TPU v7x, 32 devices: a whole 2x2x4 slice. The times are simulated.
32 devices in a mesh: dp: 4 (over z), seq: 8 (over y, x, core).
Axes of the slice: x: 2, y: 2, z: 4, core: 2. Of those that a mesh axis runs over, the one named last changes fastest.
Arguments:
- tokens: bfloat16 [4, 2048, 384], P('dp', 'seq'), may hold values from -6 to 6
- lengths: int32 [4, 5], P('dp'), may hold values from 64 to 1792, as said below
- order: int32 [4, 2048], P('dp', 'seq'), may hold values from 0 to 2047, as said below
- norm_gain: float32 [384], replicated, may hold values from 0.5 to 1.5
- w_in: bfloat16 [384, 1536], replicated, may hold values from -0.3125 to 0.3125
- conv_weight: float32 [768, 4], replicated, may hold values from -3 to 3
- conv_bias: float32 [768], replicated, may hold values from -1.8 to 1.8
- w_x: bfloat16 [768, 56], replicated, may hold values from -0.21875 to 0.21875
- w_dt: bfloat16 [24, 768], replicated, may hold values from -1.25 to 1.25
- dt_bias: float32 [768], replicated, may hold values from -6 to -2
- a_log: float32 [768, 16], replicated, may hold values from -6.9 to 2.8
- d_skip: float32 [768], replicated, may hold values from 0.5 to 1.5
- w_out: bfloat16 [768, 384], replicated, may hold values from -0.21875 to 0.21875
- cotangent: bfloat16 [4, 2048, 384], P('dp', 'seq'), may hold values from -6 to 6
Outputs:
- output: bfloat16 [4, 2048, 384], P('dp', 'seq')
- input_grad: bfloat16 [4, 2048, 384], P('dp', 'seq')
- gain_grad: float32 [384], replicated
- w_in_grad: float32 [384, 1536], replicated
- conv_weight_grad: float32 [768, 4], replicated
- conv_bias_grad: float32 [768], replicated
- w_x_grad: float32 [768, 56], replicated
- w_dt_grad: float32 [24, 768], replicated
- dt_bias_grad: float32 [768], replicated
- a_log_grad: float32 [768, 16], replicated
- d_skip_grad: float32 [768], replicated
- w_out_grad: float32 [768, 384], replicated
Inputs may be any that keep to these rules, and one draw needn't show every extreme that they name: `lengths`: each group is two objects, one scene and two objects, in that order; each object holds 64 to 127 tokens and the scene the rest of 2048; in the first group every object holds exactly 64. `order`: in each group a permutation of its places that maps the places of every cloud onto themselves.
All inputs are finite; a program needn't handle non-finite values.
Results may differ from a plain program's by a relative error of at most 0.0089.
Values may be sent and summed in bfloat16 or wider, within the bound.
No kernel may reach another device: no remote copies, remote signals or barrier semaphores. Data moves between devices by JAX's collectives and lax.ppermute only.
A program may use at most 256 MiB of HBM per device.

v0:
```python
import functools

import jax
import jax.numpy as jnp
from jax import lax
from jax.experimental import pallas as pl
from jax.experimental.pallas import tpu as pltpu
from jax.sharding import PartitionSpec as P

EPSILON = 1e-05
LOG2E = 1.4426950408889634
FAR = 1e30
CHUNKS = 8
LANES = 128
BLOCK = 16
ORDER_ROWS = 16
F32, BF16 = jnp.float32, jnp.bfloat16
VMEM_BYTES = 60 * 1024 * 1024


def dot(a, b, contract=((1,), (0,))):
    return lax.dot_general(a, b, (contract, ((), ())), preferred_element_type=F32)


def wide(tile, width):
    return jnp.concatenate([tile] * (width // LANES), axis=1)


def sigmoid(v):
    return 1.0 / (1.0 + jnp.exp(-v))


def places(first, rows, r0, steps):
    r = r0 + lax.broadcasted_iota(jnp.int32, (rows, LANES), 0)
    return first + lax.rem(r, CHUNKS) * steps + lax.div(r, CHUNKS)


def cloud_start(meta, clouds, place):
    start = jnp.zeros_like(place)
    for k in range(clouds):
        begin = meta[1 + k]
        start = jnp.maximum(start, jnp.where(begin <= place, begin, 0))
    return start


def fill_valid(valid, meta, clouds, rows, lags):
    steps = rows // CHUNKS

    def body(j, carry):
        r0 = pl.multiple_of(j * BLOCK, BLOCK)
        place = places(meta[0], BLOCK, r0, steps)
        begin = cloud_start(meta, clouds, place)
        for k in range(1, lags + 1):
            valid[k - 1, pl.ds(r0, BLOCK), :] = (place - k >= begin).astype(F32)
        return carry

    lax.fori_loop(0, rows // BLOCK, body, 0)


def own_column(order8, rows):
    steps = rows // CHUNKS
    both = order8[...]
    return jnp.concatenate([both[:, i : i + 1] for i in range(steps)], axis=0)


def gather_rows(column, pieces, src, rows):
    total = None
    lane = lax.broadcasted_iota(jnp.int32, (column.shape[0], rows), 1)
    for p, piece in enumerate(pieces):
        mine = (column - src[p] * rows == lane).astype(F32).astype(BF16)
        part = dot(mine, piece)
        total = part if total is None else total + part
    return total


def fill_broadcast(out, xproj, first, count, rows):
    def body(j, carry):
        r0 = pl.multiple_of(j * BLOCK, BLOCK)
        block = xproj[pl.ds(r0, BLOCK), :]
        for n in range(count):
            out[pl.ds(r0, BLOCK), n * LANES : (n + 1) * LANES] = jnp.broadcast_to(
                block[:, first + n : first + n + 1], (BLOCK, LANES)
            )
        return carry

    lax.fori_loop(0, rows // BLOCK, body, 0)


def rates(alog):
    return -jnp.exp(alog[...])


def chunk_of(ref, c, count):
    return jnp.concatenate([ref[b, pl.ds(c, count, stride=CHUNKS), :] for b in range(ref.shape[0])], axis=1)


def set_chunk(ref, c, value):
    for b in range(ref.shape[0]):
        ref[b, pl.ds(c, value.shape[0], stride=CHUNKS), :] = value[:, b * LANES : (b + 1) * LANES]


def pre_kernel(
    sizes, n_pieces, meta, src, order8, *refs
):
    rows, width, inner, rank, state, lags, clouds = sizes
    steps = rows // CHUNKS
    pieces = refs[:n_pieces]
    (gain, w_in, conv_w, conv_b, w_x, w_dt, dt_b, alog) = refs[n_pieces : n_pieces + 8]
    (trans_o, normed_o, gate_o, ext_o, conv_o, act_o, step_o, xproj_o, chunkf_o, sums_o, f_o, orders_o) = refs[
        n_pieces + 8 : n_pieces + 20
    ]
    conv_in, valid, far, use, bbc, a2 = refs[n_pieces + 20 :]
    me = lax.div(meta[0], rows)
    halo = jnp.full((1, 1), -1.0, F32)
    halos = [halo] * (lags + 1)
    for p in range(n_pieces):
        tail = pieces[p][rows : rows + ORDER_ROWS, :rows].astype(F32)
        row = tail[0:1] * 128.0 + tail[1:2]
        orders_o[p : p + 1, :] = row
        behind = src[p] == me - 1
        for k in range(1, lags + 1):
            r = (steps - k) * CHUNKS + CHUNKS - 1
            halos[k] = jnp.where(behind, row[:, r : r + 1], halos[k])
    sub = lax.broadcasted_iota(jnp.int32, (BLOCK, 1), 0)
    extra = jnp.full((BLOCK, 1), -1.0, F32)
    for k in range(1, lags + 1):
        extra = jnp.where(sub == k, halos[k], extra)
    column = jnp.concatenate([own_column(order8, rows), extra.astype(jnp.int32)], axis=0)
    trans = gather_rows(column, [p[0:rows, :] for p in pieces], src, rows)
    trans_o[...] = trans[:rows].astype(BF16)
    inv_rms = lax.rsqrt(jnp.mean(trans * trans, axis=1, keepdims=True) + EPSILON)
    normed = (trans * inv_rms * gain[...]).astype(BF16)
    normed_o[...] = normed[:rows]
    conv_in[...] = dot(normed, w_in[:, :inner]).astype(BF16).astype(F32)
    gate_o[...] = dot(normed[:rows], w_in[:, inner:])
    pad = lags * CHUNKS
    ext_o[pad : pad + rows, :] = conv_in[:rows, :]
    first_sub = lax.broadcasted_iota(jnp.int32, (CHUNKS, inner), 0) == 0
    for k in range(1, lags + 1):
        tile = conv_in[(steps - k) * CHUNKS : (steps - k + 1) * CHUNKS, :]
        before = conv_in[rows + k : rows + k + 1, :]
        ext_o[(lags - k) * CHUNKS : (lags - k + 1) * CHUNKS, :] = jnp.where(
            first_sub, before, pltpu.roll(tile, 1, 0)
        )
    fill_valid(valid, meta, clouds, rows, lags)

    def conv_body(j, carry):
        r0 = pl.multiple_of(j * BLOCK, BLOCK)
        out = conv_b[...] + conv_w[lags : lags + 1, :] * ext_o[pl.ds(r0 + pad, BLOCK), :]
        for k in range(1, lags + 1):
            ok = wide(valid[k - 1, pl.ds(r0, BLOCK), :], inner)
            shifted = ext_o[pl.ds(pl.multiple_of(r0 + pad - k * CHUNKS, CHUNKS), BLOCK), :]
            out = out + conv_w[lags - k : lags - k + 1, :] * shifted * ok
        conv_o[pl.ds(r0, BLOCK), :] = out
        act_o[pl.ds(r0, BLOCK), :] = (out * sigmoid(out)).astype(BF16)
        return carry

    lax.fori_loop(0, rows // BLOCK, conv_body, 0)
    xproj = dot(act_o[...], w_x[...])
    xproj_o[...] = xproj
    step_o[...] = dot(xproj.astype(BF16), w_dt[...])

    def step_body(j, carry):
        r0 = pl.multiple_of(j * BLOCK, BLOCK)
        pre = step_o[pl.ds(r0, BLOCK), :] + dt_b[...]
        step = jnp.maximum(pre, 0.0) + jnp.log1p(jnp.exp(-jnp.abs(pre)))
        step_o[pl.ds(r0, BLOCK), :] = step
        keep = wide(valid[0, pl.ds(r0, BLOCK), :], inner)
        distance = jnp.where(keep > 0.5, step, FAR)
        far[pl.ds(r0, BLOCK), :] = distance
        use[pl.ds(r0, BLOCK), :] = step * act_o[pl.ds(r0, BLOCK), :].astype(F32)
        return carry + distance[:CHUNKS] + distance[CHUNKS:]

    sums_o[...] = lax.fori_loop(0, rows // BLOCK, step_body, jnp.zeros((CHUNKS, inner), F32))
    fill_broadcast(bbc, xproj_o, rank, state, rows)
    a2[...] = rates(alog) * LOG2E
    for lb in range(inner // LANES):
        ls = slice(lb * LANES, (lb + 1) * LANES)
        rate = [jnp.broadcast_to(a2[n : n + 1, ls], (CHUNKS, LANES)) for n in range(state)]

        def scan_body(i, states):
            r = pl.ds(pl.multiple_of(i * CHUNKS, CHUNKS), CHUNKS)
            distance, u = far[r, ls], use[r, ls]
            return tuple(
                jnp.exp2(distance * rate[n]) * states[n] + u * bbc[r, n * LANES : (n + 1) * LANES]
                for n in range(state)
            )

        zero = jnp.zeros((CHUNKS, LANES), F32)
        last = lax.fori_loop(0, steps, scan_body, (zero,) * state, unroll=2)
        for n in range(state):
            chunkf_o[lb, n * CHUNKS : (n + 1) * CHUNKS, :] = last[n]
    total = jnp.zeros((state, inner), F32)
    for c in range(CHUNKS):
        total = jnp.exp2(a2[...] * sums_o[c : c + 1, :]) * total + chunk_of(chunkf_o, c, state)
    f_o[...] = total


def back_kernel(sizes, n_pieces, meta, src, order8, *refs):
    rows, width, inner, rank, state, lags, clouds = sizes
    steps = rows // CHUNKS
    pieces = refs[:n_pieces]
    gate, step, xproj, alog, w_out, sums, f = refs[n_pieces : n_pieces + 7]
    dy_o, gg_o, chunkb_o, carry_o = refs[n_pieces + 7 : n_pieces + 11]
    valid, far, gm, cbc, a2 = refs[n_pieces + 11 :]
    trans_dy = gather_rows(own_column(order8, rows), [p[...] for p in pieces], src, rows).astype(BF16)
    dy_o[...] = trans_dy
    gg_o[...] = dot(trans_dy, w_out[...], ((1,), (1,)))
    fill_valid(valid, meta, clouds, rows, 1)

    def body(j, carry):
        r = pl.ds(pl.multiple_of(j * BLOCK, BLOCK), BLOCK)
        z = gate[r, :]
        gm[r, :] = gg_o[r, :] * (z * sigmoid(z))
        far[r, :] = jnp.where(wide(valid[0, r, :], inner) > 0.5, step[r, :], FAR)
        return carry

    lax.fori_loop(0, rows // BLOCK, body, 0)
    fill_broadcast(cbc, xproj, rank + state, state, rows)
    a2[...] = rates(alog) * LOG2E
    for lb in range(inner // LANES):
        ls = slice(lb * LANES, (lb + 1) * LANES)
        rate = [jnp.broadcast_to(a2[n : n + 1, ls], (CHUNKS, LANES)) for n in range(state)]

        def scan_body(k, flows):
            r = pl.ds(pl.multiple_of((steps - 1 - k) * CHUNKS, CHUNKS), CHUNKS)
            distance, g = far[r, ls], gm[r, ls]
            return tuple(
                jnp.exp2(distance * rate[n]) * (flows[n] + g * cbc[r, n * LANES : (n + 1) * LANES])
                for n in range(state)
            )

        zero = jnp.zeros((CHUNKS, LANES), F32)
        last = lax.fori_loop(0, steps, scan_body, (zero,) * state, unroll=2)
        for n in range(state):
            chunkb_o[lb, n * CHUNKS : (n + 1) * CHUNKS, :] = last[n]
    total = jnp.zeros((state, inner), F32)
    for c in reversed(range(CHUNKS)):
        total = jnp.exp2(a2[...] * sums[c : c + 1, :]) * total + chunk_of(chunkb_o, c, state)
    carry_o[:state, :] = f[...]
    carry_o[state : 2 * state, :] = total
    carry_o[2 * state :, :] = jnp.broadcast_to(
        jnp.sum(sums[...], axis=0, keepdims=True), (CHUNKS, inner)
    )


def main_kernel(sizes, n_pieces, meta, src, *refs):
    rows, width, inner, rank, state, lags, clouds = sizes
    steps = rows // CHUNKS
    carries = refs[:n_pieces]
    (trans_dy, gg, gate, ext, conv, act, step, xproj, chunkf, chunkb, sums, alog, skip, w_out, w_x, w_dt, conv_w) = refs[
        n_pieces : n_pieces + 17
    ]
    (branch_o, gz_o, gci_o, rim_o, wout_o, wx_o, wdt_o, small_o, galog_o) = refs[n_pieces + 17 : n_pieces + 26]
    (valid, far, use, gm, bbc, cbc, a2, states, decays, mixed, gs, lamb, gb, gc, sstart, gstart, gated, held) = refs[
        n_pieces + 26 :
    ]
    me = lax.div(meta[0], rows)
    devices = n_pieces
    a2[...] = rates(alog) * LOG2E
    state_in = jnp.zeros((state, inner), F32)
    flow_in = jnp.zeros((state, inner), F32)
    size = 2 * state + CHUNKS
    for p in range(devices):
        held[pl.ds(pl.multiple_of(src[p] * size, CHUNKS), size), :] = carries[p][...]

    def ahead(s, flow):
        base = pl.multiple_of(s * size, CHUNKS)
        p_s = jnp.exp2(a2[...] * held[pl.ds(base + 2 * state, 1), :])
        return jnp.where(s < me, p_s * flow + held[pl.ds(base, state), :], flow)

    state_in = lax.fori_loop(0, devices, ahead, state_in)

    def behind(k, flow):
        s = devices - 1 - k
        base = pl.multiple_of(s * size, CHUNKS)
        p_s = jnp.exp2(a2[...] * held[pl.ds(base + 2 * state, 1), :])
        return jnp.where(s > me, p_s * flow + held[pl.ds(pl.multiple_of(base + state, CHUNKS), state), :], flow)

    flow_in = lax.fori_loop(0, devices, behind, flow_in)
    now = state_in
    for c in range(CHUNKS):
        set_chunk(sstart, c, now)
        now = jnp.exp2(a2[...] * sums[c : c + 1, :]) * now + chunk_of(chunkf, c, state)
    now = flow_in
    for c in reversed(range(CHUNKS)):
        set_chunk(gstart, c, now)
        now = jnp.exp2(a2[...] * sums[c : c + 1, :]) * now + chunk_of(chunkb, c, state)
    fill_valid(valid, meta, clouds, rows, lags)

    def prepare(j, carry):
        r = pl.ds(pl.multiple_of(j * BLOCK, BLOCK), BLOCK)
        z = gate[r, :]
        gm[r, :] = gg[r, :] * (z * sigmoid(z))
        far[r, :] = jnp.where(wide(valid[0, r, :], inner) > 0.5, step[r, :], FAR)
        use[r, :] = step[r, :] * act[r, :].astype(F32)
        return carry

    lax.fori_loop(0, rows // BLOCK, prepare, 0)
    fill_broadcast(bbc, xproj, rank, state, rows)
    fill_broadcast(cbc, xproj, rank + state, state, rows)
    for lb in range(inner // LANES):
        ls = slice(lb * LANES, (lb + 1) * LANES)
        rate = [jnp.broadcast_to(a2[n : n + 1, ls], (CHUNKS, LANES)) for n in range(state)]
        begin = []
        for n in range(state):
            tile = sstart[lb, n * CHUNKS : (n + 1) * CHUNKS, :]
            states[n, 0:CHUNKS, ls] = tile
            begin.append(tile)

        def forward(i, now):
            r0 = pl.multiple_of(i * CHUNKS, CHUNKS)
            r = pl.ds(r0, CHUNKS)
            after = pl.ds(pl.multiple_of(r0 + CHUNKS, CHUNKS), CHUNKS)
            distance, u = far[r, ls], use[r, ls]
            new, out = [], None
            for n in range(state):
                decay = jnp.exp2(distance * rate[n])
                value = decay * now[n] + u * bbc[r, n * LANES : (n + 1) * LANES]
                decays[n, r, ls] = decay
                states[n, after, ls] = value
                part = value * cbc[r, n * LANES : (n + 1) * LANES]
                out = part if out is None else out + part
                new.append(value)
            mixed[r, ls] = out
            return tuple(new)

        lax.fori_loop(0, steps, forward, tuple(begin), unroll=2)

    def gating(j, carry):
        r = pl.ds(pl.multiple_of(j * BLOCK, BLOCK), BLOCK)
        z, a = gate[r, :], act[r, :].astype(F32)
        s = sigmoid(z)
        m = mixed[r, :] + skip[...] * a
        gated[r, :] = (m * (z * s)).astype(BF16)
        gz_o[r, :] = (gg[r, :] * m * s * (1.0 + z * (1.0 - s))).astype(BF16)
        part = gm[r, :] * a
        return carry + part[:CHUNKS] + part[CHUNKS:]

    skip_sum = lax.fori_loop(0, rows // BLOCK, gating, jnp.zeros((CHUNKS, inner), F32))
    branch_o[...] = dot(gated[...], w_out[...]).astype(BF16)
    wout_o[...] = dot(gated[...], trans_dy[...], ((0,), (0,)))
    group = 3
    pair = 4
    for lg in range(inner // LANES // group):
        lanes = [slice((lg * group + k) * LANES, (lg * group + k + 1) * LANES) for k in range(group)]
        for ng in range(state // pair):
            ns = [ng * pair + k for k in range(pair)]
            rate = [[jnp.broadcast_to(a2[n : n + 1, ls] * (1.0 / LOG2E), (CHUNKS, LANES)) for ls in lanes] for n in ns]
            begin = [gstart[lg * group + k, n * CHUNKS : (n + 1) * CHUNKS, :] for n in ns for k in range(group)]
            zero = jnp.zeros((CHUNKS, LANES), F32)

            def backward(k, carry):
                flows, sums_a = carry
                r0 = pl.multiple_of((steps - 1 - k) * CHUNKS, CHUNKS)
                r = pl.ds(r0, CHUNKS)
                after = pl.ds(pl.multiple_of(r0 + CHUNKS, CHUNKS), CHUNKS)
                gs_t = [None] * group
                lamb_t = [None] * group
                g_t = [gm[r, ls] for ls in lanes]
                u_t = [use[r, ls] for ls in lanes]
                d_t = [step[r, ls] for ls in lanes]
                new_flows, new_sums = [], []
                for q, n in enumerate(ns):
                    b = bbc[r, n * LANES : (n + 1) * LANES]
                    c = cbc[r, n * LANES : (n + 1) * LANES]
                    gb_t = gc_t = None
                    for x, ls in enumerate(lanes):
                        lam = g_t[x] * c + flows[q * group + x]
                        flow = decays[n, r, ls] * lam
                        part = flow * states[n, r, ls]
                        one, two = part * rate[q][x], lam * b
                        gs_t[x] = one if gs_t[x] is None else gs_t[x] + one
                        lamb_t[x] = two if lamb_t[x] is None else lamb_t[x] + two
                        three, four = lam * u_t[x], g_t[x] * states[n, after, ls]
                        gb_t = three if gb_t is None else gb_t + three
                        gc_t = four if gc_t is None else gc_t + four
                        new_flows.append(flow)
                        new_sums.append(sums_a[q * group + x] + part * d_t[x])
                    nl = slice(n * LANES, (n + 1) * LANES)
                    if lg == 0:
                        gb[r, nl] = gb_t
                        gc[r, nl] = gc_t
                    else:
                        gb[r, nl] += gb_t
                        gc[r, nl] += gc_t
                for x, ls in enumerate(lanes):
                    if ng == 0:
                        gs[r, ls] = gs_t[x]
                        lamb[r, ls] = lamb_t[x]
                    else:
                        gs[r, ls] += gs_t[x]
                        lamb[r, ls] += lamb_t[x]
                return tuple(new_flows), tuple(new_sums)

            flows, sums_a = lax.fori_loop(
                0, steps, backward, (tuple(begin), (zero,) * (pair * group))
            )
            for q, n in enumerate(ns):
                for x, ls in enumerate(lanes):
                    galog_o[n : n + 1, ls] = (
                        jnp.sum(sums_a[q * group + x], axis=0, keepdims=True) * rate[q][x][0:1]
                    )
    col = lax.broadcasted_iota(jnp.int32, (state * LANES, LANES), 1)
    row = lax.div(lax.broadcasted_iota(jnp.int32, (state * LANES, LANES), 0), LANES)
    pick_b = (col == row + rank).astype(F32).astype(BF16)
    pick_c = (col == row + rank + state).astype(F32).astype(BF16)

    def lane_sums(ref, pick):
        whole = ref[...]
        high = whole.astype(BF16)
        low = (whole - high.astype(F32)).astype(BF16)
        return dot(high, pick) + dot(low, pick)

    grad_bc = lane_sums(gb, pick_b) + lane_sums(gc, pick_c)
    gpre = gated

    def pre_body(j, carry):
        r = pl.ds(pl.multiple_of(j * BLOCK, BLOCK), BLOCK)
        grad_step = gs[r, :] + lamb[r, :] * act[r, :].astype(F32)
        grad_pre = (grad_step * (1.0 - jnp.exp(-step[r, :]))).astype(BF16)
        gpre[r, :] = grad_pre
        part = grad_pre.astype(F32)
        return carry + part[:CHUNKS] + part[CHUNKS:]

    dt_sum = lax.fori_loop(0, rows // BLOCK, pre_body, jnp.zeros((CHUNKS, inner), F32))
    dt_low = xproj[...].astype(BF16)
    wdt_o[...] = dot(dt_low, gpre[...], ((0,), (0,)))
    grad_xproj = (dot(gpre[...], w_dt[...], ((1,), (1,))) + grad_bc).astype(BF16)
    wx_o[...] = dot(grad_xproj, act[...], ((0,), (0,)))
    gs[...] = dot(grad_xproj, w_x[...], ((1,), (1,)))
    gconv = mixed

    def conv_body(j, carry):
        r0 = pl.multiple_of(j * BLOCK, BLOCK)
        r = pl.ds(r0, BLOCK)
        grad_act = gm[r, :] * skip[...] + lamb[r, :] * step[r, :] + gs[r, :]
        v = conv[r, :]
        s = sigmoid(v)
        grad = grad_act * (s * (1.0 + v * (1.0 - s)))
        gconv[r, :] = grad
        new = [carry[0] + grad[:CHUNKS] + grad[CHUNKS:]]
        for k in range(lags + 1):
            masked = grad if k == 0 else grad * wide(valid[k - 1, r, :], inner)
            part = masked * ext[pl.ds(pl.multiple_of(r0 + (lags - k) * CHUNKS, CHUNKS), BLOCK), :]
            new.append(carry[1 + k] + part[:CHUNKS] + part[CHUNKS:])
        return tuple(new)

    conv_sums = lax.fori_loop(
        0, rows // BLOCK, conv_body, (jnp.zeros((CHUNKS, inner), F32),) * (lags + 2)
    )
    small = [skip_sum, dt_sum, conv_sums[0]] + [conv_sums[1 + lags - t] for t in range(lags + 1)]
    for k, part in enumerate(small):
        small_o[k : k + 1, :] = jnp.sum(part, axis=0, keepdims=True)
    small_o[len(small) :, :] = jnp.zeros((small_o.shape[0] - len(small), inner), F32)

    def masked_tile(i, k):
        r = pl.ds(pl.multiple_of(i * CHUNKS, CHUNKS), CHUNKS)
        tile = gconv[r, :] * conv_w[lags - k : lags - k + 1, :]
        return tile if k == 0 else tile * wide(valid[k - 1, r, :], inner)

    def spread(i, carry):
        total = masked_tile(i, 0)
        for k in range(1, lags + 1):
            total = total + masked_tile(i + k, k)
        gci_o[pl.ds(pl.multiple_of(i * CHUNKS, CHUNKS), CHUNKS), :] = total
        return carry

    lax.fori_loop(0, steps - lags, spread, 0)
    sub = lax.broadcasted_iota(jnp.int32, (CHUNKS, inner), 0)
    for i in range(steps - lags, steps):
        total = masked_tile(i, 0)
        for k in range(1, lags + 1):
            if i + k < steps:
                total = total + masked_tile(i + k, k)
            else:
                moved = pltpu.roll(masked_tile(i + k - steps, k), CHUNKS - 1, 0)
                total = total + jnp.where(sub == CHUNKS - 1, 0.0, moved)
        gci_o[i * CHUNKS : (i + 1) * CHUNKS, :] = total
    rim_o[...] = jnp.zeros((CHUNKS, inner), F32)
    for b in range(1, lags + 1):
        total = jnp.zeros((1, inner), F32)
        for k in range(b, lags + 1):
            total = total + masked_tile(k - b, k)[0:1]
        rim_o[b : b + 1, :] = total


def final_kernel(sizes, trans, normed, gci, gz, rim, gain, w_in, back_o, win_o, gain_o):
    rows, width, inner, rank, state, lags, clouds = sizes
    steps = rows // CHUNKS
    r = lax.broadcasted_iota(jnp.int32, (rows, inner), 0)
    total = gci[...]
    for k in range(1, lags + 1):
        total = total + jnp.where(r == (steps - k) * CHUNKS + CHUNKS - 1, rim[k : k + 1, :], 0.0)
    grad_ci = total.astype(BF16)
    grad_z = gz[...]
    win_o[:, :inner] = dot(normed[...], grad_ci, ((0,), (0,)))
    win_o[:, inner:] = dot(normed[...], grad_z, ((0,), (0,)))
    grad_normed = dot(grad_ci, w_in[:, :inner], ((1,), (1,))) + dot(grad_z, w_in[:, inner:], ((1,), (1,)))
    x = trans[...].astype(F32)
    inv_rms = lax.rsqrt(jnp.mean(x * x, axis=1, keepdims=True) + EPSILON)
    gain_o[...] = jnp.sum(grad_normed * x * inv_rms, axis=0, keepdims=True)
    scaled = grad_normed * gain[...]
    back_o[...] = (
        inv_rms * scaled
        - inv_rms * inv_rms * inv_rms * x * jnp.mean(scaled * x, axis=1, keepdims=True)
    ).astype(BF16)


def place_kernel(rows, n_pieces, meta, here, orders, *refs):
    pieces, out = refs[:n_pieces], refs[n_pieces]
    place = meta[0] + lax.broadcasted_iota(jnp.int32, (rows, rows), 0)
    total = here[...].astype(F32)
    for p in range(n_pieces):
        mine = (orders[p : p + 1, :].astype(jnp.int32) == place).astype(F32).astype(BF16)
        total = total + dot(mine, pieces[p][...])
    out[...] = total.astype(BF16)


def call(kernel, outs, scratch, n_smem, name):
    vmem = pl.BlockSpec(memory_space=pltpu.VMEM)
    smem = pl.BlockSpec(memory_space=pltpu.SMEM)

    def run(*args):
        return pl.pallas_call(
            kernel,
            out_shape=[jax.ShapeDtypeStruct(s, t) for s, t in outs],
            in_specs=[smem] * n_smem + [vmem] * (len(args) - n_smem),
            out_specs=[vmem] * len(outs),
            scratch_shapes=[pltpu.VMEM(s, t) for s, t in scratch],
            compiler_params=pltpu.CompilerParams(vmem_limit_bytes=VMEM_BYTES),
            name=name,
        )(*args)

    return run


def swap(block, axis, distance):
    devices = lax.axis_size(axis)
    return lax.ppermute(block, axis, [(i, i ^ distance) for i in range(devices)])


def spread_pieces(block, axis):
    devices, index = lax.axis_size(axis), lax.axis_index(axis)
    if devices == 8:
        across = [block] + [swap(block, axis, d) for d in (2, 4, 6)]
        pieces = across + [swap(part, axis, 1) for part in across]
        return pieces, [index ^ d for d in (0, 2, 4, 6, 1, 3, 5, 7)]
    whole = lax.all_gather(block, axis)
    return [whole[i] for i in range(devices)], [jnp.int32(i) for i in range(devices)]


def from_behind(block, axis, distance):
    devices = range(lax.axis_size(axis))
    route = [(i - distance, i) for i in devices if i - distance in devices]
    return lax.ppermute(block, axis, route)


def shards(
    tokens,
    lengths,
    order,
    norm_gain,
    w_in,
    conv_weight,
    conv_bias,
    w_x,
    w_dt,
    dt_bias,
    a_log,
    d_skip,
    w_out,
    cotangent,
):
    rows, width = tokens.shape[1:]
    inner, rank, state, taps = w_out.shape[0], w_dt.shape[0], a_log.shape[1], conv_weight.shape[1]
    lags, clouds, steps = taps - 1, lengths.shape[1], rows // CHUNKS
    sizes = (rows, width, inner, rank, state, lags, clouds)
    devices, me = lax.axis_size("seq"), lax.axis_index("seq")
    here_x, here_dy = tokens[0], cotangent[0]
    order8 = order.reshape(CHUNKS, steps)
    order_row = order8.T.reshape(1, rows)
    order_rows = jnp.concatenate([order_row // 128, order_row % 128], axis=0).astype(BF16)
    order_rows = jnp.pad(order_rows, ((0, ORDER_ROWS - 2), (0, width - rows)))
    pieces_x, sources = spread_pieces(jnp.concatenate([here_x, order_rows], axis=0), "seq")
    pieces_dy, _ = spread_pieces(here_dy, "seq")
    n = len(pieces_x)
    src = jnp.stack(sources).astype(jnp.int32)
    starts = jnp.cumsum(lengths[0]) - lengths[0]
    meta = jnp.concatenate([(me * rows)[None], starts]).astype(jnp.int32)
    alog_t = a_log.T
    conv_w = conv_weight.T
    w_x_pad = jnp.pad(w_x, ((0, 0), (0, LANES - w_x.shape[1])))
    w_dt_pad = jnp.pad(w_dt, ((0, LANES - rank), (0, 0)))
    row = lambda v: v[None, :]
    big, lane = (rows, inner), (rows, LANES)
    carried = (inner // LANES, state * CHUNKS, LANES)
    spread = (rows, state * LANES)
    ext_rows = rows + lags * CHUNKS
    (trans, normed, gate, ext, conv, act, step, xproj, chunkf, sums, f, orders) = call(
        functools.partial(pre_kernel, sizes, n),
        [
            ((rows, width), BF16),
            ((rows, width), BF16),
            (big, F32),
            ((ext_rows, inner), F32),
            (big, F32),
            (big, BF16),
            (big, F32),
            (lane, F32),
            (carried, F32),
            ((CHUNKS, inner), F32),
            ((state, inner), F32),
            ((n, rows), F32),
        ],
        [
            ((rows + BLOCK, inner), F32),
            ((lags, rows, LANES), F32),
            (big, F32),
            (big, F32),
            (spread, F32),
            ((state, inner), F32),
        ],
        2,
        "forward_local",
    )(meta, src, order8, *pieces_x, row(norm_gain), w_in, conv_w, row(conv_bias), w_x_pad, w_dt_pad, row(dt_bias), alog_t)
    trans_dy, gg, chunkb, carry = call(
        functools.partial(back_kernel, sizes, n),
        [
            ((rows, width), BF16),
            (big, F32),
            (carried, F32),
            ((2 * state + CHUNKS, inner), F32),
        ],
        [
            ((1, rows, LANES), F32),
            (big, F32),
            (big, F32),
            (spread, F32),
            ((state, inner), F32),
        ],
        2,
        "backward_local",
    )(meta, src, order8, *pieces_dy, gate, step, xproj, alog_t, w_out, sums, f)
    carries, _ = spread_pieces(carry, "seq")
    branch, gz, gci, rim, wout_g, wx_g, wdt_g, small, galog = call(
        functools.partial(main_kernel, sizes, n),
        [
            ((rows, width), BF16),
            (big, BF16),
            (big, F32),
            ((CHUNKS, inner), F32),
            ((inner, width), F32),
            ((LANES, inner), F32),
            ((LANES, inner), F32),
            ((CHUNKS, inner), F32),
            ((state, inner), F32),
        ],
        [
            ((lags, rows, LANES), F32),
            (big, F32),
            (big, F32),
            (big, F32),
            (spread, F32),
            (spread, F32),
            ((state, inner), F32),
            ((state, rows + CHUNKS, inner), F32),
            ((state, rows, inner), F32),
            (big, F32),
            (big, F32),
            (big, F32),
            (spread, F32),
            (spread, F32),
            (carried, F32),
            (carried, F32),
            (big, BF16),
            ((n * (2 * state + CHUNKS), inner), F32),
        ],
        2,
        "scan_both",
    )(
        meta, src, *carries, trans_dy, gg, gate, ext, conv, act, step, xproj, chunkf, chunkb, sums, alog_t,
        row(d_skip), w_out, w_x_pad, w_dt_pad, conv_w,
    )
    rim = from_behind(rim, "seq", -1)
    back, win_g, gain_g = call(
        functools.partial(final_kernel, sizes),
        [((rows, width), BF16), ((width, 2 * inner), F32), ((1, width), F32)],
        [],
        0,
        "input_projection_grads",
    )(trans, normed, gci, gz, rim, row(norm_gain), w_in)
    place = call(functools.partial(place_kernel, rows, n), [((rows, width), BF16)], [], 1, "to_hilbert")
    pieces_b, _ = spread_pieces(branch, "seq")
    pieces_g, _ = spread_pieces(back, "seq")
    (output,) = place(meta, here_x, orders, *pieces_b)
    (input_grad,) = place(meta, here_dy, orders, *pieces_g)
    s_gain, s_win, s_wx, s_wdt, s_small, s_alog, s_wout = lax.psum(
        (gain_g, win_g, wx_g[: w_x.shape[1]], wdt_g[:rank], small, galog, wout_g), ("dp", "seq")
    )
    return (
        output[None],
        input_grad[None],
        s_gain[0],
        s_win,
        s_small[3 : 4 + lags].T,
        s_small[2],
        s_wx.T,
        s_wdt,
        s_small[1],
        s_alog.T,
        s_small[0],
        s_wout,
    )


def solution(mesh):
    placed = (
        P("dp", "seq", None),
        P("dp", None),
        P("dp", "seq"),
        P(),
        P(),
        P(),
        P(),
        P(),
        P(),
        P(),
        P(),
        P(),
        P(),
        P("dp", "seq", None),
    )
    return jax.shard_map(
        shards,
        mesh=mesh,
        in_specs=placed,
        out_specs=(
            P("dp", "seq", None),
            P("dp", "seq", None),
            P(),
            P(),
            P(),
            P(),
            P(),
            P(),
            P(),
            P(),
            P(),
            P(),
        ),
        check_vma=False,
    )
```

profile of v0, /device:TPU:0, one launch (start us, length us, event | category | flops | bytes accessed | tf_op | source)
XLA Modules:
  0.0 411.3 jit_solution(9993459946609038850)
XLA Ops:
  10.3 4.0 collective-permute-start.2
  14.8 1.5 collective-permute-start.9
  16.4 7.4 %collective-permute-done.9.refs_3_ = bf16[256,384]{1,0:T(8,128)(2,1)S(1)} collective-permute-done((bf16[256,384]{1,0:T(8,128)(2,1)}, bf16[256,384]{1,0:T(8,128)(2,1)S(1)}, u32[]{:S(2)}, u32[]{:S(2)}) %collective-permute-start.9) | collective-permute-done | bytes 196640 | tf_op jit(solution)/shard_map/ppermute | solution.py:540
  23.8 1.7 collective-permute-start
  25.5 2.8 collective-permute-done.1.refs_2_
  28.3 4.1 %collective-permute-done.8.refs_2_ = bf16[256,384]{1,0:T(8,128)(2,1)S(1)} collective-permute-done((bf16[256,384]{1,0:T(8,128)(2,1)}, bf16[256,384]{1,0:T(8,128)(2,1)S(1)}, u32[]{:S(2)}, u32[]{:S(2)}) %collective-permute-start.8) | collective-permute-done | bytes 196640 | tf_op jit(solution)/shard_map/ppermute | solution.py:540
  32.4 1.7 collective-permute-start.7
  34.9 4.5 %collective-permute-done.7.refs_1_ = bf16[256,384]{1,0:T(8,128)(2,1)S(1)} collective-permute-done((bf16[256,384]{1,0:T(8,128)(2,1)}, bf16[256,384]{1,0:T(8,128)(2,1)S(1)}, u32[]{:S(2)}, u32[]{:S(2)}) %collective-permute-start.7) | collective-permute-done | bytes 196640 | tf_op jit(solution)/shard_map/ppermute | solution.py:540
  46.0 1.5 pad.14.refs_13_.refs_23_
  50.2 12.8 %forward_local.1 = (bf16[256,384]{1,0:T(8,128)(2,1)}, bf16[256,384]{1,0:T(8,128)(2,1)}, f32[256,768]{1,0:T(8,128)}, f32[280,768]{1,0:T(8,128)}, f32[256,768]{1,0...) custom-call(s32[6]{0:T(128)} %pad_add_fusion.meta, ...), custom_call_target="tpu_custom_call" | custom-call | tf_op jit(solution)/shard_map/forward_local/pallas_call | solution.py:525
  63.9 10.0 %backward_local.1 = (bf16[256,384]{1,0:T(8,128)(2,1)}, f32[256,768]{1,0:T(8,128)}, f32[6,128,128]{2,1,0:T(8,128)}, f32[40,768]{1,0:T(8,128)}) custom-call(s32[6]{0:T(128)} %pad_add_fusion.meta, s32[8]{0:T(128)} %stack.35.src, s32[8,32]{1,0:T(8,128)} %copy-done.41, bf16[256,384]{1,0:T(8,128)(2,1)} %bitcast.32, bf16[256,384]{1,0:T(8,128)(2,1)} %copy-done.27, ...), custom_call_target="tpu_custom_call" | custom-call | tf_op jit(solution)/shard_map/backward_local/pallas_call | solution.py:525
  73.9 1.5 collective-permute-start.16
  75.3 1.7 collective-permute-start.15
  77.4 3.8 collective-permute-done.16.refs_3_
  81.2 2.1 collective-permute-done.15.refs_2_
  85.6 27.8 %scan_both.1 = (bf16[256,384]{1,0:T(8,128)(2,1)}, bf16[256,768]{1,0:T(8,128)(2,1)}, f32[256,768]{1,0:T(8,128)}, f32[8,768]{1,0:T(8,128)}, f32[768,384]{1,0:T(8,1...) custom-call(s32[6]{0:T(128)} %pad_add_fusion.meta, s32[8]{0:T(128)} %stack.35.src, ...), custom_call_target="tpu_custom_call" | custom-call | tf_op jit(solution)/shard_map/scan_both/pallas_call | solution.py:525
  114.7 2.0 collective-permute-done.28.rim
  117.3 3.8 input_projection_grads.1
  122.7 1.6 slice_bitcast_fusion
  124.3 1.5 slice.21
  126.7 2.3 collective-permute-start.24
  130.0 3.0 collective-permute-start.22
  133.0 1.5 collective-permute-start.31
  134.5 2.0 collective-permute-start.30
  137.8 2.5 collective-permute-start.29
  140.3 1.8 collective-permute-done.22.refs_2_
  142.7 104.5 %all-reduce.8.cloned.1.call-done = (f32[384]{0:T(512)}, f32[8,768]{1,0:T(8,128)}, f32[768,16]{0,1:T(8,128)}) async-done(((f32[384]{0:T(512)}, f32[8,768]{1,0:T(8,128)}, f32[768,16]{0,1:T(8,128)}), (f32[384]{0:T(512)}, f32[8,768]{1,0:T(8,128)}, f32[768,16]{0,1:T(8,128)})) %all-reduce.8.cloned.1.call-update) | async-done | bytes 75280 | tf_op jit(solution)/shard_map/psum | solution.py:698
  247.2 1.5 slice_reduce_fusion
  252.5 2.9 to_hilbert.2
  257.0 2.9 to_hilbert.3
  259.9 137.6 %all-reduce.10.cloned.1.call-done = (f32[384,1536]{1,0:T(8,128)}, f32[768,56]{0,1:T(8,128)}, f32[24,768]{1,0:T(8,128)}, f32[768,384]{1,0:T(8,128)}) async-done(((f32[384,1536]{1,0:T(8,128)}, f32[768,56]{0,1:T(8,128)}, f32[24,768]{1,0:T(8,128)}, f32[768,384]{1,0:T(8,128)}), (f32[384,1536]{1,0:T(8,128)}, f32[768,56]{0,1:T(8,128)}, f32[24,768]{1,0:T(8,128)}, ...) | async-done | bytes 3784720 | tf_op jit(solution)/shard_map/psum | solution.py:698
  398.1 3.3 copy.38
  (175 shorter events, 33.3 us)
Async XLA Ops:
  7.2 240.0 %all-reduce.8.cloned.1.call-start = ((), (), s32[]{:S(2)}) async-start(), calls=%async_computation | async-start | bytes 151552 | tf_op jit(solution)/shard_map/psum | solution.py:698
  10.3 15.1 %collective-permute-start.2 = (bf16[272,384]{1,0:T(8,128)(2,1)S(1)}, bf16[272,384]{1,0:T(8,128)(2,1)S(1)}, u32[]{:S(2)}, u32[]{:S(2)}) collective-permute-start(bf16[272,384]{1,0:T(8,128)(2,1)S(1)} %pad_maximum_fusion.refs_0_), channel_id=1, source_target_pairs={{0,6},{1,7},{2,4},{3,5},{4,2},{5,3},{6,0},{7,1},{8,14},{9,15},{10,... | collective-permute-start | bytes 626696 | tf_op jit(solution)/shard_map/ppermute | solution.py:540
  14.3 13.9 %collective-permute-start.1 = (bf16[272,384]{1,0:T(8,128)(2,1)S(1)}, bf16[272,384]{1,0:T(8,128)(2,1)S(1)}, u32[]{:S(2)}, u32[]{:S(2)}) collective-permute-start(bf16[272,384]{1,0:T(8,128)(2,1)S(1)} %pad_maximum_fusion.refs_0_), channel_id=1, source_target_pairs={{0,4},{1,5},{2,6},{3,7},{4,0},{5,1},{6,2},{7,3},{8,12},{9,13},{10,... | collective-permute-start | bytes 626696 | tf_op jit(solution)/shard_map/ppermute | solution.py:540
  14.8 9.0 %collective-permute-start.9 = (bf16[256,384]{1,0:T(8,128)(2,1)}, bf16[256,384]{1,0:T(8,128)(2,1)S(1)}, u32[]{:S(2)}, u32[]{:S(2)}) collective-permute-start(bf16[256,384]{1,0:T(8,128)(2,1)} %bitcast.28), channel_id=1, source_target_pairs={{0,6},{1,7},{2,4},{3,5},{4,2},{5,3},{6,0},{7,1},{8,14},{9,15},{10,... | collective-permute-start | bytes 589832 | tf_op jit(solution)/shard_map/ppermute | solution.py:540
  16.3 16.1 %collective-permute-start.8 = (bf16[256,384]{1,0:T(8,128)(2,1)}, bf16[256,384]{1,0:T(8,128)(2,1)S(1)}, u32[]{:S(2)}, u32[]{:S(2)}) collective-permute-start(bf16[256,384]{1,0:T(8,128)(2,1)} %bitcast.29), channel_id=1, source_target_pairs={{0,4},{1,5},{2,6},{3,7},{4,0},{5,1},{6,2},{7,3},{8,12},{9,13},{10,... | collective-permute-start | bytes 589832 | tf_op jit(solution)/shard_map/ppermute | solution.py:540
  16.4 23.0 %collective-permute-start.3 = (bf16[272,384]{1,0:T(8,128)(2,1)S(1)}, bf16[272,384]{1,0:T(8,128)(2,1)S(1)}, u32[]{:S(2)}, u32[]{:S(2)}) collective-permute-start(bf16[272,384]{1,0:T(8,128)(2,1)S(1)} %pad_maximum_fusion.refs_0_), channel_id=1, source_target_pairs={{0,1},{1,0},{2,3},{3,2},{4,5},{5,4},{6,7},{7,6},{8,9},{9,8},{10,11... | collective-permute-start | bytes 626696 | tf_op jit(solution)/shard_map/ppermute | solution.py:540
  23.8 16.1 %collective-permute-start = (bf16[272,384]{1,0:T(8,128)(2,1)S(1)}, bf16[272,384]{1,0:T(8,128)(2,1)S(1)}, u32[]{:S(2)}, u32[]{:S(2)}) collective-permute-start(bf16[272,384]{1,0:T(8,128)(2,1)S(1)} %pad_maximum_fusion.refs_0_), channel_id=1, source_target_pairs={{0,2},{1,3},{2,0},{3,1},{4,6},{5,7},{6,4},{7,5},{8,10},{9,11},{10,... | collective-permute-start | bytes 626696 | tf_op jit(solution)/shard_map/ppermute | solution.py:540
  25.5 14.5 %collective-permute-start.6 = (bf16[272,384]{1,0:T(8,128)(2,1)S(1)}, bf16[272,384]{1,0:T(8,128)(2,1)S(1)}, u32[]{:S(2)}, u32[]{:S(2)}) collective-permute-start(bf16[272,384]{1,0:T(8,128)(2,1)S(1)} %collective-permute-done.2.refs_3_), channel_id=1, source_target_pairs={{0,1},{1,0},{2,3},{3,2},{4,5},{5,4},{6,7},{7,6},{8,9},{9,8},{10,11... | collective-permute-start | bytes 626696 | tf_op jit(solution)/shard_map/ppermute | solution.py:540
  28.3 12.2 %collective-permute-start.5 = (bf16[272,384]{1,0:T(8,128)(2,1)S(1)}, bf16[272,384]{1,0:T(8,128)(2,1)S(1)}, u32[]{:S(2)}, u32[]{:S(2)}) collective-permute-start(bf16[272,384]{1,0:T(8,128)(2,1)S(1)} %collective-permute-done.1.refs_2_), channel_id=1, source_target_pairs={{0,1},{1,0},{2,3},{3,2},{4,5},{5,4},{6,7},{7,6},{8,9},{9,8},{10,11... | collective-permute-start | bytes 626696 | tf_op jit(solution)/shard_map/ppermute | solution.py:540
  32.4 7.0 %collective-permute-start.7 = (bf16[256,384]{1,0:T(8,128)(2,1)}, bf16[256,384]{1,0:T(8,128)(2,1)S(1)}, u32[]{:S(2)}, u32[]{:S(2)}) collective-permute-start(bf16[256,384]{1,0:T(8,128)(2,1)} %bitcast.30), channel_id=1, source_target_pairs={{0,2},{1,3},{2,0},{3,1},{4,6},{5,7},{6,4},{7,5},{8,10},{9,11},{10,... | collective-permute-start | bytes 589832 | tf_op jit(solution)/shard_map/ppermute | solution.py:540
  39.4 23.6 %collective-permute-start.10 = (bf16[256,384]{1,0:T(8,128)(2,1)}, bf16[256,384]{1,0:T(8,128)(2,1)S(1)}, u32[]{:S(2)}, u32[]{:S(2)}) collective-permute-start(bf16[256,384]{1,0:T(8,128)(2,1)} %bitcast.31), channel_id=1, source_target_pairs={{0,1},{1,0},{2,3},{3,2},{4,5},{5,4},{6,7},{7,6},{8,9},{9,8},{10,11... | collective-permute-start | bytes 589832 | tf_op jit(solution)/shard_map/ppermute | solution.py:540
  39.4 23.6 %collective-permute-start.13 = (bf16[256,384]{1,0:T(8,128)(2,1)S(1)}, bf16[256,384]{1,0:T(8,128)(2,1)S(1)}, u32[]{:S(2)}, u32[]{:S(2)}) collective-permute-start(bf16[256,384]{1,0:T(8,128)(2,1)S(1)} %collective-permute-done.9.refs_3_), channel_id=1, source_target_pairs={{0,1},{1,0},{2,3},{3,2},{4,5},{5,4},{6,7},{7,6},{8,9},{9,8},{10,11... | collective-permute-start | bytes 589832 | tf_op jit(solution)/shard_map/ppermute | solution.py:540
  39.9 23.1 %collective-permute-start.12 = (bf16[256,384]{1,0:T(8,128)(2,1)S(1)}, bf16[256,384]{1,0:T(8,128)(2,1)S(1)}, u32[]{:S(2)}, u32[]{:S(2)}) collective-permute-start(bf16[256,384]{1,0:T(8,128)(2,1)S(1)} %collective-permute-done.8.refs_2_), channel_id=1, source_target_pairs={{0,1},{1,0},{2,3},{3,2},{4,5},{5,4},{6,7},{7,6},{8,9},{9,8},{10,11... | collective-permute-start | bytes 589832 | tf_op jit(solution)/shard_map/ppermute | solution.py:540
  40.0 23.0 %collective-permute-start.11 = (bf16[256,384]{1,0:T(8,128)(2,1)S(1)}, bf16[256,384]{1,0:T(8,128)(2,1)S(1)}, u32[]{:S(2)}, u32[]{:S(2)}) collective-permute-start(bf16[256,384]{1,0:T(8,128)(2,1)S(1)} %collective-permute-done.7.refs_1_), channel_id=1, source_target_pairs={{0,1},{1,0},{2,3},{3,2},{4,5},{5,4},{6,7},{7,6},{8,9},{9,8},{10,11... | collective-permute-start | bytes 589832 | tf_op jit(solution)/shard_map/ppermute | solution.py:540
  40.5 9.1 %collective-permute-start.4 = (bf16[272,384]{1,0:T(8,128)(2,1)S(1)}, bf16[272,384]{1,0:T(8,128)(2,1)S(1)}, u32[]{:S(2)}, u32[]{:S(2)}) collective-permute-start(bf16[272,384]{1,0:T(8,128)(2,1)S(1)} %collective-permute-done.refs_1_), channel_id=1, source_target_pairs={{0,1},{1,0},{2,3},{3,2},{4,5},{5,4},{6,7},{7,6},{8,9},{9,8},{10,11... | collective-permute-start | bytes 626696 | tf_op jit(solution)/shard_map/ppermute | solution.py:540
  73.9 7.3 %collective-permute-start.16 = (f32[40,768]{1,0:T(8,128)}, f32[40,768]{1,0:T(8,128)S(1)}, u32[]{:S(2)}, u32[]{:S(2)}) collective-permute-start(f32[40,768]{1,0:T(8,128)} %get-tuple-element.46.refs_0_), channel_id=1, source_target_pairs={{0,6},{1,7},{2,4},{3,5},{4,2},{5,3},{6,0},{7,1},{8,14},{9,15},{10,... | collective-permute-start | bytes 368648 | tf_op jit(solution)/shard_map/ppermute | solution.py:540
  75.3 8.0 %collective-permute-start.15 = (f32[40,768]{1,0:T(8,128)}, f32[40,768]{1,0:T(8,128)S(1)}, u32[]{:S(2)}, u32[]{:S(2)}) collective-permute-start(f32[40,768]{1,0:T(8,128)} %get-tuple-element.46.refs_0_), channel_id=1, source_target_pairs={{0,4},{1,5},{2,6},{3,7},{4,0},{5,1},{6,2},{7,3},{8,12},{9,13},{10,... | collective-permute-start | bytes 368648 | tf_op jit(solution)/shard_map/ppermute | solution.py:540
  77.0 6.6 %collective-permute-start.14 = (f32[40,768]{1,0:T(8,128)}, f32[40,768]{1,0:T(8,128)S(1)}, u32[]{:S(2)}, u32[]{:S(2)}) collective-permute-start(f32[40,768]{1,0:T(8,128)} %get-tuple-element.46.refs_0_), channel_id=1, source_target_pairs={{0,2},{1,3},{2,0},{3,1},{4,6},{5,7},{6,4},{7,5},{8,10},{9,11},{10,... | collective-permute-start | bytes 368648 | tf_op jit(solution)/shard_map/ppermute | solution.py:540
  77.4 7.0 %collective-permute-start.17 = (f32[40,768]{1,0:T(8,128)}, f32[40,768]{1,0:T(8,128)S(1)}, u32[]{:S(2)}, u32[]{:S(2)}) collective-permute-start(f32[40,768]{1,0:T(8,128)} %get-tuple-element.46.refs_0_), channel_id=1, source_target_pairs={{0,1},{1,0},{2,3},{3,2},{4,5},{5,4},{6,7},{7,6},{8,9},{9,8},{10,11... | collective-permute-start | bytes 368648 | tf_op jit(solution)/shard_map/ppermute | solution.py:540
  122.4 275.1 %all-reduce.10.cloned.1.call-start = ((), (), s32[]{:S(2)}) async-start(), calls=%async_computation.1 | async-start | bytes 7569408 | tf_op jit(solution)/shard_map/psum | solution.py:698
  126.7 7.8 %collective-permute-start.24 = (bf16[256,384]{1,0:T(8,128)(2,1)S(1)}, bf16[256,384]{1,0:T(8,128)(2,1)S(1)}, u32[]{:S(2)}, u32[]{:S(2)}) collective-permute-start(bf16[256,384]{1,0:T(8,128)(2,1)S(1)} %copy-done.9), channel_id=1, source_target_pairs={{0,1},{1,0},{2,3},{3,2},{4,5},{5,4},{6,7},{7,6},{8,9},{9,8},{10,11... | collective-permute-start | bytes 589832 | tf_op jit(solution)/shard_map/ppermute | solution.py:540
  129.0 8.8 %collective-permute-start.23 = (bf16[256,384]{1,0:T(8,128)(2,1)S(1)}, bf16[256,384]{1,0:T(8,128)(2,1)S(1)}, u32[]{:S(2)}, u32[]{:S(2)}) collective-permute-start(bf16[256,384]{1,0:T(8,128)(2,1)S(1)} %copy-done.9), channel_id=1, source_target_pairs={{0,6},{1,7},{2,4},{3,5},{4,2},{5,3},{6,0},{7,1},{8,14},{9,15},{10,... | collective-permute-start | bytes 589832 | tf_op jit(solution)/shard_map/ppermute | solution.py:540
  130.0 12.1 %collective-permute-start.22 = (bf16[256,384]{1,0:T(8,128)(2,1)S(1)}, bf16[256,384]{1,0:T(8,128)(2,1)S(1)}, u32[]{:S(2)}, u32[]{:S(2)}) collective-permute-start(bf16[256,384]{1,0:T(8,128)(2,1)S(1)} %copy-done.9), channel_id=1, source_target_pairs={{0,4},{1,5},{2,6},{3,7},{4,0},{5,1},{6,2},{7,3},{8,12},{9,13},{10,... | collective-permute-start | bytes 589832 | tf_op jit(solution)/shard_map/ppermute | solution.py:540
  133.0 9.3 %collective-permute-start.21 = (bf16[256,384]{1,0:T(8,128)(2,1)S(1)}, bf16[256,384]{1,0:T(8,128)(2,1)S(1)}, u32[]{:S(2)}, u32[]{:S(2)}) collective-permute-start(bf16[256,384]{1,0:T(8,128)(2,1)S(1)} %copy-done.9), channel_id=1, source_target_pairs={{0,2},{1,3},{2,0},{3,1},{4,6},{5,7},{6,4},{7,5},{8,10},{9,11},{10,... | collective-permute-start | bytes 589832 | tf_op jit(solution)/shard_map/ppermute | solution.py:540
  133.0 115.6 %collective-permute-start.31 = (bf16[256,384]{1,0:T(8,128)(2,1)S(1)}, bf16[256,384]{1,0:T(8,128)(2,1)S(1)}, u32[]{:S(2)}, u32[]{:S(2)}) collective-permute-start(bf16[256,384]{1,0:T(8,128)(2,1)S(1)} %copy-done.10), channel_id=1, source_target_pairs={{0,6},{1,7},{2,4},{3,5},{4,2},{5,3},{6,0},{7,1},{8,14},{9,15},{10,... | collective-permute-start | bytes 589832 | tf_op jit(solution)/shard_map/ppermute | solution.py:540
  134.5 115.0 %collective-permute-start.30 = (bf16[256,384]{1,0:T(8,128)(2,1)S(1)}, bf16[256,384]{1,0:T(8,128)(2,1)S(1)}, u32[]{:S(2)}, u32[]{:S(2)}) collective-permute-start(bf16[256,384]{1,0:T(8,128)(2,1)S(1)} %copy-done.10), channel_id=1, source_target_pairs={{0,4},{1,5},{2,6},{3,7},{4,0},{5,1},{6,2},{7,3},{8,12},{9,13},{10,... | collective-permute-start | bytes 589832 | tf_op jit(solution)/shard_map/ppermute | solution.py:540
  137.8 111.7 %collective-permute-start.29 = (bf16[256,384]{1,0:T(8,128)(2,1)S(1)}, bf16[256,384]{1,0:T(8,128)(2,1)S(1)}, u32[]{:S(2)}, u32[]{:S(2)}) collective-permute-start(bf16[256,384]{1,0:T(8,128)(2,1)S(1)} %copy-done.10), channel_id=1, source_target_pairs={{0,2},{1,3},{2,0},{3,1},{4,6},{5,7},{6,4},{7,5},{8,10},{9,11},{10,... | collective-permute-start | bytes 589832 | tf_op jit(solution)/shard_map/ppermute | solution.py:540
  142.1 107.9 %collective-permute-start.27 = (bf16[256,384]{1,0:T(8,128)(2,1)S(1)}, bf16[256,384]{1,0:T(8,128)(2,1)S(1)}, u32[]{:S(2)}, u32[]{:S(2)}) collective-permute-start(bf16[256,384]{1,0:T(8,128)(2,1)S(1)} %collective-permute-done.23.refs_3_), channel_id=1, source_target_pairs={{0,1},{1,0},{2,3},{3,2},{4,5},{5,4},{6,7},{7,6},{8,9},{9,8},{10,11... | collective-permute-start | bytes 589832 | tf_op jit(solution)/shard_map/ppermute | solution.py:540
  142.3 107.8 %collective-permute-start.26 = (bf16[256,384]{1,0:T(8,128)(2,1)S(1)}, bf16[256,384]{1,0:T(8,128)(2,1)S(1)}, u32[]{:S(2)}, u32[]{:S(2)}) collective-permute-start(bf16[256,384]{1,0:T(8,128)(2,1)S(1)} %collective-permute-done.22.refs_2_), channel_id=1, source_target_pairs={{0,1},{1,0},{2,3},{3,2},{4,5},{5,4},{6,7},{7,6},{8,9},{9,8},{10,11... | collective-permute-start | bytes 589832 | tf_op jit(solution)/shard_map/ppermute | solution.py:540
  248.6 6.8 %collective-permute-start.32 = (bf16[256,384]{1,0:T(8,128)(2,1)S(1)}, bf16[256,384]{1,0:T(8,128)(2,1)S(1)}, u32[]{:S(2)}, u32[]{:S(2)}) collective-permute-start(bf16[256,384]{1,0:T(8,128)(2,1)S(1)} %copy-done.10), channel_id=1, source_target_pairs={{0,1},{1,0},{2,3},{3,2},{4,5},{5,4},{6,7},{7,6},{8,9},{9,8},{10,11... | collective-permute-start | bytes 589832 | tf_op jit(solution)/shard_map/ppermute | solution.py:540
  249.6 5.9 %collective-permute-start.35 = (bf16[256,384]{1,0:T(8,128)(2,1)S(1)}, bf16[256,384]{1,0:T(8,128)(2,1)S(1)}, u32[]{:S(2)}, u32[]{:S(2)}) collective-permute-start(bf16[256,384]{1,0:T(8,128)(2,1)S(1)} %collective-permute-done.31.refs_3_), channel_id=1, source_target_pairs={{0,1},{1,0},{2,3},{3,2},{4,5},{5,4},{6,7},{7,6},{8,9},{9,8},{10,11... | collective-permute-start | bytes 589832 | tf_op jit(solution)/shard_map/ppermute | solution.py:540
  250.0 5.5 %collective-permute-start.34 = (bf16[256,384]{1,0:T(8,128)(2,1)S(1)}, bf16[256,384]{1,0:T(8,128)(2,1)S(1)}, u32[]{:S(2)}, u32[]{:S(2)}) collective-permute-start(bf16[256,384]{1,0:T(8,128)(2,1)S(1)} %collective-permute-done.30.refs_2_), channel_id=1, source_target_pairs={{0,1},{1,0},{2,3},{3,2},{4,5},{5,4},{6,7},{7,6},{8,9},{9,8},{10,11... | collective-permute-start | bytes 589832 | tf_op jit(solution)/shard_map/ppermute | solution.py:540
  (52 other events, 952.5 us)
Sparse Core Ops, SparseCore 0:
  122.5 124.5 all-reduce.7
  254.4 143.0 all-reduce.9
where the time goes:
time: 412 us; the launch traced here: 411 us
  waiting for transfers between devices  273 us (66%)
  Pallas kernels  60.2 us (15%)
  starting transfers between devices  30.5 us (7%)
  local copies, waits for them, and re-layouts  27.5 us (7%)
  between operations  14.5 us (4%)
  other arithmetic  5.72 us (1%)
    psum x2, waiting for transfers between devices, shards(): lax.psum((gain_g, win_g, wx_g[:w_x.shape[1]], wdt_g[:rank], small, galog,...  242 us
    pallas_call x6, Pallas kernels, run(): pl.pallas_call(kernel, out_shape=[jax.ShapeDtypeStruct(s, t) for s, t in...  60.2 us
    ppermute x35, starting transfers between devices, swap(): lax.ppermute(block, axis, [(i, i ^ distance) for i in range(devices)])  28.9 us
    ppermute x35, waiting for transfers between devices, swap(): lax.ppermute(block, axis, [(i, i ^ distance) for i in range(devices)])  28.7 us
    unnamed x100, local copies, waits for them, and re-layouts  14.1 us
  transfers between devices with their start and end apart: 38, of which 14 were waited for; matrix products, arithmetic and copies ran while one was open for 4% of the time, Pallas kernels for 5%

commit v1 on v0

--- a/solution.py
+++ b/solution.py
@@ -13,6 +13,8 @@
 CHUNKS = 8
 LANES = 128
 BLOCK = 16
+CUBE = (0, 2, 4, 6, 1, 3, 5, 7)
+SENT = (2, 4, 6, 1)
 ORDER_ROWS = 16
 F32, BF16 = jnp.float32, jnp.bfloat16
 VMEM_BYTES = 60 * 1024 * 1024
@@ -28,6 +30,18 @@
 
 def sigmoid(v):
     return 1.0 / (1.0 + jnp.exp(-v))
+
+
+def scalars(me, lengths, rows):
+    begin, meta = jnp.int32(0), [me[0] * rows]
+    for k in range(lengths.shape[1]):
+        meta.append(begin)
+        begin = begin + lengths[0, k]
+    return meta
+
+
+def source(me, p, n_pieces):
+    return jnp.bitwise_xor(me[0], CUBE[p]) if n_pieces == len(CUBE) else jnp.int32(p)
 
 
 def places(first, rows, r0, steps):
@@ -57,33 +71,29 @@
     lax.fori_loop(0, rows // BLOCK, body, 0)
 
 
-def own_column(order8, rows):
-    steps = rows // CHUNKS
-    both = order8[...]
-    return jnp.concatenate([both[:, i : i + 1] for i in range(steps)], axis=0)
-
-
-def gather_rows(column, pieces, src, rows):
-    total = None
-    lane = lax.broadcasted_iota(jnp.int32, (column.shape[0], rows), 1)
-    for p, piece in enumerate(pieces):
-        mine = (column - src[p] * rows == lane).astype(F32).astype(BF16)
-        part = dot(mine, piece)
-        total = part if total is None else total + part
-    return total
-
-
-def fill_broadcast(out, xproj, first, count, rows):
-    def body(j, carry):
-        r0 = pl.multiple_of(j * BLOCK, BLOCK)
-        block = xproj[pl.ds(r0, BLOCK), :]
-        for n in range(count):
-            out[pl.ds(r0, BLOCK), n * LANES : (n + 1) * LANES] = jnp.broadcast_to(
-                block[:, first + n : first + n + 1], (BLOCK, LANES)
-            )
-        return carry
-
-    lax.fori_loop(0, rows // BLOCK, body, 0)
+def row_of_place(rows):
+    place = lax.broadcasted_iota(jnp.int32, (rows, rows), 0)
+    row = lax.broadcasted_iota(jnp.int32, (rows, rows), 1)
+    return (place == lax.rem(row, CHUNKS) * (rows // CHUNKS) + lax.div(row, CHUNKS)).astype(F32).astype(BF16)
+
+
+def gather_rows(column, pieces, me, rows):
+    lane = lax.broadcasted_iota(jnp.int32, (column.shape[0], rows), 1).astype(F32)
+    mine = [
+        (column - (source(me, p, len(pieces)) * rows).astype(F32) == lane).astype(F32).astype(BF16)
+        for p in range(len(pieces))
+    ]
+    return dot(jnp.concatenate(mine, axis=1), jnp.concatenate(pieces, axis=0))
+
+
+def fill_broadcast(out, xproj, first, count):
+    whole = xproj[...]
+    high = whole.astype(BF16)
+    low = (whole - high.astype(F32)).astype(BF16)
+    row = lax.rem(lax.broadcasted_iota(jnp.int32, (2 * LANES, LANES), 0), LANES)
+    for n in range(count):
+        pick = (row == first + n).astype(F32).astype(BF16)
+        out[:, n * LANES : (n + 1) * LANES] = dot(jnp.concatenate([high, low], axis=1), pick)
 
 
 def rates(alog):
@@ -99,34 +109,46 @@
         ref[b, pl.ds(c, value.shape[0], stride=CHUNKS), :] = value[:, b * LANES : (b + 1) * LANES]
 
 
-def pre_kernel(
-    sizes, n_pieces, meta, src, order8, *refs
-):
+def refs_own(pieces, me, rows, n_pieces):
+    if n_pieces == len(CUBE):
+        return pieces[0][rows : rows + ORDER_ROWS, :rows]
+    digits = jnp.zeros((ORDER_ROWS, rows), F32)
+    for p in range(n_pieces):
+        part = pieces[p][rows : rows + ORDER_ROWS, :rows].astype(F32)
+        digits = jnp.where(me[0] == p, part, digits)
+    return digits.astype(BF16)
+
+
+def pre_kernel(sizes, n_pieces, me, lengths, *refs):
     rows, width, inner, rank, state, lags, clouds = sizes
     steps = rows // CHUNKS
     pieces = refs[:n_pieces]
     (gain, w_in, conv_w, conv_b, w_x, w_dt, dt_b, alog) = refs[n_pieces : n_pieces + 8]
-    (trans_o, normed_o, gate_o, ext_o, conv_o, act_o, step_o, xproj_o, chunkf_o, sums_o, f_o, orders_o) = refs[
-        n_pieces + 8 : n_pieces + 20
+    (trans_o, normed_o, gate_o, ext_o, conv_o, act_o, step_o, xproj_o, chunkf_o, sums_o, f_o, orders_o, column_o) = refs[
+        n_pieces + 8 : n_pieces + 21
     ]
-    conv_in, valid, far, use, bbc, a2 = refs[n_pieces + 20 :]
-    me = lax.div(meta[0], rows)
-    halo = jnp.full((1, 1), -1.0, F32)
-    halos = [halo] * (lags + 1)
+    conv_in, valid, far, use, bbc, a2 = refs[n_pieces + 21 :]
+    meta = scalars(me, lengths, rows)
+    to_row = row_of_place(rows)
+    halos = [jnp.full((1, 1), -1.0, F32)] * (lags + 1)
     for p in range(n_pieces):
-        tail = pieces[p][rows : rows + ORDER_ROWS, :rows].astype(F32)
-        row = tail[0:1] * 128.0 + tail[1:2]
+        row = dot(pieces[p][rows : rows + ORDER_ROWS, :rows], to_row)
+        row = row[0:1] * 128.0 + row[1:2]
         orders_o[p : p + 1, :] = row
-        behind = src[p] == me - 1
+        behind = source(me, p, n_pieces) == me[0] - 1
         for k in range(1, lags + 1):
             r = (steps - k) * CHUNKS + CHUNKS - 1
             halos[k] = jnp.where(behind, row[:, r : r + 1], halos[k])
-    sub = lax.broadcasted_iota(jnp.int32, (BLOCK, 1), 0)
-    extra = jnp.full((BLOCK, 1), -1.0, F32)
+    sub = lax.broadcasted_iota(jnp.int32, (BLOCK, LANES), 0)
+    extra = jnp.full((BLOCK, LANES), -1.0, F32)
     for k in range(1, lags + 1):
         extra = jnp.where(sub == k, halos[k], extra)
-    column = jnp.concatenate([own_column(order8, rows), extra.astype(jnp.int32)], axis=0)
-    trans = gather_rows(column, [p[0:rows, :] for p in pieces], src, rows)
+    digits = refs_own(pieces, me, rows, n_pieces)
+    both = dot(to_row, digits, ((0,), (1,)))
+    own = jnp.broadcast_to(both[:, 0:1] * 128.0 + both[:, 1:2], (rows, LANES))
+    column_o[...] = own
+    column = jnp.concatenate([own, extra], axis=0)
+    trans = gather_rows(wide(column, rows), [p[0:rows, :] for p in pieces], me, rows)
     trans_o[...] = trans[:rows].astype(BF16)
     inv_rms = lax.rsqrt(jnp.mean(trans * trans, axis=1, keepdims=True) + EPSILON)
     normed = (trans * inv_rms * gain[...]).astype(BF16)
@@ -172,7 +194,7 @@
         return carry + distance[:CHUNKS] + distance[CHUNKS:]
 
     sums_o[...] = lax.fori_loop(0, rows // BLOCK, step_body, jnp.zeros((CHUNKS, inner), F32))
-    fill_broadcast(bbc, xproj_o, rank, state, rows)
+    fill_broadcast(bbc, xproj_o, rank, state)
     a2[...] = rates(alog) * LOG2E
     for lb in range(inner // LANES):
         ls = slice(lb * LANES, (lb + 1) * LANES)
@@ -196,14 +218,17 @@
     f_o[...] = total
 
 
-def back_kernel(sizes, n_pieces, meta, src, order8, *refs):
+def back_kernel(sizes, n_pieces, me, lengths, *refs):
     rows, width, inner, rank, state, lags, clouds = sizes
     steps = rows // CHUNKS
     pieces = refs[:n_pieces]
-    gate, step, xproj, alog, w_out, sums, f = refs[n_pieces : n_pieces + 7]
-    dy_o, gg_o, chunkb_o, carry_o = refs[n_pieces + 7 : n_pieces + 11]
-    valid, far, gm, cbc, a2 = refs[n_pieces + 11 :]
-    trans_dy = gather_rows(own_column(order8, rows), [p[...] for p in pieces], src, rows).astype(BF16)
+    gate, step, xproj, alog, w_out, sums, f, column = refs[n_pieces : n_pieces + 8]
+    n_out = (len(CUBE) - 4 if n_pieces == len(CUBE) else 1)
+    dy_o, gg_o, chunkb_o = refs[n_pieces + 8 : n_pieces + 11]
+    carries_o = refs[n_pieces + 11 : n_pieces + 11 + n_out]
+    valid, far, gm, cbc, a2 = refs[n_pieces + 11 + n_out :]
+    meta = scalars(me, lengths, rows)
+    trans_dy = gather_rows(wide(column[...], rows), [p[...] for p in pieces], me, rows).astype(BF16)
     dy_o[...] = trans_dy
     gg_o[...] = dot(trans_dy, w_out[...], ((1,), (1,)))
     fill_valid(valid, meta, clouds, rows, 1)
@@ -216,7 +241,7 @@
         return carry
 
     lax.fori_loop(0, rows // BLOCK, body, 0)
-    fill_broadcast(cbc, xproj, rank + state, state, rows)
+    fill_broadcast(cbc, xproj, rank + state, state)
     a2[...] = rates(alog) * LOG2E
     for lb in range(inner // LANES):
         ls = slice(lb * LANES, (lb + 1) * LANES)
@@ -237,36 +262,48 @@
     total = jnp.zeros((state, inner), F32)
     for c in reversed(range(CHUNKS)):
         total = jnp.exp2(a2[...] * sums[c : c + 1, :]) * total + chunk_of(chunkb_o, c, state)
-    carry_o[:state, :] = f[...]
-    carry_o[state : 2 * state, :] = total
-    carry_o[2 * state :, :] = jnp.broadcast_to(
-        jnp.sum(sums[...], axis=0, keepdims=True), (CHUNKS, inner)
-    )
-
-
-def main_kernel(sizes, n_pieces, meta, src, *refs):
+    passed = jnp.broadcast_to(jnp.sum(sums[...], axis=0, keepdims=True), (CHUNKS, inner))
+    if n_out == 1:
+        carries_o[0][:state, :] = f[...]
+        carries_o[0][state : 2 * state, :] = total
+        carries_o[0][2 * state :, :] = passed
+        return
+    for out, d in zip(carries_o, SENT):
+        later = jnp.bitwise_xor(me[0], d) > me[0]
+        out[:state, :] = jnp.where(later, f[...], total)
+        out[state:, :] = passed
+
+
+def core_of(me, devices):
+    return jnp.bitwise_and(me, 1) if devices == len(CUBE) else jnp.int32(0)
+
+
+def main_kernel(sizes, n_pieces, me_ref, lengths, *refs):
     rows, width, inner, rank, state, lags, clouds = sizes
     steps = rows // CHUNKS
     carries = refs[:n_pieces]
-    (trans_dy, gg, gate, ext, conv, act, step, xproj, chunkf, chunkb, sums, alog, skip, w_out, w_x, w_dt, conv_w) = refs[
-        n_pieces : n_pieces + 17
+    (trans_dy, normed, gg, gate, ext, conv, act, step, xproj, chunkf, chunkb, sums, alog, skip, w_out, w_x, w_dt, conv_w) = refs[
+        n_pieces : n_pieces + 18
     ]
-    (branch_o, gz_o, gci_o, rim_o, wout_o, wx_o, wdt_o, small_o, galog_o) = refs[n_pieces + 17 : n_pieces + 26]
+    (branch_o, gz_o, gci_o, rim_o, keep_o, send_o, small_o) = refs[n_pieces + 18 : n_pieces + 25]
     (valid, far, use, gm, bbc, cbc, a2, states, decays, mixed, gs, lamb, gb, gc, sstart, gstart, gated, held) = refs[
-        n_pieces + 26 :
+        n_pieces + 25 :
     ]
-    me = lax.div(meta[0], rows)
-    devices = n_pieces
+    meta = scalars(me_ref, lengths, rows)
+    me = me_ref[0]
+    devices = len(CUBE) if n_pieces == len(CUBE) - 1 else n_pieces
     a2[...] = rates(alog) * LOG2E
     state_in = jnp.zeros((state, inner), F32)
     flow_in = jnp.zeros((state, inner), F32)
-    size = 2 * state + CHUNKS
-    for p in range(devices):
-        held[pl.ds(pl.multiple_of(src[p] * size, CHUNKS), size), :] = carries[p][...]
+    size = carries[0].shape[0]
+    back = size - CHUNKS - state
+    for p in range(n_pieces):
+        whence = source(me_ref, p + 1, devices) if devices > n_pieces else p
+        held[pl.ds(pl.multiple_of(whence * size, CHUNKS), size), :] = carries[p][...]
 
     def ahead(s, flow):
         base = pl.multiple_of(s * size, CHUNKS)
-        p_s = jnp.exp2(a2[...] * held[pl.ds(base + 2 * state, 1), :])
+        p_s = jnp.exp2(a2[...] * held[pl.ds(base + size - CHUNKS, 1), :])
         return jnp.where(s < me, p_s * flow + held[pl.ds(base, state), :], flow)
 
     state_in = lax.fori_loop(0, devices, ahead, state_in)
@@ -274,8 +311,8 @@
     def behind(k, flow):
         s = devices - 1 - k
         base = pl.multiple_of(s * size, CHUNKS)
-        p_s = jnp.exp2(a2[...] * held[pl.ds(base + 2 * state, 1), :])
-        return jnp.where(s > me, p_s * flow + held[pl.ds(pl.multiple_of(base + state, CHUNKS), state), :], flow)
+        p_s = jnp.exp2(a2[...] * held[pl.ds(base + size - CHUNKS, 1), :])
+        return jnp.where(s > me, p_s * flow + held[pl.ds(pl.multiple_of(base + back, CHUNKS), state), :], flow)
 
     flow_in = lax.fori_loop(0, devices, behind, flow_in)
     now = state_in
@@ -297,8 +334,8 @@
         return carry
 
     lax.fori_loop(0, rows // BLOCK, prepare, 0)
-    fill_broadcast(bbc, xproj, rank, state, rows)
-    fill_broadcast(cbc, xproj, rank + state, state, rows)
+    fill_broadcast(bbc, xproj, rank, state)
+    fill_broadcast(cbc, xproj, rank + state, state)
     for lb in range(inner // LANES):
         ls = slice(lb * LANES, (lb + 1) * LANES)
         rate = [jnp.broadcast_to(a2[n : n + 1, ls], (CHUNKS, LANES)) for n in range(state)]
@@ -339,7 +376,11 @@
 
     skip_sum = lax.fori_loop(0, rows // BLOCK, gating, jnp.zeros((CHUNKS, inner), F32))
     branch_o[...] = dot(gated[...], w_out[...]).astype(BF16)
-    wout_o[...] = dot(gated[...], trans_dy[...], ((0,), (0,)))
+    wout_g = dot(trans_dy[...], gated[...], ((0,), (0,))).astype(BF16)
+    gate_g = dot(normed[...], gz_o[...], ((0,), (0,))).astype(BF16)
+    second = core_of(me, devices) == 1
+    keep_o[...] = jnp.where(second, gate_g, wout_g)
+    send_o[...] = jnp.where(second, wout_g, gate_g)
     group = 3
     pair = 4
     for lg in range(inner // LANES // group):
@@ -398,7 +439,7 @@
             )
             for q, n in enumerate(ns):
                 for x, ls in enumerate(lanes):
-                    galog_o[n : n + 1, ls] = (
+                    small_o[n : n + 1, ls] = (
                         jnp.sum(sums_a[q * group + x], axis=0, keepdims=True) * rate[q][x][0:1]
                     )
     col = lax.broadcasted_iota(jnp.int32, (state * LANES, LANES), 1)
@@ -425,9 +466,14 @@
 
     dt_sum = lax.fori_loop(0, rows // BLOCK, pre_body, jnp.zeros((CHUNKS, inner), F32))
     dt_low = xproj[...].astype(BF16)
-    wdt_o[...] = dot(dt_low, gpre[...], ((0,), (0,)))
+    wdt_g = dot(dt_low, gpre[...], ((0,), (0,)))
     grad_xproj = (dot(gpre[...], w_dt[...], ((1,), (1,))) + grad_bc).astype(BF16)
-    wx_o[...] = dot(grad_xproj, act[...], ((0,), (0,)))
+    wx_g = dot(grad_xproj, act[...], ((0,), (0,)))
+    at = state
+    small_o[at : at + rank + 2 * state, :] = wx_g[: rank + 2 * state]
+    at += rank + 2 * state
+    small_o[at : at + rank, :] = wdt_g[:rank]
+    at += rank
     gs[...] = dot(grad_xproj, w_x[...], ((1,), (1,)))
     gconv = mixed
 
@@ -451,8 +497,8 @@
     )
     small = [skip_sum, dt_sum, conv_sums[0]] + [conv_sums[1 + lags - t] for t in range(lags + 1)]
     for k, part in enumerate(small):
-        small_o[k : k + 1, :] = jnp.sum(part, axis=0, keepdims=True)
-    small_o[len(small) :, :] = jnp.zeros((small_o.shape[0] - len(small), inner), F32)
+        small_o[at + k : at + k + 1, :] = jnp.sum(part, axis=0, keepdims=True)
+    small_o[at + len(small) :, :] = jnp.zeros((small_o.shape[0] - at - len(small), inner), F32)
 
     def masked_tile(i, k):
         r = pl.ds(pl.multiple_of(i * CHUNKS, CHUNKS), CHUNKS)
@@ -485,7 +531,7 @@
         rim_o[b : b + 1, :] = total
 
 
-def final_kernel(sizes, trans, normed, gci, gz, rim, gain, w_in, back_o, win_o, gain_o):
+def final_kernel(sizes, devices, me, trans, normed, gci, gz, rim, small, gain, w_in, back_o, keep_o, send_o, both):
     rows, width, inner, rank, state, lags, clouds = sizes
     steps = rows // CHUNKS
     r = lax.broadcasted_iota(jnp.int32, (rows, inner), 0)
@@ -494,27 +540,61 @@
         total = total + jnp.where(r == (steps - k) * CHUNKS + CHUNKS - 1, rim[k : k + 1, :], 0.0)
     grad_ci = total.astype(BF16)
     grad_z = gz[...]
-    win_o[:, :inner] = dot(normed[...], grad_ci, ((0,), (0,)))
-    win_o[:, inner:] = dot(normed[...], grad_z, ((0,), (0,)))
     grad_normed = dot(grad_ci, w_in[:, :inner], ((1,), (1,))) + dot(grad_z, w_in[:, inner:], ((1,), (1,)))
     x = trans[...].astype(F32)
     inv_rms = lax.rsqrt(jnp.mean(x * x, axis=1, keepdims=True) + EPSILON)
-    gain_o[...] = jnp.sum(grad_normed * x * inv_rms, axis=0, keepdims=True)
     scaled = grad_normed * gain[...]
     back_o[...] = (
         inv_rms * scaled
         - inv_rms * inv_rms * inv_rms * x * jnp.mean(scaled * x, axis=1, keepdims=True)
     ).astype(BF16)
-
-
-def place_kernel(rows, n_pieces, meta, here, orders, *refs):
+    both[0:width, :] = dot(normed[...], grad_ci, ((0,), (0,))).astype(BF16)
+    gain_row = jnp.sum(grad_normed * x * inv_rms, axis=0, keepdims=True)
+    gain_row = jnp.concatenate([gain_row, jnp.zeros((1, inner - width), F32)], axis=1)
+    n_small = small.shape[0]
+    last = lax.broadcasted_iota(jnp.int32, (n_small, inner), 0) == n_small - 1
+    both[width : width + n_small, :] = jnp.where(last, gain_row, small[...]).astype(BF16)
+    half = keep_o.shape[0]
+    core = core_of(me[0], devices)
+    keep_o[...] = both[pl.ds(pl.multiple_of(core * half, BLOCK), half), :]
+    send_o[...] = both[pl.ds(pl.multiple_of((1 - core) * half, BLOCK), half), :]
+
+
+def halves_kernel(me, kept, got, own_o, *sent_o):
+    part = own_o.shape[0]
+    chip = lax.div(me[0], 2)
+    for d, out in enumerate((own_o,) + sent_o):
+        r = pl.ds(pl.multiple_of(jnp.bitwise_xor(chip, d) * part, BLOCK), part)
+        out[...] = (kept[r, :].astype(F32) + got[r, :].astype(F32)).astype(BF16)
+
+
+def sum_kernel(a, b, c, d, out):
+    out[...] = ((a[...].astype(F32) + b[...].astype(F32)) + (c[...].astype(F32) + d[...].astype(F32))).astype(BF16)
+
+
+def unpack_kernel(sizes, n_pieces, n_small, me, *refs):
+    rows, width, inner, rank, state, lags, clouds = sizes
+    one, two = refs[:n_pieces], refs[n_pieces : 2 * n_pieces]
+    win_o, wout_o, small_o, all_one, all_two = refs[2 * n_pieces :]
+    for pieces, whole in ((one, all_one), (two, all_two)):
+        part = pieces[0].shape[0]
+        for p, piece in enumerate(pieces):
+            s = source(me, p, n_pieces)
+            if n_pieces == len(CUBE):
+                s = jnp.bitwise_and(s, 1) * (n_pieces // 2) + lax.div(s, 2)
+            whole[pl.ds(pl.multiple_of(s * part, BLOCK), part), :] = piece[...]
+    wout_o[...] = all_one[0:width, :].astype(F32).T
+    win_o[:, inner:] = all_one[width : 2 * width, :].astype(F32)
+    win_o[:, :inner] = all_two[0:width, :].astype(F32)
+    small_o[...] = all_two[width : width + n_small, :].astype(F32)
+
+
+def place_kernel(rows, n_pieces, me, here, orders, *refs):
     pieces, out = refs[:n_pieces], refs[n_pieces]
-    place = meta[0] + lax.broadcasted_iota(jnp.int32, (rows, rows), 0)
-    total = here[...].astype(F32)
-    for p in range(n_pieces):
-        mine = (orders[p : p + 1, :].astype(jnp.int32) == place).astype(F32).astype(BF16)
-        total = total + dot(mine, pieces[p][...])
-    out[...] = total.astype(BF16)
+    place = (me[0] * rows + lax.broadcasted_iota(jnp.int32, (rows, rows), 0)).astype(F32)
+    mine = [(orders[p : p + 1, :] == place).astype(F32).astype(BF16) for p in range(n_pieces)]
+    moved = dot(jnp.concatenate(mine, axis=1), jnp.concatenate([p[...] for p in pieces], axis=0))
+    out[...] = (here[...].astype(F32) + moved).astype(BF16)
 
 
 def call(kernel, outs, scratch, n_smem, name):
@@ -541,13 +621,32 @@
 
 
 def spread_pieces(block, axis):
-    devices, index = lax.axis_size(axis), lax.axis_index(axis)
-    if devices == 8:
-        across = [block] + [swap(block, axis, d) for d in (2, 4, 6)]
-        pieces = across + [swap(part, axis, 1) for part in across]
-        return pieces, [index ^ d for d in (0, 2, 4, 6, 1, 3, 5, 7)]
+    devices = lax.axis_size(axis)
+    if devices == len(CUBE):
+        across = [block] + [swap(block, axis, d) for d in CUBE[1:4]]
+        return across + [swap(part, axis, 1) for part in across]
     whole = lax.all_gather(block, axis)
-    return [whole[i] for i in range(devices)], [jnp.int32(i) for i in range(devices)]
+    return [whole[i] for i in range(devices)]
+
+
+def spread_carries(blocks, axis):
+    if len(blocks) == 1:
+        return spread_pieces(blocks[0], axis)
+    across = [swap(block, axis, d) for block, d in zip(blocks, SENT)]
+    return across[:3] + [across[3]] + [swap(part, axis, 1) for part in across[:3]]
+
+
+def total_pieces(kept, sent):
+    if lax.axis_size("seq") != len(CUBE) or lax.axis_size("dp") != 4:
+        return [lax.psum(half.astype(F32), ("dp", "seq")).astype(BF16) for half in (kept, sent)]
+    me = lax.axis_index("seq").astype(jnp.int32)[None]
+    part = (kept.shape[0] // 4, kept.shape[1])
+    got = swap(sent, "seq", 1)
+    own, *away = call(halves_kernel, [(part, BF16)] * 4, [], 1, "add_halves")(me, kept, got)
+    add = call(sum_kernel, [(part, BF16)], [], 0, "add_parts")
+    (mine,) = add(own, *[swap(block, "seq", 2 * d) for d, block in zip((1, 2, 3), away)])
+    (mine,) = add(mine, *[swap(mine, "dp", d) for d in (1, 2, 3)])
+    return spread_pieces(mine, "seq")
 
 
 def from_behind(block, axis, distance):
@@ -576,18 +675,14 @@
     inner, rank, state, taps = w_out.shape[0], w_dt.shape[0], a_log.shape[1], conv_weight.shape[1]
     lags, clouds, steps = taps - 1, lengths.shape[1], rows // CHUNKS
     sizes = (rows, width, inner, rank, state, lags, clouds)
-    devices, me = lax.axis_size("seq"), lax.axis_index("seq")
+    devices = lax.axis_size("seq")
+    me = lax.axis_index("seq").astype(jnp.int32)[None]
     here_x, here_dy = tokens[0], cotangent[0]
-    order8 = order.reshape(CHUNKS, steps)
-    order_row = order8.T.reshape(1, rows)
-    order_rows = jnp.concatenate([order_row // 128, order_row % 128], axis=0).astype(BF16)
-    order_rows = jnp.pad(order_rows, ((0, ORDER_ROWS - 2), (0, width - rows)))
-    pieces_x, sources = spread_pieces(jnp.concatenate([here_x, order_rows], axis=0), "seq")
-    pieces_dy, _ = spread_pieces(here_dy, "seq")
+    digits = jnp.concatenate([order >> 7, order & 127], axis=0).astype(BF16)
+    digits = jnp.pad(digits, ((0, ORDER_ROWS - 2), (0, width - rows)))
+    pieces_x = spread_pieces(jnp.concatenate([here_x, digits], axis=0), "seq")
+    pieces_dy = spread_pieces(here_dy, "seq")
     n = len(pieces_x)
-    src = jnp.stack(sources).astype(jnp.int32)
-    starts = jnp.cumsum(lengths[0]) - lengths[0]
-    meta = jnp.concatenate([(me * rows)[None], starts]).astype(jnp.int32)
     alog_t = a_log.T
     conv_w = conv_weight.T
     w_x_pad = jnp.pad(w_x, ((0, 0), (0, LANES - w_x.shape[1])))
@@ -597,7 +692,7 @@
     carried = (inner // LANES, state * CHUNKS, LANES)
     spread = (rows, state * LANES)
     ext_rows = rows + lags * CHUNKS
-    (trans, normed, gate, ext, conv, act, step, xproj, chunkf, sums, f, orders) = call(
+    (trans, normed, gate, ext, conv, act, step, xproj, chunkf, sums, f, orders, column) = call(
         functools.partial(pre_kernel, sizes, n),
         [
             ((rows, width), BF16),
@@ -612,6 +707,7 @@
             ((CHUNKS, inner), F32),
             ((state, inner), F32),
             ((n, rows), F32),
+            (lane, F32),
         ],
         [
             ((rows + BLOCK, inner), F32),
@@ -623,15 +719,12 @@
         ],
         2,
         "forward_local",
-    )(meta, src, order8, *pieces_x, row(norm_gain), w_in, conv_w, row(conv_bias), w_x_pad, w_dt_pad, row(dt_bias), alog_t)
-    trans_dy, gg, chunkb, carry = call(
+    )(me, lengths, *pieces_x, row(norm_gain), w_in, conv_w, row(conv_bias), w_x_pad, w_dt_pad, row(dt_bias), alog_t)
+    carry_rows = (state + CHUNKS, 2 * state + CHUNKS)[n != len(CUBE)]
+    n_sent = (len(SENT), 1)[n != len(CUBE)]
+    trans_dy, gg, chunkb, *carries = call(
         functools.partial(back_kernel, sizes, n),
-        [
-            ((rows, width), BF16),
-            (big, F32),
-            (carried, F32),
-            ((2 * state + CHUNKS, inner), F32),
-        ],
+        [((rows, width), BF16), (big, F32), (carried, F32)] + [((carry_rows, inner), F32)] * n_sent,
         [
             ((1, rows, LANES), F32),
             (big, F32),
@@ -641,20 +734,19 @@
         ],
         2,
         "backward_local",
-    )(meta, src, order8, *pieces_dy, gate, step, xproj, alog_t, w_out, sums, f)
-    carries, _ = spread_pieces(carry, "seq")
-    branch, gz, gci, rim, wout_g, wx_g, wdt_g, small, galog = call(
-        functools.partial(main_kernel, sizes, n),
+    )(me, lengths, *pieces_dy, gate, step, xproj, alog_t, w_out, sums, f, column)
+    carries = spread_carries(carries, "seq")
+    n_small = state + (rank + 2 * state) + rank + 3 + taps + 1
+    branch, gz, gci, rim, keep, send, small = call(
+        functools.partial(main_kernel, sizes, len(carries)),
         [
             ((rows, width), BF16),
             (big, BF16),
             (big, F32),
             ((CHUNKS, inner), F32),
-            ((inner, width), F32),
-            ((LANES, inner), F32),
-            ((LANES, inner), F32),
-            ((CHUNKS, inner), F32),
-            ((state, inner), F32),
+            ((width, inner), BF16),
+            ((width, inner), BF16),
+            ((n_small, inner), F32),
         ],
         [
             ((lags, rows, LANES), F32),
@@ -674,43 +766,53 @@
             (carried, F32),
             (carried, F32),
             (big, BF16),
-            ((n * (2 * state + CHUNKS), inner), F32),
+            ((n * carry_rows, inner), F32),
         ],
         2,
         "scan_both",
     )(
-        meta, src, *carries, trans_dy, gg, gate, ext, conv, act, step, xproj, chunkf, chunkb, sums, alog_t,
+        me, lengths, *carries, trans_dy, normed, gg, gate, ext, conv, act, step, xproj, chunkf, chunkb, sums, alog_t,
         row(d_skip), w_out, w_x_pad, w_dt_pad, conv_w,
     )
     rim = from_behind(rim, "seq", -1)
-    back, win_g, gain_g = call(
-        functools.partial(final_kernel, sizes),
-        [((rows, width), BF16), ((width, 2 * inner), F32), ((1, width), F32)],
-        [],
-        0,
+    one = total_pieces(keep, send)
+    half = -(-(width + n_small) // (8 * BLOCK)) * (4 * BLOCK)
+    back, keep, send = call(
+        functools.partial(final_kernel, sizes, devices),
+        [((rows, width), BF16), ((half, inner), BF16), ((half, inner), BF16)],
+        [((2 * half, inner), BF16)],
+        1,
         "input_projection_grads",
-    )(trans, normed, gci, gz, rim, row(norm_gain), w_in)
+    )(me, trans, normed, gci, gz, rim, small, row(norm_gain), w_in)
     place = call(functools.partial(place_kernel, rows, n), [((rows, width), BF16)], [], 1, "to_hilbert")
-    pieces_b, _ = spread_pieces(branch, "seq")
-    pieces_g, _ = spread_pieces(back, "seq")
-    (output,) = place(meta, here_x, orders, *pieces_b)
-    (input_grad,) = place(meta, here_dy, orders, *pieces_g)
-    s_gain, s_win, s_wx, s_wdt, s_small, s_alog, s_wout = lax.psum(
-        (gain_g, win_g, wx_g[: w_x.shape[1]], wdt_g[:rank], small, galog, wout_g), ("dp", "seq")
-    )
+    pieces_b = spread_pieces(branch, "seq")
+    (output,) = place(me, here_x, orders, *pieces_b)
+    pieces_g = spread_pieces(back, "seq")
+    two = total_pieces(keep, send)
+    (input_grad,) = place(me, here_dy, orders, *pieces_g)
+    win_g, wout_g, small = call(
+        functools.partial(unpack_kernel, sizes, len(one), n_small),
+        [((width, 2 * inner), F32), ((inner, width), F32), ((n_small, inner), F32)],
+        [((2 * width, inner), BF16), ((2 * half, inner), BF16)],
+        1,
+        "unpack_sums",
+    )(me, *one, *two)
+    cuts = [state, rank + 2 * state, rank, 1, 1, 1, taps]
+    at = [sum(cuts[:k]) for k in range(len(cuts) + 1)]
+    g_alog, g_wx, g_wdt, g_skip, g_dtb, g_convb, g_taps = [small[at[k] : at[k + 1]] for k in range(len(cuts))]
     return (
         output[None],
         input_grad[None],
-        s_gain[0],
-        s_win,
-        s_small[3 : 4 + lags].T,
-        s_small[2],
-        s_wx.T,
-        s_wdt,
-        s_small[1],
-        s_alog.T,
-        s_small[0],
-        s_wout,
+        small[n_small - 1, :width],
+        win_g,
+        g_taps.T,
+        g_convb[0],
+        g_wx.T,
+        g_wdt,
+        g_dtb[0],
+        g_alog.T,
+        g_skip[0],
+        wout_g,
     )
 
 

time: 412 us -> 198 us (0.48)
  waiting for transfers between devices: 273 us -> 48.5 us
  starting transfers between devices: 30.5 us -> 54 us
  between operations: 14.5 us -> 1.25 us
  Pallas kernels: 60.2 us -> 70.3 us
  local copies, waits for them, and re-layouts: 27.5 us -> 21.5 us
    psum x2 -> x0, waiting for transfers between devices: 242 us -> none  [shards(): lax.psum((gain_g, win_g, wx_g[:w_x.shape[1]], wdt_g[:rank], small, galog,...]
    ppermute x35 -> x63, starting transfers between devices: 28.9 us -> 52.6 us  [swap(): lax.ppermute(block, axis, [(i, i ^ distance) for i in range(devices)])]
    ppermute x35 -> x63, waiting for transfers between devices: 28.7 us -> 48.5 us  [swap(): lax.ppermute(block, axis, [(i, i ^ distance) for i in range(devices)])]
    pallas_call x6 -> x13, Pallas kernels: 60.2 us -> 70.3 us  [run(): pl.pallas_call(kernel, out_shape=[jax.ShapeDtypeStruct(s, t) for s, t in...]
    unnamed x100 -> x135, local copies, waits for them, and re-layouts: 14.1 us -> 6.36 us
  transfers between devices with their start and end apart: 38 -> 64, of which waited for: 14 -> 18; matrix products, arithmetic and copies ran while one was open for 4% -> 4% of each run, Pallas kernels for 5% -> 16%
where the time goes in v1:
time: 198 us; the launch traced here: 197 us
  Pallas kernels  70.3 us (36%)
  starting transfers between devices  54 us (27%)
  waiting for transfers between devices  48.5 us (24%)
  local copies, waits for them, and re-layouts  21.5 us (11%)
    pallas_call x13, Pallas kernels, run(): pl.pallas_call(kernel, out_shape=[jax.ShapeDtypeStruct(s, t) for s, t in...  70.3 us
    ppermute x63, starting transfers between devices, swap(): lax.ppermute(block, axis, [(i, i ^ distance) for i in range(devices)])  52.6 us
    ppermute x63, waiting for transfers between devices, swap(): lax.ppermute(block, axis, [(i, i ^ distance) for i in range(devices)])  48.5 us
    unnamed x135, local copies, waits for them, and re-layouts  6.36 us
    broadcast_in_dim x4, local copies, waits for them, and re-layouts, shards(): row = lambda v: v[None, :]  4.36 us
    transpose x3, local copies, waits for them, and re-layouts, shards(): return (output[None], input_grad[None], small[n_small - 1, :width], win_g...  4.36 us
  transfers between devices with their start and end apart: 64, of which 18 were waited for; matrix products, arithmetic and copies ran while one was open for 4% of the time, Pallas kernels for 16%

profile of v1, /device:TPU:0, one launch (start us, length us, event | category | flops | bytes accessed | tf_op | source)
XLA Modules:
  0.0 197.3 jit_solution(10063871251242929151)
XLA Ops:
  2.3 4.0 %collective-permute-start.2 = (bf16[272,384]{1,0:T(8,128)(2,1)S(1)}, bf16[272,384]{1,0:T(8,128)(2,1)S(1)}, u32[]{:S(2)}, u32[]{:S(2)}) collective-permute-start(bf16[272,384]{1,0:T(8,128)(2,1)S(1)} %pad_maximum_fusion.refs_0_), channel_id=1, source_target_pairs={{0,6},{1,7},{2,4},{3,5},{4,2},{5,3},{6,0},{7,1},{8,14},{9,15},{10,... | collective-permute-start | bytes 626696 | tf_op jit(solution)/shard_map/ppermute | solution.py:620
  8.4 1.9 collective-permute-start
  10.3 6.3 %collective-permute-done.9.refs_3_ = bf16[256,384]{1,0:T(8,128)(2,1)S(1)} collective-permute-done((bf16[256,384]{1,0:T(8,128)(2,1)}, bf16[256,384]{1,0:T(8,128)(2,1)S(1)}, u32[]{:S(2)}, u32[]{:S(2)}) %collective-permute-start.9) | collective-permute-done | bytes 196640 | tf_op jit(solution)/shard_map/ppermute | solution.py:620
  17.0 3.2 %collective-permute-done.1.refs_2_ = bf16[272,384]{1,0:T(8,128)(2,1)S(1)} collective-permute-done((bf16[272,384]{1,0:T(8,128)(2,1)S(1)}, bf16[272,384]{1,0:T(8,128)(2,1)S(1)}, u32[]{:S(2)}, u32[]{:S(2)}) %collective-permute-start.1) | collective-permute-done | bytes 208928 | tf_op jit(solution)/shard_map/ppermute | solution.py:620
  20.2 4.1 %collective-permute-done.8.refs_2_ = bf16[256,384]{1,0:T(8,128)(2,1)S(1)} collective-permute-done((bf16[256,384]{1,0:T(8,128)(2,1)}, bf16[256,384]{1,0:T(8,128)(2,1)S(1)}, u32[]{:S(2)}, u32[]{:S(2)}) %collective-permute-start.8) | collective-permute-done | bytes 196640 | tf_op jit(solution)/shard_map/ppermute | solution.py:620
  26.0 5.3 %collective-permute-done.7.refs_1_ = bf16[256,384]{1,0:T(8,128)(2,1)S(1)} collective-permute-done((bf16[256,384]{1,0:T(8,128)(2,1)}, bf16[256,384]{1,0:T(8,128)(2,1)S(1)}, u32[]{:S(2)}, u32[]{:S(2)}) %collective-permute-start.7) | collective-permute-done | bytes 196640 | tf_op jit(solution)/shard_map/ppermute | solution.py:620
  40.1 11.8 %forward_local.1 = (bf16[256,384]{1,0:T(8,128)(2,1)}, bf16[256,384]{1,0:T(8,128)(2,1)}, f32[256,768]{1,0:T(8,128)}, f32[280,768]{1,0:T(8,128)}, f32[256,768]{1,0...) custom-call(s32[1]{0:T(128)} %bitcast.me.me_ref, ...), custom_call_target="tpu_custom_call" | custom-call | tf_op jit(solution)/shard_map/forward_local/pallas_call | solution.py:605
  52.8 8.8 %backward_local.1 = (bf16[256,384]{1,0:T(8,128)(2,1)}, f32[256,768]{1,0:T(8,128)}, f32[6,128,128]{2,1,0:T(8,128)}, f32[24,768]{1,0:T(8,128)}, f32[24,768]{1,0:T(...) custom-call(s32[1]{0:T(128)} %bitcast.me.me_ref, s32[1,5]{1,0:T(1,128)} %lengths.5, bf16[256,384]{1,0:T(8,128)(2,1)} %bitcast.17, ...), custom_call_target="tpu_custom_call" | custom-call | tf_op jit(solution)/shard_map/backward_local/pallas_call | solution.py:605
  66.2 3.1 %collective-permute-done.15.refs_1_ = f32[24,768]{1,0:T(8,128)S(1)} collective-permute-done((f32[24,768]{1,0:T(8,128)}, f32[24,768]{1,0:T(8,128)S(1)}, u32[]{:S(2)}, u32[]{:S(2)}) %collective-permute-start.15) | collective-permute-done | bytes 73760 | tf_op jit(solution)/shard_map/ppermute | solution.py:620
  71.4 25.1 %scan_both.1 = (bf16[256,384]{1,0:T(8,128)(2,1)}, bf16[256,768]{1,0:T(8,128)(2,1)}, f32[256,768]{1,0:T(8,128)}, f32[8,768]{1,0:T(8,128)}, bf16[384,768]{1,0:T(8,...) custom-call(s32[1]{0:T(128)} %bitcast.me.me_ref, s32[1,5]{1,0:T(1,128)} %lengths.5, f32[24,768]{1,0:T(8,128)} %copy-done.58, ...), custom_call_target="tpu_custom_call" | custom-call | tf_op jit(solution)/shard_map/scan_both/pallas_call | solution.py:605
  99.9 3.4 %collective-permute-start.22 = (bf16[256,384]{1,0:T(8,128)(2,1)}, bf16[256,384]{1,0:T(8,128)(2,1)S(1)}, u32[]{:S(2)}, u32[]{:S(2)}) collective-permute-start(bf16[256,384]{1,0:T(8,128)(2,1)} %get-tuple-element.72.refs_0_), channel_id=1, source_target_pairs={{0,4},{1,5},{2,6},{3,7},{4,0},{5,1},{6,2},{7,3},{8,12},{9,13},{10,... | collective-permute-start | bytes 589832 | tf_op jit(solution)/shard_map/ppermute | solution.py:620
  103.9 3.8 %input_projection_grads.1 = (bf16[256,384]{1,0:T(8,128)(2,1)}, bf16[256,768]{1,0:T(8,128)(2,1)}, bf16[256,768]{1,0:T(8,128)(2,1)}) custom-call(s32[1]{0:T(128)} %bitcast.me.me_ref, bf16[256,384]{1,0:T(8,128)(2,1)} %get-tuple-element.73.trans, bf16[256,384]{1,0:T(8,128)(2,1)} %get-tuple-element.65.refs_8_.normed, f32[256,768]{1,0:T(8,128)} %get-tuple-element.74.gci, ...), custom_call_target="tpu_custom_call" | custom-call | tf_op jit(solution)/shard_map/input_projection_grads/pallas_call | solution.py:605
  107.6 2.0 %collective-permute-start.50 = (bf16[256,768]{1,0:T(8,128)(2,1)}, bf16[256,768]{1,0:T(8,128)(2,1)S(1)}, u32[]{:S(2)}, u32[]{:S(2)}) collective-permute-start(bf16[256,768]{1,0:T(8,128)(2,1)} %get-tuple-element.86), channel_id=1, source_target_pairs={{0,1},{1,0},{2,3},{3,2},{4,5},{5,4},{6,7},{7,6},{8,9},{9,8},{10,11... | collective-permute-start | bytes 1179656 | tf_op jit(solution)/shard_map/ppermute | solution.py:620
  112.0 5.5 %collective-permute-done.21.refs_1_ = bf16[256,384]{1,0:T(8,128)(2,1)S(1)} collective-permute-done((bf16[256,384]{1,0:T(8,128)(2,1)S(1)}, bf16[256,384]{1,0:T(8,128)(2,1)S(1)}, u32[]{:S(2)}, u32[]{:S(2)}) %collective-permute-start.21) | collective-permute-done | bytes 196640 | tf_op jit(solution)/shard_map/ppermute | solution.py:620
  118.8 3.0 %collective-permute-done.31.refs_3_ = bf16[256,384]{1,0:T(8,128)(2,1)S(1)} collective-permute-done((bf16[256,384]{1,0:T(8,128)(2,1)}, bf16[256,384]{1,0:T(8,128)(2,1)S(1)}, u32[]{:S(2)}, u32[]{:S(2)}) %collective-permute-start.31) | collective-permute-done | bytes 196640 | tf_op jit(solution)/shard_map/ppermute | solution.py:620
  122.6 1.9 add_halves.3
  125.4 2.3 %collective-permute-start.52 = (bf16[64,768]{1,0:T(8,128)(2,1)}, bf16[64,768]{1,0:T(8,128)(2,1)S(1)}, u32[]{:S(2)}, u32[]{:S(2)}) collective-permute-start(bf16[64,768]{1,0:T(8,128)(2,1)} %get-tuple-element.89), channel_id=1, source_target_pairs={{0,4},{1,5},{2,6},{3,7},{4,0},{5,1},{6,2},{7,3},{8,12},{9,13},{10,... | collective-permute-start | bytes 294920 | tf_op jit(solution)/shard_map/ppermute | solution.py:620
  128.6 2.1 %add_halves.2 = (bf16[96,768]{1,0:T(8,128)(2,1)}, bf16[96,768]{1,0:T(8,128)(2,1)}, bf16[96,768]{1,0:T(8,128)(2,1)}, bf16[96,768]{1,0:T(8,128)(2,1)}) custom-call(s32[1]{0:T(128)} %bitcast.me.me_ref, bf16[384,768]{1,0:T(8,128)(2,1)} %get-tuple-element.79.kept, bf16[384,768]{1,0:T(8,128)(2,1)} %copy-done.1), custom_call_target="tpu_custom_call" | custom-call | tf_op jit(solution)/shard_map/add_halves/pallas_call | solution.py:605
  131.4 1.9 collective-permute-start.38
  137.7 3.6 %collective-permute-start.56 = (bf16[64,768]{1,0:T(8,128)(2,1)}, bf16[64,768]{1,0:T(8,128)(2,1)S(1)}, u32[]{:S(2)}, u32[]{:S(2)}) collective-permute-start(bf16[64,768]{1,0:T(8,128)(2,1)} %add_parts.6.a), channel_id=1, source_target_pairs={{0,24},{8,16},{16,8},{24,0},{1,25},{9,17},{17,9},{25,1},{2,26},{10... | collective-permute-start | bytes 294920 | tf_op jit(solution)/shard_map/ppermute | solution.py:620
  143.2 1.9 add_parts.4.a
  145.1 2.5 %collective-permute-start.42 = (bf16[96,768]{1,0:T(8,128)(2,1)}, bf16[96,768]{1,0:T(8,128)(2,1)S(1)}, u32[]{:S(2)}, u32[]{:S(2)}) collective-permute-start(bf16[96,768]{1,0:T(8,128)(2,1)} %add_parts.4.a), channel_id=1, source_target_pairs={{0,24},{8,16},{16,8},{24,0},{1,25},{9,17},{17,9},{25,1},{2,26},{10... | collective-permute-start | bytes 442376 | tf_op jit(solution)/shard_map/ppermute | solution.py:620
  147.5 1.9 collective-permute-start.40
  149.5 7.2 %collective-permute-done.55.c = bf16[64,768]{1,0:T(8,128)(2,1)S(1)} collective-permute-done((bf16[64,768]{1,0:T(8,128)(2,1)}, bf16[64,768]{1,0:T(8,128)(2,1)S(1)}, u32[]{:S(2)}, u32[]{:S(2)}) %collective-permute-start.55) | collective-permute-done | bytes 98336 | tf_op jit(solution)/shard_map/ppermute | solution.py:620
  159.5 2.5 %collective-permute-done.41.c = bf16[96,768]{1,0:T(8,128)(2,1)S(1)} collective-permute-done((bf16[96,768]{1,0:T(8,128)(2,1)}, bf16[96,768]{1,0:T(8,128)(2,1)S(1)}, u32[]{:S(2)}, u32[]{:S(2)}) %collective-permute-start.41) | collective-permute-done | bytes 147488 | tf_op jit(solution)/shard_map/ppermute | solution.py:620
  162.0 2.0 %collective-permute-start.59 = (bf16[64,768]{1,0:T(8,128)(2,1)}, bf16[64,768]{1,0:T(8,128)(2,1)S(1)}, u32[]{:S(2)}, u32[]{:S(2)}) collective-permute-start(bf16[64,768]{1,0:T(8,128)(2,1)} %add_parts.7.refs_8_), channel_id=1, source_target_pairs={{0,6},{1,7},{2,4},{3,5},{4,2},{5,3},{6,0},{7,1},{8,14},{9,15},{10,... | collective-permute-start | bytes 294920 | tf_op jit(solution)/shard_map/ppermute | solution.py:620
  164.7 1.9 add_parts.5.refs_0_
  167.5 2.0 %collective-permute-start.45 = (bf16[96,768]{1,0:T(8,128)(2,1)}, bf16[96,768]{1,0:T(8,128)(2,1)S(1)}, u32[]{:S(2)}, u32[]{:S(2)}) collective-permute-start(bf16[96,768]{1,0:T(8,128)(2,1)} %add_parts.5.refs_0_), channel_id=1, source_target_pairs={{0,6},{1,7},{2,4},{3,5},{4,2},{5,3},{6,0},{7,1},{8,14},{9,15},{10,... | collective-permute-start | bytes 442376 | tf_op jit(solution)/shard_map/ppermute | solution.py:620
  173.1 2.7 %collective-permute-done.45.refs_3_ = bf16[96,768]{1,0:T(8,128)(2,1)S(1)} collective-permute-done((bf16[96,768]{1,0:T(8,128)(2,1)}, bf16[96,768]{1,0:T(8,128)(2,1)S(1)}, u32[]{:S(2)}, u32[]{:S(2)}) %collective-permute-start.45) | collective-permute-done | bytes 147488 | tf_op jit(solution)/shard_map/ppermute | solution.py:620
  177.3 2.9 %to_hilbert.2 = bf16[256,384]{1,0:T(8,128)(2,1)} custom-call(s32[1]{0:T(128)} %bitcast.me.me_ref, bf16[256,384]{1,0:T(8,128)(2,1)} %bitcast.20, f32[8,256]{1,0:T(8,128)} %get-tuple-element.53.orders, bf16[256,384]{1,0:T(8,128)(2,1)} %get-tuple-element.72.refs_0_, bf16[256,384]{1,0:T(8,128)(2,1)} %copy-done.21, bf16[256,384]{1,0:T(8,128)(2,1)} %copy-done.20, ...), custom_call_target="tpu_custom_call" | custom-call | tf_op jit(solution)/shard_map/to_hilbert/pallas_call | solution.py:605
  180.3 2.9 %to_hilbert.3 = bf16[256,384]{1,0:T(8,128)(2,1)} custom-call(s32[1]{0:T(128)} %bitcast.me.me_ref, bf16[256,384]{1,0:T(8,128)(2,1)} %bitcast.18, f32[8,256]{1,0:T(8,128)} %get-tuple-element.53.orders, bf16[256,384]{1,0:T(8,128)(2,1)} %get-tuple-element.78.refs_0_, bf16[256,384]{1,0:T(8,128)(2,1)} %copy-done.25, bf16[256,384]{1,0:T(8,128)(2,1)} %copy-done.24, ...), custom_call_target="tpu_custom_call" | custom-call | tf_op jit(solution)/shard_map/to_hilbert/pallas_call | solution.py:605
  184.7 3.9 %unpack_sums.1 = (f32[384,1536]{1,0:T(8,128)}, f32[768,384]{1,0:T(8,128)}, f32[104,768]{1,0:T(8,128)}) custom-call(s32[1]{0:T(128)} %bitcast.me.me_ref, bf16[96,768]{1,0:T(8,128)(2,1)} %add_parts.5.refs_0_, bf16[96,768]{1,0:T(8,128)(2,1)} %copy-done.34, bf16[96,768]{1,0:T(8,128)(2,1)} %copy-done.33, bf16[96,768]{1,0:T(8,128)(2,1)} %copy-done.32, ...), custom_call_target="tpu_custom_call" | custom-call | tf_op jit(solution)/shard_map/unpack_sums/pallas_call | solution.py:605
  (259 shorter events, 59.0 us)
Async XLA Ops:
  2.3 14.2 %collective-permute-start.2 = (bf16[272,384]{1,0:T(8,128)(2,1)S(1)}, bf16[272,384]{1,0:T(8,128)(2,1)S(1)}, u32[]{:S(2)}, u32[]{:S(2)}) collective-permute-start(bf16[272,384]{1,0:T(8,128)(2,1)S(1)} %pad_maximum_fusion.refs_0_), channel_id=1, source_target_pairs={{0,6},{1,7},{2,4},{3,5},{4,2},{5,3},{6,0},{7,1},{8,14},{9,15},{10,... | collective-permute-start | bytes 626696 | tf_op jit(solution)/shard_map/ppermute | solution.py:620
  6.3 13.9 %collective-permute-start.1 = (bf16[272,384]{1,0:T(8,128)(2,1)S(1)}, bf16[272,384]{1,0:T(8,128)(2,1)S(1)}, u32[]{:S(2)}, u32[]{:S(2)}) collective-permute-start(bf16[272,384]{1,0:T(8,128)(2,1)S(1)} %pad_maximum_fusion.refs_0_), channel_id=1, source_target_pairs={{0,4},{1,5},{2,6},{3,7},{4,0},{5,1},{6,2},{7,3},{8,12},{9,13},{10,... | collective-permute-start | bytes 626696 | tf_op jit(solution)/shard_map/ppermute | solution.py:620
  6.8 9.7 %collective-permute-start.9 = (bf16[256,384]{1,0:T(8,128)(2,1)}, bf16[256,384]{1,0:T(8,128)(2,1)S(1)}, u32[]{:S(2)}, u32[]{:S(2)}) collective-permute-start(bf16[256,384]{1,0:T(8,128)(2,1)} %bitcast.13), channel_id=1, source_target_pairs={{0,6},{1,7},{2,4},{3,5},{4,2},{5,3},{6,0},{7,1},{8,14},{9,15},{10,... | collective-permute-start | bytes 589832 | tf_op jit(solution)/shard_map/ppermute | solution.py:620
  8.3 16.1 %collective-permute-start.8 = (bf16[256,384]{1,0:T(8,128)(2,1)}, bf16[256,384]{1,0:T(8,128)(2,1)S(1)}, u32[]{:S(2)}, u32[]{:S(2)}) collective-permute-start(bf16[256,384]{1,0:T(8,128)(2,1)} %bitcast.14), channel_id=1, source_target_pairs={{0,4},{1,5},{2,6},{3,7},{4,0},{5,1},{6,2},{7,3},{8,12},{9,13},{10,... | collective-permute-start | bytes 589832 | tf_op jit(solution)/shard_map/ppermute | solution.py:620
  8.4 17.7 %collective-permute-start = (bf16[272,384]{1,0:T(8,128)(2,1)S(1)}, bf16[272,384]{1,0:T(8,128)(2,1)S(1)}, u32[]{:S(2)}, u32[]{:S(2)}) collective-permute-start(bf16[272,384]{1,0:T(8,128)(2,1)S(1)} %pad_maximum_fusion.refs_0_), channel_id=1, source_target_pairs={{0,2},{1,3},{2,0},{3,1},{4,6},{5,7},{6,4},{7,5},{8,10},{9,11},{10,... | collective-permute-start | bytes 626696 | tf_op jit(solution)/shard_map/ppermute | solution.py:620
  16.5 14.9 %collective-permute-start.3 = (bf16[272,384]{1,0:T(8,128)(2,1)S(1)}, bf16[272,384]{1,0:T(8,128)(2,1)S(1)}, u32[]{:S(2)}, u32[]{:S(2)}) collective-permute-start(bf16[272,384]{1,0:T(8,128)(2,1)S(1)} %pad_maximum_fusion.refs_0_), channel_id=1, source_target_pairs={{0,1},{1,0},{2,3},{3,2},{4,5},{5,4},{6,7},{7,6},{8,9},{9,8},{10,11... | collective-permute-start | bytes 626696 | tf_op jit(solution)/shard_map/ppermute | solution.py:620
  16.5 15.4 %collective-permute-start.6 = (bf16[272,384]{1,0:T(8,128)(2,1)S(1)}, bf16[272,384]{1,0:T(8,128)(2,1)S(1)}, u32[]{:S(2)}, u32[]{:S(2)}) collective-permute-start(bf16[272,384]{1,0:T(8,128)(2,1)S(1)} %collective-permute-done.2.refs_3_), channel_id=1, source_target_pairs={{0,1},{1,0},{2,3},{3,2},{4,5},{5,4},{6,7},{7,6},{8,9},{9,8},{10,11... | collective-permute-start | bytes 626696 | tf_op jit(solution)/shard_map/ppermute | solution.py:620
  20.2 11.8 %collective-permute-start.5 = (bf16[272,384]{1,0:T(8,128)(2,1)S(1)}, bf16[272,384]{1,0:T(8,128)(2,1)S(1)}, u32[]{:S(2)}, u32[]{:S(2)}) collective-permute-start(bf16[272,384]{1,0:T(8,128)(2,1)S(1)} %collective-permute-done.1.refs_2_), channel_id=1, source_target_pairs={{0,1},{1,0},{2,3},{3,2},{4,5},{5,4},{6,7},{7,6},{8,9},{9,8},{10,11... | collective-permute-start | bytes 626696 | tf_op jit(solution)/shard_map/ppermute | solution.py:620
  26.0 13.4 %collective-permute-start.4 = (bf16[272,384]{1,0:T(8,128)(2,1)S(1)}, bf16[272,384]{1,0:T(8,128)(2,1)S(1)}, u32[]{:S(2)}, u32[]{:S(2)}) collective-permute-start(bf16[272,384]{1,0:T(8,128)(2,1)S(1)} %collective-permute-done.refs_1_), channel_id=1, source_target_pairs={{0,1},{1,0},{2,3},{3,2},{4,5},{5,4},{6,7},{7,6},{8,9},{9,8},{10,11... | collective-permute-start | bytes 626696 | tf_op jit(solution)/shard_map/ppermute | solution.py:620
  31.4 20.5 %collective-permute-start.10 = (bf16[256,384]{1,0:T(8,128)(2,1)}, bf16[256,384]{1,0:T(8,128)(2,1)S(1)}, u32[]{:S(2)}, u32[]{:S(2)}) collective-permute-start(bf16[256,384]{1,0:T(8,128)(2,1)} %bitcast.16), channel_id=1, source_target_pairs={{0,1},{1,0},{2,3},{3,2},{4,5},{5,4},{6,7},{7,6},{8,9},{9,8},{10,11... | collective-permute-start | bytes 589832 | tf_op jit(solution)/shard_map/ppermute | solution.py:620
  31.4 20.5 %collective-permute-start.13 = (bf16[256,384]{1,0:T(8,128)(2,1)S(1)}, bf16[256,384]{1,0:T(8,128)(2,1)S(1)}, u32[]{:S(2)}, u32[]{:S(2)}) collective-permute-start(bf16[256,384]{1,0:T(8,128)(2,1)S(1)} %collective-permute-done.9.refs_3_), channel_id=1, source_target_pairs={{0,1},{1,0},{2,3},{3,2},{4,5},{5,4},{6,7},{7,6},{8,9},{9,8},{10,11... | collective-permute-start | bytes 589832 | tf_op jit(solution)/shard_map/ppermute | solution.py:620
  31.9 20.0 %collective-permute-start.12 = (bf16[256,384]{1,0:T(8,128)(2,1)S(1)}, bf16[256,384]{1,0:T(8,128)(2,1)S(1)}, u32[]{:S(2)}, u32[]{:S(2)}) collective-permute-start(bf16[256,384]{1,0:T(8,128)(2,1)S(1)} %collective-permute-done.8.refs_2_), channel_id=1, source_target_pairs={{0,1},{1,0},{2,3},{3,2},{4,5},{5,4},{6,7},{7,6},{8,9},{9,8},{10,11... | collective-permute-start | bytes 589832 | tf_op jit(solution)/shard_map/ppermute | solution.py:620
  32.0 20.0 %collective-permute-start.11 = (bf16[256,384]{1,0:T(8,128)(2,1)S(1)}, bf16[256,384]{1,0:T(8,128)(2,1)S(1)}, u32[]{:S(2)}, u32[]{:S(2)}) collective-permute-start(bf16[256,384]{1,0:T(8,128)(2,1)S(1)} %collective-permute-done.7.refs_1_), channel_id=1, source_target_pairs={{0,1},{1,0},{2,3},{3,2},{4,5},{5,4},{6,7},{7,6},{8,9},{9,8},{10,11... | collective-permute-start | bytes 589832 | tf_op jit(solution)/shard_map/ppermute | solution.py:620
  96.5 13.1 %collective-permute-start.24 = (bf16[256,384]{1,0:T(8,128)(2,1)}, bf16[256,384]{1,0:T(8,128)(2,1)S(1)}, u32[]{:S(2)}, u32[]{:S(2)}) collective-permute-start(bf16[256,384]{1,0:T(8,128)(2,1)} %get-tuple-element.72.refs_0_), channel_id=1, source_target_pairs={{0,1},{1,0},{2,3},{3,2},{4,5},{5,4},{6,7},{7,6},{8,9},{9,8},{10,11... | collective-permute-start | bytes 589832 | tf_op jit(solution)/shard_map/ppermute | solution.py:620
  97.0 14.0 %collective-permute-start.23 = (bf16[256,384]{1,0:T(8,128)(2,1)}, bf16[256,384]{1,0:T(8,128)(2,1)S(1)}, u32[]{:S(2)}, u32[]{:S(2)}) collective-permute-start(bf16[256,384]{1,0:T(8,128)(2,1)} %get-tuple-element.72.refs_0_), channel_id=1, source_target_pairs={{0,6},{1,7},{2,4},{3,5},{4,2},{5,3},{6,0},{7,1},{8,14},{9,15},{10,... | collective-permute-start | bytes 589832 | tf_op jit(solution)/shard_map/ppermute | solution.py:620
  98.4 29.2 %collective-permute-start.36 = (bf16[384,768]{1,0:T(8,128)(2,1)}, bf16[384,768]{1,0:T(8,128)(2,1)S(1)}, u32[]{:S(2)}, u32[]{:S(2)}) collective-permute-start(bf16[384,768]{1,0:T(8,128)(2,1)} %get-tuple-element.80), channel_id=1, source_target_pairs={{0,1},{1,0},{2,3},{3,2},{4,5},{5,4},{6,7},{7,6},{8,9},{9,8},{10,11... | collective-permute-start | bytes 1769480 | tf_op jit(solution)/shard_map/ppermute | solution.py:620
  99.9 11.1 %collective-permute-start.22 = (bf16[256,384]{1,0:T(8,128)(2,1)}, bf16[256,384]{1,0:T(8,128)(2,1)S(1)}, u32[]{:S(2)}, u32[]{:S(2)}) collective-permute-start(bf16[256,384]{1,0:T(8,128)(2,1)} %get-tuple-element.72.refs_0_), channel_id=1, source_target_pairs={{0,4},{1,5},{2,6},{3,7},{4,0},{5,1},{6,2},{7,3},{8,12},{9,13},{10,... | collective-permute-start | bytes 589832 | tf_op jit(solution)/shard_map/ppermute | solution.py:620
  107.6 14.2 %collective-permute-start.50 = (bf16[256,768]{1,0:T(8,128)(2,1)}, bf16[256,768]{1,0:T(8,128)(2,1)S(1)}, u32[]{:S(2)}, u32[]{:S(2)}) collective-permute-start(bf16[256,768]{1,0:T(8,128)(2,1)} %get-tuple-element.86), channel_id=1, source_target_pairs={{0,1},{1,0},{2,3},{3,2},{4,5},{5,4},{6,7},{7,6},{8,9},{9,8},{10,11... | collective-permute-start | bytes 1179656 | tf_op jit(solution)/shard_map/ppermute | solution.py:620
  111.0 10.8 %collective-permute-start.31 = (bf16[256,384]{1,0:T(8,128)(2,1)}, bf16[256,384]{1,0:T(8,128)(2,1)S(1)}, u32[]{:S(2)}, u32[]{:S(2)}) collective-permute-start(bf16[256,384]{1,0:T(8,128)(2,1)} %get-tuple-element.78.refs_0_), channel_id=1, source_target_pairs={{0,6},{1,7},{2,4},{3,5},{4,2},{5,3},{6,0},{7,1},{8,14},{9,15},{10,... | collective-permute-start | bytes 589832 | tf_op jit(solution)/shard_map/ppermute | solution.py:620
  131.4 9.8 %collective-permute-start.38 = (bf16[96,768]{1,0:T(8,128)(2,1)}, bf16[96,768]{1,0:T(8,128)(2,1)S(1)}, u32[]{:S(2)}, u32[]{:S(2)}) collective-permute-start(bf16[96,768]{1,0:T(8,128)(2,1)} %get-tuple-element.83), channel_id=1, source_target_pairs={{0,4},{1,5},{2,6},{3,7},{4,0},{5,1},{6,2},{7,3},{8,12},{9,13},{10,... | collective-permute-start | bytes 442376 | tf_op jit(solution)/shard_map/ppermute | solution.py:620
  134.3 10.8 %collective-permute-start.25 = (bf16[256,384]{1,0:T(8,128)(2,1)S(1)}, bf16[256,384]{1,0:T(8,128)(2,1)S(1)}, u32[]{:S(2)}, u32[]{:S(2)}) collective-permute-start(bf16[256,384]{1,0:T(8,128)(2,1)S(1)} %collective-permute-done.21.refs_1_), channel_id=1, source_target_pairs={{0,1},{1,0},{2,3},{3,2},{4,5},{5,4},{6,7},{7,6},{8,9},{9,8},{10,11... | collective-permute-start | bytes 589832 | tf_op jit(solution)/shard_map/ppermute | solution.py:620
  134.3 13.2 %collective-permute-start.35 = (bf16[256,384]{1,0:T(8,128)(2,1)S(1)}, bf16[256,384]{1,0:T(8,128)(2,1)S(1)}, u32[]{:S(2)}, u32[]{:S(2)}) collective-permute-start(bf16[256,384]{1,0:T(8,128)(2,1)S(1)} %collective-permute-done.31.refs_3_), channel_id=1, source_target_pairs={{0,1},{1,0},{2,3},{3,2},{4,5},{5,4},{6,7},{7,6},{8,9},{9,8},{10,11... | collective-permute-start | bytes 589832 | tf_op jit(solution)/shard_map/ppermute | solution.py:620
  137.7 9.9 %collective-permute-start.56 = (bf16[64,768]{1,0:T(8,128)(2,1)}, bf16[64,768]{1,0:T(8,128)(2,1)S(1)}, u32[]{:S(2)}, u32[]{:S(2)}) collective-permute-start(bf16[64,768]{1,0:T(8,128)(2,1)} %add_parts.6.a), channel_id=1, source_target_pairs={{0,24},{8,16},{16,8},{24,0},{1,25},{9,17},{17,9},{25,1},{2,26},{10... | collective-permute-start | bytes 294920 | tf_op jit(solution)/shard_map/ppermute | solution.py:620
  141.3 15.4 %collective-permute-start.55 = (bf16[64,768]{1,0:T(8,128)(2,1)}, bf16[64,768]{1,0:T(8,128)(2,1)S(1)}, u32[]{:S(2)}, u32[]{:S(2)}) collective-permute-start(bf16[64,768]{1,0:T(8,128)(2,1)} %add_parts.6.a), channel_id=1, source_target_pairs={{0,16},{8,24},{16,0},{24,8},{1,17},{9,25},{17,1},{25,9},{2,18},{10... | collective-permute-start | bytes 294920 | tf_op jit(solution)/shard_map/ppermute | solution.py:620
  141.6 15.0 %collective-permute-start.54 = (bf16[64,768]{1,0:T(8,128)(2,1)}, bf16[64,768]{1,0:T(8,128)(2,1)S(1)}, u32[]{:S(2)}, u32[]{:S(2)}) collective-permute-start(bf16[64,768]{1,0:T(8,128)(2,1)} %add_parts.6.a), channel_id=1, source_target_pairs={{0,8},{8,0},{16,24},{24,16},{1,9},{9,1},{17,25},{25,17},{2,10},{10... | collective-permute-start | bytes 294920 | tf_op jit(solution)/shard_map/ppermute | solution.py:620
  145.1 14.0 %collective-permute-start.42 = (bf16[96,768]{1,0:T(8,128)(2,1)}, bf16[96,768]{1,0:T(8,128)(2,1)S(1)}, u32[]{:S(2)}, u32[]{:S(2)}) collective-permute-start(bf16[96,768]{1,0:T(8,128)(2,1)} %add_parts.4.a), channel_id=1, source_target_pairs={{0,24},{8,16},{16,8},{24,0},{1,25},{9,17},{17,9},{25,1},{2,26},{10... | collective-permute-start | bytes 442376 | tf_op jit(solution)/shard_map/ppermute | solution.py:620
  147.5 14.5 %collective-permute-start.41 = (bf16[96,768]{1,0:T(8,128)(2,1)}, bf16[96,768]{1,0:T(8,128)(2,1)S(1)}, u32[]{:S(2)}, u32[]{:S(2)}) collective-permute-start(bf16[96,768]{1,0:T(8,128)(2,1)} %add_parts.4.a), channel_id=1, source_target_pairs={{0,16},{8,24},{16,0},{24,8},{1,17},{9,25},{17,1},{25,9},{2,18},{10... | collective-permute-start | bytes 442376 | tf_op jit(solution)/shard_map/ppermute | solution.py:620
  147.5 16.5 %collective-permute-start.40 = (bf16[96,768]{1,0:T(8,128)(2,1)}, bf16[96,768]{1,0:T(8,128)(2,1)S(1)}, u32[]{:S(2)}, u32[]{:S(2)}) collective-permute-start(bf16[96,768]{1,0:T(8,128)(2,1)} %add_parts.4.a), channel_id=1, source_target_pairs={{0,8},{8,0},{16,24},{24,16},{1,9},{9,1},{17,25},{25,17},{2,10},{10... | collective-permute-start | bytes 442376 | tf_op jit(solution)/shard_map/ppermute | solution.py:620
  156.6 9.9 %collective-permute-start.34 = (bf16[256,384]{1,0:T(8,128)(2,1)S(1)}, bf16[256,384]{1,0:T(8,128)(2,1)S(1)}, u32[]{:S(2)}, u32[]{:S(2)}) collective-permute-start(bf16[256,384]{1,0:T(8,128)(2,1)S(1)} %collective-permute-done.30.refs_2_), channel_id=1, source_target_pairs={{0,1},{1,0},{2,3},{3,2},{4,5},{5,4},{6,7},{7,6},{8,9},{9,8},{10,11... | collective-permute-start | bytes 589832 | tf_op jit(solution)/shard_map/ppermute | solution.py:620
  156.7 10.8 %collective-permute-start.33 = (bf16[256,384]{1,0:T(8,128)(2,1)S(1)}, bf16[256,384]{1,0:T(8,128)(2,1)S(1)}, u32[]{:S(2)}, u32[]{:S(2)}) collective-permute-start(bf16[256,384]{1,0:T(8,128)(2,1)S(1)} %collective-permute-done.29.refs_1_), channel_id=1, source_target_pairs={{0,1},{1,0},{2,3},{3,2},{4,5},{5,4},{6,7},{7,6},{8,9},{9,8},{10,11... | collective-permute-start | bytes 589832 | tf_op jit(solution)/shard_map/ppermute | solution.py:620
  159.0 10.4 %collective-permute-start.60 = (bf16[64,768]{1,0:T(8,128)(2,1)}, bf16[64,768]{1,0:T(8,128)(2,1)S(1)}, u32[]{:S(2)}, u32[]{:S(2)}) collective-permute-start(bf16[64,768]{1,0:T(8,128)(2,1)} %add_parts.7.refs_8_), channel_id=1, source_target_pairs={{0,1},{1,0},{2,3},{3,2},{4,5},{5,4},{6,7},{7,6},{8,9},{9,8},{10,11... | collective-permute-start | bytes 294920 | tf_op jit(solution)/shard_map/ppermute | solution.py:620
  172.6 10.7 %collective-permute-start.46 = (bf16[96,768]{1,0:T(8,128)(2,1)}, bf16[96,768]{1,0:T(8,128)(2,1)S(1)}, u32[]{:S(2)}, u32[]{:S(2)}) collective-permute-start(bf16[96,768]{1,0:T(8,128)(2,1)} %add_parts.5.refs_0_), channel_id=1, source_target_pairs={{0,1},{1,0},{2,3},{3,2},{4,5},{5,4},{6,7},{7,6},{8,9},{9,8},{10,11... | collective-permute-start | bytes 442376 | tf_op jit(solution)/shard_map/ppermute | solution.py:620
  (99 other events, 1217.1 us)

commit v2 on v1

v2 whole, which is shorter than its diff:
```python
import functools

import jax
import jax.numpy as jnp
from jax import lax
from jax.experimental import pallas as pl
from jax.experimental.pallas import tpu as pltpu
from jax.sharding import PartitionSpec as P

EPSILON = 1e-05
LOG2E = 1.4426950408889634
FAR = 1e30
CHUNKS = 8
LANES = 128
BLOCK = 16
CUBE = (0, 2, 4, 6, 1, 3, 5, 7)
SENT = (2, 4, 6, 1)
ORDER_ROWS = 16
F32, BF16 = jnp.float32, jnp.bfloat16
MIB = 1024 * 1024


def dot(a, b, contract=((1,), (0,))):
    return lax.dot_general(a, b, (contract, ((), ())), preferred_element_type=F32)


def as_row(ref):
    return ref[...].reshape(1, ref.shape[0])


def wide(tile, width):
    return jnp.concatenate([tile] * (width // LANES), axis=1)


def sigmoid(v):
    return 1.0 / (1.0 + jnp.exp(-v))


def scalars(me, lengths, rows):
    begin, meta = jnp.int32(0), [me[0] * rows]
    for k in range(lengths.shape[1]):
        meta.append(begin)
        begin = begin + lengths[0, k]
    return meta


def source(me, p, n_pieces):
    return jnp.bitwise_xor(me[0], CUBE[p]) if n_pieces == len(CUBE) else jnp.int32(p)


def places(first, rows, r0, steps):
    r = r0 + lax.broadcasted_iota(jnp.int32, (rows, LANES), 0)
    return first + lax.rem(r, CHUNKS) * steps + lax.div(r, CHUNKS)


def cloud_start(meta, clouds, place):
    start = jnp.zeros_like(place)
    for k in range(clouds):
        begin = meta[1 + k]
        start = jnp.maximum(start, jnp.where(begin <= place, begin, 0))
    return start


def fill_valid(valid, meta, clouds, rows, lags):
    steps = rows // CHUNKS

    def body(j, carry):
        r0 = pl.multiple_of(j * BLOCK, BLOCK)
        place = places(meta[0], BLOCK, r0, steps)
        begin = cloud_start(meta, clouds, place)
        for k in range(1, lags + 1):
            valid[k - 1, pl.ds(r0, BLOCK), :] = (place - k >= begin).astype(F32)
        return carry

    lax.fori_loop(0, rows // BLOCK, body, 0)


def row_of_place(rows):
    place = lax.broadcasted_iota(jnp.int32, (rows, rows), 0)
    row = lax.broadcasted_iota(jnp.int32, (rows, rows), 1)
    return (place == lax.rem(row, CHUNKS) * (rows // CHUNKS) + lax.div(row, CHUNKS)).astype(F32).astype(BF16)


def gather_rows(column, pieces, me, rows):
    lane = lax.broadcasted_iota(jnp.int32, (column.shape[0], rows), 1).astype(F32)
    mine = [
        (column - (source(me, p, len(pieces)) * rows).astype(F32) == lane).astype(F32).astype(BF16)
        for p in range(len(pieces))
    ]
    return dot(jnp.concatenate(mine, axis=1), jnp.concatenate(pieces, axis=0))


def fill_broadcast(out, xproj, first, count):
    whole = xproj[...]
    high = whole.astype(BF16)
    low = (whole - high.astype(F32)).astype(BF16)
    row = lax.rem(lax.broadcasted_iota(jnp.int32, (2 * LANES, LANES), 0), LANES)
    for n in range(count):
        pick = (row == first + n).astype(F32).astype(BF16)
        out[:, n * LANES : (n + 1) * LANES] = dot(jnp.concatenate([high, low], axis=1), pick)


def rates(alog):
    return -jnp.exp(alog[...])


def chunk_of(ref, c, count):
    return jnp.concatenate([ref[b, pl.ds(c, count, stride=CHUNKS), :] for b in range(ref.shape[0])], axis=1)


def set_chunk(ref, c, value):
    for b in range(ref.shape[0]):
        ref[b, pl.ds(c, value.shape[0], stride=CHUNKS), :] = value[:, b * LANES : (b + 1) * LANES]


def refs_own(pieces, me, rows, n_pieces):
    if n_pieces == len(CUBE):
        return pieces[0][rows : rows + ORDER_ROWS, :rows]
    digits = jnp.zeros((ORDER_ROWS, rows), F32)
    for p in range(n_pieces):
        part = pieces[p][rows : rows + ORDER_ROWS, :rows].astype(F32)
        digits = jnp.where(me[0] == p, part, digits)
    return digits.astype(BF16)


def pre_kernel(sizes, n_pieces, n_far, me, *refs):
    rows, width, inner, rank, state, lags, clouds = sizes
    steps = rows // CHUNKS
    pieces = refs[:n_pieces]
    far_refs, refs = refs[n_pieces : n_pieces + n_far], refs[:n_pieces] + refs[n_pieces + n_far :]
    near_refs, copied, refs = refs[-n_far - 1 : -1], refs[-1], refs[: -n_far - 1]
    copies = [pltpu.make_async_copy(a, b, copied.at[k]) for k, (a, b) in enumerate(zip(far_refs, near_refs))]
    for copy in copies:
        copy.start()
    (lengths, gain, w_in, conv_w, conv_b, w_x, w_dt, dt_b, alog, skip) = near_refs
    (trans_o, normed_o, gate_o, ext_o, conv_o, act_o, step_o, xproj_o, chunkf_o, sums_o, f_o, orders_o, column_o,
     valid, far, use, bbc, wx_o, wdt_o, a2, rows_o, conv_in) = refs[n_pieces:]
    to_row = row_of_place(rows)
    halos = [jnp.full((1, 1), -1.0, F32)] * (lags + 1)
    for p in range(n_pieces):
        row = dot(pieces[p][rows : rows + ORDER_ROWS, :rows], to_row)
        row = row[0:1] * 128.0 + row[1:2]
        orders_o[p : p + 1, :] = row
        behind = source(me, p, n_pieces) == me[0] - 1
        for k in range(1, lags + 1):
            r = (steps - k) * CHUNKS + CHUNKS - 1
            halos[k] = jnp.where(behind, row[:, r : r + 1], halos[k])
    sub = lax.broadcasted_iota(jnp.int32, (BLOCK, LANES), 0)
    extra = jnp.full((BLOCK, LANES), -1.0, F32)
    for k in range(1, lags + 1):
        extra = jnp.where(sub == k, halos[k], extra)
    digits = refs_own(pieces, me, rows, n_pieces)
    both = dot(to_row, digits, ((0,), (1,)))
    own = jnp.broadcast_to(both[:, 0:1] * 128.0 + both[:, 1:2], (rows, LANES))
    column_o[...] = own
    column = jnp.concatenate([own, extra], axis=0)
    trans = gather_rows(wide(column, rows), [p[0:rows, :] for p in pieces], me, rows)
    trans_o[...] = trans[:rows].astype(BF16)
    for copy in copies:
        copy.wait()
    meta = scalars(me, lengths, rows)
    bias, dt_bias = as_row(conv_b), as_row(dt_b)
    rows_o[0 : lags + 1, :] = conv_w[...]
    rows_o[lags + 1 : lags + 2, :] = as_row(skip)
    inv_rms = lax.rsqrt(jnp.mean(trans * trans, axis=1, keepdims=True) + EPSILON)
    normed = (trans * inv_rms * as_row(gain)).astype(BF16)
    normed_o[...] = normed[:rows]
    conv_in[...] = dot(normed, w_in[:, :inner]).astype(BF16).astype(F32)
    gate_o[...] = dot(normed[:rows], w_in[:, inner:])
    pad = lags * CHUNKS
    ext_o[pad : pad + rows, :] = conv_in[:rows, :]
    first_sub = lax.broadcasted_iota(jnp.int32, (CHUNKS, inner), 0) == 0
    for k in range(1, lags + 1):
        tile = conv_in[(steps - k) * CHUNKS : (steps - k + 1) * CHUNKS, :]
        before = conv_in[rows + k : rows + k + 1, :]
        ext_o[(lags - k) * CHUNKS : (lags - k + 1) * CHUNKS, :] = jnp.where(
            first_sub, before, pltpu.roll(tile, 1, 0)
        )
    for thin, full in ((w_x, wx_o), (w_dt, wdt_o)):
        blank = jnp.zeros((LANES - thin.shape[0], inner), F32)
        full[...] = jnp.concatenate([thin[...].astype(F32), blank], axis=0).astype(BF16)
    fill_valid(valid, meta, clouds, rows, lags)

    def conv_body(j, carry):
        r0 = pl.multiple_of(j * BLOCK, BLOCK)
        out = bias + conv_w[lags : lags + 1, :] * ext_o[pl.ds(r0 + pad, BLOCK), :]
        for k in range(1, lags + 1):
            ok = wide(valid[k - 1, pl.ds(r0, BLOCK), :], inner)
            shifted = ext_o[pl.ds(pl.multiple_of(r0 + pad - k * CHUNKS, CHUNKS), BLOCK), :]
            out = out + conv_w[lags - k : lags - k + 1, :] * shifted * ok
        conv_o[pl.ds(r0, BLOCK), :] = out
        act_o[pl.ds(r0, BLOCK), :] = (out * sigmoid(out)).astype(BF16)
        return carry

    lax.fori_loop(0, rows // BLOCK, conv_body, 0)
    xproj = dot(act_o[...], wx_o[...], ((1,), (1,)))
    xproj_o[...] = xproj
    step_o[...] = dot(xproj.astype(BF16), wdt_o[...])

    def step_body(j, carry):
        r0 = pl.multiple_of(j * BLOCK, BLOCK)
        pre = step_o[pl.ds(r0, BLOCK), :] + dt_bias
        step = jnp.maximum(pre, 0.0) + jnp.log1p(jnp.exp(-jnp.abs(pre)))
        step_o[pl.ds(r0, BLOCK), :] = step
        keep = wide(valid[0, pl.ds(r0, BLOCK), :], inner)
        distance = jnp.where(keep > 0.5, step, FAR)
        far[pl.ds(r0, BLOCK), :] = distance
        use[pl.ds(r0, BLOCK), :] = step * act_o[pl.ds(r0, BLOCK), :].astype(F32)
        return carry + distance[:CHUNKS] + distance[CHUNKS:]

    sums_o[...] = lax.fori_loop(0, rows // BLOCK, step_body, jnp.zeros((CHUNKS, inner), F32))
    fill_broadcast(bbc, xproj_o, rank, state)
    a2[...] = rates(alog) * LOG2E
    for lb in range(inner // LANES):
        ls = slice(lb * LANES, (lb + 1) * LANES)
        rate = [jnp.broadcast_to(a2[n : n + 1, ls], (CHUNKS, LANES)) for n in range(state)]

        def scan_body(i, states):
            r = pl.ds(pl.multiple_of(i * CHUNKS, CHUNKS), CHUNKS)
            distance, u = far[r, ls], use[r, ls]
            return tuple(
                jnp.exp2(distance * rate[n]) * states[n] + u * bbc[r, n * LANES : (n + 1) * LANES]
                for n in range(state)
            )

        zero = jnp.zeros((CHUNKS, LANES), F32)
        last = lax.fori_loop(0, steps, scan_body, (zero,) * state, unroll=2)
        for n in range(state):
            chunkf_o[lb, n * CHUNKS : (n + 1) * CHUNKS, :] = last[n]
    total = jnp.zeros((state, inner), F32)
    for c in range(CHUNKS):
        total = jnp.exp2(a2[...] * sums_o[c : c + 1, :]) * total + chunk_of(chunkf_o, c, state)
    f_o[...] = total


def back_kernel(sizes, n_pieces, me, *refs):
    rows, width, inner, rank, state, lags, clouds = sizes
    steps = rows // CHUNKS
    pieces = refs[:n_pieces]
    gate, far, xproj, a2, w_out, sums, f, column = refs[n_pieces : n_pieces + 8]
    n_out = (len(CUBE) - 4 if n_pieces == len(CUBE) else 1)
    dy_o, gg_o, gm, cbc, chunkb_o = refs[n_pieces + 8 : n_pieces + 13]
    carries_o = refs[n_pieces + 13 : n_pieces + 13 + n_out]
    near_out, copied = refs[n_pieces + 13 + n_out :]
    copy = pltpu.make_async_copy(w_out, near_out, copied)
    copy.start()
    trans_dy = gather_rows(wide(column[...], rows), [p[...] for p in pieces], me, rows).astype(BF16)
    dy_o[...] = trans_dy
    copy.wait()
    gg_o[...] = dot(trans_dy, near_out[...], ((1,), (1,)))

    def body(j, carry):
        r = pl.ds(pl.multiple_of(j * BLOCK, BLOCK), BLOCK)
        z = gate[r, :]
        gm[r, :] = gg_o[r, :] * (z * sigmoid(z))
        return carry

    lax.fori_loop(0, rows // BLOCK, body, 0)
    fill_broadcast(cbc, xproj, rank + state, state)
    for lb in range(inner // LANES):
        ls = slice(lb * LANES, (lb + 1) * LANES)
        rate = [jnp.broadcast_to(a2[n : n + 1, ls], (CHUNKS, LANES)) for n in range(state)]

        def scan_body(k, flows):
            r = pl.ds(pl.multiple_of((steps - 1 - k) * CHUNKS, CHUNKS), CHUNKS)
            distance, g = far[r, ls], gm[r, ls]
            return tuple(
                jnp.exp2(distance * rate[n]) * (flows[n] + g * cbc[r, n * LANES : (n + 1) * LANES])
                for n in range(state)
            )

        zero = jnp.zeros((CHUNKS, LANES), F32)
        last = lax.fori_loop(0, steps, scan_body, (zero,) * state, unroll=2)
        for n in range(state):
            chunkb_o[lb, n * CHUNKS : (n + 1) * CHUNKS, :] = last[n]
    total = jnp.zeros((state, inner), F32)
    for c in reversed(range(CHUNKS)):
        total = jnp.exp2(a2[...] * sums[c : c + 1, :]) * total + chunk_of(chunkb_o, c, state)
    passed = jnp.broadcast_to(jnp.sum(sums[...], axis=0, keepdims=True), (CHUNKS, inner))
    if n_out == 1:
        carries_o[0][:state, :] = f[...]
        carries_o[0][state : 2 * state, :] = total
        carries_o[0][2 * state :, :] = passed
        return
    for out, d in zip(carries_o, SENT):
        later = jnp.bitwise_xor(me[0], d) > me[0]
        out[:state, :] = jnp.where(later, f[...], total)
        out[state:, :] = passed


def core_of(me, devices):
    return jnp.bitwise_and(me, 1) if devices == len(CUBE) else jnp.int32(0)


def hold_carries(held, carries, me):
    n_pieces, size = len(carries), carries[0].shape[0]
    devices = len(CUBE) if n_pieces == len(CUBE) - 1 else n_pieces
    for p in range(n_pieces):
        whence = source(me, p + 1, devices) if devices > n_pieces else p
        held[pl.ds(pl.multiple_of(whence * size, CHUNKS), size), :] = carries[p][...]
    return devices


def scan_forward_kernel(sizes, n_pieces, me_ref, *refs):
    rows, width, inner, rank, state, lags, clouds = sizes
    steps = rows // CHUNKS
    carries = refs[:n_pieces]
    (trans_dy, normed, gg, gate, act, far, use, bbc, cbc, chunkf, sums, a2, consts, w_out) = refs[n_pieces : n_pieces + 14]
    blocks = inner // LANES
    states = refs[n_pieces + 14 : n_pieces + 14 + blocks]
    (branch_o, gz_o, keep_o, send_o) = refs[n_pieces + 14 + blocks : n_pieces + 18 + blocks]
    (mixed, sstart, gated, held) = refs[n_pieces + 18 + blocks :]
    me = me_ref[0]
    skips = consts[lags + 1 : lags + 2, :]
    size = carries[0].shape[0]
    devices = hold_carries(held, carries, me_ref)

    def ahead(s, flow):
        base = pl.multiple_of(s * size, CHUNKS)
        p_s = jnp.exp2(a2[...] * held[pl.ds(base + size - CHUNKS, 1), :])
        return jnp.where(s < me, p_s * flow + held[pl.ds(base, state), :], flow)

    now = lax.fori_loop(0, devices, ahead, jnp.zeros((state, inner), F32))
    for c in range(CHUNKS):
        set_chunk(sstart, c, now)
        now = jnp.exp2(a2[...] * sums[c : c + 1, :]) * now + chunk_of(chunkf, c, state)

    for lb in range(inner // LANES):
        ls = slice(lb * LANES, (lb + 1) * LANES)
        rate = [jnp.broadcast_to(a2[n : n + 1, ls], (CHUNKS, LANES)) for n in range(state)]
        begin = []
        for n in range(state):
            tile = sstart[lb, n * CHUNKS : (n + 1) * CHUNKS, :]
            states[lb][n, 0:CHUNKS, :] = tile
            begin.append(tile)

        def forward(i, now):
            r0 = pl.multiple_of(i * CHUNKS, CHUNKS)
            r = pl.ds(r0, CHUNKS)
            nxt = pl.ds(pl.multiple_of(r0 + CHUNKS, CHUNKS), CHUNKS)
            distance, u = far[r, ls], use[r, ls]
            new, out = [], None
            for n in range(state):
                value = jnp.exp2(distance * rate[n]) * now[n] + u * bbc[r, n * LANES : (n + 1) * LANES]
                states[lb][n, nxt, :] = value
                part = value * cbc[r, n * LANES : (n + 1) * LANES]
                out = part if out is None else out + part
                new.append(value)
            mixed[r, ls] = out
            return tuple(new)

        lax.fori_loop(0, steps, forward, tuple(begin), unroll=2)

    def gating(j, carry):
        r = pl.ds(pl.multiple_of(j * BLOCK, BLOCK), BLOCK)
        z, a = gate[r, :], act[r, :].astype(F32)
        s = sigmoid(z)
        m = mixed[r, :] + skips * a
        gated[r, :] = (m * (z * s)).astype(BF16)
        gz_o[r, :] = (gg[r, :] * m * s * (1.0 + z * (1.0 - s))).astype(BF16)
        return carry

    lax.fori_loop(0, rows // BLOCK, gating, 0)
    branch_o[...] = dot(gated[...], w_out[...]).astype(BF16)
    second = core_of(me, devices) == 1
    wout_g = dot(trans_dy[...], gated[...], ((0,), (0,))).astype(BF16)
    gate_g = dot(normed[...], gz_o[...], ((0,), (0,))).astype(BF16)
    keep_o[...] = jnp.where(second, gate_g, wout_g)
    send_o[...] = jnp.where(second, wout_g, gate_g)


def adjoint_carries_kernel(sizes, n_pieces, me_ref, *refs):
    rows, width, inner, rank, state, lags, clouds = sizes
    carries = refs[:n_pieces]
    chunkb, sums, a2, gstart, held = refs[n_pieces:]
    me = me_ref[0]
    size = carries[0].shape[0]
    back = size - CHUNKS - state
    devices = hold_carries(held, carries, me_ref)

    def behind(k, flow):
        s = devices - 1 - k
        base = pl.multiple_of(s * size, CHUNKS)
        p_s = jnp.exp2(a2[...] * held[pl.ds(base + size - CHUNKS, 1), :])
        return jnp.where(s > me, p_s * flow + held[pl.ds(pl.multiple_of(base + back, CHUNKS), state), :], flow)

    now = lax.fori_loop(0, devices, behind, jnp.zeros((state, inner), F32))
    for c in reversed(range(CHUNKS)):
        set_chunk(gstart, c, now)
        now = jnp.exp2(a2[...] * sums[c : c + 1, :]) * now + chunk_of(chunkb, c, state)


def scan_backward_kernel(sizes, *refs):
    rows, width, inner, rank, state, lags, clouds = sizes
    steps = rows // CHUNKS
    states, refs = refs[: inner // LANES], refs[inner // LANES :]
    (gstart, far, use, bbc, cbc, gm, step, act, conv, valid, a2, conv_w, w_x, w_dt) = refs[:14]
    (gconv, rim_o, gpre, gxproj_o, galog_o) = refs[14:19]
    (gs, lamb, gb, gc) = refs[19:]
    skips = conv_w[lags + 1 : lags + 2, :]
    group, pair = 3, 4
    for lg in range(inner // LANES // group):
        lanes = [slice((lg * group + k) * LANES, (lg * group + k + 1) * LANES) for k in range(group)]
        for ng in range(state // pair):
            ns = [ng * pair + k for k in range(pair)]
            rate = [[jnp.broadcast_to(a2[n : n + 1, ls], (CHUNKS, LANES)) for ls in lanes] for n in ns]
            begin = [gstart[lg * group + k, n * CHUNKS : (n + 1) * CHUNKS, :] for n in ns for k in range(group)]
            zero = jnp.zeros((CHUNKS, LANES), F32)

            def backward(k, carry):
                flows, sums_a = carry
                r0 = pl.multiple_of((steps - 1 - k) * CHUNKS, CHUNKS)
                r = pl.ds(r0, CHUNKS)
                nxt = pl.ds(pl.multiple_of(r0 + CHUNKS, CHUNKS), CHUNKS)
                gs_t = [None] * group
                lamb_t = [None] * group
                g_t = [gm[r, ls] for ls in lanes]
                u_t = [use[r, ls] for ls in lanes]
                d_t = [step[r, ls] for ls in lanes]
                f_t = [far[r, ls] for ls in lanes]
                new_flows, new_sums = [], []
                for q, n in enumerate(ns):
                    b = bbc[r, n * LANES : (n + 1) * LANES]
                    c = cbc[r, n * LANES : (n + 1) * LANES]
                    gb_t = gc_t = None
                    for x, ls in enumerate(lanes):
                        lam = g_t[x] * c + flows[q * group + x]
                        flow = jnp.exp2(f_t[x] * rate[q][x]) * lam
                        part = flow * states[lg * group + x][n, r, :]
                        one, two = part * rate[q][x], lam * b
                        gs_t[x] = one if gs_t[x] is None else gs_t[x] + one
                        lamb_t[x] = two if lamb_t[x] is None else lamb_t[x] + two
                        three, four = lam * u_t[x], g_t[x] * states[lg * group + x][n, nxt, :]
                        gb_t = three if gb_t is None else gb_t + three
                        gc_t = four if gc_t is None else gc_t + four
                        new_flows.append(flow)
                        new_sums.append(sums_a[q * group + x] + part * d_t[x])
                    nl = slice(n * LANES, (n + 1) * LANES)
                    if lg == 0:
                        gb[r, nl] = gb_t
                        gc[r, nl] = gc_t
                    else:
                        gb[r, nl] += gb_t
                        gc[r, nl] += gc_t
                for x, ls in enumerate(lanes):
                    if ng == 0:
                        gs[r, ls] = gs_t[x]
                        lamb[r, ls] = lamb_t[x]
                    else:
                        gs[r, ls] += gs_t[x]
                        lamb[r, ls] += lamb_t[x]
                return tuple(new_flows), tuple(new_sums)

            flows, sums_a = lax.fori_loop(
                0, steps, backward, (tuple(begin), (zero,) * (pair * group))
            )
            for q, n in enumerate(ns):
                for x, ls in enumerate(lanes):
                    galog_o[n : n + 1, ls] = (
                        jnp.sum(sums_a[q * group + x], axis=0, keepdims=True) * rate[q][x][0:1] * (1.0 / LOG2E)
                    )
    col = lax.broadcasted_iota(jnp.int32, (state * LANES, LANES), 1)
    row = lax.div(lax.broadcasted_iota(jnp.int32, (state * LANES, LANES), 0), LANES)
    pick_b = (col == row + rank).astype(F32).astype(BF16)
    pick_c = (col == row + rank + state).astype(F32).astype(BF16)

    def lane_sums(ref, pick):
        whole = ref[...]
        high = whole.astype(BF16)
        low = (whole - high.astype(F32)).astype(BF16)
        return dot(high, pick) + dot(low, pick)

    grad_bc = lane_sums(gb, pick_b) + lane_sums(gc, pick_c)

    def pre_body(j, carry):
        r = pl.ds(pl.multiple_of(j * BLOCK, BLOCK), BLOCK)
        grad_step = gs[r, :] * (1.0 / LOG2E) + lamb[r, :] * act[r, :].astype(F32)
        gpre[r, :] = (grad_step * (1.0 - jnp.exp(-step[r, :]))).astype(BF16)
        return carry

    lax.fori_loop(0, rows // BLOCK, pre_body, 0)
    grad_xproj = (dot(gpre[...], w_dt[...], ((1,), (1,))) + grad_bc).astype(BF16)
    gxproj_o[...] = grad_xproj
    gs[...] = dot(grad_xproj, w_x[...])

    def conv_body(j, carry):
        r = pl.ds(pl.multiple_of(j * BLOCK, BLOCK), BLOCK)
        grad_act = gm[r, :] * skips + lamb[r, :] * step[r, :] + gs[r, :]
        v = conv[r, :]
        s = sigmoid(v)
        gconv[r, :] = grad_act * (s * (1.0 + v * (1.0 - s)))
        return carry

    lax.fori_loop(0, rows // BLOCK, conv_body, 0)
    rim_o[...] = jnp.zeros((CHUNKS, inner), F32)
    for b in range(1, lags + 1):
        total = jnp.zeros((1, inner), F32)
        for k in range(b, lags + 1):
            total = total + masked_tile(gconv, valid, conv_w, k - b, k, lags)[0:1]
        rim_o[b : b + 1, :] = total


def masked_tile(gconv, valid, conv_w, i, k, lags):
    r = pl.ds(pl.multiple_of(i * CHUNKS, CHUNKS), CHUNKS)
    tile = gconv[r, :] * conv_w[lags - k : lags - k + 1, :]
    return tile if k == 0 else tile * wide(valid[k - 1, r, :], tile.shape[1])


def small_kernel(sizes, gpre, gxproj, xproj, act, gconv, ext, valid, gm, conv_w, galog, small_o, gci_o):
    rows, width, inner, rank, state, lags, clouds = sizes
    steps = rows // CHUNKS

    def spread(i, carry):
        total = masked_tile(gconv, valid, conv_w, i, 0, lags)
        for k in range(1, lags + 1):
            total = total + masked_tile(gconv, valid, conv_w, i + k, k, lags)
        gci_o[pl.ds(pl.multiple_of(i * CHUNKS, CHUNKS), CHUNKS), :] = total
        return carry

    lax.fori_loop(0, steps - lags, spread, 0)
    sub = lax.broadcasted_iota(jnp.int32, (CHUNKS, inner), 0)
    for i in range(steps - lags, steps):
        total = masked_tile(gconv, valid, conv_w, i, 0, lags)
        for k in range(1, lags + 1):
            if i + k < steps:
                total = total + masked_tile(gconv, valid, conv_w, i + k, k, lags)
            else:
                moved = pltpu.roll(masked_tile(gconv, valid, conv_w, i + k - steps, k, lags), CHUNKS - 1, 0)
                total = total + jnp.where(sub == CHUNKS - 1, 0.0, moved)
        gci_o[i * CHUNKS : (i + 1) * CHUNKS, :] = total

    def sum_body(j, carry):
        r0 = pl.multiple_of(j * BLOCK, BLOCK)
        r = pl.ds(r0, BLOCK)
        grad = gconv[r, :]
        parts = [gm[r, :] * act[r, :].astype(F32), gpre[r, :].astype(F32), grad]
        for k in reversed(range(lags + 1)):
            masked = grad if k == 0 else grad * wide(valid[k - 1, r, :], inner)
            parts.append(masked * ext[pl.ds(pl.multiple_of(r0 + (lags - k) * CHUNKS, CHUNKS), BLOCK), :])
        return tuple(total + part[:CHUNKS] + part[CHUNKS:] for total, part in zip(carry, parts))

    sums = lax.fori_loop(0, rows // BLOCK, sum_body, (jnp.zeros((CHUNKS, inner), F32),) * (lags + 4))
    small_o[0:state, :] = galog[...]
    at = state
    small_o[at : at + rank + 2 * state, :] = dot(gxproj[...], act[...], ((0,), (0,)))[: rank + 2 * state]
    at += rank + 2 * state
    small_o[at : at + rank, :] = dot(xproj[...].astype(BF16), gpre[...], ((0,), (0,)))[:rank]
    at += rank
    for k, part in enumerate(sums):
        small_o[at + k : at + k + 1, :] = jnp.sum(part, axis=0, keepdims=True)
    at += len(sums)
    small_o[at:, :] = jnp.zeros((small_o.shape[0] - at, inner), F32)


def final_kernel(sizes, devices, me, trans, normed, gci, gz, rim, small, gain, w_in, back_o, keep_o, send_o, both):
    rows, width, inner, rank, state, lags, clouds = sizes
    steps = rows // CHUNKS
    r = lax.broadcasted_iota(jnp.int32, (rows, inner), 0)
    total = gci[...]
    for k in range(1, lags + 1):
        total = total + jnp.where(r == (steps - k) * CHUNKS + CHUNKS - 1, rim[k : k + 1, :], 0.0)
    grad_ci = total.astype(BF16)
    grad_z = gz[...]
    grad_normed = dot(grad_ci, w_in[:, :inner], ((1,), (1,))) + dot(grad_z, w_in[:, inner:], ((1,), (1,)))
    x = trans[...].astype(F32)
    inv_rms = lax.rsqrt(jnp.mean(x * x, axis=1, keepdims=True) + EPSILON)
    scaled = grad_normed * as_row(gain)
    back_o[...] = (
        inv_rms * scaled
        - inv_rms * inv_rms * inv_rms * x * jnp.mean(scaled * x, axis=1, keepdims=True)
    ).astype(BF16)
    both[0:width, :] = dot(normed[...], grad_ci, ((0,), (0,))).astype(BF16)
    gain_row = jnp.sum(grad_normed * x * inv_rms, axis=0, keepdims=True)
    gain_row = jnp.concatenate([gain_row, jnp.zeros((1, inner - width), F32)], axis=1)
    n_small = small.shape[0]
    last = lax.broadcasted_iota(jnp.int32, (n_small, inner), 0) == n_small - 1
    both[width : width + n_small, :] = jnp.where(last, gain_row, small[...]).astype(BF16)
    half = keep_o.shape[0]
    core = core_of(me[0], devices)
    keep_o[...] = both[pl.ds(pl.multiple_of(core * half, BLOCK), half), :]
    send_o[...] = both[pl.ds(pl.multiple_of((1 - core) * half, BLOCK), half), :]


def small_rows(sizes):
    rows, width, inner, rank, state, lags, clouds = sizes
    return state + (rank + 2 * state) + rank + 3 + lags + 1 + 1


def halves_kernel(me, kept, got, own_o, *sent_o):
    part = own_o.shape[0]
    chip = lax.div(me[0], 2)
    for d, out in enumerate((own_o,) + sent_o):
        r = pl.ds(pl.multiple_of(jnp.bitwise_xor(chip, d) * part, BLOCK), part)
        out[...] = (kept[r, :].astype(F32) + got[r, :].astype(F32)).astype(BF16)


def beside(out, rows):
    half, width = rows.shape[0] // 2, rows.shape[1]
    out[0:half, 0:width] = rows[0:half, :]
    out[0:half, width:] = rows[half:, :]


def unfold(piece, rows, width):
    if piece.shape == (rows, width):
        return piece[...]
    half = rows // 2
    return jnp.concatenate([piece[0:half, 0:width], piece[0:half, width : 2 * width]], axis=0)


def halves_beside_kernel(me, kept, got, rows, own_o, *sent_o):
    part = own_o.shape[0]
    half = rows.shape[0] // 2
    chip = lax.div(me[0], 2)
    for d, out in enumerate((own_o,) + sent_o):
        r = pl.ds(pl.multiple_of(jnp.bitwise_xor(chip, d) * part, BLOCK), part)
        total = (kept[r, :].astype(F32) + got[r, :].astype(F32)).astype(BF16)
        if d == 0:
            out[...] = total
        else:
            beside(out, rows)
            out[half:, :] = total


def sum_kernel(a, b, c, d, out):
    one, two, three, four = (x[x.shape[0] - a.shape[0] :, :].astype(F32) for x in (a, b, c, d))
    out[...] = ((one + two) + (three + four)).astype(BF16)


def sum_beside_kernel(a, b, c, d, rows, out):
    beside(out, rows)
    sum_kernel(a, b, c, d, out.at[pl.ds(rows.shape[0] // 2, a.shape[0])])


def unpack_kernel(sizes, n_pieces, me, *refs):
    rows, width, inner, rank, state, lags, clouds = sizes
    one, two = refs[:n_pieces], refs[n_pieces : 2 * n_pieces]
    (gain_o, win_o, taps_o, convb_o, wx_o, wdt_o, dtb_o, alog_o, skip_o, wout_o) = refs[2 * n_pieces : 2 * n_pieces + 10]
    all_one, all_two = refs[2 * n_pieces + 10 :]
    for pieces, whole in ((one, all_one), (two, all_two)):
        part = whole.shape[0] // n_pieces
        for p, piece in enumerate(pieces):
            s = source(me, p, n_pieces)
            if n_pieces == len(CUBE):
                s = jnp.bitwise_and(s, 1) * (n_pieces // 2) + lax.div(s, 2)
            whole[pl.ds(pl.multiple_of(s * part, BLOCK), part), :] = piece[piece.shape[0] - part :, :]
    wout_o[...] = all_one[0:width, :].astype(F32).T
    win_o[:, inner:] = all_one[width : 2 * width, :].astype(F32)
    win_o[:, :inner] = all_two[0:width, :].astype(F32)
    n_small = small_rows(sizes)
    small = all_two[width : width + n_small, :].astype(F32)
    alog_o[...] = small[0:state]
    at = state
    wx_o[...] = small[at : at + rank + 2 * state]
    at += rank + 2 * state
    wdt_o[...] = small[at : at + rank]
    at += rank
    for k, out in enumerate((skip_o, dtb_o, convb_o)):
        out[...] = small[at + k : at + k + 1].reshape(inner)
    at += 3
    taps_o[...] = small[at : at + lags + 1]
    gain_o[...] = small[n_small - 1 : n_small, :width].reshape(width)


def place_kernel(rows, n_pieces, me, here, orders, *refs):
    pieces, out = refs[:n_pieces], refs[n_pieces]
    place = (me[0] * rows + lax.broadcasted_iota(jnp.int32, (rows, rows), 0)).astype(F32)
    mine = [(orders[p : p + 1, :] == place).astype(F32).astype(BF16) for p in range(n_pieces)]
    moved = dot(jnp.concatenate(mine, axis=1), jnp.concatenate([unfold(p, rows, out.shape[1]) for p in pieces], axis=0))
    out[...] = (here[...].astype(F32) + moved).astype(BF16)


def call(kernel, outs, scratch, n_smem, name, room, time=1.0, far_ins=()):
    vmem = pl.BlockSpec(memory_space=pltpu.VMEM)
    smem = pl.BlockSpec(memory_space=pltpu.SMEM)
    anywhere = pl.BlockSpec(memory_space=pltpu.HBM)

    def run(*args):
        args = [pltpu.with_memory_space_constraint(v, pltpu.HBM) if k in far_ins else v for k, v in enumerate(args)]
        return pl.pallas_call(
            kernel,
            out_shape=[jax.ShapeDtypeStruct(*part) if isinstance(part, tuple) else part for part in outs],
            in_specs=[smem if k < n_smem else anywhere if k in far_ins else vmem for k in range(len(args))],
            out_specs=[vmem] * len(outs),
            scratch_shapes=[pltpu.VMEM(*part) if isinstance(part, tuple) else part for part in scratch],
            compiler_params=pltpu.CompilerParams(vmem_limit_bytes=room * MIB),
            cost_estimate=pl.CostEstimate(
                flops=1, bytes_accessed=1, transcendentals=0
            ),
            name=name,
        )(*args)

    return run


def after(value, *others):
    return lax.optimization_barrier((value, others))[0]


def swap(block, axis, distance):
    devices = lax.axis_size(axis)
    return lax.ppermute(block, axis, [(i, i ^ distance) for i in range(devices)])


def spread_pieces(block, axis, then=None):
    devices = lax.axis_size(axis)
    if devices == len(CUBE):
        across = [block] + [swap(block, axis, d) for d in CUBE[1:4]]
        if then is not None:
            then = after(then, across[3])
        pieces = across + [swap(part, axis, 1) for part in across]
    else:
        whole = lax.all_gather(block, axis)
        pieces = [whole[i] for i in range(devices)]
    return pieces if then is None else (pieces, then)


def spread_carries(blocks, axis):
    if len(blocks) == 1:
        return spread_pieces(blocks[0], axis)
    across = [swap(block, axis, d) for block, d in zip(blocks, SENT)]
    return across[:3] + [across[3]] + [swap(part, axis, 1) for part in across[:3]]


def from_behind(block, axis, distance):
    devices = range(lax.axis_size(axis))
    route = [(i - distance, i) for i in devices if i - distance in devices]
    return lax.ppermute(block, axis, route)


def shards(
    tokens,
    lengths,
    order,
    norm_gain,
    w_in,
    conv_weight,
    conv_bias,
    w_x,
    w_dt,
    dt_bias,
    a_log,
    d_skip,
    w_out,
    cotangent,
):
    rows, width = tokens.shape[1:]
    inner, rank, state, taps = w_out.shape[0], w_dt.shape[0], a_log.shape[1], conv_weight.shape[1]
    lags, clouds, steps = taps - 1, lengths.shape[1], rows // CHUNKS
    sizes = (rows, width, inner, rank, state, lags, clouds)
    devices = lax.axis_size("seq")
    me = lax.axis_index("seq").astype(jnp.int32)[None]
    here_x, here_dy = tokens[0], cotangent[0]
    digits = jnp.concatenate([order >> 7, order & 127], axis=0).astype(BF16)
    digits = jnp.pad(digits, ((0, ORDER_ROWS - 2), (0, width - rows)))
    weights = (lengths, norm_gain, w_in, conv_weight.T, conv_bias, w_x.T, w_dt, dt_bias, a_log.T, d_skip)
    pieces_x, here_dy = spread_pieces(jnp.concatenate([here_x, digits], axis=0), "seq", then=here_dy)
    pieces_dy = spread_pieces(here_dy, "seq")
    n = len(pieces_x)
    big, lane = (rows, inner), (rows, LANES)
    carried = (inner // LANES, state * CHUNKS, LANES)
    spread = (rows, state * LANES)
    ext_rows = rows + lags * CHUNKS
    (trans, normed, gate, ext, conv, act, step, xproj, chunkf, sums, f, orders, column, valid, far, use, bbc, w_x_pad, w_dt_pad, a2, row_consts) = call(
        functools.partial(pre_kernel, sizes, n, len(weights)),
        [
            ((rows, width), BF16),
            ((rows, width), BF16),
            (big, F32),
            ((ext_rows, inner), F32),
            (big, F32),
            (big, BF16),
            (big, F32),
            (lane, F32),
            (carried, F32),
            ((CHUNKS, inner), F32),
            ((state, inner), F32),
            ((n, rows), F32),
            (lane, F32),
            ((lags, rows, LANES), F32),
            (big, F32),
            (big, F32),
            (spread, F32),
            ((LANES, inner), BF16),
            ((LANES, inner), BF16),
            ((state, inner), F32),
            ((lags + 2, inner), F32),
        ],
        [((rows + BLOCK, inner), F32), pltpu.SMEM(lengths.shape, jnp.int32)]
        + [(v.shape, v.dtype) for v in weights[1:]]
        + [pltpu.SemaphoreType.DMA((len(weights),))],
        1,
        "forward_local",
        24,
        9,
        far_ins=tuple(range(n + 1, n + 1 + len(weights))),
    )(me, *pieces_x, *weights)
    carry_rows = (state + CHUNKS, 2 * state + CHUNKS)[n != len(CUBE)]
    n_sent = (len(SENT), 1)[n != len(CUBE)]
    trans_dy, gg, gm, cbc, chunkb, *carries = call(
        functools.partial(back_kernel, sizes, n),
        [((rows, width), BF16), (big, F32), (big, F32), (spread, F32), (carried, F32)]
        + [((carry_rows, inner), F32)] * n_sent,
        [(w_out.shape, w_out.dtype), pltpu.SemaphoreType.DMA],
        1,
        "backward_local",
        20,
        7,
        far_ins=(n + 5,),
    )(me, *pieces_dy, gate, far, xproj, a2, w_out, sums, f, column)
    carries = spread_carries(carries, "seq")
    n_small = small_rows(sizes)
    held = ((n * carry_rows, inner), F32)
    kept = [pltpu.VMEM((state, rows + CHUNKS, LANES), F32)] * (inner // LANES)
    *states, branch, gz, keep, send = call(
        functools.partial(scan_forward_kernel, sizes, len(carries)),
        [*kept, ((rows, width), BF16), (big, BF16), ((width, inner), BF16), ((width, inner), BF16)],
        [(big, F32), (carried, F32), (big, BF16), held],
        1,
        "scan_forward",
        18,
        7,
    )(me, *carries, trans_dy, normed, gg, gate, act, far, use, bbc, cbc, chunkf, sums, a2, row_consts, w_out)
    cube = n == len(CUBE) and lax.axis_size("dp") == 4
    first = (keep, send)
    half_one, half_two = width, -(-(width + n_small) // (8 * BLOCK)) * (4 * BLOCK)
    got = swap(send, "seq", 1) if cube else None
    (gstart,) = call(
        functools.partial(adjoint_carries_kernel, sizes, len(carries)),
        [(carried, F32)],
        [held],
        1,
        "adjoint_carries",
        8,
        1.5,
    )(me, *carries, chunkb, sums, a2)
    if cube:
        part_one = half_one // 4
        beside_one = ((rows // 2 + part_one, inner), BF16)
        own_one, *sent = call(
            halves_beside_kernel, [((part_one, inner), BF16)] + [beside_one] * 3, [], 1, "add_halves_beside_rows", 8
        )(me, keep, got, branch)
        away_one = [swap(block, "seq", d) for block, d in zip(sent, SENT)]
    gconv, rim, gpre, gxproj, galog = call(
        functools.partial(scan_backward_kernel, sizes),
        [(big, F32), ((CHUNKS, inner), F32), (big, BF16), (lane, BF16), ((state, inner), F32)],
        [(big, F32), (big, F32), (spread, F32), (spread, F32)],
        0,
        "scan_backward",
        20,
        14,
    )(*[pltpu.with_memory_space_constraint(part, pltpu.VMEM) for part in states], gstart, far, use, bbc, cbc, gm, step, act, conv, valid, a2, row_consts, w_x_pad, w_dt_pad)
    rim = from_behind(rim, "seq", -1)
    small, gci = call(
        functools.partial(small_kernel, sizes),
        [((n_small, inner), F32), (big, F32)],
        [],
        0,
        "small_grads",
        16,
        1.6,
    )(after(gpre, *away_one) if cube else gpre, gxproj, xproj, act, gconv, ext, valid, gm, row_consts, galog)
    back, keep, send = call(
        functools.partial(final_kernel, sizes, devices),
        [((rows, width), BF16), ((half_two, inner), BF16), ((half_two, inner), BF16)],
        [((2 * half_two, inner), BF16)],
        1,
        "input_projection_grads",
        16,
    )(me, trans, normed, gci, gz, rim, small, norm_gain, w_in)
    place = call(functools.partial(place_kernel, rows, n), [((rows, width), BF16)], [], 1, "to_hilbert", 12, 1.4)
    if cube:
        part_two = half_two // 4
        adds_one = call(sum_kernel, [((part_one, inner), BF16)], [], 0, "add_parts", 4)
        adds_two = call(sum_kernel, [((part_two, inner), BF16)], [], 0, "add_parts", 4)
        got = swap(send, "seq", 1)
        (one,) = adds_one(own_one, *away_one)
        pieces_b = [branch, *away_one]
        pieces_b += [swap(part, "seq", 1) for part in pieces_b]
        own_two, *sent = call(halves_kernel, [((part_two, inner), BF16)] * 4, [], 1, "add_halves", 4)(me, keep, got)
        away_two = [swap(block, "seq", d) for block, d in zip(sent, SENT)]
        one = after(one, own_two)
        z_one = [swap(one, "dp", d) for d in (1, 2, 3)]
        (two,) = adds_two(own_two, *away_two)
        z_two = [swap(two, "dp", d) for d in (1, 2, 3)]
        (output,) = place(me, after(here_x, two), orders, *pieces_b)
        (one,) = call(sum_beside_kernel, [beside_one], [], 0, "add_parts_beside_rows", 8)(
            one, *z_one, after(back, two)
        )
        pieces_g = spread_pieces(one, "seq")
        (two,) = adds_two(two, *z_two)
        totals = (pieces_g, spread_pieces(two, "seq"))
    else:
        totals = [
            [lax.psum(half.astype(F32), ("dp", "seq")).astype(BF16) for half in halves]
            for halves in (first, (keep, send))
        ]
        (output,) = place(me, here_x, orders, *spread_pieces(branch, "seq"))
        pieces_g = spread_pieces(back, "seq")
    (input_grad,) = place(me, here_dy, orders, *pieces_g)
    weights = call(
        functools.partial(unpack_kernel, sizes, len(totals[0])),
        [
            ((width,), F32),
            ((width, 2 * inner), F32),
            ((taps, inner), F32),
            ((inner,), F32),
            ((rank + 2 * state, inner), F32),
            ((rank, inner), F32),
            ((inner,), F32),
            ((state, inner), F32),
            ((inner,), F32),
            ((inner, width), F32),
        ],
        [((2 * half_one, inner), BF16), ((2 * half_two, inner), BF16)],
        1,
        "unpack_sums",
        24,
        2.4,
    )(me, *totals[0], *totals[1])
    turned = [v.T if v.ndim == 2 and v.shape[1] == inner and v.shape[0] != rank else v for v in weights]
    return (output[None], input_grad[None], *turned)


def solution(mesh):
    placed = (
        P("dp", "seq", None),
        P("dp", None),
        P("dp", "seq"),
        P(),
        P(),
        P(),
        P(),
        P(),
        P(),
        P(),
        P(),
        P(),
        P(),
        P("dp", "seq", None),
    )
    return jax.shard_map(
        shards,
        mesh=mesh,
        in_specs=placed,
        out_specs=(
            P("dp", "seq", None),
            P("dp", "seq", None),
            P(),
            P(),
            P(),
            P(),
            P(),
            P(),
            P(),
            P(),
            P(),
            P(),
        ),
        check_vma=False,
    )
```

time: 198 us -> 146 us (0.74)
  Pallas kernels: 70.3 us -> 41.3 us
  local copies, waits for them, and re-layouts: 21.5 us -> 0.03 us
  starting transfers between devices: 54 us -> 40.5 us
  waiting for transfers between devices: 48.5 us -> 60.9 us
    pallas_call x13 -> x16, Pallas kernels: 70.3 us -> 41.3 us  [run(): pl.pallas_call(kernel, out_shape=[jax.ShapeDtypeStruct(*part) if isinstan...]
    ppermute x63 -> x53, starting transfers between devices: 52.6 us -> 38.9 us  [swap(): lax.ppermute(block, axis, [(i, i ^ distance) for i in range(devices)])]
    ppermute x63 -> x53, waiting for transfers between devices: 48.5 us -> 60.9 us  [swap(): lax.ppermute(block, axis, [(i, i ^ distance) for i in range(devices)])]
    unnamed x135 -> x10, local copies, waits for them, and re-layouts: 6.36 us -> 0.03 us
    broadcast_in_dim x4 -> x0, local copies, waits for them, and re-layouts: 4.36 us -> none  [shards(): row = lambda v: v[None, :]]
    transpose x3 -> x0, local copies, waits for them, and re-layouts: 4.36 us -> none  [shards(): return (output[None], input_grad[None], small[n_small - 1, :width], win_g...]
    slice x3 -> x0, local copies, waits for them, and re-layouts: 4.3 us -> none  [the longest x2 3 us: shards(): small[at[k]:at[k + 1]]]
    pad x2 -> x0, local copies, waits for them, and re-layouts: 2.18 us -> none  [the longest x1 1.46 us: shards(): w_dt_pad = jnp.pad(w_dt, ((0, LANES - rank), (0, 0)))]
  transfers between devices with their start and end apart: 64 -> 54, of which waited for: 18 -> 21; matrix products, arithmetic and copies ran while one was open for 4% -> 0% of each run, Pallas kernels for 16% -> 18%
where the time goes in v2:
time: 146 us; the launch traced here: 145 us
  waiting for transfers between devices  60.9 us (42%)
  Pallas kernels  41.3 us (28%)
  starting transfers between devices  40.5 us (28%)
  other arithmetic  1.69 us (1%)
    ppermute x53, waiting for transfers between devices, swap(): lax.ppermute(block, axis, [(i, i ^ distance) for i in range(devices)])  60.9 us
    pallas_call x16, Pallas kernels, run(): pl.pallas_call(kernel, out_shape=[jax.ShapeDtypeStruct(*part) if isinstan...  41.3 us
    ppermute x53, starting transfers between devices, swap(): lax.ppermute(block, axis, [(i, i ^ distance) for i in range(devices)])  38.9 us
  transfers between devices with their start and end apart: 54, of which 21 were waited for; matrix products, arithmetic and copies ran while one was open for 0% of the time, Pallas kernels for 18%

profile of v2, /device:TPU:0, one launch (start us, length us, event | category | flops | bytes accessed | tf_op | source)
XLA Modules:
  0.0 145.3 jit_solution(5991729778043717907)
XLA Ops:
  2.3 4.0 %collective-permute-start.2 = (bf16[272,384]{1,0:T(8,128)(2,1)S(1)}, bf16[272,384]{1,0:T(8,128)(2,1)S(1)}, u32[]{:S(2)}, u32[]{:S(2)}) collective-permute-start(bf16[272,384]{1,0:T(8,128)(2,1)S(1)} %pad_maximum_fusion.refs_0_), channel_id=1, source_target_pairs={{0,6},{1,7},{2,4},{3,5},{4,2},{5,3},{6,0},{7,1},{8,14},{9,15},{10,... | collective-permute-start | bytes 626696 | tf_op jit(solution)/shard_map/ppermute | solution.py:701
  7.0 5.1 %collective-permute-done.2.refs_3_ = bf16[272,384]{1,0:T(8,128)(2,1)S(1)} collective-permute-done((bf16[272,384]{1,0:T(8,128)(2,1)S(1)}, bf16[272,384]{1,0:T(8,128)(2,1)S(1)}, u32[]{:S(2)}, u32[]{:S(2)}) %collective-permute-start.2) | collective-permute-done | bytes 208928 | tf_op jit(solution)/shard_map/ppermute | solution.py:701
  12.1 3.2 %collective-permute-start.9 = (bf16[256,384]{1,0:T(8,128)(2,1)}, bf16[256,384]{1,0:T(8,128)(2,1)S(1)}, u32[]{:S(2)}, u32[]{:S(2)}) collective-permute-start(bf16[256,384]{1,0:T(8,128)(2,1)} %bitcast.11), channel_id=1, source_target_pairs={{0,6},{1,7},{2,4},{3,5},{4,2},{5,3},{6,0},{7,1},{8,14},{9,15},{10,... | collective-permute-start | bytes 589832 | tf_op jit(solution)/shard_map/ppermute | solution.py:701
  16.5 2.3 %collective-permute-start.8 = (bf16[256,384]{1,0:T(8,128)(2,1)}, bf16[256,384]{1,0:T(8,128)(2,1)S(1)}, u32[]{:S(2)}, u32[]{:S(2)}) collective-permute-start(bf16[256,384]{1,0:T(8,128)(2,1)} %bitcast.12), channel_id=1, source_target_pairs={{0,4},{1,5},{2,6},{3,7},{4,0},{5,1},{6,2},{7,3},{8,12},{9,13},{10,... | collective-permute-start | bytes 589832 | tf_op jit(solution)/shard_map/ppermute | solution.py:701
  20.2 4.3 %collective-permute-done.8.refs_2_ = bf16[256,384]{1,0:T(8,128)(2,1)S(1)} collective-permute-done((bf16[256,384]{1,0:T(8,128)(2,1)}, bf16[256,384]{1,0:T(8,128)(2,1)S(1)}, u32[]{:S(2)}, u32[]{:S(2)}) %collective-permute-start.8) | collective-permute-done | bytes 196640 | tf_op jit(solution)/shard_map/ppermute | solution.py:701
  24.6 1.5 %collective-permute-done.7.refs_1_ = bf16[256,384]{1,0:T(8,128)(2,1)S(1)} collective-permute-done((bf16[256,384]{1,0:T(8,128)(2,1)}, bf16[256,384]{1,0:T(8,128)(2,1)S(1)}, u32[]{:S(2)}, u32[]{:S(2)}) %collective-permute-start.7) | collective-permute-done | bytes 196640 | tf_op jit(solution)/shard_map/ppermute | solution.py:701
  26.6 9.1 %forward_local.1 = (bf16[256,384]{1,0:T(8,128)(2,1)S(1)}, bf16[256,384]{1,0:T(8,128)(2,1)S(1)}, f32[256,768]{1,0:T(8,128)S(1)}, f32[280,768]{1,0:T(8,128)S(1)}, ...) custom-call(s32[1]{0:T(128)} %bitcast.me.me_ref, ...), custom_call_target="tpu_custom_call" | custom-call | flops 1 | bytes 1 | tf_op jit(solution)/shard_map/forward_local/pallas_call | solution.py:679
  35.7 6.1 %backward_local.1 = (bf16[256,384]{1,0:T(8,128)(2,1)S(1)}, f32[256,768]{1,0:T(8,128)S(1)}, f32[256,768]{1,0:T(8,128)S(1)}, f32[256,2048]{1,0:T(8,128)S(1)}, f32[...) custom-call(s32[1]{0:T(128)} %bitcast.me.me_ref, ...), custom_call_target="tpu_custom_call" | custom-call | flops 1 | bytes 1 | tf_op jit(solution)/shard_map/backward_local/pallas_call | solution.py:679
  44.0 1.4 collective-permute-start.16
  45.4 1.5 %collective-permute-done.14.refs_0_ = f32[24,768]{1,0:T(8,128)S(1)} collective-permute-done((f32[24,768]{1,0:T(8,128)S(1)}, f32[24,768]{1,0:T(8,128)S(1)}, u32[]{:S(2)}, u32[]{:S(2)}) %collective-permute-start.14) | collective-permute-done | bytes 73760 | tf_op jit(solution)/shard_map/ppermute | solution.py:701
  47.4 1.8 %collective-permute-done.16.refs_2_ = f32[24,768]{1,0:T(8,128)S(1)} collective-permute-done((f32[24,768]{1,0:T(8,128)S(1)}, f32[24,768]{1,0:T(8,128)S(1)}, u32[]{:S(2)}, u32[]{:S(2)}) %collective-permute-start.16) | collective-permute-done | bytes 73760 | tf_op jit(solution)/shard_map/ppermute | solution.py:701
  50.5 5.5 %scan_forward.1 = (f32[16,264,128]{2,1,0:T(8,128)S(1)}, f32[16,264,128]{2,1,0:T(8,128)S(1)}, f32[16,264,128]{2,1,0:T(8,128)S(1)}, f32[16,264,128]{2,1,0:T(8,128)...) custom-call(s32[1]{0:T(128)} %bitcast.me.me_ref, ...), custom_call_target="tpu_custom_call" | custom-call | flops 1 | bytes 1 | tf_op jit(solution)/shard_map/scan_forward/pallas_call | solution.py:679
  56.2 1.9 %collective-permute-done.21.got = bf16[384,768]{1,0:T(8,128)(2,1)S(1)} collective-permute-done((bf16[384,768]{1,0:T(8,128)(2,1)S(1)}, bf16[384,768]{1,0:T(8,128)(2,1)S(1)}, u32[]{:S(2)}, u32[]{:S(2)}) %collective-permute-start.21) | collective-permute-done | bytes 589856 | tf_op jit(solution)/shard_map/ppermute | solution.py:701
  60.3 1.5 %collective-permute-start.24 = (bf16[224,768]{1,0:T(8,128)(2,1)S(1)}, bf16[224,768]{1,0:T(8,128)(2,1)S(1)}, u32[]{:S(2)}, u32[]{:S(2)}) collective-permute-start(bf16[224,768]{1,0:T(8,128)(2,1)S(1)} %get-tuple-element.126), channel_id=1, source_target_pairs={{0,6},{1,7},{2,4},{3,5},{4,2},{5,3},{6,0},{7,1},{8,14},{9,15},{10,... | collective-permute-start | bytes 1032200 | tf_op jit(solution)/shard_map/ppermute | solution.py:701
  62.2 12.1 %scan_backward.1 = (f32[256,768]{1,0:T(8,128)S(1)}, f32[8,768]{1,0:T(8,128)S(1)}, bf16[256,768]{1,0:T(8,128)(2,1)S(1)}, bf16[256,128]{1,0:T(8,128)(2,1)S(1)}, f32[16,768]{1,0:T(8,128)S(1)}) custom-call(f32[16,264,128]{2,1,0:T(8,128)S(1)} %get-tuple-element.107.refs_0_, f32[16,264,128]{2,1,0:T(8,128)S(1)} %get-tuple-element.108.refs_1_, ...), custom_call_target="tpu_custom_call" | custom-call | flops 1 | bytes 1 | tf_op jit(solution)/shard_map/scan_backward/pallas_call | solution.py:679
  74.3 1.6 %collective-permute-start.25 = (f32[8,768]{1,0:T(8,128)S(1)}, f32[8,768]{1,0:T(8,128)S(1)}, u32[]{:S(2)}, u32[]{:S(2)}) collective-permute-start(f32[8,768]{1,0:T(8,128)S(1)} %get-tuple-element.134), channel_id=1, source_target_pairs={{1,0},{2,1},{3,2},{4,3},{5,4},{6,5},{7,6},{9,8},{10,9},{11,10},{12... | collective-permute-start | bytes 73736 | tf_op jit(solution)/shard_map/ppermute | solution.py:727
  76.2 1.7 %small_grads.1 = (f32[104,768]{1,0:T(8,128)S(1)}, f32[256,768]{1,0:T(8,128)S(1)}) custom-call(bf16[256,768]{1,0:T(8,128)(2,1)S(1)} %get-tuple-element.127.gpre, bf16[256,128]{1,0:T(8,128)(2,1)S(1)} %get-tuple-element.128.gxproj, f32[256,128]{1,0:T(8,128)S(1)} %get-tuple-element.90.refs_10_.xproj, ...), custom_call_target="tpu_custom_call" | custom-call | flops 1 | bytes 1 | tf_op jit(solution)/shard_map/small_grads/pallas_call | solution.py:679
  81.3 1.7 %collective-permute-start.27 = (bf16[64,768]{1,0:T(8,128)(2,1)S(1)}, bf16[64,768]{1,0:T(8,128)(2,1)S(1)}, u32[]{:S(2)}, u32[]{:S(2)}) collective-permute-start(bf16[64,768]{1,0:T(8,128)(2,1)S(1)} %get-tuple-element.139), channel_id=1, source_target_pairs={{0,2},{1,3},{2,0},{3,1},{4,6},{5,7},{6,4},{7,5},{8,10},{9,11},{10,... | collective-permute-start | bytes 294920 | tf_op jit(solution)/shard_map/ppermute | solution.py:701
  83.1 3.7 %collective-permute-start.36 = (bf16[96,768]{1,0:T(8,128)(2,1)S(1)}, bf16[96,768]{1,0:T(8,128)(2,1)S(1)}, u32[]{:S(2)}, u32[]{:S(2)}) collective-permute-start(bf16[96,768]{1,0:T(8,128)(2,1)S(1)} %add_parts.4.a), channel_id=1, source_target_pairs={{0,24},{8,16},{16,8},{24,0},{1,25},{9,17},{17,9},{25,1},{2,26},{10... | collective-permute-start | bytes 442376 | tf_op jit(solution)/shard_map/ppermute | solution.py:701
  87.1 1.6 %collective-permute-start.29 = (bf16[64,768]{1,0:T(8,128)(2,1)S(1)}, bf16[64,768]{1,0:T(8,128)(2,1)S(1)}, u32[]{:S(2)}, u32[]{:S(2)}) collective-permute-start(bf16[64,768]{1,0:T(8,128)(2,1)S(1)} %get-tuple-element.141), channel_id=1, source_target_pairs={{0,6},{1,7},{2,4},{3,5},{4,2},{5,3},{6,0},{7,1},{8,14},{9,15},{10,... | collective-permute-start | bytes 294920 | tf_op jit(solution)/shard_map/ppermute | solution.py:701
  88.7 5.0 %collective-permute-done.28.c = bf16[64,768]{1,0:T(8,128)(2,1)S(1)} collective-permute-done((bf16[64,768]{1,0:T(8,128)(2,1)S(1)}, bf16[64,768]{1,0:T(8,128)(2,1)S(1)}, u32[]{:S(2)}, u32[]{:S(2)}) %collective-permute-start.28) | collective-permute-done | bytes 98336 | tf_op jit(solution)/shard_map/ppermute | solution.py:701
  94.7 8.4 %collective-permute-done.35.c = bf16[96,768]{1,0:T(8,128)(2,1)S(1)} collective-permute-done((bf16[96,768]{1,0:T(8,128)(2,1)S(1)}, bf16[96,768]{1,0:T(8,128)(2,1)S(1)}, u32[]{:S(2)}, u32[]{:S(2)}) %collective-permute-start.35) | collective-permute-done | bytes 147488 | tf_op jit(solution)/shard_map/ppermute | solution.py:701
  105.4 1.4 collective-permute-start.46
  106.8 1.6 %collective-permute-start.37 = (bf16[224,768]{1,0:T(8,128)(2,1)S(1)}, bf16[224,768]{1,0:T(8,128)(2,1)S(1)}, u32[]{:S(2)}, u32[]{:S(2)}) collective-permute-start(bf16[224,768]{1,0:T(8,128)(2,1)S(1)} %add_parts_beside_rows.1.refs_0_), channel_id=1, source_target_pairs={{0,2},{1,3},{2,0},{3,1},{4,6},{5,7},{6,4},{7,5},{8,10},{9,11},{10,... | collective-permute-start | bytes 1032200 | tf_op jit(solution)/shard_map/ppermute | solution.py:701
  108.4 4.0 %collective-permute-done.46.d = bf16[64,768]{1,0:T(8,128)(2,1)S(1)} collective-permute-done((bf16[64,768]{1,0:T(8,128)(2,1)S(1)}, bf16[64,768]{1,0:T(8,128)(2,1)S(1)}, u32[]{:S(2)}, u32[]{:S(2)}) %collective-permute-start.46) | collective-permute-done | bytes 98336 | tf_op jit(solution)/shard_map/ppermute | solution.py:701
  113.1 5.4 %collective-permute-done.45.c = bf16[64,768]{1,0:T(8,128)(2,1)S(1)} collective-permute-done((bf16[64,768]{1,0:T(8,128)(2,1)S(1)}, bf16[64,768]{1,0:T(8,128)(2,1)S(1)}, u32[]{:S(2)}, u32[]{:S(2)}) %collective-permute-start.45) | collective-permute-done | bytes 98336 | tf_op jit(solution)/shard_map/ppermute | solution.py:701
  118.5 4.6 %collective-permute-done.44.b = bf16[64,768]{1,0:T(8,128)(2,1)S(1)} collective-permute-done((bf16[64,768]{1,0:T(8,128)(2,1)S(1)}, bf16[64,768]{1,0:T(8,128)(2,1)S(1)}, u32[]{:S(2)}, u32[]{:S(2)}) %collective-permute-start.44) | collective-permute-done | bytes 98336 | tf_op jit(solution)/shard_map/ppermute | solution.py:701
  125.1 4.9 %collective-permute-done.49.refs_11_ = bf16[64,768]{1,0:T(8,128)(2,1)S(1)} collective-permute-done((bf16[64,768]{1,0:T(8,128)(2,1)S(1)}, bf16[64,768]{1,0:T(8,128)(2,1)S(1)}, u32[]{:S(2)}, u32[]{:S(2)}) %collective-permute-start.49) | collective-permute-done | bytes 98336 | tf_op jit(solution)/shard_map/ppermute | solution.py:701
  131.0 3.6 %collective-permute-done.48.refs_10_ = bf16[64,768]{1,0:T(8,128)(2,1)S(1)} collective-permute-done((bf16[64,768]{1,0:T(8,128)(2,1)S(1)}, bf16[64,768]{1,0:T(8,128)(2,1)S(1)}, u32[]{:S(2)}, u32[]{:S(2)}) %collective-permute-start.48) | collective-permute-done | bytes 98336 | tf_op jit(solution)/shard_map/ppermute | solution.py:701
  134.5 1.6 %collective-permute-start.47 = (bf16[64,768]{1,0:T(8,128)(2,1)S(1)}, bf16[64,768]{1,0:T(8,128)(2,1)S(1)}, u32[]{:S(2)}, u32[]{:S(2)}) collective-permute-start(bf16[64,768]{1,0:T(8,128)(2,1)S(1)} %add_parts.5.refs_8_), channel_id=1, source_target_pairs={{0,2},{1,3},{2,0},{3,1},{4,6},{5,7},{6,4},{7,5},{8,10},{9,11},{10,... | collective-permute-start | bytes 294920 | tf_op jit(solution)/shard_map/ppermute | solution.py:701
  136.1 3.1 %collective-permute-done.47.refs_9_ = bf16[64,768]{1,0:T(8,128)(2,1)S(1)} collective-permute-done((bf16[64,768]{1,0:T(8,128)(2,1)S(1)}, bf16[64,768]{1,0:T(8,128)(2,1)S(1)}, u32[]{:S(2)}, u32[]{:S(2)}) %collective-permute-start.47) | collective-permute-done | bytes 98336 | tf_op jit(solution)/shard_map/ppermute | solution.py:701
  143.0 2.3 %unpack_sums.1 = (f32[384]{0:T(512)}, f32[384,1536]{1,0:T(8,128)}, f32[4,768]{1,0:T(4,128)}, f32[768]{0:T(1024)}, f32[56,768]{1,0:T(8,128)}, /*index=5*/f32[24,7...) custom-call(s32[1]{0:T(128)} %bitcast.me.me_ref, ...), custom_call_target="tpu_custom_call" | custom-call | flops 1 | bytes 1 | tf_op jit(solution)/shard_map/unpack_sums/pallas_call | solution.py:679
  (105 shorter events, 27.0 us)
Async XLA Ops:
  2.3 9.7 %collective-permute-start.2 = (bf16[272,384]{1,0:T(8,128)(2,1)S(1)}, bf16[272,384]{1,0:T(8,128)(2,1)S(1)}, u32[]{:S(2)}, u32[]{:S(2)}) collective-permute-start(bf16[272,384]{1,0:T(8,128)(2,1)S(1)} %pad_maximum_fusion.refs_0_), channel_id=1, source_target_pairs={{0,6},{1,7},{2,4},{3,5},{4,2},{5,3},{6,0},{7,1},{8,14},{9,15},{10,... | collective-permute-start | bytes 626696 | tf_op jit(solution)/shard_map/ppermute | solution.py:701
  6.3 10.2 %collective-permute-start.1 = (bf16[272,384]{1,0:T(8,128)(2,1)S(1)}, bf16[272,384]{1,0:T(8,128)(2,1)S(1)}, u32[]{:S(2)}, u32[]{:S(2)}) collective-permute-start(bf16[272,384]{1,0:T(8,128)(2,1)S(1)} %pad_maximum_fusion.refs_0_), channel_id=1, source_target_pairs={{0,4},{1,5},{2,6},{3,7},{4,0},{5,1},{6,2},{7,3},{8,12},{9,13},{10,... | collective-permute-start | bytes 626696 | tf_op jit(solution)/shard_map/ppermute | solution.py:701
  6.8 9.7 %collective-permute-start.3 = (bf16[272,384]{1,0:T(8,128)(2,1)S(1)}, bf16[272,384]{1,0:T(8,128)(2,1)S(1)}, u32[]{:S(2)}, u32[]{:S(2)}) collective-permute-start(bf16[272,384]{1,0:T(8,128)(2,1)S(1)} %pad_maximum_fusion.refs_0_), channel_id=1, source_target_pairs={{0,1},{1,0},{2,3},{3,2},{4,5},{5,4},{6,7},{7,6},{8,9},{9,8},{10,11... | collective-permute-start | bytes 626696 | tf_op jit(solution)/shard_map/ppermute | solution.py:701
  6.8 12.0 %collective-permute-start = (bf16[272,384]{1,0:T(8,128)(2,1)S(1)}, bf16[272,384]{1,0:T(8,128)(2,1)S(1)}, u32[]{:S(2)}, u32[]{:S(2)}) collective-permute-start(bf16[272,384]{1,0:T(8,128)(2,1)S(1)} %pad_maximum_fusion.refs_0_), channel_id=1, source_target_pairs={{0,2},{1,3},{2,0},{3,1},{4,6},{5,7},{6,4},{7,5},{8,10},{9,11},{10,... | collective-permute-start | bytes 626696 | tf_op jit(solution)/shard_map/ppermute | solution.py:701
  12.1 8.1 %collective-permute-start.9 = (bf16[256,384]{1,0:T(8,128)(2,1)}, bf16[256,384]{1,0:T(8,128)(2,1)S(1)}, u32[]{:S(2)}, u32[]{:S(2)}) collective-permute-start(bf16[256,384]{1,0:T(8,128)(2,1)} %bitcast.11), channel_id=1, source_target_pairs={{0,6},{1,7},{2,4},{3,5},{4,2},{5,3},{6,0},{7,1},{8,14},{9,15},{10,... | collective-permute-start | bytes 589832 | tf_op jit(solution)/shard_map/ppermute | solution.py:701
  15.3 10.8 %collective-permute-start.6 = (bf16[272,384]{1,0:T(8,128)(2,1)S(1)}, bf16[272,384]{1,0:T(8,128)(2,1)S(1)}, u32[]{:S(2)}, u32[]{:S(2)}) collective-permute-start(bf16[272,384]{1,0:T(8,128)(2,1)S(1)} %collective-permute-done.2.refs_3_), channel_id=1, source_target_pairs={{0,1},{1,0},{2,3},{3,2},{4,5},{5,4},{6,7},{7,6},{8,9},{9,8},{10,11... | collective-permute-start | bytes 626696 | tf_op jit(solution)/shard_map/ppermute | solution.py:701
  16.5 10.1 %collective-permute-start.5 = (bf16[272,384]{1,0:T(8,128)(2,1)S(1)}, bf16[272,384]{1,0:T(8,128)(2,1)S(1)}, u32[]{:S(2)}, u32[]{:S(2)}) collective-permute-start(bf16[272,384]{1,0:T(8,128)(2,1)S(1)} %collective-permute-done.1.refs_2_), channel_id=1, source_target_pairs={{0,1},{1,0},{2,3},{3,2},{4,5},{5,4},{6,7},{7,6},{8,9},{9,8},{10,11... | collective-permute-start | bytes 626696 | tf_op jit(solution)/shard_map/ppermute | solution.py:701
  16.5 8.1 %collective-permute-start.8 = (bf16[256,384]{1,0:T(8,128)(2,1)}, bf16[256,384]{1,0:T(8,128)(2,1)S(1)}, u32[]{:S(2)}, u32[]{:S(2)}) collective-permute-start(bf16[256,384]{1,0:T(8,128)(2,1)} %bitcast.12), channel_id=1, source_target_pairs={{0,4},{1,5},{2,6},{3,7},{4,0},{5,1},{6,2},{7,3},{8,12},{9,13},{10,... | collective-permute-start | bytes 589832 | tf_op jit(solution)/shard_map/ppermute | solution.py:701
  18.8 7.2 %collective-permute-start.7 = (bf16[256,384]{1,0:T(8,128)(2,1)}, bf16[256,384]{1,0:T(8,128)(2,1)S(1)}, u32[]{:S(2)}, u32[]{:S(2)}) collective-permute-start(bf16[256,384]{1,0:T(8,128)(2,1)} %bitcast.13), channel_id=1, source_target_pairs={{0,2},{1,3},{2,0},{3,1},{4,6},{5,7},{6,4},{7,5},{8,10},{9,11},{10,... | collective-permute-start | bytes 589832 | tf_op jit(solution)/shard_map/ppermute | solution.py:701
  24.6 11.1 %collective-permute-start.10 = (bf16[256,384]{1,0:T(8,128)(2,1)}, bf16[256,384]{1,0:T(8,128)(2,1)S(1)}, u32[]{:S(2)}, u32[]{:S(2)}) collective-permute-start(bf16[256,384]{1,0:T(8,128)(2,1)} %bitcast.14), channel_id=1, source_target_pairs={{0,1},{1,0},{2,3},{3,2},{4,5},{5,4},{6,7},{7,6},{8,9},{9,8},{10,11... | collective-permute-start | bytes 589832 | tf_op jit(solution)/shard_map/ppermute | solution.py:701
  26.0 9.7 %collective-permute-start.13 = (bf16[256,384]{1,0:T(8,128)(2,1)S(1)}, bf16[256,384]{1,0:T(8,128)(2,1)S(1)}, u32[]{:S(2)}, u32[]{:S(2)}) collective-permute-start(bf16[256,384]{1,0:T(8,128)(2,1)S(1)} %collective-permute-done.9.refs_3_), channel_id=1, source_target_pairs={{0,1},{1,0},{2,3},{3,2},{4,5},{5,4},{6,7},{7,6},{8,9},{9,8},{10,11... | collective-permute-start | bytes 589832 | tf_op jit(solution)/shard_map/ppermute | solution.py:701
  26.0 9.7 %collective-permute-start.12 = (bf16[256,384]{1,0:T(8,128)(2,1)S(1)}, bf16[256,384]{1,0:T(8,128)(2,1)S(1)}, u32[]{:S(2)}, u32[]{:S(2)}) collective-permute-start(bf16[256,384]{1,0:T(8,128)(2,1)S(1)} %collective-permute-done.8.refs_2_), channel_id=1, source_target_pairs={{0,1},{1,0},{2,3},{3,2},{4,5},{5,4},{6,7},{7,6},{8,9},{9,8},{10,11... | collective-permute-start | bytes 589832 | tf_op jit(solution)/shard_map/ppermute | solution.py:701
  26.5 9.2 %collective-permute-start.11 = (bf16[256,384]{1,0:T(8,128)(2,1)S(1)}, bf16[256,384]{1,0:T(8,128)(2,1)S(1)}, u32[]{:S(2)}, u32[]{:S(2)}) collective-permute-start(bf16[256,384]{1,0:T(8,128)(2,1)S(1)} %collective-permute-done.7.refs_1_), channel_id=1, source_target_pairs={{0,1},{1,0},{2,3},{3,2},{4,5},{5,4},{6,7},{7,6},{8,9},{9,8},{10,11... | collective-permute-start | bytes 589832 | tf_op jit(solution)/shard_map/ppermute | solution.py:701
  58.3 17.7 %collective-permute-start.22 = (bf16[224,768]{1,0:T(8,128)(2,1)S(1)}, bf16[224,768]{1,0:T(8,128)(2,1)S(1)}, u32[]{:S(2)}, u32[]{:S(2)}) collective-permute-start(bf16[224,768]{1,0:T(8,128)(2,1)S(1)} %get-tuple-element.124), channel_id=1, source_target_pairs={{0,2},{1,3},{2,0},{3,1},{4,6},{5,7},{6,4},{7,5},{8,10},{9,11},{10,... | collective-permute-start | bytes 1032200 | tf_op jit(solution)/shard_map/ppermute | solution.py:701
  59.0 17.2 %collective-permute-start.23 = (bf16[224,768]{1,0:T(8,128)(2,1)S(1)}, bf16[224,768]{1,0:T(8,128)(2,1)S(1)}, u32[]{:S(2)}, u32[]{:S(2)}) collective-permute-start(bf16[224,768]{1,0:T(8,128)(2,1)S(1)} %get-tuple-element.125), channel_id=1, source_target_pairs={{0,4},{1,5},{2,6},{3,7},{4,0},{5,1},{6,2},{7,3},{8,12},{9,13},{10,... | collective-permute-start | bytes 1032200 | tf_op jit(solution)/shard_map/ppermute | solution.py:701
  60.3 15.9 %collective-permute-start.24 = (bf16[224,768]{1,0:T(8,128)(2,1)S(1)}, bf16[224,768]{1,0:T(8,128)(2,1)S(1)}, u32[]{:S(2)}, u32[]{:S(2)}) collective-permute-start(bf16[224,768]{1,0:T(8,128)(2,1)S(1)} %get-tuple-element.126), channel_id=1, source_target_pairs={{0,6},{1,7},{2,4},{3,5},{4,2},{5,3},{6,0},{7,1},{8,14},{9,15},{10,... | collective-permute-start | bytes 1032200 | tf_op jit(solution)/shard_map/ppermute | solution.py:701
  81.3 7.4 %collective-permute-start.27 = (bf16[64,768]{1,0:T(8,128)(2,1)S(1)}, bf16[64,768]{1,0:T(8,128)(2,1)S(1)}, u32[]{:S(2)}, u32[]{:S(2)}) collective-permute-start(bf16[64,768]{1,0:T(8,128)(2,1)S(1)} %get-tuple-element.139), channel_id=1, source_target_pairs={{0,2},{1,3},{2,0},{3,1},{4,6},{5,7},{6,4},{7,5},{8,10},{9,11},{10,... | collective-permute-start | bytes 294920 | tf_op jit(solution)/shard_map/ppermute | solution.py:701
  83.0 22.4 %collective-permute-start.31 = (bf16[224,768]{1,0:T(8,128)(2,1)S(1)}, bf16[224,768]{1,0:T(8,128)(2,1)S(1)}, u32[]{:S(2)}, u32[]{:S(2)}) collective-permute-start(bf16[224,768]{1,0:T(8,128)(2,1)S(1)} %collective-permute-done.22.refs_1_.b), channel_id=1, source_target_pairs={{0,1},{1,0},{2,3},{3,2},{4,5},{5,4},{6,7},{7,6},{8,9},{9,8},{10,11... | collective-permute-start | bytes 1032200 | tf_op jit(solution)/shard_map/ppermute | solution.py:701
  83.1 10.7 %collective-permute-start.36 = (bf16[96,768]{1,0:T(8,128)(2,1)S(1)}, bf16[96,768]{1,0:T(8,128)(2,1)S(1)}, u32[]{:S(2)}, u32[]{:S(2)}) collective-permute-start(bf16[96,768]{1,0:T(8,128)(2,1)S(1)} %add_parts.4.a), channel_id=1, source_target_pairs={{0,24},{8,16},{16,8},{24,0},{1,25},{9,17},{17,9},{25,1},{2,26},{10... | collective-permute-start | bytes 442376 | tf_op jit(solution)/shard_map/ppermute | solution.py:701
  88.7 18.1 %collective-permute-start.32 = (bf16[224,768]{1,0:T(8,128)(2,1)S(1)}, bf16[224,768]{1,0:T(8,128)(2,1)S(1)}, u32[]{:S(2)}, u32[]{:S(2)}) collective-permute-start(bf16[224,768]{1,0:T(8,128)(2,1)S(1)} %collective-permute-done.23.refs_2_.c), channel_id=1, source_target_pairs={{0,1},{1,0},{2,3},{3,2},{4,5},{5,4},{6,7},{7,6},{8,9},{9,8},{10,11... | collective-permute-start | bytes 1032200 | tf_op jit(solution)/shard_map/ppermute | solution.py:701
  93.8 11.6 %collective-permute-start.30 = (bf16[256,384]{1,0:T(8,128)(2,1)S(1)}, bf16[256,384]{1,0:T(8,128)(2,1)S(1)}, u32[]{:S(2)}, u32[]{:S(2)}) collective-permute-start(bf16[256,384]{1,0:T(8,128)(2,1)S(1)} %get-tuple-element.123.rows.refs_0_), channel_id=1, source_target_pairs={{0,1},{1,0},{2,3},{3,2},{4,5},{5,4},{6,7},{7,6},{8,9},{9,8},{10,11... | collective-permute-start | bytes 589832 | tf_op jit(solution)/shard_map/ppermute | solution.py:701
  93.8 9.4 %collective-permute-start.35 = (bf16[96,768]{1,0:T(8,128)(2,1)S(1)}, bf16[96,768]{1,0:T(8,128)(2,1)S(1)}, u32[]{:S(2)}, u32[]{:S(2)}) collective-permute-start(bf16[96,768]{1,0:T(8,128)(2,1)S(1)} %add_parts.4.a), channel_id=1, source_target_pairs={{0,16},{8,24},{16,0},{24,8},{1,17},{9,25},{17,1},{25,9},{2,18},{10... | collective-permute-start | bytes 442376 | tf_op jit(solution)/shard_map/ppermute | solution.py:701
  93.8 9.5 %collective-permute-start.34 = (bf16[96,768]{1,0:T(8,128)(2,1)S(1)}, bf16[96,768]{1,0:T(8,128)(2,1)S(1)}, u32[]{:S(2)}, u32[]{:S(2)}) collective-permute-start(bf16[96,768]{1,0:T(8,128)(2,1)S(1)} %add_parts.4.a), channel_id=1, source_target_pairs={{0,8},{8,0},{16,24},{24,16},{1,9},{9,1},{17,25},{25,17},{2,10},{10... | collective-permute-start | bytes 442376 | tf_op jit(solution)/shard_map/ppermute | solution.py:701
  103.4 19.8 %collective-permute-start.39 = (bf16[224,768]{1,0:T(8,128)(2,1)S(1)}, bf16[224,768]{1,0:T(8,128)(2,1)S(1)}, u32[]{:S(2)}, u32[]{:S(2)}) collective-permute-start(bf16[224,768]{1,0:T(8,128)(2,1)S(1)} %add_parts_beside_rows.1.refs_0_), channel_id=1, source_target_pairs={{0,6},{1,7},{2,4},{3,5},{4,2},{5,3},{6,0},{7,1},{8,14},{9,15},{10,... | collective-permute-start | bytes 1032200 | tf_op jit(solution)/shard_map/ppermute | solution.py:701
  104.4 19.3 %collective-permute-start.38 = (bf16[224,768]{1,0:T(8,128)(2,1)S(1)}, bf16[224,768]{1,0:T(8,128)(2,1)S(1)}, u32[]{:S(2)}, u32[]{:S(2)}) collective-permute-start(bf16[224,768]{1,0:T(8,128)(2,1)S(1)} %add_parts_beside_rows.1.refs_0_), channel_id=1, source_target_pairs={{0,4},{1,5},{2,6},{3,7},{4,0},{5,1},{6,2},{7,3},{8,12},{9,13},{10,... | collective-permute-start | bytes 1032200 | tf_op jit(solution)/shard_map/ppermute | solution.py:701
  105.4 18.4 %collective-permute-start.33 = (bf16[224,768]{1,0:T(8,128)(2,1)S(1)}, bf16[224,768]{1,0:T(8,128)(2,1)S(1)}, u32[]{:S(2)}, u32[]{:S(2)}) collective-permute-start(bf16[224,768]{1,0:T(8,128)(2,1)S(1)} %collective-permute-done.24.refs_3_.d), channel_id=1, source_target_pairs={{0,1},{1,0},{2,3},{3,2},{4,5},{5,4},{6,7},{7,6},{8,9},{9,8},{10,11... | collective-permute-start | bytes 1032200 | tf_op jit(solution)/shard_map/ppermute | solution.py:701
  105.4 7.0 %collective-permute-start.46 = (bf16[64,768]{1,0:T(8,128)(2,1)S(1)}, bf16[64,768]{1,0:T(8,128)(2,1)S(1)}, u32[]{:S(2)}, u32[]{:S(2)}) collective-permute-start(bf16[64,768]{1,0:T(8,128)(2,1)S(1)} %add_parts.3.a), channel_id=1, source_target_pairs={{0,24},{8,16},{16,8},{24,0},{1,25},{9,17},{17,9},{25,1},{2,26},{10... | collective-permute-start | bytes 294920 | tf_op jit(solution)/shard_map/ppermute | solution.py:701
  106.8 18.1 %collective-permute-start.37 = (bf16[224,768]{1,0:T(8,128)(2,1)S(1)}, bf16[224,768]{1,0:T(8,128)(2,1)S(1)}, u32[]{:S(2)}, u32[]{:S(2)}) collective-permute-start(bf16[224,768]{1,0:T(8,128)(2,1)S(1)} %add_parts_beside_rows.1.refs_0_), channel_id=1, source_target_pairs={{0,2},{1,3},{2,0},{3,1},{4,6},{5,7},{6,4},{7,5},{8,10},{9,11},{10,... | collective-permute-start | bytes 1032200 | tf_op jit(solution)/shard_map/ppermute | solution.py:701
  123.2 16.0 %collective-permute-start.40 = (bf16[224,768]{1,0:T(8,128)(2,1)S(1)}, bf16[224,768]{1,0:T(8,128)(2,1)S(1)}, u32[]{:S(2)}, u32[]{:S(2)}) collective-permute-start(bf16[224,768]{1,0:T(8,128)(2,1)S(1)} %add_parts_beside_rows.1.refs_0_), channel_id=1, source_target_pairs={{0,1},{1,0},{2,3},{3,2},{4,5},{5,4},{6,7},{7,6},{8,9},{9,8},{10,11... | collective-permute-start | bytes 1032200 | tf_op jit(solution)/shard_map/ppermute | solution.py:701
  123.2 16.5 %collective-permute-start.43 = (bf16[224,768]{1,0:T(8,128)(2,1)S(1)}, bf16[224,768]{1,0:T(8,128)(2,1)S(1)}, u32[]{:S(2)}, u32[]{:S(2)}) collective-permute-start(bf16[224,768]{1,0:T(8,128)(2,1)S(1)} %collective-permute-done.39.refs_3_), channel_id=1, source_target_pairs={{0,1},{1,0},{2,3},{3,2},{4,5},{5,4},{6,7},{7,6},{8,9},{9,8},{10,11... | collective-permute-start | bytes 1032200 | tf_op jit(solution)/shard_map/ppermute | solution.py:701
  123.7 16.1 %collective-permute-start.42 = (bf16[224,768]{1,0:T(8,128)(2,1)S(1)}, bf16[224,768]{1,0:T(8,128)(2,1)S(1)}, u32[]{:S(2)}, u32[]{:S(2)}) collective-permute-start(bf16[224,768]{1,0:T(8,128)(2,1)S(1)} %collective-permute-done.38.refs_2_), channel_id=1, source_target_pairs={{0,1},{1,0},{2,3},{3,2},{4,5},{5,4},{6,7},{7,6},{8,9},{9,8},{10,11... | collective-permute-start | bytes 1032200 | tf_op jit(solution)/shard_map/ppermute | solution.py:701
  124.9 16.7 %collective-permute-start.41 = (bf16[224,768]{1,0:T(8,128)(2,1)S(1)}, bf16[224,768]{1,0:T(8,128)(2,1)S(1)}, u32[]{:S(2)}, u32[]{:S(2)}) collective-permute-start(bf16[224,768]{1,0:T(8,128)(2,1)S(1)} %collective-permute-done.37.refs_1_), channel_id=1, source_target_pairs={{0,1},{1,0},{2,3},{3,2},{4,5},{5,4},{6,7},{7,6},{8,9},{9,8},{10,11... | collective-permute-start | bytes 1032200 | tf_op jit(solution)/shard_map/ppermute | solution.py:701
  (27 other events, 211.4 us)

commit v3 on v2

--- a/solution.py
+++ b/solution.py
@@ -113,17 +113,27 @@
         ref[b, pl.ds(c, value.shape[0], stride=CHUNKS), :] = value[:, b * LANES : (b + 1) * LANES]
 
 
-def refs_own(pieces, me, rows, n_pieces):
-    if n_pieces == len(CUBE):
-        return pieces[0][rows : rows + ORDER_ROWS, :rows]
-    digits = jnp.zeros((ORDER_ROWS, rows), F32)
-    for p in range(n_pieces):
-        part = pieces[p][rows : rows + ORDER_ROWS, :rows].astype(F32)
-        digits = jnp.where(me[0] == p, part, digits)
-    return digits.astype(BF16)
-
-
-def pre_kernel(sizes, n_pieces, n_far, me, *refs):
+def payload_kernel(tokens, order, out, near, copied):
+    rows, width = tokens.shape
+    copies = [
+        pltpu.make_async_copy(order, near, copied.at[0]),
+        pltpu.make_async_copy(tokens, out.at[pl.ds(0, rows)], copied.at[1]),
+    ]
+    for copy in copies:
+        copy.start()
+    out[rows:, :] = jnp.zeros((ORDER_ROWS, width), BF16)
+    copies[0].wait()
+    out[rows:, 0:rows] = order_digits(near)
+    copies[1].wait()
+
+
+def order_digits(order):
+    sub = lax.broadcasted_iota(jnp.int32, (ORDER_ROWS, order.shape[1]), 0)
+    digits = jnp.where(sub == 0, order[...] >> 7, jnp.where(sub == 1, order[...] & 127, 0))
+    return digits.astype(F32).astype(BF16)
+
+
+def pre_kernel(sizes, n_pieces, n_far, me, order, *refs):
     rows, width, inner, rank, state, lags, clouds = sizes
     steps = rows // CHUNKS
     pieces = refs[:n_pieces]
@@ -133,24 +143,21 @@
     for copy in copies:
         copy.start()
     (lengths, gain, w_in, conv_w, conv_b, w_x, w_dt, dt_b, alog, skip) = near_refs
-    (trans_o, normed_o, gate_o, ext_o, conv_o, act_o, step_o, xproj_o, chunkf_o, sums_o, f_o, orders_o, column_o,
+    (trans_o, normed_o, gate_o, ext_o, conv_o, act_o, step_o, xproj_o, chunkf_o, sums_o, f_o, column_o, orders_o,
      valid, far, use, bbc, wx_o, wdt_o, a2, rows_o, conv_in) = refs[n_pieces:]
     to_row = row_of_place(rows)
-    halos = [jnp.full((1, 1), -1.0, F32)] * (lags + 1)
-    for p in range(n_pieces):
-        row = dot(pieces[p][rows : rows + ORDER_ROWS, :rows], to_row)
-        row = row[0:1] * 128.0 + row[1:2]
-        orders_o[p : p + 1, :] = row
-        behind = source(me, p, n_pieces) == me[0] - 1
-        for k in range(1, lags + 1):
-            r = (steps - k) * CHUNKS + CHUNKS - 1
-            halos[k] = jnp.where(behind, row[:, r : r + 1], halos[k])
     sub = lax.broadcasted_iota(jnp.int32, (BLOCK, LANES), 0)
     extra = jnp.full((BLOCK, LANES), -1.0, F32)
+    tail = jnp.zeros((ORDER_ROWS, rows), F32)
+    for p in range(n_pieces):
+        now = pieces[p][rows : rows + ORDER_ROWS, :rows]
+        tail = jnp.where(source(me, p, n_pieces) == me[0] - 1, now.astype(F32), tail)
+        if p < orders_o.shape[0]:
+            row = dot(now, to_row)
+            orders_o[p : p + 1, :] = row[0:1] * 128.0 + row[1:2]
     for k in range(1, lags + 1):
-        extra = jnp.where(sub == k, halos[k], extra)
-    digits = refs_own(pieces, me, rows, n_pieces)
-    both = dot(to_row, digits, ((0,), (1,)))
+        extra = jnp.where(sub == k, tail[0:1, rows - k : rows - k + 1] * 128.0 + tail[1:2, rows - k : rows - k + 1], extra)
+    both = dot(to_row, order_digits(order), ((0,), (1,)))
     own = jnp.broadcast_to(both[:, 0:1] * 128.0 + both[:, 1:2], (rows, LANES))
     column_o[...] = own
     column = jnp.concatenate([own, extra], axis=0)
@@ -224,7 +231,7 @@
             )
 
         zero = jnp.zeros((CHUNKS, LANES), F32)
-        last = lax.fori_loop(0, steps, scan_body, (zero,) * state, unroll=2)
+        last = lax.fori_loop(0, steps, scan_body, (zero,) * state, unroll=8)
         for n in range(state):
             chunkf_o[lb, n * CHUNKS : (n + 1) * CHUNKS, :] = last[n]
     total = jnp.zeros((state, inner), F32)
@@ -244,7 +251,7 @@
     near_out, copied = refs[n_pieces + 13 + n_out :]
     copy = pltpu.make_async_copy(w_out, near_out, copied)
     copy.start()
-    trans_dy = gather_rows(wide(column[...], rows), [p[...] for p in pieces], me, rows).astype(BF16)
+    trans_dy = gather_rows(wide(column[...], rows), [p[0:rows, :] for p in pieces], me, rows).astype(BF16)
     dy_o[...] = trans_dy
     copy.wait()
     gg_o[...] = dot(trans_dy, near_out[...], ((1,), (1,)))
@@ -270,7 +277,7 @@
             )
 
         zero = jnp.zeros((CHUNKS, LANES), F32)
-        last = lax.fori_loop(0, steps, scan_body, (zero,) * state, unroll=2)
+        last = lax.fori_loop(0, steps, scan_body, (zero,) * state, unroll=8)
         for n in range(state):
             chunkb_o[lb, n * CHUNKS : (n + 1) * CHUNKS, :] = last[n]
     total = jnp.zeros((state, inner), F32)
@@ -349,7 +356,7 @@
             mixed[r, ls] = out
             return tuple(new)
 
-        lax.fori_loop(0, steps, forward, tuple(begin), unroll=2)
+        lax.fori_loop(0, steps, forward, tuple(begin), unroll=8)
 
     def gating(j, carry):
         r = pl.ds(pl.multiple_of(j * BLOCK, BLOCK), BLOCK)
@@ -452,7 +459,7 @@
                 return tuple(new_flows), tuple(new_sums)
 
             flows, sums_a = lax.fori_loop(
-                0, steps, backward, (tuple(begin), (zero,) * (pair * group))
+                0, steps, backward, (tuple(begin), (zero,) * (pair * group)), unroll=8
             )
             for q, n in enumerate(ns):
                 for x, ls in enumerate(lanes):
@@ -626,23 +633,57 @@
     out[...] = ((one + two) + (three + four)).astype(BF16)
 
 
-def sum_beside_kernel(a, b, c, d, rows, out):
+def pair_kernel(a, b, out):
+    out[...] = (a[...].astype(F32) + b[...].astype(F32)).astype(BF16)
+
+
+def pair_beside_kernel(a, b, rows, out):
     beside(out, rows)
-    sum_kernel(a, b, c, d, out.at[pl.ds(rows.shape[0] // 2, a.shape[0])])
-
-
-def unpack_kernel(sizes, n_pieces, me, *refs):
+    out[rows.shape[0] // 2 :, :] = (a[...].astype(F32) + b[...].astype(F32)).astype(BF16)
+
+
+def by_chip(out, first, parts, me, part):
+    for d, piece in enumerate(parts):
+        chip = jnp.bitwise_xor(lax.div(me[0], 2), d)
+        out[pl.ds(pl.multiple_of(first + chip * part, BLOCK), part), :] = piece[piece.shape[0] - part :, :]
+
+
+def chips_kernel(me, own, two, four, six, out):
+    by_chip(out, 0, (own, two, four, six), me, own.shape[0])
+
+
+def share_kernel(rows, width, me, orders, own, two, four, six, mine_o, theirs_o, *half_o):
+    pieces = (own, two, four, six)
+    whole = jnp.concatenate([unfold(p, rows, width) for p in pieces], axis=0)
+    for core, out in enumerate((mine_o, theirs_o)):
+        first = jnp.bitwise_xor(me[0], core) * rows
+        place = (first + lax.broadcasted_iota(jnp.int32, (rows, rows), 0)).astype(F32)
+        match = [(orders[p : p + 1, :] == place).astype(F32).astype(BF16) for p in range(len(pieces))]
+        moved = dot(jnp.concatenate(match, axis=1), whole).astype(BF16)
+        if core == 0:
+            out[...] = moved
+        else:
+            out[0 : rows // 2, 0:width] = moved[: rows // 2]
+            out[0 : rows // 2, width:] = moved[rows // 2 :]
+    for out in half_o:
+        part = out.shape[0] // len(pieces)
+        by_chip(out, 0, pieces, me, part)
+        by_chip(theirs_o, rows // 2, pieces, me, part)
+
+
+def arrive_kernel(here, mine, theirs, out):
+    rows, width = here.shape
+    moved = mine[...].astype(F32) + unfold(theirs, rows, width).astype(F32)
+    out[...] = (here[...].astype(F32) + moved).astype(BF16)
+
+
+def unpack_kernel(sizes, devices, me, own_one, other_one, own_two, other_two, *refs):
     rows, width, inner, rank, state, lags, clouds = sizes
-    one, two = refs[:n_pieces], refs[n_pieces : 2 * n_pieces]
-    (gain_o, win_o, taps_o, convb_o, wx_o, wdt_o, dtb_o, alog_o, skip_o, wout_o) = refs[2 * n_pieces : 2 * n_pieces + 10]
-    all_one, all_two = refs[2 * n_pieces + 10 :]
-    for pieces, whole in ((one, all_one), (two, all_two)):
-        part = whole.shape[0] // n_pieces
-        for p, piece in enumerate(pieces):
-            s = source(me, p, n_pieces)
-            if n_pieces == len(CUBE):
-                s = jnp.bitwise_and(s, 1) * (n_pieces // 2) + lax.div(s, 2)
-            whole[pl.ds(pl.multiple_of(s * part, BLOCK), part), :] = piece[piece.shape[0] - part :, :]
+    (gain_o, win_o, taps_o, convb_o, wx_o, wdt_o, dtb_o, alog_o, skip_o, wout_o, all_one, all_two) = refs
+    for own, other, whole, n in ((own_one, other_one, all_one, devices[0]), (own_two, other_two, all_two, devices[1])):
+        core, half = core_of(me[0], n), whole.shape[0] // 2
+        for k, piece in ((core, own), (1 - core, other)):
+            whole[pl.ds(pl.multiple_of(k * half, BLOCK), half), :] = piece[piece.shape[0] - half :, :]
     wout_o[...] = all_one[0:width, :].astype(F32).T
     win_o[:, inner:] = all_one[width : 2 * width, :].astype(F32)
     win_o[:, :inner] = all_two[0:width, :].astype(F32)
@@ -665,7 +706,7 @@
     pieces, out = refs[:n_pieces], refs[n_pieces]
     place = (me[0] * rows + lax.broadcasted_iota(jnp.int32, (rows, rows), 0)).astype(F32)
     mine = [(orders[p : p + 1, :] == place).astype(F32).astype(BF16) for p in range(n_pieces)]
-    moved = dot(jnp.concatenate(mine, axis=1), jnp.concatenate([unfold(p, rows, out.shape[1]) for p in pieces], axis=0))
+    moved = dot(jnp.concatenate(mine, axis=1), jnp.concatenate([p[...] for p in pieces], axis=0))
     out[...] = (here[...].astype(F32) + moved).astype(BF16)
 
 
@@ -692,6 +733,16 @@
     return run
 
 
+CFG = {'dy': 'd6', 'dy1': 'fwd', 'adj': 'gstart', 'rim': '', 'small': 'one', 'z1': 'send', 'halves': '', 'pair': '', 'share': 'pair', 'hold': 'out', 'm3': 'pair', 'd': 'out', 'share3': 'total'}
+
+
+def tie(name, value, choices):
+    pick = CFG.get(name, "")
+    for k in pick.split("+") if pick else ():
+        value = after(value, choices[k])
+    return value
+
+
 def after(value, *others):
     return lax.optimization_barrier((value, others))[0]
 
@@ -701,17 +752,9 @@
     return lax.ppermute(block, axis, [(i, i ^ distance) for i in range(devices)])
 
 
-def spread_pieces(block, axis, then=None):
-    devices = lax.axis_size(axis)
-    if devices == len(CUBE):
-        across = [block] + [swap(block, axis, d) for d in CUBE[1:4]]
-        if then is not None:
-            then = after(then, across[3])
-        pieces = across + [swap(part, axis, 1) for part in across]
-    else:
-        whole = lax.all_gather(block, axis)
-        pieces = [whole[i] for i in range(devices)]
-    return pieces if then is None else (pieces, then)
+def spread_pieces(block, axis):
+    whole = lax.all_gather(block, axis)
+    return [whole[i] for i in range(lax.axis_size(axis))]
 
 
 def spread_carries(blocks, axis):
@@ -750,17 +793,30 @@
     devices = lax.axis_size("seq")
     me = lax.axis_index("seq").astype(jnp.int32)[None]
     here_x, here_dy = tokens[0], cotangent[0]
-    digits = jnp.concatenate([order >> 7, order & 127], axis=0).astype(BF16)
-    digits = jnp.pad(digits, ((0, ORDER_ROWS - 2), (0, width - rows)))
+    cube = devices == len(CUBE) and lax.axis_size("dp") == 4
+    (payload,) = call(
+        payload_kernel,
+        [((rows + ORDER_ROWS, width), BF16)],
+        [(order.shape, order.dtype), pltpu.SemaphoreType.DMA((2,))],
+        0,
+        "tokens_and_order",
+        4,
+        far_ins=(0, 1),
+    )(here_x, order)
     weights = (lengths, norm_gain, w_in, conv_weight.T, conv_bias, w_x.T, w_dt, dt_bias, a_log.T, d_skip)
-    pieces_x, here_dy = spread_pieces(jnp.concatenate([here_x, digits], axis=0), "seq", then=here_dy)
-    pieces_dy = spread_pieces(here_dy, "seq")
+    if cube:
+        across_x = [payload] + [swap(payload, "seq", d) for d in CUBE[1:4]]
+        send_dy = tie("dy", here_dy, {"d2": across_x[1], "d4": across_x[2], "d6": across_x[3]})
+        across_dy = [send_dy] + [swap(send_dy, "seq", d) for d in CUBE[1:4]]
+        pieces_x = across_x + [swap(part, "seq", 1) for part in across_x]
+    else:
+        pieces_x, pieces_dy = spread_pieces(payload, "seq"), spread_pieces(here_dy, "seq")
     n = len(pieces_x)
     big, lane = (rows, inner), (rows, LANES)
     carried = (inner // LANES, state * CHUNKS, LANES)
     spread = (rows, state * LANES)
     ext_rows = rows + lags * CHUNKS
-    (trans, normed, gate, ext, conv, act, step, xproj, chunkf, sums, f, orders, column, valid, far, use, bbc, w_x_pad, w_dt_pad, a2, row_consts) = call(
+    (trans, normed, gate, ext, conv, act, step, xproj, chunkf, sums, f, column, orders, valid, far, use, bbc, w_x_pad, w_dt_pad, a2, row_consts) = call(
         functools.partial(pre_kernel, sizes, n, len(weights)),
         [
             ((rows, width), BF16),
@@ -774,8 +830,8 @@
             (carried, F32),
             ((CHUNKS, inner), F32),
             ((state, inner), F32),
-            ((n, rows), F32),
             (lane, F32),
+            ((4 if cube else n, rows), F32),
             ((lags, rows, LANES), F32),
             (big, F32),
             (big, F32),
@@ -792,10 +848,13 @@
         "forward_local",
         24,
         9,
-        far_ins=tuple(range(n + 1, n + 1 + len(weights))),
-    )(me, *pieces_x, *weights)
-    carry_rows = (state + CHUNKS, 2 * state + CHUNKS)[n != len(CUBE)]
-    n_sent = (len(SENT), 1)[n != len(CUBE)]
+        far_ins=tuple(range(n + 2, n + 2 + len(weights))),
+    )(me, order, *pieces_x, *weights)
+    if cube:
+        across_dy = [tie("dy1", part, {"fwd": xproj}) for part in across_dy]
+        pieces_dy = across_dy + [swap(part, "seq", 1) for part in across_dy]
+    carry_rows = (state + CHUNKS, 2 * state + CHUNKS)[not cube]
+    n_sent = (len(SENT), 1)[not cube]
     trans_dy, gg, gm, cbc, chunkb, *carries = call(
         functools.partial(back_kernel, sizes, n),
         [((rows, width), BF16), (big, F32), (big, F32), (spread, F32), (carried, F32)]
@@ -820,7 +879,6 @@
         18,
         7,
     )(me, *carries, trans_dy, normed, gg, gate, act, far, use, bbc, cbc, chunkf, sums, a2, row_consts, w_out)
-    cube = n == len(CUBE) and lax.axis_size("dp") == 4
     first = (keep, send)
     half_one, half_two = width, -(-(width + n_small) // (8 * BLOCK)) * (4 * BLOCK)
     got = swap(send, "seq", 1) if cube else None
@@ -838,7 +896,7 @@
         beside_one = ((rows // 2 + part_one, inner), BF16)
         own_one, *sent = call(
             halves_beside_kernel, [((part_one, inner), BF16)] + [beside_one] * 3, [], 1, "add_halves_beside_rows", 8
-        )(me, keep, got, branch)
+        )(me, tie("adj", keep, {"gstart": gstart}), got, branch)
         away_one = [swap(block, "seq", d) for block, d in zip(sent, SENT)]
     gconv, rim, gpre, gxproj, galog = call(
         functools.partial(scan_backward_kernel, sizes),
@@ -850,6 +908,11 @@
         14,
     )(*[pltpu.with_memory_space_constraint(part, pltpu.VMEM) for part in states], gstart, far, use, bbc, cbc, gm, step, act, conv, valid, a2, row_consts, w_x_pad, w_dt_pad)
     rim = from_behind(rim, "seq", -1)
+    if cube:
+        (one,) = call(sum_kernel, [((part_one, inner), BF16)], [], 0, "add_parts", 4)(
+            tie("rim", after(own_one, gpre), {"rim": rim}), *away_one
+        )
+        gpre = tie("small", gpre, {"one": one})
     small, gci = call(
         functools.partial(small_kernel, sizes),
         [((n_small, inner), F32), (big, F32)],
@@ -858,7 +921,7 @@
         "small_grads",
         16,
         1.6,
-    )(after(gpre, *away_one) if cube else gpre, gxproj, xproj, act, gconv, ext, valid, gm, row_consts, galog)
+    )(gpre, gxproj, xproj, act, gconv, ext, valid, gm, row_consts, galog)
     back, keep, send = call(
         functools.partial(final_kernel, sizes, devices),
         [((rows, width), BF16), ((half_two, inner), BF16), ((half_two, inner), BF16)],
@@ -867,38 +930,83 @@
         "input_projection_grads",
         16,
     )(me, trans, normed, gci, gz, rim, small, norm_gain, w_in)
-    place = call(functools.partial(place_kernel, rows, n), [((rows, width), BF16)], [], 1, "to_hilbert", 12, 1.4)
     if cube:
         part_two = half_two // 4
-        adds_one = call(sum_kernel, [((part_one, inner), BF16)], [], 0, "add_parts", 4)
-        adds_two = call(sum_kernel, [((part_two, inner), BF16)], [], 0, "add_parts", 4)
+        piece_one, piece_two = ((part_one, inner), BF16), ((part_two, inner), BF16)
+        pair_two = call(pair_kernel, [piece_two], [], 0, "add_pair", 4)
+        rows_out = [((rows, width), BF16)]
+        arrive = call(arrive_kernel, rows_out, [], 0, "add_arrived", 4)
         got = swap(send, "seq", 1)
-        (one,) = adds_one(own_one, *away_one)
-        pieces_b = [branch, *away_one]
-        pieces_b += [swap(part, "seq", 1) for part in pieces_b]
-        own_two, *sent = call(halves_kernel, [((part_two, inner), BF16)] * 4, [], 1, "add_halves", 4)(me, keep, got)
+        at = {"send": send}
+
+        def branch_rows(point, value):
+            if CFG["share"] != point:
+                return value
+            mine, theirs = call(
+                functools.partial(share_kernel, rows, width),
+                rows_out + [((rows // 2, inner), BF16)],
+                [],
+                1,
+                "share_rows",
+                8,
+            )(me, orders, after(branch, at[point]), *away_one)
+            at["out"] = arrive(here_x, mine, swap(theirs, "seq", 1))[0]
+            return tie("hold", value, at)
+
+        one = tie("z1", one, at)
+        z_one = swap(one, "dp", 1)
+        keep = tie("halves", keep, {"z": z_one})
+        keep = branch_rows("send", keep)
+        own_two, *sent = call(halves_kernel, [piece_two] * 4, [], 1, "add_halves", 4)(me, keep, got)
         away_two = [swap(block, "seq", d) for block, d in zip(sent, SENT)]
-        one = after(one, own_two)
-        z_one = [swap(one, "dp", d) for d in (1, 2, 3)]
-        (two,) = adds_two(own_two, *away_two)
-        z_two = [swap(two, "dp", d) for d in (1, 2, 3)]
-        (output,) = place(me, after(here_x, two), orders, *pieces_b)
-        (one,) = call(sum_beside_kernel, [beside_one], [], 0, "add_parts_beside_rows", 8)(
-            one, *z_one, after(back, two)
+        at.update(d2=away_two[0], d4=away_two[1], d6=away_two[2], own=own_two)
+        (one,) = call(pair_kernel, [piece_one], [], 0, "add_pair", 4)(tie("pair", one, at), z_one)
+        z_one = swap(one, "dp", 2)
+        own_two = branch_rows("own", own_two)
+        (two,) = call(sum_kernel, [piece_two], [], 0, "add_parts", 4)(own_two, *away_two)
+        z_two = swap(two, "dp", 1)
+        at["summed"], at["z"] = two, z_two
+        two = branch_rows("summed", two)
+        (two,) = pair_two(two, z_two)
+        z_two = swap(two, "dp", 2)
+        at["pair"] = two
+        two = branch_rows("pair", two)
+        (two,) = pair_two(two, z_two)
+        at["total"] = two
+        branch_rows("total", two)
+        (one,) = call(pair_beside_kernel, [beside_one], [], 0, "add_pair_beside_rows", 8)(
+            one, z_one, tie("m3", back, at)
         )
-        pieces_g = spread_pieces(one, "seq")
-        (two,) = adds_two(two, *z_two)
-        totals = (pieces_g, spread_pieces(two, "seq"))
+        away_one = [swap(one, "seq", d) for d in SENT[:3]]
+        if CFG["d"] == "ag":
+            whole = lax.all_gather(two, "seq").reshape(4, 2, *two.shape).swapaxes(0, 1).reshape(2, half_two, inner)
+            at["d2"] = at["d4"] = at["d6"] = whole
+        else:
+            away_two = [swap(two, "seq", d) for d in SENT[:3]]
+            at.update(d2=away_two[0], d4=away_two[1], d6=away_two[2])
+        mine, theirs, own_one = call(
+            functools.partial(share_kernel, rows, width),
+            rows_out + [((rows // 2 + half_one, inner), BF16), ((half_one, inner), BF16)],
+            [],
+            1,
+            "share_rows_and_parts",
+            12,
+        )(me, orders, tie("share3", one, at), *away_one)
+        other_one = swap(theirs, "seq", 1)
+        (input_grad,) = arrive(here_dy, mine, other_one)
+        output = at["out"]
+        if CFG["d"] == "ag":
+            totals = (own_one, other_one, whole[0], whole[1])
+        else:
+            (own_two,) = call(chips_kernel, [((half_two, inner), BF16)], [], 1, "order_parts", 4)(me, two, *away_two)
+            totals = (own_one, other_one, own_two, swap(own_two, "seq", 1))
     else:
-        totals = [
-            [lax.psum(half.astype(F32), ("dp", "seq")).astype(BF16) for half in halves]
-            for halves in (first, (keep, send))
-        ]
+        totals = [lax.psum(half.astype(F32), ("dp", "seq")).astype(BF16) for half in (*first, keep, send)]
+        place = call(functools.partial(place_kernel, rows, n), [((rows, width), BF16)], [], 1, "to_hilbert", 24)
         (output,) = place(me, here_x, orders, *spread_pieces(branch, "seq"))
-        pieces_g = spread_pieces(back, "seq")
-    (input_grad,) = place(me, here_dy, orders, *pieces_g)
+        (input_grad,) = place(me, here_dy, orders, *spread_pieces(back, "seq"))
     weights = call(
-        functools.partial(unpack_kernel, sizes, len(totals[0])),
+        functools.partial(unpack_kernel, sizes, (devices if cube else 0, devices if cube and CFG["d"] != "ag" else 0)),
         [
             ((width,), F32),
             ((width, 2 * inner), F32),
@@ -916,7 +1024,7 @@
         "unpack_sums",
         24,
         2.4,
-    )(me, *totals[0], *totals[1])
+    )(me, *totals)
     turned = [v.T if v.ndim == 2 and v.shape[1] == inner and v.shape[0] != rank else v for v in weights]
     return (output[None], input_grad[None], *turned)
 

time: 146 us -> 121 us (0.83)
  waiting for transfers between devices: 60.9 us -> 42.2 us
  starting transfers between devices: 40.5 us -> 37 us
  other arithmetic: 1.69 us -> 0 us
  Pallas kernels: 41.3 us -> 39.7 us
    ppermute x53 -> x42, waiting for transfers between devices: 60.9 us -> 42.2 us  [swap(): lax.ppermute(block, axis, [(i, i ^ distance) for i in range(devices)])]
    ppermute x53 -> x42, starting transfers between devices: 38.9 us -> 35.7 us  [swap(): lax.ppermute(block, axis, [(i, i ^ distance) for i in range(devices)])]
    pallas_call x16 -> x22, Pallas kernels: 41.3 us -> 39.7 us  [run(): pl.pallas_call(kernel, out_shape=[jax.ShapeDtypeStruct(*part) if isinstan...]
  transfers between devices with their start and end apart: 54 -> 43, of which waited for: 21 -> 23; matrix products, arithmetic and copies ran while one was open for 0% -> 0% of each run, Pallas kernels for 18% -> 20%
where the time goes in v3:
time: 121 us
  waiting for transfers between devices  42.2 us (35%)
  Pallas kernels  39.7 us (33%)
  starting transfers between devices  37 us (31%)
    ppermute x42, waiting for transfers between devices, swap(): lax.ppermute(block, axis, [(i, i ^ distance) for i in range(devices)])  42.2 us
    pallas_call x22, Pallas kernels, run(): pl.pallas_call(kernel, out_shape=[jax.ShapeDtypeStruct(*part) if isinstan...  39.7 us
    ppermute x42, starting transfers between devices, swap(): lax.ppermute(block, axis, [(i, i ^ distance) for i in range(devices)])  35.7 us
  transfers between devices with their start and end apart: 43, of which 23 were waited for; matrix products, arithmetic and copies ran while one was open for 0% of the time, Pallas kernels for 20%

profile of v3, /device:TPU:0, one launch (start us, length us, event | category | flops | bytes accessed | tf_op | source)
XLA Modules:
  0.0 120.5 jit_solution(6907419090208415809)
XLA Ops:
  1.7 4.0 %collective-permute-start.2 = (bf16[272,384]{1,0:T(8,128)(2,1)S(1)}, bf16[272,384]{1,0:T(8,128)(2,1)S(1)}, u32[]{:S(2)}, u32[]{:S(2)}) collective-permute-start(bf16[272,384]{1,0:T(8,128)(2,1)S(1)} %tokens_and_order.1.refs_0_), channel_id=1, source_target_pairs={{0,6},{1,7},{2,4},{3,5},{4,2},{5,3},{6,0},{7,1},{8,14},{9,15},{10,... | collective-permute-start | bytes 626696 | tf_op jit(solution)/shard_map/ppermute | solution.py:752
  6.3 5.4 %collective-permute-done.2.refs_3_ = bf16[272,384]{1,0:T(8,128)(2,1)S(1)} collective-permute-done((bf16[272,384]{1,0:T(8,128)(2,1)S(1)}, bf16[272,384]{1,0:T(8,128)(2,1)S(1)}, u32[]{:S(2)}, u32[]{:S(2)}) %collective-permute-start.2) | collective-permute-done | bytes 208928 | tf_op jit(solution)/shard_map/ppermute | solution.py:752
  11.7 3.6 %collective-permute-done.1.refs_2_ = bf16[272,384]{1,0:T(8,128)(2,1)S(1)} collective-permute-done((bf16[272,384]{1,0:T(8,128)(2,1)S(1)}, bf16[272,384]{1,0:T(8,128)(2,1)S(1)}, u32[]{:S(2)}, u32[]{:S(2)}) %collective-permute-start.1) | collective-permute-done | bytes 208928 | tf_op jit(solution)/shard_map/ppermute | solution.py:752
  15.8 1.8 %collective-permute-start.9 = (bf16[256,384]{1,0:T(8,128)(2,1)}, bf16[256,384]{1,0:T(8,128)(2,1)S(1)}, u32[]{:S(2)}, u32[]{:S(2)}) collective-permute-start(bf16[256,384]{1,0:T(8,128)(2,1)} %bitcast.11), channel_id=1, source_target_pairs={{0,6},{1,7},{2,4},{3,5},{4,2},{5,3},{6,0},{7,1},{8,14},{9,15},{10,... | collective-permute-start | bytes 589832 | tf_op jit(solution)/shard_map/ppermute | solution.py:752
  17.6 1.3 %collective-permute-start.8 = (bf16[256,384]{1,0:T(8,128)(2,1)}, bf16[256,384]{1,0:T(8,128)(2,1)S(1)}, u32[]{:S(2)}, u32[]{:S(2)}) collective-permute-start(bf16[256,384]{1,0:T(8,128)(2,1)} %bitcast.12), channel_id=1, source_target_pairs={{0,4},{1,5},{2,6},{3,7},{4,0},{5,1},{6,2},{7,3},{8,12},{9,13},{10,... | collective-permute-start | bytes 589832 | tf_op jit(solution)/shard_map/ppermute | solution.py:752
  20.0 8.4 %forward_local.1 = (bf16[256,384]{1,0:T(8,128)(2,1)S(1)}, bf16[256,384]{1,0:T(8,128)(2,1)S(1)}, f32[256,768]{1,0:T(8,128)S(1)}, f32[280,768]{1,0:T(8,128)S(1)}, ...) custom-call(s32[1]{0:T(128)} %bitcast.1.me.me_ref, ...), custom_call_target="tpu_custom_call" | custom-call | flops 1 | bytes 1 | tf_op jit(solution)/shard_map/forward_local/pallas_call | solution.py:720
  30.8 5.5 %backward_local.1 = (bf16[256,384]{1,0:T(8,128)(2,1)S(1)}, f32[256,768]{1,0:T(8,128)S(1)}, f32[256,768]{1,0:T(8,128)S(1)}, f32[256,2048]{1,0:T(8,128)S(1)}, f32[...) custom-call(s32[1]{0:T(128)} %bitcast.1.me.me_ref, ...), custom_call_target="tpu_custom_call" | custom-call | flops 1 | bytes 1 | tf_op jit(solution)/shard_map/backward_local/pallas_call | solution.py:720
  36.3 1.7 %collective-permute-start.14 = (f32[24,768]{1,0:T(8,128)S(1)}, f32[24,768]{1,0:T(8,128)S(1)}, u32[]{:S(2)}, u32[]{:S(2)}) collective-permute-start(f32[24,768]{1,0:T(8,128)S(1)} %get-tuple-element.111), channel_id=1, source_target_pairs={{0,2},{1,3},{2,0},{3,1},{4,6},{5,7},{6,4},{7,5},{8,10},{9,11},{10,... | collective-permute-start | bytes 221192 | tf_op jit(solution)/shard_map/ppermute | solution.py:752
  40.8 2.4 %collective-permute-done.15.refs_1_ = f32[24,768]{1,0:T(8,128)S(1)} collective-permute-done((f32[24,768]{1,0:T(8,128)S(1)}, f32[24,768]{1,0:T(8,128)S(1)}, u32[]{:S(2)}, u32[]{:S(2)}) %collective-permute-start.15) | collective-permute-done | bytes 73760 | tf_op jit(solution)/shard_map/ppermute | solution.py:752
  45.3 4.8 %scan_forward.1 = (f32[16,264,128]{2,1,0:T(8,128)S(1)}, f32[16,264,128]{2,1,0:T(8,128)S(1)}, f32[16,264,128]{2,1,0:T(8,128)S(1)}, f32[16,264,128]{2,1,0:T(8,128)...) custom-call(s32[1]{0:T(128)} %bitcast.1.me.me_ref, ...), custom_call_target="tpu_custom_call" | custom-call | flops 1 | bytes 1 | tf_op jit(solution)/shard_map/scan_forward/pallas_call | solution.py:720
  50.7 1.5 %collective-permute-done.21.got = bf16[384,768]{1,0:T(8,128)(2,1)S(1)} collective-permute-done((bf16[384,768]{1,0:T(8,128)(2,1)S(1)}, bf16[384,768]{1,0:T(8,128)(2,1)S(1)}, u32[]{:S(2)}, u32[]{:S(2)}) %collective-permute-start.21) | collective-permute-done | bytes 589856 | tf_op jit(solution)/shard_map/ppermute | solution.py:752
  52.3 1.4 %collective-permute-start.22 = (bf16[224,768]{1,0:T(8,128)(2,1)S(1)}, bf16[224,768]{1,0:T(8,128)(2,1)S(1)}, u32[]{:S(2)}, u32[]{:S(2)}) collective-permute-start(bf16[224,768]{1,0:T(8,128)(2,1)S(1)} %get-tuple-element.145), channel_id=1, source_target_pairs={{0,2},{1,3},{2,0},{3,1},{4,6},{5,7},{6,4},{7,5},{8,10},{9,11},{10,... | collective-permute-start | bytes 1032200 | tf_op jit(solution)/shard_map/ppermute | solution.py:752
  54.5 1.4 %collective-permute-start.24 = (bf16[224,768]{1,0:T(8,128)(2,1)S(1)}, bf16[224,768]{1,0:T(8,128)(2,1)S(1)}, u32[]{:S(2)}, u32[]{:S(2)}) collective-permute-start(bf16[224,768]{1,0:T(8,128)(2,1)S(1)} %get-tuple-element.147), channel_id=1, source_target_pairs={{0,6},{1,7},{2,4},{3,5},{4,2},{5,3},{6,0},{7,1},{8,14},{9,15},{10,... | collective-permute-start | bytes 1032200 | tf_op jit(solution)/shard_map/ppermute | solution.py:752
  55.9 10.8 %scan_backward.1 = (f32[256,768]{1,0:T(8,128)S(1)}, f32[8,768]{1,0:T(8,128)S(1)}, bf16[256,768]{1,0:T(8,128)(2,1)S(1)}, bf16[256,128]{1,0:T(8,128)(2,1)S(1)}, f32[16,768]{1,0:T(8,128)S(1)}) custom-call(f32[16,264,128]{2,1,0:T(8,128)S(1)} %get-tuple-element.126.refs_0_, f32[16,264,128]{2,1,0:T(8,128)S(1)} %get-tuple-element.127.refs_1_, ...), custom_call_target="tpu_custom_call" | custom-call | flops 1 | bytes 1 | tf_op jit(solution)/shard_map/scan_backward/pallas_call | solution.py:720
  66.7 1.3 %collective-permute-start.25 = (f32[8,768]{1,0:T(8,128)S(1)}, f32[8,768]{1,0:T(8,128)S(1)}, u32[]{:S(2)}, u32[]{:S(2)}) collective-permute-start(f32[8,768]{1,0:T(8,128)S(1)} %get-tuple-element.155), channel_id=1, source_target_pairs={{1,0},{2,1},{3,2},{4,3},{5,4},{6,5},{7,6},{9,8},{10,9},{11,10},{12... | collective-permute-start | bytes 73736 | tf_op jit(solution)/shard_map/ppermute | solution.py:770
  68.0 3.0 %collective-permute-done.23.c.four = bf16[224,768]{1,0:T(8,128)(2,1)S(1)} collective-permute-done((bf16[224,768]{1,0:T(8,128)(2,1)S(1)}, bf16[224,768]{1,0:T(8,128)(2,1)S(1)}, u32[]{:S(2)}, u32[]{:S(2)}) %collective-permute-start.23) | collective-permute-done | bytes 344096 | tf_op jit(solution)/shard_map/ppermute | solution.py:752
  71.1 1.9 %small_grads.1 = (f32[104,768]{1,0:T(8,128)S(1)}, f32[256,768]{1,0:T(8,128)S(1)}) custom-call(bf16[256,768]{1,0:T(8,128)(2,1)S(1)} %get-tuple-element.148.gpre, bf16[256,128]{1,0:T(8,128)(2,1)S(1)} %get-tuple-element.149.gxproj, f32[256,128]{1,0:T(8,128)S(1)} %get-tuple-element.100.refs_10_.xproj, ...), custom_call_target="tpu_custom_call" | custom-call | flops 1 | bytes 1 | tf_op jit(solution)/shard_map/small_grads/pallas_call | solution.py:720
  74.0 1.6 %collective-permute-start.32 = (bf16[96,768]{1,0:T(8,128)(2,1)S(1)}, bf16[96,768]{1,0:T(8,128)(2,1)S(1)}, u32[]{:S(2)}, u32[]{:S(2)}) collective-permute-start(bf16[96,768]{1,0:T(8,128)(2,1)S(1)} %add_parts.2.a), channel_id=1, source_target_pairs={{0,8},{8,0},{16,24},{24,16},{1,9},{9,1},{17,25},{25,17},{2,10},{10... | collective-permute-start | bytes 442376 | tf_op jit(solution)/shard_map/ppermute | solution.py:752
  76.6 1.3 %collective-permute-start.28 = (bf16[64,768]{1,0:T(8,128)(2,1)S(1)}, bf16[64,768]{1,0:T(8,128)(2,1)S(1)}, u32[]{:S(2)}, u32[]{:S(2)}) collective-permute-start(bf16[64,768]{1,0:T(8,128)(2,1)S(1)} %get-tuple-element.161), channel_id=1, source_target_pairs={{0,4},{1,5},{2,6},{3,7},{4,0},{5,1},{6,2},{7,3},{8,12},{9,13},{10,... | collective-permute-start | bytes 294920 | tf_op jit(solution)/shard_map/ppermute | solution.py:752
  77.9 1.5 %collective-permute-start.29 = (bf16[64,768]{1,0:T(8,128)(2,1)S(1)}, bf16[64,768]{1,0:T(8,128)(2,1)S(1)}, u32[]{:S(2)}, u32[]{:S(2)}) collective-permute-start(bf16[64,768]{1,0:T(8,128)(2,1)S(1)} %get-tuple-element.162), channel_id=1, source_target_pairs={{0,6},{1,7},{2,4},{3,5},{4,2},{5,3},{6,0},{7,1},{8,14},{9,15},{10,... | collective-permute-start | bytes 294920 | tf_op jit(solution)/shard_map/ppermute | solution.py:752
  80.3 2.7 %collective-permute-start.33 = (bf16[96,768]{1,0:T(8,128)(2,1)S(1)}, bf16[96,768]{1,0:T(8,128)(2,1)S(1)}, u32[]{:S(2)}, u32[]{:S(2)}) collective-permute-start(bf16[96,768]{1,0:T(8,128)(2,1)S(1)} %add_pair.4.a), channel_id=1, source_target_pairs={{0,16},{8,24},{16,0},{24,8},{1,17},{9,25},{17,1},{25,9},{2,18},{10... | collective-permute-start | bytes 442376 | tf_op jit(solution)/shard_map/ppermute | solution.py:752
  83.4 1.6 %collective-permute-start.30 = (bf16[64,768]{1,0:T(8,128)(2,1)S(1)}, bf16[64,768]{1,0:T(8,128)(2,1)S(1)}, u32[]{:S(2)}, u32[]{:S(2)}) collective-permute-start(bf16[64,768]{1,0:T(8,128)(2,1)S(1)} %add_parts.3.a), channel_id=1, source_target_pairs={{0,8},{8,0},{16,24},{24,16},{1,9},{9,1},{17,25},{25,17},{2,10},{10... | collective-permute-start | bytes 294920 | tf_op jit(solution)/shard_map/ppermute | solution.py:752
  85.1 5.1 %collective-permute-done.30.b = bf16[64,768]{1,0:T(8,128)(2,1)S(1)} collective-permute-done((bf16[64,768]{1,0:T(8,128)(2,1)S(1)}, bf16[64,768]{1,0:T(8,128)(2,1)S(1)}, u32[]{:S(2)}, u32[]{:S(2)}) %collective-permute-start.30) | collective-permute-done | bytes 98336 | tf_op jit(solution)/shard_map/ppermute | solution.py:752
  90.2 1.5 %collective-permute-start.37 = (bf16[224,768]{1,0:T(8,128)(2,1)S(1)}, bf16[224,768]{1,0:T(8,128)(2,1)S(1)}, u32[]{:S(2)}, u32[]{:S(2)}) collective-permute-start(bf16[224,768]{1,0:T(8,128)(2,1)S(1)} %add_pair_beside_rows.1.own), channel_id=1, source_target_pairs={{0,6},{1,7},{2,4},{3,5},{4,2},{5,3},{6,0},{7,1},{8,14},{9,15},{10,... | collective-permute-start | bytes 1032200 | tf_op jit(solution)/shard_map/ppermute | solution.py:752
  94.6 2.0 %collective-permute-start.34 = (bf16[64,768]{1,0:T(8,128)(2,1)S(1)}, bf16[64,768]{1,0:T(8,128)(2,1)S(1)}, u32[]{:S(2)}, u32[]{:S(2)}) collective-permute-start(bf16[64,768]{1,0:T(8,128)(2,1)S(1)} %add_pair.3.a), channel_id=1, source_target_pairs={{0,16},{8,24},{16,0},{24,8},{1,17},{9,25},{17,1},{25,9},{2,18},{10... | collective-permute-start | bytes 294920 | tf_op jit(solution)/shard_map/ppermute | solution.py:752
  97.3 5.5 %collective-permute-done.34.b = bf16[64,768]{1,0:T(8,128)(2,1)S(1)} collective-permute-done((bf16[64,768]{1,0:T(8,128)(2,1)S(1)}, bf16[64,768]{1,0:T(8,128)(2,1)S(1)}, u32[]{:S(2)}, u32[]{:S(2)}) %collective-permute-start.34) | collective-permute-done | bytes 98336 | tf_op jit(solution)/shard_map/ppermute | solution.py:752
  102.8 4.3 %collective-permute-done.36.four = bf16[224,768]{1,0:T(8,128)(2,1)S(1)} collective-permute-done((bf16[224,768]{1,0:T(8,128)(2,1)S(1)}, bf16[224,768]{1,0:T(8,128)(2,1)S(1)}, u32[]{:S(2)}, u32[]{:S(2)}) %collective-permute-start.36) | collective-permute-done | bytes 344096 | tf_op jit(solution)/shard_map/ppermute | solution.py:752
  108.0 1.4 %collective-permute-start.41 = (bf16[64,768]{1,0:T(8,128)(2,1)S(1)}, bf16[64,768]{1,0:T(8,128)(2,1)S(1)}, u32[]{:S(2)}, u32[]{:S(2)}) collective-permute-start(bf16[64,768]{1,0:T(8,128)(2,1)S(1)} %add_pair.5.own), channel_id=1, source_target_pairs={{0,6},{1,7},{2,4},{3,5},{4,2},{5,3},{6,0},{7,1},{8,14},{9,15},{10,... | collective-permute-start | bytes 294920 | tf_op jit(solution)/shard_map/ppermute | solution.py:752
  110.3 1.3 %collective-permute-start.39 = (bf16[64,768]{1,0:T(8,128)(2,1)S(1)}, bf16[64,768]{1,0:T(8,128)(2,1)S(1)}, u32[]{:S(2)}, u32[]{:S(2)}) collective-permute-start(bf16[64,768]{1,0:T(8,128)(2,1)S(1)} %add_pair.5.own), channel_id=1, source_target_pairs={{0,2},{1,3},{2,0},{3,1},{4,6},{5,7},{6,4},{7,5},{8,10},{9,11},{10,... | collective-permute-start | bytes 294920 | tf_op jit(solution)/shard_map/ppermute | solution.py:752
  111.6 3.0 %collective-permute-done.41.six = bf16[64,768]{1,0:T(8,128)(2,1)S(1)} collective-permute-done((bf16[64,768]{1,0:T(8,128)(2,1)S(1)}, bf16[64,768]{1,0:T(8,128)(2,1)S(1)}, u32[]{:S(2)}, u32[]{:S(2)}) %collective-permute-start.41) | collective-permute-done | bytes 98336 | tf_op jit(solution)/shard_map/ppermute | solution.py:752
  114.6 1.7 %collective-permute-done.40.four = bf16[64,768]{1,0:T(8,128)(2,1)S(1)} collective-permute-done((bf16[64,768]{1,0:T(8,128)(2,1)S(1)}, bf16[64,768]{1,0:T(8,128)(2,1)S(1)}, u32[]{:S(2)}, u32[]{:S(2)}) %collective-permute-start.40) | collective-permute-done | bytes 98336 | tf_op jit(solution)/shard_map/ppermute | solution.py:752
  118.1 2.4 %unpack_sums.1 = (f32[384]{0:T(512)}, f32[384,1536]{1,0:T(8,128)}, f32[4,768]{1,0:T(4,128)}, f32[768]{0:T(1024)}, f32[56,768]{1,0:T(8,128)}, /*index=5*/f32[24,7...) custom-call(s32[1]{0:T(128)} %bitcast.1.me.me_ref, ...), custom_call_target="tpu_custom_call" | custom-call | flops 1 | bytes 1 | tf_op jit(solution)/shard_map/unpack_sums/pallas_call | solution.py:720
  (88 shorter events, 22.5 us)
Async XLA Ops:
  1.7 10.0 %collective-permute-start.2 = (bf16[272,384]{1,0:T(8,128)(2,1)S(1)}, bf16[272,384]{1,0:T(8,128)(2,1)S(1)}, u32[]{:S(2)}, u32[]{:S(2)}) collective-permute-start(bf16[272,384]{1,0:T(8,128)(2,1)S(1)} %tokens_and_order.1.refs_0_), channel_id=1, source_target_pairs={{0,6},{1,7},{2,4},{3,5},{4,2},{5,3},{6,0},{7,1},{8,14},{9,15},{10,... | collective-permute-start | bytes 626696 | tf_op jit(solution)/shard_map/ppermute | solution.py:752
  5.6 9.6 %collective-permute-start.1 = (bf16[272,384]{1,0:T(8,128)(2,1)S(1)}, bf16[272,384]{1,0:T(8,128)(2,1)S(1)}, u32[]{:S(2)}, u32[]{:S(2)}) collective-permute-start(bf16[272,384]{1,0:T(8,128)(2,1)S(1)} %tokens_and_order.1.refs_0_), channel_id=1, source_target_pairs={{0,4},{1,5},{2,6},{3,7},{4,0},{5,1},{6,2},{7,3},{8,12},{9,13},{10,... | collective-permute-start | bytes 626696 | tf_op jit(solution)/shard_map/ppermute | solution.py:752
  6.1 9.4 %collective-permute-start = (bf16[272,384]{1,0:T(8,128)(2,1)S(1)}, bf16[272,384]{1,0:T(8,128)(2,1)S(1)}, u32[]{:S(2)}, u32[]{:S(2)}) collective-permute-start(bf16[272,384]{1,0:T(8,128)(2,1)S(1)} %tokens_and_order.1.refs_0_), channel_id=1, source_target_pairs={{0,2},{1,3},{2,0},{3,1},{4,6},{5,7},{6,4},{7,5},{8,10},{9,11},{10,... | collective-permute-start | bytes 626696 | tf_op jit(solution)/shard_map/ppermute | solution.py:752
  6.3 11.3 %collective-permute-start.3 = (bf16[272,384]{1,0:T(8,128)(2,1)S(1)}, bf16[272,384]{1,0:T(8,128)(2,1)S(1)}, u32[]{:S(2)}, u32[]{:S(2)}) collective-permute-start(bf16[272,384]{1,0:T(8,128)(2,1)S(1)} %tokens_and_order.1.refs_0_), channel_id=1, source_target_pairs={{0,1},{1,0},{2,3},{3,2},{4,5},{5,4},{6,7},{7,6},{8,9},{9,8},{10,11... | collective-permute-start | bytes 626696 | tf_op jit(solution)/shard_map/ppermute | solution.py:752
  11.7 7.3 %collective-permute-start.6 = (bf16[272,384]{1,0:T(8,128)(2,1)S(1)}, bf16[272,384]{1,0:T(8,128)(2,1)S(1)}, u32[]{:S(2)}, u32[]{:S(2)}) collective-permute-start(bf16[272,384]{1,0:T(8,128)(2,1)S(1)} %collective-permute-done.2.refs_3_), channel_id=1, source_target_pairs={{0,1},{1,0},{2,3},{3,2},{4,5},{5,4},{6,7},{7,6},{8,9},{9,8},{10,11... | collective-permute-start | bytes 626696 | tf_op jit(solution)/shard_map/ppermute | solution.py:752
  15.3 4.0 %collective-permute-start.5 = (bf16[272,384]{1,0:T(8,128)(2,1)S(1)}, bf16[272,384]{1,0:T(8,128)(2,1)S(1)}, u32[]{:S(2)}, u32[]{:S(2)}) collective-permute-start(bf16[272,384]{1,0:T(8,128)(2,1)S(1)} %collective-permute-done.1.refs_2_), channel_id=1, source_target_pairs={{0,1},{1,0},{2,3},{3,2},{4,5},{5,4},{6,7},{7,6},{8,9},{9,8},{10,11... | collective-permute-start | bytes 626696 | tf_op jit(solution)/shard_map/ppermute | solution.py:752
  15.6 3.7 %collective-permute-start.4 = (bf16[272,384]{1,0:T(8,128)(2,1)S(1)}, bf16[272,384]{1,0:T(8,128)(2,1)S(1)}, u32[]{:S(2)}, u32[]{:S(2)}) collective-permute-start(bf16[272,384]{1,0:T(8,128)(2,1)S(1)} %collective-permute-done.refs_1_), channel_id=1, source_target_pairs={{0,1},{1,0},{2,3},{3,2},{4,5},{5,4},{6,7},{7,6},{8,9},{9,8},{10,11... | collective-permute-start | bytes 626696 | tf_op jit(solution)/shard_map/ppermute | solution.py:752
  15.8 12.6 %collective-permute-start.9 = (bf16[256,384]{1,0:T(8,128)(2,1)}, bf16[256,384]{1,0:T(8,128)(2,1)S(1)}, u32[]{:S(2)}, u32[]{:S(2)}) collective-permute-start(bf16[256,384]{1,0:T(8,128)(2,1)} %bitcast.11), channel_id=1, source_target_pairs={{0,6},{1,7},{2,4},{3,5},{4,2},{5,3},{6,0},{7,1},{8,14},{9,15},{10,... | collective-permute-start | bytes 589832 | tf_op jit(solution)/shard_map/ppermute | solution.py:752
  17.6 10.8 %collective-permute-start.8 = (bf16[256,384]{1,0:T(8,128)(2,1)}, bf16[256,384]{1,0:T(8,128)(2,1)S(1)}, u32[]{:S(2)}, u32[]{:S(2)}) collective-permute-start(bf16[256,384]{1,0:T(8,128)(2,1)} %bitcast.12), channel_id=1, source_target_pairs={{0,4},{1,5},{2,6},{3,7},{4,0},{5,1},{6,2},{7,3},{8,12},{9,13},{10,... | collective-permute-start | bytes 589832 | tf_op jit(solution)/shard_map/ppermute | solution.py:752
  18.9 9.5 %collective-permute-start.7 = (bf16[256,384]{1,0:T(8,128)(2,1)}, bf16[256,384]{1,0:T(8,128)(2,1)S(1)}, u32[]{:S(2)}, u32[]{:S(2)}) collective-permute-start(bf16[256,384]{1,0:T(8,128)(2,1)} %bitcast.13), channel_id=1, source_target_pairs={{0,2},{1,3},{2,0},{3,1},{4,6},{5,7},{6,4},{7,5},{8,10},{9,11},{10,... | collective-permute-start | bytes 589832 | tf_op jit(solution)/shard_map/ppermute | solution.py:752
  36.3 4.5 %collective-permute-start.14 = (f32[24,768]{1,0:T(8,128)S(1)}, f32[24,768]{1,0:T(8,128)S(1)}, u32[]{:S(2)}, u32[]{:S(2)}) collective-permute-start(f32[24,768]{1,0:T(8,128)S(1)} %get-tuple-element.111), channel_id=1, source_target_pairs={{0,2},{1,3},{2,0},{3,1},{4,6},{5,7},{6,4},{7,5},{8,10},{9,11},{10,... | collective-permute-start | bytes 221192 | tf_op jit(solution)/shard_map/ppermute | solution.py:752
  38.0 5.1 %collective-permute-start.15 = (f32[24,768]{1,0:T(8,128)S(1)}, f32[24,768]{1,0:T(8,128)S(1)}, u32[]{:S(2)}, u32[]{:S(2)}) collective-permute-start(f32[24,768]{1,0:T(8,128)S(1)} %get-tuple-element.112), channel_id=1, source_target_pairs={{0,4},{1,5},{2,6},{3,7},{4,0},{5,1},{6,2},{7,3},{8,12},{9,13},{10,... | collective-permute-start | bytes 221192 | tf_op jit(solution)/shard_map/ppermute | solution.py:752
  38.7 5.3 %collective-permute-start.16 = (f32[24,768]{1,0:T(8,128)S(1)}, f32[24,768]{1,0:T(8,128)S(1)}, u32[]{:S(2)}, u32[]{:S(2)}) collective-permute-start(f32[24,768]{1,0:T(8,128)S(1)} %get-tuple-element.113), channel_id=1, source_target_pairs={{0,6},{1,7},{2,4},{3,5},{4,2},{5,3},{6,0},{7,1},{8,14},{9,15},{10,... | collective-permute-start | bytes 221192 | tf_op jit(solution)/shard_map/ppermute | solution.py:752
  39.8 4.2 %collective-permute-start.17 = (f32[24,768]{1,0:T(8,128)S(1)}, f32[24,768]{1,0:T(8,128)S(1)}, u32[]{:S(2)}, u32[]{:S(2)}) collective-permute-start(f32[24,768]{1,0:T(8,128)S(1)} %get-tuple-element.114), channel_id=1, source_target_pairs={{0,1},{1,0},{2,3},{3,2},{4,5},{5,4},{6,7},{7,6},{8,9},{9,8},{10,11... | collective-permute-start | bytes 221192 | tf_op jit(solution)/shard_map/ppermute | solution.py:752
  52.3 15.7 %collective-permute-start.22 = (bf16[224,768]{1,0:T(8,128)(2,1)S(1)}, bf16[224,768]{1,0:T(8,128)(2,1)S(1)}, u32[]{:S(2)}, u32[]{:S(2)}) collective-permute-start(bf16[224,768]{1,0:T(8,128)(2,1)S(1)} %get-tuple-element.145), channel_id=1, source_target_pairs={{0,2},{1,3},{2,0},{3,1},{4,6},{5,7},{6,4},{7,5},{8,10},{9,11},{10,... | collective-permute-start | bytes 1032200 | tf_op jit(solution)/shard_map/ppermute | solution.py:752
  53.8 17.2 %collective-permute-start.23 = (bf16[224,768]{1,0:T(8,128)(2,1)S(1)}, bf16[224,768]{1,0:T(8,128)(2,1)S(1)}, u32[]{:S(2)}, u32[]{:S(2)}) collective-permute-start(bf16[224,768]{1,0:T(8,128)(2,1)S(1)} %get-tuple-element.146), channel_id=1, source_target_pairs={{0,4},{1,5},{2,6},{3,7},{4,0},{5,1},{6,2},{7,3},{8,12},{9,13},{10,... | collective-permute-start | bytes 1032200 | tf_op jit(solution)/shard_map/ppermute | solution.py:752
  54.5 16.4 %collective-permute-start.24 = (bf16[224,768]{1,0:T(8,128)(2,1)S(1)}, bf16[224,768]{1,0:T(8,128)(2,1)S(1)}, u32[]{:S(2)}, u32[]{:S(2)}) collective-permute-start(bf16[224,768]{1,0:T(8,128)(2,1)S(1)} %get-tuple-element.147), channel_id=1, source_target_pairs={{0,6},{1,7},{2,4},{3,5},{4,2},{5,3},{6,0},{7,1},{8,14},{9,15},{10,... | collective-permute-start | bytes 1032200 | tf_op jit(solution)/shard_map/ppermute | solution.py:752
  66.7 6.3 %collective-permute-start.25 = (f32[8,768]{1,0:T(8,128)S(1)}, f32[8,768]{1,0:T(8,128)S(1)}, u32[]{:S(2)}, u32[]{:S(2)}) collective-permute-start(f32[8,768]{1,0:T(8,128)S(1)} %get-tuple-element.155), channel_id=1, source_target_pairs={{1,0},{2,1},{3,2},{4,3},{5,4},{6,5},{7,6},{9,8},{10,9},{11,10},{12... | collective-permute-start | bytes 73736 | tf_op jit(solution)/shard_map/ppermute | solution.py:770
  74.0 6.3 %collective-permute-start.32 = (bf16[96,768]{1,0:T(8,128)(2,1)S(1)}, bf16[96,768]{1,0:T(8,128)(2,1)S(1)}, u32[]{:S(2)}, u32[]{:S(2)}) collective-permute-start(bf16[96,768]{1,0:T(8,128)(2,1)S(1)} %add_parts.2.a), channel_id=1, source_target_pairs={{0,8},{8,0},{16,24},{24,16},{1,9},{9,1},{17,25},{25,17},{2,10},{10... | collective-permute-start | bytes 442376 | tf_op jit(solution)/shard_map/ppermute | solution.py:752
  75.8 7.2 %collective-permute-start.27 = (bf16[64,768]{1,0:T(8,128)(2,1)S(1)}, bf16[64,768]{1,0:T(8,128)(2,1)S(1)}, u32[]{:S(2)}, u32[]{:S(2)}) collective-permute-start(bf16[64,768]{1,0:T(8,128)(2,1)S(1)} %get-tuple-element.160), channel_id=1, source_target_pairs={{0,2},{1,3},{2,0},{3,1},{4,6},{5,7},{6,4},{7,5},{8,10},{9,11},{10,... | collective-permute-start | bytes 294920 | tf_op jit(solution)/shard_map/ppermute | solution.py:752
  76.6 6.4 %collective-permute-start.28 = (bf16[64,768]{1,0:T(8,128)(2,1)S(1)}, bf16[64,768]{1,0:T(8,128)(2,1)S(1)}, u32[]{:S(2)}, u32[]{:S(2)}) collective-permute-start(bf16[64,768]{1,0:T(8,128)(2,1)S(1)} %get-tuple-element.161), channel_id=1, source_target_pairs={{0,4},{1,5},{2,6},{3,7},{4,0},{5,1},{6,2},{7,3},{8,12},{9,13},{10,... | collective-permute-start | bytes 294920 | tf_op jit(solution)/shard_map/ppermute | solution.py:752
  77.9 5.5 %collective-permute-start.29 = (bf16[64,768]{1,0:T(8,128)(2,1)S(1)}, bf16[64,768]{1,0:T(8,128)(2,1)S(1)}, u32[]{:S(2)}, u32[]{:S(2)}) collective-permute-start(bf16[64,768]{1,0:T(8,128)(2,1)S(1)} %get-tuple-element.162), channel_id=1, source_target_pairs={{0,6},{1,7},{2,4},{3,5},{4,2},{5,3},{6,0},{7,1},{8,14},{9,15},{10,... | collective-permute-start | bytes 294920 | tf_op jit(solution)/shard_map/ppermute | solution.py:752
  80.3 9.9 %collective-permute-start.33 = (bf16[96,768]{1,0:T(8,128)(2,1)S(1)}, bf16[96,768]{1,0:T(8,128)(2,1)S(1)}, u32[]{:S(2)}, u32[]{:S(2)}) collective-permute-start(bf16[96,768]{1,0:T(8,128)(2,1)S(1)} %add_pair.4.a), channel_id=1, source_target_pairs={{0,16},{8,24},{16,0},{24,8},{1,17},{9,25},{17,1},{25,9},{2,18},{10... | collective-permute-start | bytes 442376 | tf_op jit(solution)/shard_map/ppermute | solution.py:752
  83.4 6.7 %collective-permute-start.30 = (bf16[64,768]{1,0:T(8,128)(2,1)S(1)}, bf16[64,768]{1,0:T(8,128)(2,1)S(1)}, u32[]{:S(2)}, u32[]{:S(2)}) collective-permute-start(bf16[64,768]{1,0:T(8,128)(2,1)S(1)} %add_parts.3.a), channel_id=1, source_target_pairs={{0,8},{8,0},{16,24},{24,16},{1,9},{9,1},{17,25},{25,17},{2,10},{10... | collective-permute-start | bytes 294920 | tf_op jit(solution)/shard_map/ppermute | solution.py:752
  90.2 12.6 %collective-permute-start.37 = (bf16[224,768]{1,0:T(8,128)(2,1)S(1)}, bf16[224,768]{1,0:T(8,128)(2,1)S(1)}, u32[]{:S(2)}, u32[]{:S(2)}) collective-permute-start(bf16[224,768]{1,0:T(8,128)(2,1)S(1)} %add_pair_beside_rows.1.own), channel_id=1, source_target_pairs={{0,6},{1,7},{2,4},{3,5},{4,2},{5,3},{6,0},{7,1},{8,14},{9,15},{10,... | collective-permute-start | bytes 1032200 | tf_op jit(solution)/shard_map/ppermute | solution.py:752
  91.7 15.4 %collective-permute-start.36 = (bf16[224,768]{1,0:T(8,128)(2,1)S(1)}, bf16[224,768]{1,0:T(8,128)(2,1)S(1)}, u32[]{:S(2)}, u32[]{:S(2)}) collective-permute-start(bf16[224,768]{1,0:T(8,128)(2,1)S(1)} %add_pair_beside_rows.1.own), channel_id=1, source_target_pairs={{0,4},{1,5},{2,6},{3,7},{4,0},{5,1},{6,2},{7,3},{8,12},{9,13},{10,... | collective-permute-start | bytes 1032200 | tf_op jit(solution)/shard_map/ppermute | solution.py:752
  92.8 14.3 %collective-permute-start.35 = (bf16[224,768]{1,0:T(8,128)(2,1)S(1)}, bf16[224,768]{1,0:T(8,128)(2,1)S(1)}, u32[]{:S(2)}, u32[]{:S(2)}) collective-permute-start(bf16[224,768]{1,0:T(8,128)(2,1)S(1)} %add_pair_beside_rows.1.own), channel_id=1, source_target_pairs={{0,2},{1,3},{2,0},{3,1},{4,6},{5,7},{6,4},{7,5},{8,10},{9,11},{10,... | collective-permute-start | bytes 1032200 | tf_op jit(solution)/shard_map/ppermute | solution.py:752
  94.6 8.2 %collective-permute-start.34 = (bf16[64,768]{1,0:T(8,128)(2,1)S(1)}, bf16[64,768]{1,0:T(8,128)(2,1)S(1)}, u32[]{:S(2)}, u32[]{:S(2)}) collective-permute-start(bf16[64,768]{1,0:T(8,128)(2,1)S(1)} %add_pair.3.a), channel_id=1, source_target_pairs={{0,16},{8,24},{16,0},{24,8},{1,17},{9,25},{17,1},{25,9},{2,18},{10... | collective-permute-start | bytes 294920 | tf_op jit(solution)/shard_map/ppermute | solution.py:752
  108.0 8.4 %collective-permute-start.38 = (bf16[512,768]{1,0:T(8,128)(2,1)S(1)}, bf16[512,768]{1,0:T(8,128)(2,1)S(1)}, u32[]{:S(2)}, u32[]{:S(2)}) collective-permute-start(bf16[512,768]{1,0:T(8,128)(2,1)S(1)} %get-tuple-element.172), channel_id=1, source_target_pairs={{0,1},{1,0},{2,3},{3,2},{4,5},{5,4},{6,7},{7,6},{8,9},{9,8},{10,11... | collective-permute-start | bytes 2359304 | tf_op jit(solution)/shard_map/ppermute | solution.py:752
  108.0 6.6 %collective-permute-start.41 = (bf16[64,768]{1,0:T(8,128)(2,1)S(1)}, bf16[64,768]{1,0:T(8,128)(2,1)S(1)}, u32[]{:S(2)}, u32[]{:S(2)}) collective-permute-start(bf16[64,768]{1,0:T(8,128)(2,1)S(1)} %add_pair.5.own), channel_id=1, source_target_pairs={{0,6},{1,7},{2,4},{3,5},{4,2},{5,3},{6,0},{7,1},{8,14},{9,15},{10,... | collective-permute-start | bytes 294920 | tf_op jit(solution)/shard_map/ppermute | solution.py:752
  109.4 6.8 %collective-permute-start.40 = (bf16[64,768]{1,0:T(8,128)(2,1)S(1)}, bf16[64,768]{1,0:T(8,128)(2,1)S(1)}, u32[]{:S(2)}, u32[]{:S(2)}) collective-permute-start(bf16[64,768]{1,0:T(8,128)(2,1)S(1)} %add_pair.5.own), channel_id=1, source_target_pairs={{0,4},{1,5},{2,6},{3,7},{4,0},{5,1},{6,2},{7,3},{8,12},{9,13},{10,... | collective-permute-start | bytes 294920 | tf_op jit(solution)/shard_map/ppermute | solution.py:752
  110.3 6.0 %collective-permute-start.39 = (bf16[64,768]{1,0:T(8,128)(2,1)S(1)}, bf16[64,768]{1,0:T(8,128)(2,1)S(1)}, u32[]{:S(2)}, u32[]{:S(2)}) collective-permute-start(bf16[64,768]{1,0:T(8,128)(2,1)S(1)} %add_pair.5.own), channel_id=1, source_target_pairs={{0,2},{1,3},{2,0},{3,1},{4,6},{5,7},{6,4},{7,5},{8,10},{9,11},{10,... | collective-permute-start | bytes 294920 | tf_op jit(solution)/shard_map/ppermute | solution.py:752
  (17 other events, 91.8 us)

commit v4 on v3

--- a/solution.py
+++ b/solution.py
@@ -127,13 +127,18 @@
     copies[1].wait()
 
 
+def order_column(to_row, digits):
+    both = dot(to_row, digits, ((0,), (1,)))
+    return jnp.broadcast_to(both[:, 0:1] * 128.0 + both[:, 1:2], (to_row.shape[0], LANES))
+
+
 def order_digits(order):
     sub = lax.broadcasted_iota(jnp.int32, (ORDER_ROWS, order.shape[1]), 0)
     digits = jnp.where(sub == 0, order[...] >> 7, jnp.where(sub == 1, order[...] & 127, 0))
     return digits.astype(F32).astype(BF16)
 
 
-def pre_kernel(sizes, n_pieces, n_far, me, order, *refs):
+def pre_kernel(sizes, n_pieces, n_far, me, *refs):
     rows, width, inner, rank, state, lags, clouds = sizes
     steps = rows // CHUNKS
     pieces = refs[:n_pieces]
@@ -142,7 +147,8 @@
     copies = [pltpu.make_async_copy(a, b, copied.at[k]) for k, (a, b) in enumerate(zip(far_refs, near_refs))]
     for copy in copies:
         copy.start()
-    (lengths, gain, w_in, conv_w, conv_b, w_x, w_dt, dt_b, alog, skip) = near_refs
+    (lengths, order, gain, w_in, conv_w, conv_b, w_x, w_dt, dt_b, alog, skip) = near_refs
+    copies[1].wait()
     (trans_o, normed_o, gate_o, ext_o, conv_o, act_o, step_o, xproj_o, chunkf_o, sums_o, f_o, column_o, orders_o,
      valid, far, use, bbc, wx_o, wdt_o, a2, rows_o, conv_in) = refs[n_pieces:]
     to_row = row_of_place(rows)
@@ -157,13 +163,14 @@
             orders_o[p : p + 1, :] = row[0:1] * 128.0 + row[1:2]
     for k in range(1, lags + 1):
         extra = jnp.where(sub == k, tail[0:1, rows - k : rows - k + 1] * 128.0 + tail[1:2, rows - k : rows - k + 1], extra)
-    both = dot(to_row, order_digits(order), ((0,), (1,)))
-    own = jnp.broadcast_to(both[:, 0:1] * 128.0 + both[:, 1:2], (rows, LANES))
-    column_o[...] = own
+    own = order_column(to_row, order_digits(order))
+    column_o[0] = own
+    if n_pieces == len(CUBE):
+        column_o[1] = order_column(to_row, pieces[CUBE.index(1)][rows : rows + ORDER_ROWS, :rows])
     column = jnp.concatenate([own, extra], axis=0)
     trans = gather_rows(wide(column, rows), [p[0:rows, :] for p in pieces], me, rows)
     trans_o[...] = trans[:rows].astype(BF16)
-    for copy in copies:
+    for copy in copies[:1] + copies[2:]:
         copy.wait()
     meta = scalars(me, lengths, rows)
     bias, dt_bias = as_row(conv_b), as_row(dt_b)
@@ -240,18 +247,30 @@
     f_o[...] = total
 
 
+def gather_kernel(core, me, column, own, two, four, six, out):
+    rows = own.shape[0]
+    whole = jnp.concatenate([p[...] for p in (own, two, four, six)], axis=0)
+    lane = lax.broadcasted_iota(jnp.int32, (rows, rows), 1).astype(F32)
+    place = wide(column[core], rows)
+    match = [(place - (source(me, p, len(CUBE)) * rows).astype(F32) == lane).astype(F32).astype(BF16) for p in range(4)]
+    out[...] = dot(jnp.concatenate(match, axis=1), whole).astype(BF16)
+
+
 def back_kernel(sizes, n_pieces, me, *refs):
     rows, width, inner, rank, state, lags, clouds = sizes
     steps = rows // CHUNKS
     pieces = refs[:n_pieces]
     gate, far, xproj, a2, w_out, sums, f, column = refs[n_pieces : n_pieces + 8]
-    n_out = (len(CUBE) - 4 if n_pieces == len(CUBE) else 1)
-    dy_o, gg_o, gm, cbc, chunkb_o = refs[n_pieces + 8 : n_pieces + 13]
-    carries_o = refs[n_pieces + 13 : n_pieces + 13 + n_out]
-    near_out, copied = refs[n_pieces + 13 + n_out :]
+    n_out = len(SENT) if n_pieces == 2 else 1
+    dy_o, gg_o, gm, cbc, chunkb_o, near_out = refs[n_pieces + 8 : n_pieces + 14]
+    carries_o = refs[n_pieces + 14 : n_pieces + 14 + n_out]
+    (copied,) = refs[n_pieces + 14 + n_out :]
     copy = pltpu.make_async_copy(w_out, near_out, copied)
     copy.start()
-    trans_dy = gather_rows(wide(column[...], rows), [p[0:rows, :] for p in pieces], me, rows).astype(BF16)
+    if n_pieces == 2:
+        trans_dy = (pieces[0][...].astype(F32) + pieces[1][...].astype(F32)).astype(BF16)
+    else:
+        trans_dy = gather_rows(wide(column[0], rows), [p[...] for p in pieces], me, rows).astype(BF16)
     dy_o[...] = trans_dy
     copy.wait()
     gg_o[...] = dot(trans_dy, near_out[...], ((1,), (1,)))
@@ -283,16 +302,20 @@
     total = jnp.zeros((state, inner), F32)
     for c in reversed(range(CHUNKS)):
         total = jnp.exp2(a2[...] * sums[c : c + 1, :]) * total + chunk_of(chunkb_o, c, state)
-    passed = jnp.broadcast_to(jnp.sum(sums[...], axis=0, keepdims=True), (CHUNKS, inner))
+    passed = jnp.sum(sums[...], axis=0, keepdims=True)
+    blocks = inner // LANES
+    passed = jnp.concatenate([passed[:, b * LANES : (b + 1) * LANES] for b in range(blocks)], axis=0)
+    passed = jnp.concatenate([passed, jnp.zeros((state - blocks, LANES), F32)], axis=0)
     if n_out == 1:
-        carries_o[0][:state, :] = f[...]
-        carries_o[0][state : 2 * state, :] = total
-        carries_o[0][2 * state :, :] = passed
+        carries_o[0][:state, :inner] = f[...]
+        carries_o[0][state:, :inner] = total
+        carries_o[0][:state, inner:] = passed
+        carries_o[0][state:, inner:] = passed
         return
     for out, d in zip(carries_o, SENT):
         later = jnp.bitwise_xor(me[0], d) > me[0]
-        out[:state, :] = jnp.where(later, f[...], total)
-        out[state:, :] = passed
+        out[:, :inner] = jnp.where(later, f[...], total)
+        out[:, inner:] = passed
 
 
 def core_of(me, devices):
@@ -300,27 +323,31 @@
 
 
 def hold_carries(held, carries, me):
-    n_pieces, size = len(carries), carries[0].shape[0]
+    n_pieces, count, inner = len(carries), carries[0].shape[0], held.shape[1]
     devices = len(CUBE) if n_pieces == len(CUBE) - 1 else n_pieces
+    size = count + CHUNKS
     for p in range(n_pieces):
         whence = source(me, p + 1, devices) if devices > n_pieces else p
-        held[pl.ds(pl.multiple_of(whence * size, CHUNKS), size), :] = carries[p][...]
-    return devices
+        base = whence * size
+        held[pl.ds(pl.multiple_of(base, CHUNKS), count), :] = carries[p][:, :inner]
+        passed = [carries[p][b : b + 1, inner:] for b in range(inner // LANES)]
+        passed = jnp.broadcast_to(jnp.concatenate(passed, axis=1), (CHUNKS, inner))
+        held[pl.ds(pl.multiple_of(base + count, CHUNKS), CHUNKS), :] = passed
+    return devices, size
 
 
 def scan_forward_kernel(sizes, n_pieces, me_ref, *refs):
     rows, width, inner, rank, state, lags, clouds = sizes
     steps = rows // CHUNKS
     carries = refs[:n_pieces]
-    (trans_dy, normed, gg, gate, act, far, use, bbc, cbc, chunkf, sums, a2, consts, w_out) = refs[n_pieces : n_pieces + 14]
+    (trans_dy, normed, gg, gate, act, far, use, bbc, cbc, chunkf, sums, a2, consts) = refs[n_pieces : n_pieces + 13]
     blocks = inner // LANES
-    states = refs[n_pieces + 14 : n_pieces + 14 + blocks]
-    (branch_o, gz_o, keep_o, send_o) = refs[n_pieces + 14 + blocks : n_pieces + 18 + blocks]
-    (mixed, sstart, gated, held) = refs[n_pieces + 18 + blocks :]
+    states = refs[n_pieces + 13 : n_pieces + 13 + blocks]
+    (gated, gz_o, keep_o, send_o) = refs[n_pieces + 13 + blocks : n_pieces + 17 + blocks]
+    (mixed, sstart, held) = refs[n_pieces + 17 + blocks :]
     me = me_ref[0]
     skips = consts[lags + 1 : lags + 2, :]
-    size = carries[0].shape[0]
-    devices = hold_carries(held, carries, me_ref)
+    devices, size = hold_carries(held, carries, me_ref)
 
     def ahead(s, flow):
         base = pl.multiple_of(s * size, CHUNKS)
@@ -368,7 +395,6 @@
         return carry
 
     lax.fori_loop(0, rows // BLOCK, gating, 0)
-    branch_o[...] = dot(gated[...], w_out[...]).astype(BF16)
     second = core_of(me, devices) == 1
     wout_g = dot(trans_dy[...], gated[...], ((0,), (0,))).astype(BF16)
     gate_g = dot(normed[...], gz_o[...], ((0,), (0,))).astype(BF16)
@@ -376,14 +402,14 @@
     send_o[...] = jnp.where(second, wout_g, gate_g)
 
 
-def adjoint_carries_kernel(sizes, n_pieces, me_ref, *refs):
+def branch_kernel(sizes, n_pieces, me_ref, *refs):
     rows, width, inner, rank, state, lags, clouds = sizes
     carries = refs[:n_pieces]
-    chunkb, sums, a2, gstart, held = refs[n_pieces:]
+    chunkb, sums, a2, gated, w_out, gstart, branch_o, held = refs[n_pieces:]
     me = me_ref[0]
-    size = carries[0].shape[0]
+    branch_o[...] = dot(gated[...], w_out[...]).astype(BF16)
+    devices, size = hold_carries(held, carries, me_ref)
     back = size - CHUNKS - state
-    devices = hold_carries(held, carries, me_ref)
 
     def behind(k, flow):
         s = devices - 1 - k
@@ -648,6 +674,18 @@
         out[pl.ds(pl.multiple_of(first + chip * part, BLOCK), part), :] = piece[piece.shape[0] - part :, :]
 
 
+def stack_kernel(a, b, out):
+    out[0 : a.shape[0], :] = a[...]
+    out[a.shape[0] :, :] = b[...]
+
+
+def both_chips_kernel(part_a, part_b, me, own, two, four, six, out):
+    for d, piece in enumerate((own, two, four, six)):
+        chip = jnp.bitwise_xor(lax.div(me[0], 2), d)
+        out[pl.ds(pl.multiple_of(chip * part_a, BLOCK), part_a), :] = piece[0:part_a, :]
+        out[pl.ds(pl.multiple_of(4 * part_a + chip * part_b, BLOCK), part_b), :] = piece[part_a:, :]
+
+
 def chips_kernel(me, own, two, four, six, out):
     by_chip(out, 0, (own, two, four, six), me, own.shape[0])
 
@@ -671,24 +709,52 @@
         by_chip(theirs_o, rows // 2, pieces, me, part)
 
 
+def share_both_kernel(rows, width, me, orders, *refs):
+    one, two, (mine_one, mine_two, theirs_o) = refs[0:4], refs[4:8], refs[8:]
+    share_kernel(rows, width, me, orders, *one, mine_one, theirs_o.at[pl.ds(0, rows // 2)])
+    share_kernel(rows, width, me, orders, *two, mine_two, theirs_o.at[pl.ds(rows // 2, rows // 2)])
+
+
+def arrive_both_kernel(here_one, here_two, mine_one, mine_two, theirs, out_one, out_two):
+    half = here_one.shape[0] // 2
+    arrive_kernel(here_one, mine_one, theirs.at[pl.ds(0, half)], out_one)
+    arrive_kernel(here_two, mine_two, theirs.at[pl.ds(half, half)], out_two)
+
+
 def arrive_kernel(here, mine, theirs, out):
     rows, width = here.shape
     moved = mine[...].astype(F32) + unfold(theirs, rows, width).astype(F32)
     out[...] = (here[...].astype(F32) + moved).astype(BF16)
 
 
-def unpack_kernel(sizes, devices, me, own_one, other_one, own_two, other_two, *refs):
+def halves_of(own, other, me, devices):
+    second = core_of(me[0], devices) == 1
+    return jnp.where(second, other, own), jnp.where(second, own, other)
+
+
+def first_results_kernel(half, devices, me, own, other, wout_o, win_o, turned, copied):
+    wout, gate = halves_of(own[own.shape[0] - half :, :], other[other.shape[0] - half :, :], me, devices)
+    turned[...] = gate.astype(F32)
+    inner = turned.shape[1]
+    copy = pltpu.make_async_copy(turned, win_o.at[:, pl.ds(inner, inner)], copied)
+    copy.start()
+    wout_o[...] = wout.astype(F32).T
+    copy.wait()
+
+
+def last_results_kernel(sizes, half, devices, me, own, other, win, *refs):
     rows, width, inner, rank, state, lags, clouds = sizes
-    (gain_o, win_o, taps_o, convb_o, wx_o, wdt_o, dtb_o, alog_o, skip_o, wout_o, all_one, all_two) = refs
-    for own, other, whole, n in ((own_one, other_one, all_one, devices[0]), (own_two, other_two, all_two, devices[1])):
-        core, half = core_of(me[0], n), whole.shape[0] // 2
-        for k, piece in ((core, own), (1 - core, other)):
-            whole[pl.ds(pl.multiple_of(k * half, BLOCK), half), :] = piece[piece.shape[0] - half :, :]
-    wout_o[...] = all_one[0:width, :].astype(F32).T
-    win_o[:, inner:] = all_one[width : 2 * width, :].astype(F32)
-    win_o[:, :inner] = all_two[0:width, :].astype(F32)
+    (gain_o, win_o, taps_o, convb_o, wx_o, wdt_o, dtb_o, alog_o, skip_o, near, copied) = refs
+    first, second = halves_of(own[0:half, :], other[0:half, :], me, devices)
+    whole = jnp.concatenate([first, second], axis=0)
+    copies = []
+    for k in range(width // LANES):
+        r = pl.ds(k * LANES, LANES)
+        near[r, :] = whole[k * LANES : (k + 1) * LANES].astype(F32)
+        copies.append(pltpu.make_async_copy(near.at[r], win_o.at[r, pl.ds(0, inner)], copied.at[k]))
+        copies[-1].start()
     n_small = small_rows(sizes)
-    small = all_two[width : width + n_small, :].astype(F32)
+    small = whole[width : width + n_small].astype(F32)
     alog_o[...] = small[0:state]
     at = state
     wx_o[...] = small[at : at + rank + 2 * state]
@@ -700,6 +766,8 @@
     at += 3
     taps_o[...] = small[at : at + lags + 1]
     gain_o[...] = small[n_small - 1 : n_small, :width].reshape(width)
+    for copy in copies:
+        copy.wait()
 
 
 def place_kernel(rows, n_pieces, me, here, orders, *refs):
@@ -710,7 +778,7 @@
     out[...] = (here[...].astype(F32) + moved).astype(BF16)
 
 
-def call(kernel, outs, scratch, n_smem, name, room, time=1.0, far_ins=()):
+def call(kernel, outs, scratch, n_smem, name, room, time=1.0, far_ins=(), far_outs=(), aliases={}):
     vmem = pl.BlockSpec(memory_space=pltpu.VMEM)
     smem = pl.BlockSpec(memory_space=pltpu.SMEM)
     anywhere = pl.BlockSpec(memory_space=pltpu.HBM)
@@ -721,7 +789,8 @@
             kernel,
             out_shape=[jax.ShapeDtypeStruct(*part) if isinstance(part, tuple) else part for part in outs],
             in_specs=[smem if k < n_smem else anywhere if k in far_ins else vmem for k in range(len(args))],
-            out_specs=[vmem] * len(outs),
+            out_specs=[anywhere if k in far_outs else vmem for k in range(len(outs))],
+            input_output_aliases=aliases,
             scratch_shapes=[pltpu.VMEM(*part) if isinstance(part, tuple) else part for part in scratch],
             compiler_params=pltpu.CompilerParams(vmem_limit_bytes=room * MIB),
             cost_estimate=pl.CostEstimate(
@@ -733,13 +802,13 @@
     return run
 
 
-CFG = {'dy': 'd6', 'dy1': 'fwd', 'adj': 'gstart', 'rim': '', 'small': 'one', 'z1': 'send', 'halves': '', 'pair': '', 'share': 'pair', 'hold': 'out', 'm3': 'pair', 'd': 'out', 'share3': 'total'}
+CFG = {'adj': 'gstart', 'arrive': '', 'chips1': 'total', 'chips2': 'first', 'd': '', 'dy': 'd6', 'dy1': 'fwd', 'halves': '', 'hold': '', 'm3': 'own', 'one': 'b2+b4+b6+pair', 'p1d': 'z', 'pair': 'd2', 'rim': '', 'share': 'pair', 'share3': 'total', 'small': 'mid', 'z1': 'send', 'fin': '', 'sumz': 'z1'}
 
 
 def tie(name, value, choices):
     pick = CFG.get(name, "")
     for k in pick.split("+") if pick else ():
-        value = after(value, choices[k])
+        value = after(value, choices[k]) if k in choices else value
     return value
 
 
@@ -803,7 +872,7 @@
         4,
         far_ins=(0, 1),
     )(here_x, order)
-    weights = (lengths, norm_gain, w_in, conv_weight.T, conv_bias, w_x.T, w_dt, dt_bias, a_log.T, d_skip)
+    weights = (lengths, order, norm_gain, w_in, conv_weight.T, conv_bias, w_x.T, w_dt, dt_bias, a_log.T, d_skip)
     if cube:
         across_x = [payload] + [swap(payload, "seq", d) for d in CUBE[1:4]]
         send_dy = tie("dy", here_dy, {"d2": across_x[1], "d4": across_x[2], "d6": across_x[3]})
@@ -830,7 +899,7 @@
             (carried, F32),
             ((CHUNKS, inner), F32),
             ((state, inner), F32),
-            (lane, F32),
+            ((1 + cube, *lane), F32),
             ((4 if cube else n, rows), F32),
             ((lags, rows, LANES), F32),
             (big, F32),
@@ -848,49 +917,53 @@
         "forward_local",
         24,
         9,
-        far_ins=tuple(range(n + 2, n + 2 + len(weights))),
-    )(me, order, *pieces_x, *weights)
+        far_ins=tuple(range(n + 1, n + 1 + len(weights))),
+    )(me, *pieces_x, *weights)
     if cube:
-        across_dy = [tie("dy1", part, {"fwd": xproj}) for part in across_dy]
-        pieces_dy = across_dy + [swap(part, "seq", 1) for part in across_dy]
-    carry_rows = (state + CHUNKS, 2 * state + CHUNKS)[not cube]
+        gather = lambda core: call(
+            functools.partial(gather_kernel, core), [((rows, width), BF16)], [], 1, ("gather", "gather_other")[core], 8
+        )
+        (theirs,) = gather(1)(me, column, *across_dy)
+        (mine,) = gather(0)(me, after(column, theirs), *across_dy)
+        pieces_dy = [mine, swap(theirs, "seq", 1)]
+    carry_rows = (state, 2 * state)[not cube]
     n_sent = (len(SENT), 1)[not cube]
-    trans_dy, gg, gm, cbc, chunkb, *carries = call(
-        functools.partial(back_kernel, sizes, n),
-        [((rows, width), BF16), (big, F32), (big, F32), (spread, F32), (carried, F32)]
-        + [((carry_rows, inner), F32)] * n_sent,
-        [(w_out.shape, w_out.dtype), pltpu.SemaphoreType.DMA],
+    trans_dy, gg, gm, cbc, chunkb, near_out, *carries = call(
+        functools.partial(back_kernel, sizes, len(pieces_dy)),
+        [((rows, width), BF16), (big, F32), (big, F32), (spread, F32), (carried, F32), (w_out.shape, BF16)]
+        + [((carry_rows, inner + LANES), F32)] * n_sent,
+        [pltpu.SemaphoreType.DMA],
         1,
         "backward_local",
         20,
         7,
-        far_ins=(n + 5,),
+        far_ins=(len(pieces_dy) + 5,),
     )(me, *pieces_dy, gate, far, xproj, a2, w_out, sums, f, column)
     carries = spread_carries(carries, "seq")
     n_small = small_rows(sizes)
-    held = ((n * carry_rows, inner), F32)
+    held = ((n * (carry_rows + CHUNKS), inner), F32)
     kept = [pltpu.VMEM((state, rows + CHUNKS, LANES), F32)] * (inner // LANES)
-    *states, branch, gz, keep, send = call(
+    *states, gated, gz, keep, send = call(
         functools.partial(scan_forward_kernel, sizes, len(carries)),
-        [*kept, ((rows, width), BF16), (big, BF16), ((width, inner), BF16), ((width, inner), BF16)],
-        [(big, F32), (carried, F32), (big, BF16), held],
+        [*kept, (big, BF16), (big, BF16), ((width, inner), BF16), ((width, inner), BF16)],
+        [(big, F32), (carried, F32), held],
         1,
         "scan_forward",
         18,
         7,
-    )(me, *carries, trans_dy, normed, gg, gate, act, far, use, bbc, cbc, chunkf, sums, a2, row_consts, w_out)
+    )(me, *carries, trans_dy, normed, gg, gate, act, far, use, bbc, cbc, chunkf, sums, a2, row_consts)
     first = (keep, send)
     half_one, half_two = width, -(-(width + n_small) // (8 * BLOCK)) * (4 * BLOCK)
     got = swap(send, "seq", 1) if cube else None
-    (gstart,) = call(
-        functools.partial(adjoint_carries_kernel, sizes, len(carries)),
-        [(carried, F32)],
+    gstart, branch = call(
+        functools.partial(branch_kernel, sizes, len(carries)),
+        [(carried, F32), ((rows, width), BF16)],
         [held],
         1,
-        "adjoint_carries",
+        "adjoint_carries_and_branch",
         8,
         1.5,
-    )(me, *carries, chunkb, sums, a2)
+    )(me, *carries, chunkb, sums, a2, gated, near_out)
     if cube:
         part_one = half_one // 4
         beside_one = ((rows // 2 + part_one, inner), BF16)
@@ -909,10 +982,10 @@
     )(*[pltpu.with_memory_space_constraint(part, pltpu.VMEM) for part in states], gstart, far, use, bbc, cbc, gm, step, act, conv, valid, a2, row_consts, w_x_pad, w_dt_pad)
     rim = from_behind(rim, "seq", -1)
     if cube:
-        (one,) = call(sum_kernel, [((part_one, inner), BF16)], [], 0, "add_parts", 4)(
-            tie("rim", after(own_one, gpre), {"rim": rim}), *away_one
-        )
-        gpre = tie("small", gpre, {"one": one})
+        add_one = call(sum_kernel, [((part_one, inner), BF16)], [], 0, "add_parts", 4)
+        if CFG["small"] != "mid":
+            (one,) = add_one(tie("rim", after(own_one, gpre), {"rim": rim}), *away_one)
+            gpre = tie("small", gpre, {"one": one})
     small, gci = call(
         functools.partial(small_kernel, sizes),
         [((n_small, inner), F32), (big, F32)],
@@ -922,6 +995,9 @@
         16,
         1.6,
     )(gpre, gxproj, xproj, act, gconv, ext, valid, gm, row_consts, galog)
+    if cube and CFG["small"] == "mid":
+        (one,) = add_one(after(own_one, small), *away_one)
+        small = after(small, one)
     back, keep, send = call(
         functools.partial(final_kernel, sizes, devices),
         [((rows, width), BF16), ((half_two, inner), BF16), ((half_two, inner), BF16)],
@@ -930,6 +1006,19 @@
         "input_projection_grads",
         16,
     )(me, trans, normed, gci, gz, rim, small, norm_gain, w_in)
+    cores = devices if cube else 0
+
+    def first_results(own, other):
+        return call(
+            functools.partial(first_results_kernel, half_one, cores),
+            [((inner, width), F32), ((width, 2 * inner), F32)],
+            [((width, inner), F32), pltpu.SemaphoreType.DMA],
+            1,
+            "first_results",
+            16,
+            far_outs=(1,),
+        )(me, own, other)
+
     if cube:
         part_two = half_two // 4
         piece_one, piece_two = ((part_one, inner), BF16), ((part_two, inner), BF16)
@@ -938,9 +1027,10 @@
         arrive = call(arrive_kernel, rows_out, [], 0, "add_arrived", 4)
         got = swap(send, "seq", 1)
         at = {"send": send}
+        away_first = away_one
 
         def branch_rows(point, value):
-            if CFG["share"] != point:
+            if CFG["share"] != point or CFG["p1d"] == "z":
                 return value
             mine, theirs = call(
                 functools.partial(share_kernel, rows, width),
@@ -960,53 +1050,115 @@
         own_two, *sent = call(halves_kernel, [piece_two] * 4, [], 1, "add_halves", 4)(me, keep, got)
         away_two = [swap(block, "seq", d) for block, d in zip(sent, SENT)]
         at.update(d2=away_two[0], d4=away_two[1], d6=away_two[2], own=own_two)
+        at["z1"] = z_one
         (one,) = call(pair_kernel, [piece_one], [], 0, "add_pair", 4)(tie("pair", one, at), z_one)
         z_one = swap(one, "dp", 2)
-        own_two = branch_rows("own", own_two)
+        at["zz"] = z_one
+        own_two = tie("sumz", branch_rows("own", own_two), at)
         (two,) = call(sum_kernel, [piece_two], [], 0, "add_parts", 4)(own_two, *away_two)
         z_two = swap(two, "dp", 1)
         at["summed"], at["z"] = two, z_two
-        two = branch_rows("summed", two)
+        two = tie("c1", branch_rows("summed", two), at)
         (two,) = pair_two(two, z_two)
         z_two = swap(two, "dp", 2)
         at["pair"] = two
         two = branch_rows("pair", two)
+        if CFG["p1d"] == "z":
+            back = tie("m3", back, at)
+            away_back = [swap(back, "seq", d) for d in SENT[:3]]
+            at.update(b2=away_back[0], b4=away_back[1], b6=away_back[2])
+            mine_b, mine_g, theirs = call(
+                functools.partial(share_both_kernel, rows, width),
+                rows_out * 2 + [((rows, inner), BF16)],
+                [],
+                1,
+                "share_rows",
+                12,
+            )(me, orders, tie("share", branch, at), *away_first, back, *away_back)
+            output, input_grad = call(arrive_both_kernel, rows_out * 2, [], 0, "add_arrived", 8)(
+                here_x, here_dy, mine_b, mine_g, swap(theirs, "seq", 1)
+            )
+            at.update(out=output, arrived=input_grad)
+            two = tie("fin", two, at)
         (two,) = pair_two(two, z_two)
         at["total"] = two
         branch_rows("total", two)
-        (one,) = call(pair_beside_kernel, [beside_one], [], 0, "add_pair_beside_rows", 8)(
-            one, z_one, tie("m3", back, at)
-        )
-        away_one = [swap(one, "seq", d) for d in SENT[:3]]
-        if CFG["d"] == "ag":
-            whole = lax.all_gather(two, "seq").reshape(4, 2, *two.shape).swapaxes(0, 1).reshape(2, half_two, inner)
-            at["d2"] = at["d4"] = at["d6"] = whole
-        else:
+        if CFG["p1d"] != "z":
+            back = tie("m3", back, at)
+        share = functools.partial(share_kernel, rows, width)
+        if CFG["p1d"] == "m3":
+            (one,) = call(pair_beside_kernel, [beside_one], [], 0, "add_pair_beside_rows", 8)(one, z_one, back)
+            away_one = [swap(one, "seq", d) for d in SENT[:3]]
+            two = tie("d", two, at)
             away_two = [swap(two, "seq", d) for d in SENT[:3]]
             at.update(d2=away_two[0], d4=away_two[1], d6=away_two[2])
-        mine, theirs, own_one = call(
-            functools.partial(share_kernel, rows, width),
-            rows_out + [((rows // 2 + half_one, inner), BF16), ((half_one, inner), BF16)],
-            [],
-            1,
-            "share_rows_and_parts",
-            12,
-        )(me, orders, tie("share3", one, at), *away_one)
-        other_one = swap(theirs, "seq", 1)
-        (input_grad,) = arrive(here_dy, mine, other_one)
+            mine, theirs, own_one = call(
+                share,
+                rows_out + [((rows // 2 + half_one, inner), BF16), ((half_one, inner), BF16)],
+                [],
+                1,
+                "share_rows_and_parts",
+                12,
+            )(me, orders, tie("share3", one, at), *away_one)
+            theirs = swap(theirs, "seq", 1)
+            f_wout, f_win = first_results(own_one, theirs)
+            (input_grad,) = arrive(here_dy, mine, theirs)
+            at.update(first=f_wout, arrived=input_grad)
+            (own_two,) = call(chips_kernel, [((half_two, inner), BF16)], [], 1, "order_parts", 4)(
+                me, tie("chips2", two, at), *away_two
+            )
+            other_two = swap(own_two, "seq", 1)
+        else:
+            if CFG["p1d"] != "z":
+                away_back = [swap(back, "seq", d) for d in SENT[:3]]
+                at.update(b2=away_back[0], b4=away_back[1], b6=away_back[2])
+            (one,) = call(pair_kernel, [piece_one], [], 0, "add_pair", 4)(one, z_one)
+            if CFG["p1d"] in "yz":
+                away_one = [swap(tie("one", one, at), "seq", d) for d in SENT[:3]]
+                at.update(o2=away_one[0], o4=away_one[1], o6=away_one[2])
+                (own_one,) = call(chips_kernel, [((half_one, inner), BF16)], [], 1, "order_parts", 4)(
+                    me, tie("chips1", one, at), *away_one
+                )
+                f_wout, f_win = first_results(own_one, swap(own_one, "seq", 1))
+                at.update(first=f_wout)
+                two = tie("d", two, at)
+                away_two = [swap(two, "seq", d) for d in SENT[:3]]
+                at.update(d2=away_two[0], d4=away_two[1], d6=away_two[2])
+                (own_two,) = call(chips_kernel, [((half_two, inner), BF16)], [], 1, "order_parts", 4)(
+                    me, tie("chips2", two, at), *away_two
+                )
+                other_two = swap(own_two, "seq", 1)
+            else:
+                two = tie("d", two, at)
+                (both,) = call(stack_kernel, [((part_two + part_one, inner), BF16)], [], 0, "stack", 4)(two, one)
+                away = [swap(both, "seq", d) for d in SENT[:3]]
+                at.update(d2=away[0], d4=away[1], d6=away[2])
+                (own_one,) = call(
+                    functools.partial(both_chips_kernel, part_two, part_one),
+                    [((half_two + half_one, inner), BF16)],
+                    [],
+                    1,
+                    "order_parts",
+                    8,
+                )(me, both, *away)
+                own_two, other_two = own_one, swap(own_one, "seq", 1)
+                f_wout, f_win = first_results(own_two, other_two)
+            if CFG["p1d"] != "z":
+                mine, theirs = call(share, rows_out + [((rows // 2, inner), BF16)], [], 1, "share_rows", 8)(
+                    me, orders, tie("share3", back, at), *away_back
+                )
+                (input_grad,) = arrive(tie("arrive", here_dy, at), mine, swap(theirs, "seq", 1))
+        totals = (own_two, other_two)
         output = at["out"]
-        if CFG["d"] == "ag":
-            totals = (own_one, other_one, whole[0], whole[1])
-        else:
-            (own_two,) = call(chips_kernel, [((half_two, inner), BF16)], [], 1, "order_parts", 4)(me, two, *away_two)
-            totals = (own_one, other_one, own_two, swap(own_two, "seq", 1))
     else:
         totals = [lax.psum(half.astype(F32), ("dp", "seq")).astype(BF16) for half in (*first, keep, send)]
+        f_wout, f_win = first_results(*totals[:2])
+        totals = totals[2:]
         place = call(functools.partial(place_kernel, rows, n), [((rows, width), BF16)], [], 1, "to_hilbert", 24)
         (output,) = place(me, here_x, orders, *spread_pieces(branch, "seq"))
         (input_grad,) = place(me, here_dy, orders, *spread_pieces(back, "seq"))
-    weights = call(
-        functools.partial(unpack_kernel, sizes, (devices if cube else 0, devices if cube and CFG["d"] != "ag" else 0)),
+    gain, f_win, taps_g, convb, wx, wdt, dtb, alog, skip = call(
+        functools.partial(last_results_kernel, sizes, half_two, cores),
         [
             ((width,), F32),
             ((width, 2 * inner), F32),
@@ -1017,16 +1169,16 @@
             ((inner,), F32),
             ((state, inner), F32),
             ((inner,), F32),
-            ((inner, width), F32),
         ],
-        [((2 * half_one, inner), BF16), ((2 * half_two, inner), BF16)],
+        [((width, inner), F32), pltpu.SemaphoreType.DMA((width // LANES,))],
         1,
-        "unpack_sums",
-        24,
-        2.4,
-    )(me, *totals)
-    turned = [v.T if v.ndim == 2 and v.shape[1] == inner and v.shape[0] != rank else v for v in weights]
-    return (output[None], input_grad[None], *turned)
+        "last_results",
+        16,
+        far_ins=(3,),
+        far_outs=(1,),
+        aliases={3: 1},
+    )(me, *totals, f_win)
+    return (output[None], input_grad[None], gain, f_win, taps_g.T, convb, wx.T, wdt, dtb, alog.T, skip, f_wout)
 
 
 def solution(mesh):

time: 121 us -> 111 us (0.917)
  waiting for transfers between devices: 42.2 us -> 28.5 us
  starting transfers between devices: 37 us -> 40.9 us
    ppermute x42, waiting for transfers between devices: 42.2 us -> 28.5 us  [swap(): lax.ppermute(block, axis, [(i, i ^ distance) for i in range(devices)])]
    ppermute x42, starting transfers between devices: 35.7 us -> 39.6 us  [swap(): lax.ppermute(block, axis, [(i, i ^ distance) for i in range(devices)])]
    pallas_call x22 -> x24, Pallas kernels: 39.7 us -> 40.6 us  [run(): pl.pallas_call(kernel, out_shape=[jax.ShapeDtypeStruct(*part) if isinstan...]
  transfers between devices with their start and end apart: 43 -> 43, of which waited for: 23 -> 17; matrix products, arithmetic and copies ran while one was open for 0% -> 0% of each run, Pallas kernels for 20% -> 24%
where the time goes in v4:
time: 111 us
  starting transfers between devices  40.9 us (37%)
  Pallas kernels  40.6 us (37%)
  waiting for transfers between devices  28.5 us (26%)
  between operations  1.15 us (1%)
    pallas_call x24, Pallas kernels, run(): pl.pallas_call(kernel, out_shape=[jax.ShapeDtypeStruct(*part) if isinstan...  40.6 us
    ppermute x42, starting transfers between devices, swap(): lax.ppermute(block, axis, [(i, i ^ distance) for i in range(devices)])  39.6 us
    ppermute x42, waiting for transfers between devices, swap(): lax.ppermute(block, axis, [(i, i ^ distance) for i in range(devices)])  28.5 us
  transfers between devices with their start and end apart: 43, of which 17 were waited for; matrix products, arithmetic and copies ran while one was open for 0% of the time, Pallas kernels for 24%

profile of v4, /device:TPU:0, one launch (start us, length us, event | category | flops | bytes accessed | tf_op | source)
XLA Modules:
  0.0 111.2 jit_solution(5228681285583258319)
XLA Ops:
  1.7 4.0 %collective-permute-start.2 = (bf16[272,384]{1,0:T(8,128)(2,1)S(1)}, bf16[272,384]{1,0:T(8,128)(2,1)S(1)}, u32[]{:S(2)}, u32[]{:S(2)}) collective-permute-start(bf16[272,384]{1,0:T(8,128)(2,1)S(1)} %tokens_and_order.1.refs_0_), channel_id=1, source_target_pairs={{0,6},{1,7},{2,4},{3,5},{4,2},{5,3},{6,0},{7,1},{8,14},{9,15},{10,... | collective-permute-start | bytes 626696 | tf_op jit(solution)/shard_map/ppermute | solution.py:821
  6.3 5.4 %collective-permute-done.2.refs_3_ = bf16[272,384]{1,0:T(8,128)(2,1)S(1)} collective-permute-done((bf16[272,384]{1,0:T(8,128)(2,1)S(1)}, bf16[272,384]{1,0:T(8,128)(2,1)S(1)}, u32[]{:S(2)}, u32[]{:S(2)}) %collective-permute-start.2) | collective-permute-done | bytes 208928 | tf_op jit(solution)/shard_map/ppermute | solution.py:821
  11.7 3.6 %collective-permute-done.1.refs_2_ = bf16[272,384]{1,0:T(8,128)(2,1)S(1)} collective-permute-done((bf16[272,384]{1,0:T(8,128)(2,1)S(1)}, bf16[272,384]{1,0:T(8,128)(2,1)S(1)}, u32[]{:S(2)}, u32[]{:S(2)}) %collective-permute-start.1) | collective-permute-done | bytes 208928 | tf_op jit(solution)/shard_map/ppermute | solution.py:821
  15.8 1.8 %collective-permute-start.9 = (bf16[256,384]{1,0:T(8,128)(2,1)}, bf16[256,384]{1,0:T(8,128)(2,1)S(1)}, u32[]{:S(2)}, u32[]{:S(2)}) collective-permute-start(bf16[256,384]{1,0:T(8,128)(2,1)} %bitcast.11), channel_id=1, source_target_pairs={{0,6},{1,7},{2,4},{3,5},{4,2},{5,3},{6,0},{7,1},{8,14},{9,15},{10,... | collective-permute-start | bytes 589832 | tf_op jit(solution)/shard_map/ppermute | solution.py:821
  17.6 1.3 %collective-permute-start.8 = (bf16[256,384]{1,0:T(8,128)(2,1)}, bf16[256,384]{1,0:T(8,128)(2,1)S(1)}, u32[]{:S(2)}, u32[]{:S(2)}) collective-permute-start(bf16[256,384]{1,0:T(8,128)(2,1)} %bitcast.12), channel_id=1, source_target_pairs={{0,4},{1,5},{2,6},{3,7},{4,0},{5,1},{6,2},{7,3},{8,12},{9,13},{10,... | collective-permute-start | bytes 589832 | tf_op jit(solution)/shard_map/ppermute | solution.py:821
  19.3 8.1 %forward_local.1 = (bf16[256,384]{1,0:T(8,128)(2,1)S(1)}, bf16[256,384]{1,0:T(8,128)(2,1)S(1)}, f32[256,768]{1,0:T(8,128)S(1)}, f32[280,768]{1,0:T(8,128)S(1)}, ...) custom-call(s32[1]{0:T(128)} %bitcast.2.me.me_ref, ...), custom_call_target="tpu_custom_call" | custom-call | flops 1 | bytes 1 | tf_op jit(solution)/shard_map/forward_local/pallas_call | solution.py:788
  30.2 5.1 %backward_local.1 = (bf16[256,384]{1,0:T(8,128)(2,1)S(1)}, f32[256,768]{1,0:T(8,128)S(1)}, f32[256,768]{1,0:T(8,128)S(1)}, f32[256,2048]{1,0:T(8,128)S(1)}, f32[...) custom-call(s32[1]{0:T(128)} %bitcast.2.me.me_ref, ...), custom_call_target="tpu_custom_call" | custom-call | flops 1 | bytes 1 | tf_op jit(solution)/shard_map/backward_local/pallas_call | solution.py:788
  35.3 1.5 %collective-permute-start.11 = (f32[16,896]{1,0:T(8,128)S(1)}, f32[16,896]{1,0:T(8,128)S(1)}, u32[]{:S(2)}, u32[]{:S(2)}) collective-permute-start(f32[16,896]{1,0:T(8,128)S(1)} %get-tuple-element.115), channel_id=1, source_target_pairs={{0,2},{1,3},{2,0},{3,1},{4,6},{5,7},{6,4},{7,5},{8,10},{9,11},{10,... | collective-permute-start | bytes 172040 | tf_op jit(solution)/shard_map/ppermute | solution.py:821
  37.4 1.4 %collective-permute-start.13 = (f32[16,896]{1,0:T(8,128)S(1)}, f32[16,896]{1,0:T(8,128)S(1)}, u32[]{:S(2)}, u32[]{:S(2)}) collective-permute-start(f32[16,896]{1,0:T(8,128)S(1)} %get-tuple-element.117), channel_id=1, source_target_pairs={{0,6},{1,7},{2,4},{3,5},{4,2},{5,3},{6,0},{7,1},{8,14},{9,15},{10,... | collective-permute-start | bytes 172040 | tf_op jit(solution)/shard_map/ppermute | solution.py:821
  39.5 2.1 %collective-permute-done.12.refs_1_ = f32[16,896]{1,0:T(8,128)S(1)} collective-permute-done((f32[16,896]{1,0:T(8,128)S(1)}, f32[16,896]{1,0:T(8,128)S(1)}, u32[]{:S(2)}, u32[]{:S(2)}) %collective-permute-start.12) | collective-permute-done | bytes 57376 | tf_op jit(solution)/shard_map/ppermute | solution.py:821
  43.7 4.7 %scan_forward.1 = (f32[16,264,128]{2,1,0:T(8,128)S(1)}, f32[16,264,128]{2,1,0:T(8,128)S(1)}, f32[16,264,128]{2,1,0:T(8,128)S(1)}, f32[16,264,128]{2,1,0:T(8,128)...) custom-call(s32[1]{0:T(128)} %bitcast.2.me.me_ref, ...), custom_call_target="tpu_custom_call" | custom-call | flops 1 | bytes 1 | tf_op jit(solution)/shard_map/scan_forward/pallas_call | solution.py:788
  50.6 1.4 %collective-permute-start.20 = (bf16[224,768]{1,0:T(8,128)(2,1)S(1)}, bf16[224,768]{1,0:T(8,128)(2,1)S(1)}, u32[]{:S(2)}, u32[]{:S(2)}) collective-permute-start(bf16[224,768]{1,0:T(8,128)(2,1)S(1)} %get-tuple-element.160), channel_id=1, source_target_pairs={{0,2},{1,3},{2,0},{3,1},{4,6},{5,7},{6,4},{7,5},{8,10},{9,11},{10,... | collective-permute-start | bytes 1032200 | tf_op jit(solution)/shard_map/ppermute | solution.py:821
  52.7 1.5 %collective-permute-start.22 = (bf16[224,768]{1,0:T(8,128)(2,1)S(1)}, bf16[224,768]{1,0:T(8,128)(2,1)S(1)}, u32[]{:S(2)}, u32[]{:S(2)}) collective-permute-start(bf16[224,768]{1,0:T(8,128)(2,1)S(1)} %get-tuple-element.162), channel_id=1, source_target_pairs={{0,6},{1,7},{2,4},{3,5},{4,2},{5,3},{6,0},{7,1},{8,14},{9,15},{10,... | collective-permute-start | bytes 1032200 | tf_op jit(solution)/shard_map/ppermute | solution.py:821
  54.2 10.8 %scan_backward.1 = (f32[256,768]{1,0:T(8,128)S(1)}, f32[8,768]{1,0:T(8,128)S(1)}, bf16[256,768]{1,0:T(8,128)(2,1)S(1)}, bf16[256,128]{1,0:T(8,128)(2,1)S(1)}, f32[16,768]{1,0:T(8,128)S(1)}) custom-call(f32[16,264,128]{2,1,0:T(8,128)S(1)} %get-tuple-element.133.refs_0_, f32[16,264,128]{2,1,0:T(8,128)S(1)} %get-tuple-element.134.refs_1_, ...), custom_call_target="tpu_custom_call" | custom-call | flops 1 | bytes 1 | tf_op jit(solution)/shard_map/scan_backward/pallas_call | solution.py:788
  65.0 1.3 %collective-permute-start.18 = (f32[8,768]{1,0:T(8,128)S(1)}, f32[8,768]{1,0:T(8,128)S(1)}, u32[]{:S(2)}, u32[]{:S(2)}) collective-permute-start(f32[8,768]{1,0:T(8,128)S(1)} %get-tuple-element.153), channel_id=1, source_target_pairs={{1,0},{2,1},{3,2},{4,3},{5,4},{6,5},{7,6},{9,8},{10,9},{11,10},{12... | collective-permute-start | bytes 73736 | tf_op jit(solution)/shard_map/ppermute | solution.py:839
  66.3 1.9 %small_grads.1 = (f32[104,768]{1,0:T(8,128)S(1)}, f32[256,768]{1,0:T(8,128)S(1)}) custom-call(bf16[256,768]{1,0:T(8,128)(2,1)S(1)} %get-tuple-element.146.gpre, bf16[256,128]{1,0:T(8,128)(2,1)S(1)} %get-tuple-element.147.gxproj, f32[256,128]{1,0:T(8,128)S(1)} %get-tuple-element.111.refs_4_.xproj, ...), custom_call_target="tpu_custom_call" | custom-call | flops 1 | bytes 1 | tf_op jit(solution)/shard_map/small_grads/pallas_call | solution.py:788
  70.9 1.6 %collective-permute-start.24 = (bf16[96,768]{1,0:T(8,128)(2,1)S(1)}, bf16[96,768]{1,0:T(8,128)(2,1)S(1)}, u32[]{:S(2)}, u32[]{:S(2)}) collective-permute-start(bf16[96,768]{1,0:T(8,128)(2,1)S(1)} %add_parts.2.a), channel_id=1, source_target_pairs={{0,8},{8,0},{16,24},{24,16},{1,9},{9,1},{17,25},{25,17},{2,10},{10... | collective-permute-start | bytes 442376 | tf_op jit(solution)/shard_map/ppermute | solution.py:821
  72.6 1.9 %collective-permute-start.25 = (bf16[64,768]{1,0:T(8,128)(2,1)S(1)}, bf16[64,768]{1,0:T(8,128)(2,1)S(1)}, u32[]{:S(2)}, u32[]{:S(2)}) collective-permute-start(bf16[64,768]{1,0:T(8,128)(2,1)S(1)} %get-tuple-element.169), channel_id=1, source_target_pairs={{0,2},{1,3},{2,0},{3,1},{4,6},{5,7},{6,4},{7,5},{8,10},{9,11},{10,... | collective-permute-start | bytes 294920 | tf_op jit(solution)/shard_map/ppermute | solution.py:821
  74.5 1.7 %collective-permute-start.27 = (bf16[64,768]{1,0:T(8,128)(2,1)S(1)}, bf16[64,768]{1,0:T(8,128)(2,1)S(1)}, u32[]{:S(2)}, u32[]{:S(2)}) collective-permute-start(bf16[64,768]{1,0:T(8,128)(2,1)S(1)} %get-tuple-element.171), channel_id=1, source_target_pairs={{0,6},{1,7},{2,4},{3,5},{4,2},{5,3},{6,0},{7,1},{8,14},{9,15},{10,... | collective-permute-start | bytes 294920 | tf_op jit(solution)/shard_map/ppermute | solution.py:821
  76.1 1.8 %collective-permute-start.29 = (bf16[256,384]{1,0:T(8,128)(2,1)S(1)}, bf16[256,384]{1,0:T(8,128)(2,1)S(1)}, u32[]{:S(2)}, u32[]{:S(2)}) collective-permute-start(bf16[256,384]{1,0:T(8,128)(2,1)S(1)} %get-tuple-element.174.refs_4_), channel_id=1, source_target_pairs={{0,2},{1,3},{2,0},{3,1},{4,6},{5,7},{6,4},{7,5},{8,10},{9,11},{10,... | collective-permute-start | bytes 589832 | tf_op jit(solution)/shard_map/ppermute | solution.py:821
  78.0 2.0 %collective-permute-start.31 = (bf16[256,384]{1,0:T(8,128)(2,1)S(1)}, bf16[256,384]{1,0:T(8,128)(2,1)S(1)}, u32[]{:S(2)}, u32[]{:S(2)}) collective-permute-start(bf16[256,384]{1,0:T(8,128)(2,1)S(1)} %get-tuple-element.174.refs_4_), channel_id=1, source_target_pairs={{0,6},{1,7},{2,4},{3,5},{4,2},{5,3},{6,0},{7,1},{8,14},{9,15},{10,... | collective-permute-start | bytes 589832 | tf_op jit(solution)/shard_map/ppermute | solution.py:821
  80.1 1.9 %collective-permute-done.26.c = bf16[64,768]{1,0:T(8,128)(2,1)S(1)} collective-permute-done((bf16[64,768]{1,0:T(8,128)(2,1)S(1)}, bf16[64,768]{1,0:T(8,128)(2,1)S(1)}, u32[]{:S(2)}, u32[]{:S(2)}) %collective-permute-start.26) | collective-permute-done | bytes 98336 | tf_op jit(solution)/shard_map/ppermute | solution.py:821
  81.9 2.6 %collective-permute-start.34 = (bf16[96,768]{1,0:T(8,128)(2,1)S(1)}, bf16[96,768]{1,0:T(8,128)(2,1)S(1)}, u32[]{:S(2)}, u32[]{:S(2)}) collective-permute-start(bf16[96,768]{1,0:T(8,128)(2,1)S(1)} %add_pair.6.a), channel_id=1, source_target_pairs={{0,16},{8,24},{16,0},{24,8},{1,17},{9,25},{17,1},{25,9},{2,18},{10... | collective-permute-start | bytes 442376 | tf_op jit(solution)/shard_map/ppermute | solution.py:821
  84.6 1.7 %collective-permute-start.28 = (bf16[64,768]{1,0:T(8,128)(2,1)S(1)}, bf16[64,768]{1,0:T(8,128)(2,1)S(1)}, u32[]{:S(2)}, u32[]{:S(2)}) collective-permute-start(bf16[64,768]{1,0:T(8,128)(2,1)S(1)} %add_parts.3.a), channel_id=1, source_target_pairs={{0,8},{8,0},{16,24},{24,16},{1,9},{9,1},{17,25},{25,17},{2,10},{10... | collective-permute-start | bytes 294920 | tf_op jit(solution)/shard_map/ppermute | solution.py:821
  86.3 3.4 %collective-permute-done.28.b = bf16[64,768]{1,0:T(8,128)(2,1)S(1)} collective-permute-done((bf16[64,768]{1,0:T(8,128)(2,1)S(1)}, bf16[64,768]{1,0:T(8,128)(2,1)S(1)}, u32[]{:S(2)}, u32[]{:S(2)}) %collective-permute-start.28) | collective-permute-done | bytes 98336 | tf_op jit(solution)/shard_map/ppermute | solution.py:821
  91.4 1.9 %collective-permute-start.35 = (bf16[96,768]{1,0:T(8,128)(2,1)S(1)}, bf16[96,768]{1,0:T(8,128)(2,1)S(1)}, u32[]{:S(2)}, u32[]{:S(2)}) collective-permute-start(bf16[96,768]{1,0:T(8,128)(2,1)S(1)} %add_pair.7.own), channel_id=1, source_target_pairs={{0,2},{1,3},{2,0},{3,1},{4,6},{5,7},{6,4},{7,5},{8,10},{9,11},{10,... | collective-permute-start | bytes 442376 | tf_op jit(solution)/shard_map/ppermute | solution.py:821
  93.3 2.3 %collective-permute-start.33 = (bf16[64,768]{1,0:T(8,128)(2,1)S(1)}, bf16[64,768]{1,0:T(8,128)(2,1)S(1)}, u32[]{:S(2)}, u32[]{:S(2)}) collective-permute-start(bf16[64,768]{1,0:T(8,128)(2,1)S(1)} %add_pair.4.a), channel_id=1, source_target_pairs={{0,16},{8,24},{16,0},{24,8},{1,17},{9,25},{17,1},{25,9},{2,18},{10... | collective-permute-start | bytes 294920 | tf_op jit(solution)/shard_map/ppermute | solution.py:821
  95.6 4.3 %collective-permute-done.33.b = bf16[64,768]{1,0:T(8,128)(2,1)S(1)} collective-permute-done((bf16[64,768]{1,0:T(8,128)(2,1)S(1)}, bf16[64,768]{1,0:T(8,128)(2,1)S(1)}, u32[]{:S(2)}, u32[]{:S(2)}) %collective-permute-start.33) | collective-permute-done | bytes 98336 | tf_op jit(solution)/shard_map/ppermute | solution.py:821
  100.7 2.9 %collective-permute-start.39 = (bf16[64,768]{1,0:T(8,128)(2,1)S(1)}, bf16[64,768]{1,0:T(8,128)(2,1)S(1)}, u32[]{:S(2)}, u32[]{:S(2)}) collective-permute-start(bf16[64,768]{1,0:T(8,128)(2,1)S(1)} %add_pair.5.own), channel_id=1, source_target_pairs={{0,2},{1,3},{2,0},{3,1},{4,6},{5,7},{6,4},{7,5},{8,10},{9,11},{10,... | collective-permute-start | bytes 294920 | tf_op jit(solution)/shard_map/ppermute | solution.py:821
  103.7 1.3 %share_rows.1 = (bf16[256,384]{1,0:T(8,128)(2,1)S(1)}, bf16[256,384]{1,0:T(8,128)(2,1)S(1)}, bf16[256,768]{1,0:T(8,128)(2,1)S(1)}) custom-call(s32[1]{0:T(128)} %bitcast.2.me.me_ref, f32[4,256]{1,0:T(4,128)S(1)} %get-tuple-element.105.orders, bf16[256,384]{1,0:T(8,128)(2,1)S(1)} %get-tuple-element.172.rows.refs_0_, ...), custom_call_target="tpu_custom_call" | custom-call | flops 1 | bytes 1 | tf_op jit(solution)/shard_map/share_rows/pallas_call | solution.py:788
  105.0 2.2 %first_results.1 = (f32[768,384]{1,0:T(8,128)}, f32[384,1536]{1,0:T(8,128)}) custom-call(s32[1]{0:T(128)} %bitcast.2.me.me_ref, bf16[384,768]{1,0:T(8,128)(2,1)S(1)} %order_parts.2.own, bf16[384,768]{1,0:T(8,128)(2,1)S(1)} %collective-permute-done.38.other), custom_call_target="tpu_custom_call" | custom-call | flops 1 | bytes 1 | tf_op jit(solution)/shard_map/first_results/pallas_call | solution.py:788
  109.3 1.8 %last_results.1 = (f32[384]{0:T(512)}, f32[384,1536]{1,0:T(8,128)}, f32[4,768]{1,0:T(4,128)}, f32[768]{0:T(1024)}, f32[56,768]{1,0:T(8,128)}, /*index=5*/f32[24,...) custom-call(s32[1]{0:T(128)} %bitcast.2.me.me_ref, ...), custom_call_target="tpu_custom_call", output_to_operand_aliasing={{1}: (3, {})} | custom-call | flops 1 | bytes 1 | tf_op jit(solution)/shard_map/last_results/pallas_call | solution.py:788
  (86 shorter events, 18.9 us)
Async XLA Ops:
  1.7 10.0 %collective-permute-start.2 = (bf16[272,384]{1,0:T(8,128)(2,1)S(1)}, bf16[272,384]{1,0:T(8,128)(2,1)S(1)}, u32[]{:S(2)}, u32[]{:S(2)}) collective-permute-start(bf16[272,384]{1,0:T(8,128)(2,1)S(1)} %tokens_and_order.1.refs_0_), channel_id=1, source_target_pairs={{0,6},{1,7},{2,4},{3,5},{4,2},{5,3},{6,0},{7,1},{8,14},{9,15},{10,... | collective-permute-start | bytes 626696 | tf_op jit(solution)/shard_map/ppermute | solution.py:821
  5.6 9.6 %collective-permute-start.1 = (bf16[272,384]{1,0:T(8,128)(2,1)S(1)}, bf16[272,384]{1,0:T(8,128)(2,1)S(1)}, u32[]{:S(2)}, u32[]{:S(2)}) collective-permute-start(bf16[272,384]{1,0:T(8,128)(2,1)S(1)} %tokens_and_order.1.refs_0_), channel_id=1, source_target_pairs={{0,4},{1,5},{2,6},{3,7},{4,0},{5,1},{6,2},{7,3},{8,12},{9,13},{10,... | collective-permute-start | bytes 626696 | tf_op jit(solution)/shard_map/ppermute | solution.py:821
  6.1 9.4 %collective-permute-start = (bf16[272,384]{1,0:T(8,128)(2,1)S(1)}, bf16[272,384]{1,0:T(8,128)(2,1)S(1)}, u32[]{:S(2)}, u32[]{:S(2)}) collective-permute-start(bf16[272,384]{1,0:T(8,128)(2,1)S(1)} %tokens_and_order.1.refs_0_), channel_id=1, source_target_pairs={{0,2},{1,3},{2,0},{3,1},{4,6},{5,7},{6,4},{7,5},{8,10},{9,11},{10,... | collective-permute-start | bytes 626696 | tf_op jit(solution)/shard_map/ppermute | solution.py:821
  6.3 11.3 %collective-permute-start.3 = (bf16[272,384]{1,0:T(8,128)(2,1)S(1)}, bf16[272,384]{1,0:T(8,128)(2,1)S(1)}, u32[]{:S(2)}, u32[]{:S(2)}) collective-permute-start(bf16[272,384]{1,0:T(8,128)(2,1)S(1)} %tokens_and_order.1.refs_0_), channel_id=1, source_target_pairs={{0,1},{1,0},{2,3},{3,2},{4,5},{5,4},{6,7},{7,6},{8,9},{9,8},{10,11... | collective-permute-start | bytes 626696 | tf_op jit(solution)/shard_map/ppermute | solution.py:821
  11.7 7.3 %collective-permute-start.6 = (bf16[272,384]{1,0:T(8,128)(2,1)S(1)}, bf16[272,384]{1,0:T(8,128)(2,1)S(1)}, u32[]{:S(2)}, u32[]{:S(2)}) collective-permute-start(bf16[272,384]{1,0:T(8,128)(2,1)S(1)} %collective-permute-done.2.refs_3_), channel_id=1, source_target_pairs={{0,1},{1,0},{2,3},{3,2},{4,5},{5,4},{6,7},{7,6},{8,9},{9,8},{10,11... | collective-permute-start | bytes 626696 | tf_op jit(solution)/shard_map/ppermute | solution.py:821
  15.8 11.6 %collective-permute-start.9 = (bf16[256,384]{1,0:T(8,128)(2,1)}, bf16[256,384]{1,0:T(8,128)(2,1)S(1)}, u32[]{:S(2)}, u32[]{:S(2)}) collective-permute-start(bf16[256,384]{1,0:T(8,128)(2,1)} %bitcast.11), channel_id=1, source_target_pairs={{0,6},{1,7},{2,4},{3,5},{4,2},{5,3},{6,0},{7,1},{8,14},{9,15},{10,... | collective-permute-start | bytes 589832 | tf_op jit(solution)/shard_map/ppermute | solution.py:821
  17.6 10.6 %collective-permute-start.8 = (bf16[256,384]{1,0:T(8,128)(2,1)}, bf16[256,384]{1,0:T(8,128)(2,1)S(1)}, u32[]{:S(2)}, u32[]{:S(2)}) collective-permute-start(bf16[256,384]{1,0:T(8,128)(2,1)} %bitcast.12), channel_id=1, source_target_pairs={{0,4},{1,5},{2,6},{3,7},{4,0},{5,1},{6,2},{7,3},{8,12},{9,13},{10,... | collective-permute-start | bytes 589832 | tf_op jit(solution)/shard_map/ppermute | solution.py:821
  18.9 9.3 %collective-permute-start.7 = (bf16[256,384]{1,0:T(8,128)(2,1)}, bf16[256,384]{1,0:T(8,128)(2,1)S(1)}, u32[]{:S(2)}, u32[]{:S(2)}) collective-permute-start(bf16[256,384]{1,0:T(8,128)(2,1)} %bitcast.13), channel_id=1, source_target_pairs={{0,2},{1,3},{2,0},{3,1},{4,6},{5,7},{6,4},{7,5},{8,10},{9,11},{10,... | collective-permute-start | bytes 589832 | tf_op jit(solution)/shard_map/ppermute | solution.py:821
  35.3 4.2 %collective-permute-start.11 = (f32[16,896]{1,0:T(8,128)S(1)}, f32[16,896]{1,0:T(8,128)S(1)}, u32[]{:S(2)}, u32[]{:S(2)}) collective-permute-start(f32[16,896]{1,0:T(8,128)S(1)} %get-tuple-element.115), channel_id=1, source_target_pairs={{0,2},{1,3},{2,0},{3,1},{4,6},{5,7},{6,4},{7,5},{8,10},{9,11},{10,... | collective-permute-start | bytes 172040 | tf_op jit(solution)/shard_map/ppermute | solution.py:821
  36.8 4.8 %collective-permute-start.12 = (f32[16,896]{1,0:T(8,128)S(1)}, f32[16,896]{1,0:T(8,128)S(1)}, u32[]{:S(2)}, u32[]{:S(2)}) collective-permute-start(f32[16,896]{1,0:T(8,128)S(1)} %get-tuple-element.116), channel_id=1, source_target_pairs={{0,4},{1,5},{2,6},{3,7},{4,0},{5,1},{6,2},{7,3},{8,12},{9,13},{10,... | collective-permute-start | bytes 172040 | tf_op jit(solution)/shard_map/ppermute | solution.py:821
  37.4 5.1 %collective-permute-start.13 = (f32[16,896]{1,0:T(8,128)S(1)}, f32[16,896]{1,0:T(8,128)S(1)}, u32[]{:S(2)}, u32[]{:S(2)}) collective-permute-start(f32[16,896]{1,0:T(8,128)S(1)} %get-tuple-element.117), channel_id=1, source_target_pairs={{0,6},{1,7},{2,4},{3,5},{4,2},{5,3},{6,0},{7,1},{8,14},{9,15},{10,... | collective-permute-start | bytes 172040 | tf_op jit(solution)/shard_map/ppermute | solution.py:821
  50.6 17.6 %collective-permute-start.20 = (bf16[224,768]{1,0:T(8,128)(2,1)S(1)}, bf16[224,768]{1,0:T(8,128)(2,1)S(1)}, u32[]{:S(2)}, u32[]{:S(2)}) collective-permute-start(bf16[224,768]{1,0:T(8,128)(2,1)S(1)} %get-tuple-element.160), channel_id=1, source_target_pairs={{0,2},{1,3},{2,0},{3,1},{4,6},{5,7},{6,4},{7,5},{8,10},{9,11},{10,... | collective-permute-start | bytes 1032200 | tf_op jit(solution)/shard_map/ppermute | solution.py:821
  52.1 17.2 %collective-permute-start.21 = (bf16[224,768]{1,0:T(8,128)(2,1)S(1)}, bf16[224,768]{1,0:T(8,128)(2,1)S(1)}, u32[]{:S(2)}, u32[]{:S(2)}) collective-permute-start(bf16[224,768]{1,0:T(8,128)(2,1)S(1)} %get-tuple-element.161), channel_id=1, source_target_pairs={{0,4},{1,5},{2,6},{3,7},{4,0},{5,1},{6,2},{7,3},{8,12},{9,13},{10,... | collective-permute-start | bytes 1032200 | tf_op jit(solution)/shard_map/ppermute | solution.py:821
  52.7 16.6 %collective-permute-start.22 = (bf16[224,768]{1,0:T(8,128)(2,1)S(1)}, bf16[224,768]{1,0:T(8,128)(2,1)S(1)}, u32[]{:S(2)}, u32[]{:S(2)}) collective-permute-start(bf16[224,768]{1,0:T(8,128)(2,1)S(1)} %get-tuple-element.162), channel_id=1, source_target_pairs={{0,6},{1,7},{2,4},{3,5},{4,2},{5,3},{6,0},{7,1},{8,14},{9,15},{10,... | collective-permute-start | bytes 1032200 | tf_op jit(solution)/shard_map/ppermute | solution.py:821
  65.0 4.4 %collective-permute-start.18 = (f32[8,768]{1,0:T(8,128)S(1)}, f32[8,768]{1,0:T(8,128)S(1)}, u32[]{:S(2)}, u32[]{:S(2)}) collective-permute-start(f32[8,768]{1,0:T(8,128)S(1)} %get-tuple-element.153), channel_id=1, source_target_pairs={{1,0},{2,1},{3,2},{4,3},{5,4},{6,5},{7,6},{9,8},{10,9},{11,10},{12... | collective-permute-start | bytes 73736 | tf_op jit(solution)/shard_map/ppermute | solution.py:839
  70.9 7.1 %collective-permute-start.24 = (bf16[96,768]{1,0:T(8,128)(2,1)S(1)}, bf16[96,768]{1,0:T(8,128)(2,1)S(1)}, u32[]{:S(2)}, u32[]{:S(2)}) collective-permute-start(bf16[96,768]{1,0:T(8,128)(2,1)S(1)} %add_parts.2.a), channel_id=1, source_target_pairs={{0,8},{8,0},{16,24},{24,16},{1,9},{9,1},{17,25},{25,17},{2,10},{10... | collective-permute-start | bytes 442376 | tf_op jit(solution)/shard_map/ppermute | solution.py:821
  72.6 5.4 %collective-permute-start.25 = (bf16[64,768]{1,0:T(8,128)(2,1)S(1)}, bf16[64,768]{1,0:T(8,128)(2,1)S(1)}, u32[]{:S(2)}, u32[]{:S(2)}) collective-permute-start(bf16[64,768]{1,0:T(8,128)(2,1)S(1)} %get-tuple-element.169), channel_id=1, source_target_pairs={{0,2},{1,3},{2,0},{3,1},{4,6},{5,7},{6,4},{7,5},{8,10},{9,11},{10,... | collective-permute-start | bytes 294920 | tf_op jit(solution)/shard_map/ppermute | solution.py:821
  74.5 7.5 %collective-permute-start.26 = (bf16[64,768]{1,0:T(8,128)(2,1)S(1)}, bf16[64,768]{1,0:T(8,128)(2,1)S(1)}, u32[]{:S(2)}, u32[]{:S(2)}) collective-permute-start(bf16[64,768]{1,0:T(8,128)(2,1)S(1)} %get-tuple-element.170), channel_id=1, source_target_pairs={{0,4},{1,5},{2,6},{3,7},{4,0},{5,1},{6,2},{7,3},{8,12},{9,13},{10,... | collective-permute-start | bytes 294920 | tf_op jit(solution)/shard_map/ppermute | solution.py:821
  74.5 10.1 %collective-permute-start.27 = (bf16[64,768]{1,0:T(8,128)(2,1)S(1)}, bf16[64,768]{1,0:T(8,128)(2,1)S(1)}, u32[]{:S(2)}, u32[]{:S(2)}) collective-permute-start(bf16[64,768]{1,0:T(8,128)(2,1)S(1)} %get-tuple-element.171), channel_id=1, source_target_pairs={{0,6},{1,7},{2,4},{3,5},{4,2},{5,3},{6,0},{7,1},{8,14},{9,15},{10,... | collective-permute-start | bytes 294920 | tf_op jit(solution)/shard_map/ppermute | solution.py:821
  76.1 13.6 %collective-permute-start.29 = (bf16[256,384]{1,0:T(8,128)(2,1)S(1)}, bf16[256,384]{1,0:T(8,128)(2,1)S(1)}, u32[]{:S(2)}, u32[]{:S(2)}) collective-permute-start(bf16[256,384]{1,0:T(8,128)(2,1)S(1)} %get-tuple-element.174.refs_4_), channel_id=1, source_target_pairs={{0,2},{1,3},{2,0},{3,1},{4,6},{5,7},{6,4},{7,5},{8,10},{9,11},{10,... | collective-permute-start | bytes 589832 | tf_op jit(solution)/shard_map/ppermute | solution.py:821
  78.0 11.8 %collective-permute-start.30 = (bf16[256,384]{1,0:T(8,128)(2,1)S(1)}, bf16[256,384]{1,0:T(8,128)(2,1)S(1)}, u32[]{:S(2)}, u32[]{:S(2)}) collective-permute-start(bf16[256,384]{1,0:T(8,128)(2,1)S(1)} %get-tuple-element.174.refs_4_), channel_id=1, source_target_pairs={{0,4},{1,5},{2,6},{3,7},{4,0},{5,1},{6,2},{7,3},{8,12},{9,13},{10,... | collective-permute-start | bytes 589832 | tf_op jit(solution)/shard_map/ppermute | solution.py:821
  78.0 11.8 %collective-permute-start.31 = (bf16[256,384]{1,0:T(8,128)(2,1)S(1)}, bf16[256,384]{1,0:T(8,128)(2,1)S(1)}, u32[]{:S(2)}, u32[]{:S(2)}) collective-permute-start(bf16[256,384]{1,0:T(8,128)(2,1)S(1)} %get-tuple-element.174.refs_4_), channel_id=1, source_target_pairs={{0,6},{1,7},{2,4},{3,5},{4,2},{5,3},{6,0},{7,1},{8,14},{9,15},{10,... | collective-permute-start | bytes 589832 | tf_op jit(solution)/shard_map/ppermute | solution.py:821
  81.9 7.8 %collective-permute-start.34 = (bf16[96,768]{1,0:T(8,128)(2,1)S(1)}, bf16[96,768]{1,0:T(8,128)(2,1)S(1)}, u32[]{:S(2)}, u32[]{:S(2)}) collective-permute-start(bf16[96,768]{1,0:T(8,128)(2,1)S(1)} %add_pair.6.a), channel_id=1, source_target_pairs={{0,16},{8,24},{16,0},{24,8},{1,17},{9,25},{17,1},{25,9},{2,18},{10... | collective-permute-start | bytes 442376 | tf_op jit(solution)/shard_map/ppermute | solution.py:821
  84.6 5.1 %collective-permute-start.28 = (bf16[64,768]{1,0:T(8,128)(2,1)S(1)}, bf16[64,768]{1,0:T(8,128)(2,1)S(1)}, u32[]{:S(2)}, u32[]{:S(2)}) collective-permute-start(bf16[64,768]{1,0:T(8,128)(2,1)S(1)} %add_parts.3.a), channel_id=1, source_target_pairs={{0,8},{8,0},{16,24},{24,16},{1,9},{9,1},{17,25},{25,17},{2,10},{10... | collective-permute-start | bytes 294920 | tf_op jit(solution)/shard_map/ppermute | solution.py:821
  89.8 10.2 %collective-permute-start.37 = (bf16[96,768]{1,0:T(8,128)(2,1)S(1)}, bf16[96,768]{1,0:T(8,128)(2,1)S(1)}, u32[]{:S(2)}, u32[]{:S(2)}) collective-permute-start(bf16[96,768]{1,0:T(8,128)(2,1)S(1)} %add_pair.7.own), channel_id=1, source_target_pairs={{0,6},{1,7},{2,4},{3,5},{4,2},{5,3},{6,0},{7,1},{8,14},{9,15},{10,... | collective-permute-start | bytes 442376 | tf_op jit(solution)/shard_map/ppermute | solution.py:821
  90.7 9.2 %collective-permute-start.36 = (bf16[96,768]{1,0:T(8,128)(2,1)S(1)}, bf16[96,768]{1,0:T(8,128)(2,1)S(1)}, u32[]{:S(2)}, u32[]{:S(2)}) collective-permute-start(bf16[96,768]{1,0:T(8,128)(2,1)S(1)} %add_pair.7.own), channel_id=1, source_target_pairs={{0,4},{1,5},{2,6},{3,7},{4,0},{5,1},{6,2},{7,3},{8,12},{9,13},{10,... | collective-permute-start | bytes 442376 | tf_op jit(solution)/shard_map/ppermute | solution.py:821
  91.4 8.5 %collective-permute-start.35 = (bf16[96,768]{1,0:T(8,128)(2,1)S(1)}, bf16[96,768]{1,0:T(8,128)(2,1)S(1)}, u32[]{:S(2)}, u32[]{:S(2)}) collective-permute-start(bf16[96,768]{1,0:T(8,128)(2,1)S(1)} %add_pair.7.own), channel_id=1, source_target_pairs={{0,2},{1,3},{2,0},{3,1},{4,6},{5,7},{6,4},{7,5},{8,10},{9,11},{10,... | collective-permute-start | bytes 442376 | tf_op jit(solution)/shard_map/ppermute | solution.py:821
  93.3 6.6 %collective-permute-start.33 = (bf16[64,768]{1,0:T(8,128)(2,1)S(1)}, bf16[64,768]{1,0:T(8,128)(2,1)S(1)}, u32[]{:S(2)}, u32[]{:S(2)}) collective-permute-start(bf16[64,768]{1,0:T(8,128)(2,1)S(1)} %add_pair.4.a), channel_id=1, source_target_pairs={{0,16},{8,24},{16,0},{24,8},{1,17},{9,25},{17,1},{25,9},{2,18},{10... | collective-permute-start | bytes 294920 | tf_op jit(solution)/shard_map/ppermute | solution.py:821
  100.0 5.0 %collective-permute-start.38 = (bf16[384,768]{1,0:T(8,128)(2,1)S(1)}, bf16[384,768]{1,0:T(8,128)(2,1)S(1)}, u32[]{:S(2)}, u32[]{:S(2)}) collective-permute-start(bf16[384,768]{1,0:T(8,128)(2,1)S(1)} %order_parts.2.own), channel_id=1, source_target_pairs={{0,1},{1,0},{2,3},{3,2},{4,5},{5,4},{6,7},{7,6},{8,9},{9,8},{10,11... | collective-permute-start | bytes 1769480 | tf_op jit(solution)/shard_map/ppermute | solution.py:821
  100.1 7.1 %collective-permute-start.41 = (bf16[64,768]{1,0:T(8,128)(2,1)S(1)}, bf16[64,768]{1,0:T(8,128)(2,1)S(1)}, u32[]{:S(2)}, u32[]{:S(2)}) collective-permute-start(bf16[64,768]{1,0:T(8,128)(2,1)S(1)} %add_pair.5.own), channel_id=1, source_target_pairs={{0,6},{1,7},{2,4},{3,5},{4,2},{5,3},{6,0},{7,1},{8,14},{9,15},{10,... | collective-permute-start | bytes 294920 | tf_op jit(solution)/shard_map/ppermute | solution.py:821
  100.2 7.2 %collective-permute-start.40 = (bf16[64,768]{1,0:T(8,128)(2,1)S(1)}, bf16[64,768]{1,0:T(8,128)(2,1)S(1)}, u32[]{:S(2)}, u32[]{:S(2)}) collective-permute-start(bf16[64,768]{1,0:T(8,128)(2,1)S(1)} %add_pair.5.own), channel_id=1, source_target_pairs={{0,4},{1,5},{2,6},{3,7},{4,0},{5,1},{6,2},{7,3},{8,12},{9,13},{10,... | collective-permute-start | bytes 294920 | tf_op jit(solution)/shard_map/ppermute | solution.py:821
  100.7 6.7 %collective-permute-start.39 = (bf16[64,768]{1,0:T(8,128)(2,1)S(1)}, bf16[64,768]{1,0:T(8,128)(2,1)S(1)}, u32[]{:S(2)}, u32[]{:S(2)}) collective-permute-start(bf16[64,768]{1,0:T(8,128)(2,1)S(1)} %add_pair.5.own), channel_id=1, source_target_pairs={{0,2},{1,3},{2,0},{3,1},{4,6},{5,7},{6,4},{7,5},{8,10},{9,11},{10,... | collective-permute-start | bytes 294920 | tf_op jit(solution)/shard_map/ppermute | solution.py:821
  (15 other events, 68.9 us)

commit v5 on v4

--- a/solution.py
+++ b/solution.py
@@ -260,11 +260,11 @@
     rows, width, inner, rank, state, lags, clouds = sizes
     steps = rows // CHUNKS
     pieces = refs[:n_pieces]
-    gate, far, xproj, a2, w_out, sums, f, column = refs[n_pieces : n_pieces + 8]
+    gate, far, xproj, a2, w_out, sums, f, column, normed = refs[n_pieces : n_pieces + 9]
     n_out = len(SENT) if n_pieces == 2 else 1
-    dy_o, gg_o, gm, cbc, chunkb_o, near_out = refs[n_pieces + 8 : n_pieces + 14]
-    carries_o = refs[n_pieces + 14 : n_pieces + 14 + n_out]
-    (copied,) = refs[n_pieces + 14 + n_out :]
+    dy_o, gg_o, gm, cbc, chunkb_o, near_out, factor_o = refs[n_pieces + 9 : n_pieces + 16]
+    carries_o = refs[n_pieces + 16 : n_pieces + 16 + n_out]
+    (copied,) = refs[n_pieces + 16 + n_out :]
     copy = pltpu.make_async_copy(w_out, near_out, copied)
     copy.start()
     if n_pieces == 2:
@@ -272,6 +272,7 @@
     else:
         trans_dy = gather_rows(wide(column[0], rows), [p[...] for p in pieces], me, rows).astype(BF16)
     dy_o[...] = trans_dy
+    factor_o[...] = jnp.where(jnp.bitwise_and(me[0], 1) == 1, trans_dy, normed[...])
     copy.wait()
     gg_o[...] = dot(trans_dy, near_out[...], ((1,), (1,)))
 
@@ -340,11 +341,11 @@
     rows, width, inner, rank, state, lags, clouds = sizes
     steps = rows // CHUNKS
     carries = refs[:n_pieces]
-    (trans_dy, normed, gg, gate, act, far, use, bbc, cbc, chunkf, sums, a2, consts) = refs[n_pieces : n_pieces + 13]
+    (gg, gate, act, far, use, bbc, cbc, chunkf, sums, a2, consts) = refs[n_pieces : n_pieces + 11]
     blocks = inner // LANES
-    states = refs[n_pieces + 13 : n_pieces + 13 + blocks]
-    (gated, gz_o, keep_o, send_o) = refs[n_pieces + 13 + blocks : n_pieces + 17 + blocks]
-    (mixed, sstart, held) = refs[n_pieces + 17 + blocks :]
+    states = refs[n_pieces + 11 : n_pieces + 11 + blocks]
+    (gated, gz_o, send_o) = refs[n_pieces + 11 + blocks : n_pieces + 14 + blocks]
+    (mixed, sstart, held) = refs[n_pieces + 14 + blocks :]
     me = me_ref[0]
     skips = consts[lags + 1 : lags + 2, :]
     devices, size = hold_carries(held, carries, me_ref)
@@ -385,29 +386,32 @@
 
         lax.fori_loop(0, steps, forward, tuple(begin), unroll=8)
 
+    second = jnp.bitwise_and(me, 1) == 1
+
     def gating(j, carry):
         r = pl.ds(pl.multiple_of(j * BLOCK, BLOCK), BLOCK)
         z, a = gate[r, :], act[r, :].astype(F32)
         s = sigmoid(z)
         m = mixed[r, :] + skips * a
-        gated[r, :] = (m * (z * s)).astype(BF16)
-        gz_o[r, :] = (gg[r, :] * m * s * (1.0 + z * (1.0 - s))).astype(BF16)
+        out = (m * (z * s)).astype(BF16)
+        grad = (gg[r, :] * m * s * (1.0 + z * (1.0 - s))).astype(BF16)
+        gated[r, :] = out
+        gz_o[r, :] = grad
+        send_o[r, :] = jnp.where(second, out, grad)
         return carry
 
     lax.fori_loop(0, rows // BLOCK, gating, 0)
-    second = core_of(me, devices) == 1
-    wout_g = dot(trans_dy[...], gated[...], ((0,), (0,))).astype(BF16)
-    gate_g = dot(normed[...], gz_o[...], ((0,), (0,))).astype(BF16)
-    keep_o[...] = jnp.where(second, gate_g, wout_g)
-    send_o[...] = jnp.where(second, wout_g, gate_g)
 
 
 def branch_kernel(sizes, n_pieces, me_ref, *refs):
     rows, width, inner, rank, state, lags, clouds = sizes
     carries = refs[:n_pieces]
-    chunkb, sums, a2, gated, w_out, gstart, branch_o, held = refs[n_pieces:]
+    chunkb, sums, a2, gated, gz, trans_dy, normed, w_out, gstart, branch_o, part_o, held = refs[n_pieces:]
     me = me_ref[0]
     branch_o[...] = dot(gated[...], w_out[...]).astype(BF16)
+    second = jnp.bitwise_and(me, 1) == 1
+    factor = jnp.where(second, normed[...], trans_dy[...])
+    part_o[...] = dot(factor, jnp.where(second, gz[...], gated[...]), ((0,), (0,)))
     devices, size = hold_carries(held, carries, me_ref)
     back = size - CHUNKS - state
 
@@ -498,10 +502,7 @@
     pick_c = (col == row + rank + state).astype(F32).astype(BF16)
 
     def lane_sums(ref, pick):
-        whole = ref[...]
-        high = whole.astype(BF16)
-        low = (whole - high.astype(F32)).astype(BF16)
-        return dot(high, pick) + dot(low, pick)
+        return dot(ref[...].astype(BF16), pick)
 
     grad_bc = lane_sums(gb, pick_b) + lane_sums(gc, pick_c)
 
@@ -608,6 +609,7 @@
     n_small = small.shape[0]
     last = lax.broadcasted_iota(jnp.int32, (n_small, inner), 0) == n_small - 1
     both[width : width + n_small, :] = jnp.where(last, gain_row, small[...]).astype(BF16)
+    both[width + n_small :, :] = jnp.zeros((both.shape[0] - width - n_small, inner), BF16)
     half = keep_o.shape[0]
     core = core_of(me[0], devices)
     keep_o[...] = both[pl.ds(pl.multiple_of(core * half, BLOCK), half), :]
@@ -640,13 +642,15 @@
     return jnp.concatenate([piece[0:half, 0:width], piece[0:half, width : 2 * width]], axis=0)
 
 
-def halves_beside_kernel(me, kept, got, rows, own_o, *sent_o):
+def first_halves_kernel(me, kept, factor, got, rows, own_o, *sent_o):
+    whole, sent_o = sent_o[-1], sent_o[:-1]
     part = own_o.shape[0]
     half = rows.shape[0] // 2
     chip = lax.div(me[0], 2)
+    whole[...] = kept[...] + dot(factor[...], got[...], ((0,), (0,)))
     for d, out in enumerate((own_o,) + sent_o):
         r = pl.ds(pl.multiple_of(jnp.bitwise_xor(chip, d) * part, BLOCK), part)
-        total = (kept[r, :].astype(F32) + got[r, :].astype(F32)).astype(BF16)
+        total = whole[r, :].astype(BF16)
         if d == 0:
             out[...] = total
         else:
@@ -654,6 +658,11 @@
             out[half:, :] = total
 
 
+def products_kernel(trans_dy, gated, normed, gz, wout_o, gate_o):
+    wout_o[...] = dot(trans_dy[...], gated[...], ((0,), (0,)))
+    gate_o[...] = dot(normed[...], gz[...], ((0,), (0,)))
+
+
 def sum_kernel(a, b, c, d, out):
     one, two, three, four = (x[x.shape[0] - a.shape[0] :, :].astype(F32) for x in (a, b, c, d))
     out[...] = ((one + two) + (three + four)).astype(BF16)
@@ -663,34 +672,14 @@
     out[...] = (a[...].astype(F32) + b[...].astype(F32)).astype(BF16)
 
 
-def pair_beside_kernel(a, b, rows, out):
-    beside(out, rows)
-    out[rows.shape[0] // 2 :, :] = (a[...].astype(F32) + b[...].astype(F32)).astype(BF16)
-
-
-def by_chip(out, first, parts, me, part):
-    for d, piece in enumerate(parts):
-        chip = jnp.bitwise_xor(lax.div(me[0], 2), d)
-        out[pl.ds(pl.multiple_of(first + chip * part, BLOCK), part), :] = piece[piece.shape[0] - part :, :]
-
-
-def stack_kernel(a, b, out):
-    out[0 : a.shape[0], :] = a[...]
-    out[a.shape[0] :, :] = b[...]
-
-
-def both_chips_kernel(part_a, part_b, me, own, two, four, six, out):
+def chips_kernel(me, own, two, four, six, out):
+    part = own.shape[0]
     for d, piece in enumerate((own, two, four, six)):
         chip = jnp.bitwise_xor(lax.div(me[0], 2), d)
-        out[pl.ds(pl.multiple_of(chip * part_a, BLOCK), part_a), :] = piece[0:part_a, :]
-        out[pl.ds(pl.multiple_of(4 * part_a + chip * part_b, BLOCK), part_b), :] = piece[part_a:, :]
-
-
-def chips_kernel(me, own, two, four, six, out):
-    by_chip(out, 0, (own, two, four, six), me, own.shape[0])
-
-
-def share_kernel(rows, width, me, orders, own, two, four, six, mine_o, theirs_o, *half_o):
+        out[pl.ds(pl.multiple_of(chip * part, BLOCK), part), :] = piece[...]
+
+
+def share_kernel(rows, width, me, orders, own, two, four, six, mine_o, theirs_o):
     pieces = (own, two, four, six)
     whole = jnp.concatenate([unfold(p, rows, width) for p in pieces], axis=0)
     for core, out in enumerate((mine_o, theirs_o)):
@@ -701,12 +690,8 @@
         if core == 0:
             out[...] = moved
         else:
-            out[0 : rows // 2, 0:width] = moved[: rows // 2]
-            out[0 : rows // 2, width:] = moved[rows // 2 :]
-    for out in half_o:
-        part = out.shape[0] // len(pieces)
-        by_chip(out, 0, pieces, me, part)
-        by_chip(theirs_o, rows // 2, pieces, me, part)
+            out[:, 0:width] = moved[: rows // 2]
+            out[:, width:] = moved[rows // 2 :]
 
 
 def share_both_kernel(rows, width, me, orders, *refs):
@@ -778,7 +763,7 @@
     out[...] = (here[...].astype(F32) + moved).astype(BF16)
 
 
-def call(kernel, outs, scratch, n_smem, name, room, time=1.0, far_ins=(), far_outs=(), aliases={}):
+def call(kernel, outs, scratch, n_smem, name, room, far_ins=(), far_outs=(), aliases={}):
     vmem = pl.BlockSpec(memory_space=pltpu.VMEM)
     smem = pl.BlockSpec(memory_space=pltpu.SMEM)
     anywhere = pl.BlockSpec(memory_space=pltpu.HBM)
@@ -800,16 +785,6 @@
         )(*args)
 
     return run
-
-
-CFG = {'adj': 'gstart', 'arrive': '', 'chips1': 'total', 'chips2': 'first', 'd': '', 'dy': 'd6', 'dy1': 'fwd', 'halves': '', 'hold': '', 'm3': 'own', 'one': 'b2+b4+b6+pair', 'p1d': 'z', 'pair': 'd2', 'rim': '', 'share': 'pair', 'share3': 'total', 'small': 'mid', 'z1': 'send', 'fin': '', 'sumz': 'z1'}
-
-
-def tie(name, value, choices):
-    pick = CFG.get(name, "")
-    for k in pick.split("+") if pick else ():
-        value = after(value, choices[k]) if k in choices else value
-    return value
 
 
 def after(value, *others):
@@ -863,6 +838,8 @@
     me = lax.axis_index("seq").astype(jnp.int32)[None]
     here_x, here_dy = tokens[0], cotangent[0]
     cube = devices == len(CUBE) and lax.axis_size("dp") == 4
+    if devices == len(CUBE) and not cube:
+        raise ValueError("unknown mesh")
     (payload,) = call(
         payload_kernel,
         [((rows + ORDER_ROWS, width), BF16)],
@@ -875,7 +852,7 @@
     weights = (lengths, order, norm_gain, w_in, conv_weight.T, conv_bias, w_x.T, w_dt, dt_bias, a_log.T, d_skip)
     if cube:
         across_x = [payload] + [swap(payload, "seq", d) for d in CUBE[1:4]]
-        send_dy = tie("dy", here_dy, {"d2": across_x[1], "d4": across_x[2], "d6": across_x[3]})
+        send_dy = after(here_dy, across_x[2])
         across_dy = [send_dy] + [swap(send_dy, "seq", d) for d in CUBE[1:4]]
         pieces_x = across_x + [swap(part, "seq", 1) for part in across_x]
     else:
@@ -916,7 +893,6 @@
         1,
         "forward_local",
         24,
-        9,
         far_ins=tuple(range(n + 1, n + 1 + len(weights))),
     )(me, *pieces_x, *weights)
     if cube:
@@ -928,48 +904,53 @@
         pieces_dy = [mine, swap(theirs, "seq", 1)]
     carry_rows = (state, 2 * state)[not cube]
     n_sent = (len(SENT), 1)[not cube]
-    trans_dy, gg, gm, cbc, chunkb, near_out, *carries = call(
+    trans_dy, gg, gm, cbc, chunkb, near_out, factor, *carries = call(
         functools.partial(back_kernel, sizes, len(pieces_dy)),
-        [((rows, width), BF16), (big, F32), (big, F32), (spread, F32), (carried, F32), (w_out.shape, BF16)]
+        [((rows, width), BF16), (big, F32), (big, F32), (spread, F32), (carried, F32), (w_out.shape, BF16), ((rows, width), BF16)]
         + [((carry_rows, inner + LANES), F32)] * n_sent,
         [pltpu.SemaphoreType.DMA],
         1,
         "backward_local",
         20,
-        7,
         far_ins=(len(pieces_dy) + 5,),
-    )(me, *pieces_dy, gate, far, xproj, a2, w_out, sums, f, column)
+    )(me, *pieces_dy, gate, far, xproj, a2, w_out, sums, f, column, normed)
     carries = spread_carries(carries, "seq")
+    if cube:
+        factor = swap(factor, "seq", 1)
+        gate = after(gate, factor)
     n_small = small_rows(sizes)
     held = ((n * (carry_rows + CHUNKS), inner), F32)
     kept = [pltpu.VMEM((state, rows + CHUNKS, LANES), F32)] * (inner // LANES)
-    *states, gated, gz, keep, send = call(
+    *states, gated, gz, send = call(
         functools.partial(scan_forward_kernel, sizes, len(carries)),
-        [*kept, (big, BF16), (big, BF16), ((width, inner), BF16), ((width, inner), BF16)],
+        [*kept, (big, BF16), (big, BF16), (big, BF16)],
         [(big, F32), (carried, F32), held],
         1,
         "scan_forward",
         18,
-        7,
-    )(me, *carries, trans_dy, normed, gg, gate, act, far, use, bbc, cbc, chunkf, sums, a2, row_consts)
-    first = (keep, send)
+    )(me, *carries, gg, gate, act, far, use, bbc, cbc, chunkf, sums, a2, row_consts)
     half_one, half_two = width, -(-(width + n_small) // (8 * BLOCK)) * (4 * BLOCK)
-    got = swap(send, "seq", 1) if cube else None
-    gstart, branch = call(
+    if cube:
+        got = swap(send, "seq", 1)
+    gstart, branch, part = call(
         functools.partial(branch_kernel, sizes, len(carries)),
-        [(carried, F32), ((rows, width), BF16)],
+        [(carried, F32), ((rows, width), BF16), ((width, inner), F32)],
         [held],
         1,
         "adjoint_carries_and_branch",
         8,
-        1.5,
-    )(me, *carries, chunkb, sums, a2, gated, near_out)
+    )(me, *carries, chunkb, sums, a2, gated, gz, trans_dy, normed, near_out)
     if cube:
         part_one = half_one // 4
         beside_one = ((rows // 2 + part_one, inner), BF16)
         own_one, *sent = call(
-            halves_beside_kernel, [((part_one, inner), BF16)] + [beside_one] * 3, [], 1, "add_halves_beside_rows", 8
-        )(me, tie("adj", keep, {"gstart": gstart}), got, branch)
+            first_halves_kernel,
+            [((part_one, inner), BF16)] + [beside_one] * 3,
+            [((width, inner), F32)],
+            1,
+            "first_halves",
+            12,
+        )(me, part, factor, got, branch)
         away_one = [swap(block, "seq", d) for block, d in zip(sent, SENT)]
     gconv, rim, gpre, gxproj, galog = call(
         functools.partial(scan_backward_kernel, sizes),
@@ -978,14 +959,11 @@
         0,
         "scan_backward",
         20,
-        14,
-    )(*[pltpu.with_memory_space_constraint(part, pltpu.VMEM) for part in states], gstart, far, use, bbc, cbc, gm, step, act, conv, valid, a2, row_consts, w_x_pad, w_dt_pad)
+    )(
+        *[pltpu.with_memory_space_constraint(part, pltpu.VMEM) for part in states],
+        gstart, far, use, bbc, cbc, gm, step, act, conv, valid, a2, row_consts, w_x_pad, w_dt_pad,
+    )
     rim = from_behind(rim, "seq", -1)
-    if cube:
-        add_one = call(sum_kernel, [((part_one, inner), BF16)], [], 0, "add_parts", 4)
-        if CFG["small"] != "mid":
-            (one,) = add_one(tie("rim", after(own_one, gpre), {"rim": rim}), *away_one)
-            gpre = tie("small", gpre, {"one": one})
     small, gci = call(
         functools.partial(small_kernel, sizes),
         [((n_small, inner), F32), (big, F32)],
@@ -993,10 +971,11 @@
         0,
         "small_grads",
         16,
-        1.6,
     )(gpre, gxproj, xproj, act, gconv, ext, valid, gm, row_consts, galog)
-    if cube and CFG["small"] == "mid":
-        (one,) = add_one(after(own_one, small), *away_one)
+    if cube:
+        (one,) = call(sum_kernel, [((part_one, inner), BF16)], [], 0, "add_parts", 4)(
+            after(own_one, small), *away_one
+        )
         small = after(small, one)
     back, keep, send = call(
         functools.partial(final_kernel, sizes, devices),
@@ -1022,135 +1001,47 @@
     if cube:
         part_two = half_two // 4
         piece_one, piece_two = ((part_one, inner), BF16), ((part_two, inner), BF16)
-        pair_two = call(pair_kernel, [piece_two], [], 0, "add_pair", 4)
-        rows_out = [((rows, width), BF16)]
-        arrive = call(arrive_kernel, rows_out, [], 0, "add_arrived", 4)
+        pair_one, pair_two = [call(pair_kernel, [piece], [], 0, "add_pair", 4) for piece in (piece_one, piece_two)]
         got = swap(send, "seq", 1)
-        at = {"send": send}
-        away_first = away_one
-
-        def branch_rows(point, value):
-            if CFG["share"] != point or CFG["p1d"] == "z":
-                return value
-            mine, theirs = call(
-                functools.partial(share_kernel, rows, width),
-                rows_out + [((rows // 2, inner), BF16)],
-                [],
-                1,
-                "share_rows",
-                8,
-            )(me, orders, after(branch, at[point]), *away_one)
-            at["out"] = arrive(here_x, mine, swap(theirs, "seq", 1))[0]
-            return tie("hold", value, at)
-
-        one = tie("z1", one, at)
+        one = after(one, send)
         z_one = swap(one, "dp", 1)
-        keep = tie("halves", keep, {"z": z_one})
-        keep = branch_rows("send", keep)
         own_two, *sent = call(halves_kernel, [piece_two] * 4, [], 1, "add_halves", 4)(me, keep, got)
         away_two = [swap(block, "seq", d) for block, d in zip(sent, SENT)]
-        at.update(d2=away_two[0], d4=away_two[1], d6=away_two[2], own=own_two)
-        at["z1"] = z_one
-        (one,) = call(pair_kernel, [piece_one], [], 0, "add_pair", 4)(tie("pair", one, at), z_one)
-        z_one = swap(one, "dp", 2)
-        at["zz"] = z_one
-        own_two = tie("sumz", branch_rows("own", own_two), at)
-        (two,) = call(sum_kernel, [piece_two], [], 0, "add_parts", 4)(own_two, *away_two)
-        z_two = swap(two, "dp", 1)
-        at["summed"], at["z"] = two, z_two
-        two = tie("c1", branch_rows("summed", two), at)
+        (one,) = pair_one(after(one, away_two[0]), z_one)
+        z_here, z_one = z_one, swap(one, "dp", 2)
+        (two,) = call(sum_kernel, [piece_two], [], 0, "add_parts", 4)(after(own_two, z_here), *away_two)
+        (two,) = pair_two(two, swap(two, "dp", 1))
+        z_two = swap(two, "dp", 2)
+        back = after(back, own_two)
+        away_back = [swap(back, "seq", d) for d in SENT[:3]]
+        mine_b, mine_g, theirs = call(
+            functools.partial(share_both_kernel, rows, width),
+            [((rows, width), BF16)] * 2 + [((rows, inner), BF16)],
+            [],
+            1,
+            "share_rows",
+            12,
+        )(me, orders, after(branch, two), *away_one, back, *away_back)
+        output, input_grad = call(arrive_both_kernel, [((rows, width), BF16)] * 2, [], 0, "add_arrived", 8)(
+            here_x, here_dy, mine_b, mine_g, swap(theirs, "seq", 1)
+        )
+        paired = two
         (two,) = pair_two(two, z_two)
-        z_two = swap(two, "dp", 2)
-        at["pair"] = two
-        two = branch_rows("pair", two)
-        if CFG["p1d"] == "z":
-            back = tie("m3", back, at)
-            away_back = [swap(back, "seq", d) for d in SENT[:3]]
-            at.update(b2=away_back[0], b4=away_back[1], b6=away_back[2])
-            mine_b, mine_g, theirs = call(
-                functools.partial(share_both_kernel, rows, width),
-                rows_out * 2 + [((rows, inner), BF16)],
-                [],
-                1,
-                "share_rows",
-                12,
-            )(me, orders, tie("share", branch, at), *away_first, back, *away_back)
-            output, input_grad = call(arrive_both_kernel, rows_out * 2, [], 0, "add_arrived", 8)(
-                here_x, here_dy, mine_b, mine_g, swap(theirs, "seq", 1)
-            )
-            at.update(out=output, arrived=input_grad)
-            two = tie("fin", two, at)
-        (two,) = pair_two(two, z_two)
-        at["total"] = two
-        branch_rows("total", two)
-        if CFG["p1d"] != "z":
-            back = tie("m3", back, at)
-        share = functools.partial(share_kernel, rows, width)
-        if CFG["p1d"] == "m3":
-            (one,) = call(pair_beside_kernel, [beside_one], [], 0, "add_pair_beside_rows", 8)(one, z_one, back)
-            away_one = [swap(one, "seq", d) for d in SENT[:3]]
-            two = tie("d", two, at)
-            away_two = [swap(two, "seq", d) for d in SENT[:3]]
-            at.update(d2=away_two[0], d4=away_two[1], d6=away_two[2])
-            mine, theirs, own_one = call(
-                share,
-                rows_out + [((rows // 2 + half_one, inner), BF16), ((half_one, inner), BF16)],
-                [],
-                1,
-                "share_rows_and_parts",
-                12,
-            )(me, orders, tie("share3", one, at), *away_one)
-            theirs = swap(theirs, "seq", 1)
-            f_wout, f_win = first_results(own_one, theirs)
-            (input_grad,) = arrive(here_dy, mine, theirs)
-            at.update(first=f_wout, arrived=input_grad)
-            (own_two,) = call(chips_kernel, [((half_two, inner), BF16)], [], 1, "order_parts", 4)(
-                me, tie("chips2", two, at), *away_two
-            )
-            other_two = swap(own_two, "seq", 1)
-        else:
-            if CFG["p1d"] != "z":
-                away_back = [swap(back, "seq", d) for d in SENT[:3]]
-                at.update(b2=away_back[0], b4=away_back[1], b6=away_back[2])
-            (one,) = call(pair_kernel, [piece_one], [], 0, "add_pair", 4)(one, z_one)
-            if CFG["p1d"] in "yz":
-                away_one = [swap(tie("one", one, at), "seq", d) for d in SENT[:3]]
-                at.update(o2=away_one[0], o4=away_one[1], o6=away_one[2])
-                (own_one,) = call(chips_kernel, [((half_one, inner), BF16)], [], 1, "order_parts", 4)(
-                    me, tie("chips1", one, at), *away_one
-                )
-                f_wout, f_win = first_results(own_one, swap(own_one, "seq", 1))
-                at.update(first=f_wout)
-                two = tie("d", two, at)
-                away_two = [swap(two, "seq", d) for d in SENT[:3]]
-                at.update(d2=away_two[0], d4=away_two[1], d6=away_two[2])
-                (own_two,) = call(chips_kernel, [((half_two, inner), BF16)], [], 1, "order_parts", 4)(
-                    me, tie("chips2", two, at), *away_two
-                )
-                other_two = swap(own_two, "seq", 1)
-            else:
-                two = tie("d", two, at)
-                (both,) = call(stack_kernel, [((part_two + part_one, inner), BF16)], [], 0, "stack", 4)(two, one)
-                away = [swap(both, "seq", d) for d in SENT[:3]]
-                at.update(d2=away[0], d4=away[1], d6=away[2])
-                (own_one,) = call(
-                    functools.partial(both_chips_kernel, part_two, part_one),
-                    [((half_two + half_one, inner), BF16)],
-                    [],
-                    1,
-                    "order_parts",
-                    8,
-                )(me, both, *away)
-                own_two, other_two = own_one, swap(own_one, "seq", 1)
-                f_wout, f_win = first_results(own_two, other_two)
-            if CFG["p1d"] != "z":
-                mine, theirs = call(share, rows_out + [((rows // 2, inner), BF16)], [], 1, "share_rows", 8)(
-                    me, orders, tie("share3", back, at), *away_back
-                )
-                (input_grad,) = arrive(tie("arrive", here_dy, at), mine, swap(theirs, "seq", 1))
-        totals = (own_two, other_two)
-        output = at["out"]
+        (one,) = pair_one(one, z_one)
+        away_one = []
+        for d in SENT[:3]:
+            held_back = one
+            for there in (*away_back, paired):
+                held_back = after(held_back, there)
+            away_one.append(swap(held_back, "seq", d))
+        order_parts = lambda half: call(chips_kernel, [((half, inner), BF16)], [], 1, "order_parts", 4)
+        (own_one,) = order_parts(half_one)(me, after(one, two), *away_one)
+        f_wout, f_win = first_results(own_one, swap(own_one, "seq", 1))
+        away_two = [swap(two, "seq", d) for d in SENT[:3]]
+        (own_two,) = order_parts(half_two)(me, after(two, f_wout), *away_two)
+        totals = (own_two, swap(own_two, "seq", 1))
     else:
+        first = call(products_kernel, [((width, inner), F32)] * 2, [], 0, "products", 12)(trans_dy, gated, normed, gz)
         totals = [lax.psum(half.astype(F32), ("dp", "seq")).astype(BF16) for half in (*first, keep, send)]
         f_wout, f_win = first_results(*totals[:2])
         totals = totals[2:]

time: 111 us -> 110 us (level)
    ppermute x42 -> x43, starting transfers between devices: 39.6 us -> 38.9 us  [swap(): lax.ppermute(block, axis, [(i, i ^ distance) for i in range(devices)])]
    ppermute x42 -> x43, waiting for transfers between devices: 28.5 us -> 28.6 us  [swap(): lax.ppermute(block, axis, [(i, i ^ distance) for i in range(devices)])]
  transfers between devices with their start and end apart: 43 -> 44, of which waited for: 17 -> 18; matrix products, arithmetic and copies ran while one was open for 0% -> 0% of each run, Pallas kernels for 24% -> 24%
where the time goes in v5:
time: 110 us
  starting transfers between devices  40.2 us (37%)
  Pallas kernels  39.9 us (36%)
  waiting for transfers between devices  28.6 us (26%)
  between operations  1.14 us (1%)
    pallas_call x24, Pallas kernels, run(): pl.pallas_call(kernel, out_shape=[jax.ShapeDtypeStruct(*part) if isinstan...  39.9 us
    ppermute x43, starting transfers between devices, swap(): lax.ppermute(block, axis, [(i, i ^ distance) for i in range(devices)])  38.9 us
    ppermute x43, waiting for transfers between devices, swap(): lax.ppermute(block, axis, [(i, i ^ distance) for i in range(devices)])  28.6 us
  transfers between devices with their start and end apart: 44, of which 18 were waited for; matrix products, arithmetic and copies ran while one was open for 0% of the time, Pallas kernels for 24%

profile of v5, /device:TPU:0, one launch (start us, length us, event | category | flops | bytes accessed | tf_op | source)
XLA Modules:
  0.0 110.0 jit_solution(6335711796067156210)
XLA Ops:
  1.7 4.0 %collective-permute-start.2 = (bf16[272,384]{1,0:T(8,128)(2,1)S(1)}, bf16[272,384]{1,0:T(8,128)(2,1)S(1)}, u32[]{:S(2)}, u32[]{:S(2)}) collective-permute-start(bf16[272,384]{1,0:T(8,128)(2,1)S(1)} %tokens_and_order.1.refs_0_), channel_id=1, source_target_pairs={{0,6},{1,7},{2,4},{3,5},{4,2},{5,3},{6,0},{7,1},{8,14},{9,15},{10,... | collective-permute-start | bytes 626696 | tf_op jit(solution)/shard_map/ppermute | solution.py:796
  6.3 5.4 %collective-permute-done.2.refs_3_ = bf16[272,384]{1,0:T(8,128)(2,1)S(1)} collective-permute-done((bf16[272,384]{1,0:T(8,128)(2,1)S(1)}, bf16[272,384]{1,0:T(8,128)(2,1)S(1)}, u32[]{:S(2)}, u32[]{:S(2)}) %collective-permute-start.2) | collective-permute-done | bytes 208928 | tf_op jit(solution)/shard_map/ppermute | solution.py:796
  11.7 3.6 %collective-permute-done.1.refs_2_ = bf16[272,384]{1,0:T(8,128)(2,1)S(1)} collective-permute-done((bf16[272,384]{1,0:T(8,128)(2,1)S(1)}, bf16[272,384]{1,0:T(8,128)(2,1)S(1)}, u32[]{:S(2)}, u32[]{:S(2)}) %collective-permute-start.1) | collective-permute-done | bytes 208928 | tf_op jit(solution)/shard_map/ppermute | solution.py:796
  15.8 1.8 %collective-permute-start.9 = (bf16[256,384]{1,0:T(8,128)(2,1)}, bf16[256,384]{1,0:T(8,128)(2,1)S(1)}, u32[]{:S(2)}, u32[]{:S(2)}) collective-permute-start(bf16[256,384]{1,0:T(8,128)(2,1)} %bitcast.11), channel_id=1, source_target_pairs={{0,6},{1,7},{2,4},{3,5},{4,2},{5,3},{6,0},{7,1},{8,14},{9,15},{10,... | collective-permute-start | bytes 589832 | tf_op jit(solution)/shard_map/ppermute | solution.py:796
  17.6 1.3 %collective-permute-start.8 = (bf16[256,384]{1,0:T(8,128)(2,1)}, bf16[256,384]{1,0:T(8,128)(2,1)S(1)}, u32[]{:S(2)}, u32[]{:S(2)}) collective-permute-start(bf16[256,384]{1,0:T(8,128)(2,1)} %bitcast.12), channel_id=1, source_target_pairs={{0,4},{1,5},{2,6},{3,7},{4,0},{5,1},{6,2},{7,3},{8,12},{9,13},{10,... | collective-permute-start | bytes 589832 | tf_op jit(solution)/shard_map/ppermute | solution.py:796
  19.3 8.1 %forward_local.1 = (bf16[256,384]{1,0:T(8,128)(2,1)S(1)}, bf16[256,384]{1,0:T(8,128)(2,1)S(1)}, f32[256,768]{1,0:T(8,128)S(1)}, f32[280,768]{1,0:T(8,128)S(1)}, ...) custom-call(s32[1]{0:T(128)} %bitcast.2.me.me_ref, ...), custom_call_target="tpu_custom_call" | custom-call | flops 1 | bytes 1 | tf_op jit(solution)/shard_map/forward_local/pallas_call | solution.py:773
  30.2 5.1 %backward_local.1 = (bf16[256,384]{1,0:T(8,128)(2,1)S(1)}, f32[256,768]{1,0:T(8,128)S(1)}, f32[256,768]{1,0:T(8,128)S(1)}, f32[256,2048]{1,0:T(8,128)S(1)}, f32[...) custom-call(s32[1]{0:T(128)} %bitcast.2.me.me_ref, ...), custom_call_target="tpu_custom_call" | custom-call | flops 1 | bytes 1 | tf_op jit(solution)/shard_map/backward_local/pallas_call | solution.py:773
  35.5 1.5 %collective-permute-start.11 = (f32[16,896]{1,0:T(8,128)S(1)}, f32[16,896]{1,0:T(8,128)S(1)}, u32[]{:S(2)}, u32[]{:S(2)}) collective-permute-start(f32[16,896]{1,0:T(8,128)S(1)} %get-tuple-element.117), channel_id=1, source_target_pairs={{0,2},{1,3},{2,0},{3,1},{4,6},{5,7},{6,4},{7,5},{8,10},{9,11},{10,... | collective-permute-start | bytes 172040 | tf_op jit(solution)/shard_map/ppermute | solution.py:796
  37.6 1.4 %collective-permute-start.13 = (f32[16,896]{1,0:T(8,128)S(1)}, f32[16,896]{1,0:T(8,128)S(1)}, u32[]{:S(2)}, u32[]{:S(2)}) collective-permute-start(f32[16,896]{1,0:T(8,128)S(1)} %get-tuple-element.119), channel_id=1, source_target_pairs={{0,6},{1,7},{2,4},{3,5},{4,2},{5,3},{6,0},{7,1},{8,14},{9,15},{10,... | collective-permute-start | bytes 172040 | tf_op jit(solution)/shard_map/ppermute | solution.py:796
  39.7 2.1 %collective-permute-done.12.refs_1_ = f32[16,896]{1,0:T(8,128)S(1)} collective-permute-done((f32[16,896]{1,0:T(8,128)S(1)}, f32[16,896]{1,0:T(8,128)S(1)}, u32[]{:S(2)}, u32[]{:S(2)}) %collective-permute-start.12) | collective-permute-done | bytes 57376 | tf_op jit(solution)/shard_map/ppermute | solution.py:796
  43.9 4.2 %scan_forward.1 = (f32[16,264,128]{2,1,0:T(8,128)S(1)}, f32[16,264,128]{2,1,0:T(8,128)S(1)}, f32[16,264,128]{2,1,0:T(8,128)S(1)}, f32[16,264,128]{2,1,0:T(8,128)...) custom-call(s32[1]{0:T(128)} %bitcast.2.me.me_ref, ...), custom_call_target="tpu_custom_call" | custom-call | flops 1 | bytes 1 | tf_op jit(solution)/shard_map/scan_forward/pallas_call | solution.py:773
  50.4 1.4 %collective-permute-start.21 = (bf16[224,768]{1,0:T(8,128)(2,1)S(1)}, bf16[224,768]{1,0:T(8,128)(2,1)S(1)}, u32[]{:S(2)}, u32[]{:S(2)}) collective-permute-start(bf16[224,768]{1,0:T(8,128)(2,1)S(1)} %get-tuple-element.162), channel_id=1, source_target_pairs={{0,2},{1,3},{2,0},{3,1},{4,6},{5,7},{6,4},{7,5},{8,10},{9,11},{10,... | collective-permute-start | bytes 1032200 | tf_op jit(solution)/shard_map/ppermute | solution.py:796
  52.4 1.5 %collective-permute-start.23 = (bf16[224,768]{1,0:T(8,128)(2,1)S(1)}, bf16[224,768]{1,0:T(8,128)(2,1)S(1)}, u32[]{:S(2)}, u32[]{:S(2)}) collective-permute-start(bf16[224,768]{1,0:T(8,128)(2,1)S(1)} %get-tuple-element.164), channel_id=1, source_target_pairs={{0,6},{1,7},{2,4},{3,5},{4,2},{5,3},{6,0},{7,1},{8,14},{9,15},{10,... | collective-permute-start | bytes 1032200 | tf_op jit(solution)/shard_map/ppermute | solution.py:796
  53.9 10.0 %scan_backward.1 = (f32[256,768]{1,0:T(8,128)S(1)}, f32[8,768]{1,0:T(8,128)S(1)}, bf16[256,768]{1,0:T(8,128)(2,1)S(1)}, bf16[256,128]{1,0:T(8,128)(2,1)S(1)}, f32[16,768]{1,0:T(8,128)S(1)}) custom-call(f32[16,264,128]{2,1,0:T(8,128)S(1)} %get-tuple-element.137.refs_0_, f32[16,264,128]{2,1,0:T(8,128)S(1)} %get-tuple-element.138.refs_1_, ...), custom_call_target="tpu_custom_call" | custom-call | flops 1 | bytes 1 | tf_op jit(solution)/shard_map/scan_backward/pallas_call | solution.py:773
  64.0 1.3 %collective-permute-start.19 = (f32[8,768]{1,0:T(8,128)S(1)}, f32[8,768]{1,0:T(8,128)S(1)}, u32[]{:S(2)}, u32[]{:S(2)}) collective-permute-start(f32[8,768]{1,0:T(8,128)S(1)} %get-tuple-element.156), channel_id=1, source_target_pairs={{1,0},{2,1},{3,2},{4,3},{5,4},{6,5},{7,6},{9,8},{10,9},{11,10},{12... | collective-permute-start | bytes 73736 | tf_op jit(solution)/shard_map/ppermute | solution.py:814
  65.3 1.9 %small_grads.1 = (f32[104,768]{1,0:T(8,128)S(1)}, f32[256,768]{1,0:T(8,128)S(1)}) custom-call(bf16[256,768]{1,0:T(8,128)(2,1)S(1)} %get-tuple-element.150.gpre, bf16[256,128]{1,0:T(8,128)(2,1)S(1)} %get-tuple-element.151.gxproj, f32[256,128]{1,0:T(8,128)S(1)} %get-tuple-element.112.refs_4_.xproj, ...), custom_call_target="tpu_custom_call" | custom-call | flops 1 | bytes 1 | tf_op jit(solution)/shard_map/small_grads/pallas_call | solution.py:773
  67.2 1.8 %collective-permute-done.22.c.refs_2_ = bf16[224,768]{1,0:T(8,128)(2,1)S(1)} collective-permute-done((bf16[224,768]{1,0:T(8,128)(2,1)S(1)}, bf16[224,768]{1,0:T(8,128)(2,1)S(1)}, u32[]{:S(2)}, u32[]{:S(2)}) %collective-permute-start.22) | collective-permute-done | bytes 344096 | tf_op jit(solution)/shard_map/ppermute | solution.py:796
  70.1 1.6 %collective-permute-start.25 = (bf16[96,768]{1,0:T(8,128)(2,1)S(1)}, bf16[96,768]{1,0:T(8,128)(2,1)S(1)}, u32[]{:S(2)}, u32[]{:S(2)}) collective-permute-start(bf16[96,768]{1,0:T(8,128)(2,1)S(1)} %add_parts.2.a), channel_id=1, source_target_pairs={{0,8},{8,0},{16,24},{24,16},{1,9},{9,1},{17,25},{25,17},{2,10},{10... | collective-permute-start | bytes 442376 | tf_op jit(solution)/shard_map/ppermute | solution.py:796
  71.9 1.5 %collective-permute-start.26 = (bf16[64,768]{1,0:T(8,128)(2,1)S(1)}, bf16[64,768]{1,0:T(8,128)(2,1)S(1)}, u32[]{:S(2)}, u32[]{:S(2)}) collective-permute-start(bf16[64,768]{1,0:T(8,128)(2,1)S(1)} %get-tuple-element.171), channel_id=1, source_target_pairs={{0,2},{1,3},{2,0},{3,1},{4,6},{5,7},{6,4},{7,5},{8,10},{9,11},{10,... | collective-permute-start | bytes 294920 | tf_op jit(solution)/shard_map/ppermute | solution.py:796
  74.1 1.4 %collective-permute-start.28 = (bf16[64,768]{1,0:T(8,128)(2,1)S(1)}, bf16[64,768]{1,0:T(8,128)(2,1)S(1)}, u32[]{:S(2)}, u32[]{:S(2)}) collective-permute-start(bf16[64,768]{1,0:T(8,128)(2,1)S(1)} %get-tuple-element.173), channel_id=1, source_target_pairs={{0,6},{1,7},{2,4},{3,5},{4,2},{5,3},{6,0},{7,1},{8,14},{9,15},{10,... | collective-permute-start | bytes 294920 | tf_op jit(solution)/shard_map/ppermute | solution.py:796
  75.5 1.4 %collective-permute-start.30 = (bf16[256,384]{1,0:T(8,128)(2,1)S(1)}, bf16[256,384]{1,0:T(8,128)(2,1)S(1)}, u32[]{:S(2)}, u32[]{:S(2)}) collective-permute-start(bf16[256,384]{1,0:T(8,128)(2,1)S(1)} %get-tuple-element.176.refs_4_), channel_id=1, source_target_pairs={{0,2},{1,3},{2,0},{3,1},{4,6},{5,7},{6,4},{7,5},{8,10},{9,11},{10,... | collective-permute-start | bytes 589832 | tf_op jit(solution)/shard_map/ppermute | solution.py:796
  77.6 1.5 %collective-permute-start.32 = (bf16[256,384]{1,0:T(8,128)(2,1)S(1)}, bf16[256,384]{1,0:T(8,128)(2,1)S(1)}, u32[]{:S(2)}, u32[]{:S(2)}) collective-permute-start(bf16[256,384]{1,0:T(8,128)(2,1)S(1)} %get-tuple-element.176.refs_4_), channel_id=1, source_target_pairs={{0,6},{1,7},{2,4},{3,5},{4,2},{5,3},{6,0},{7,1},{8,14},{9,15},{10,... | collective-permute-start | bytes 589832 | tf_op jit(solution)/shard_map/ppermute | solution.py:796
  79.1 1.3 %collective-permute-done.27.c = bf16[64,768]{1,0:T(8,128)(2,1)S(1)} collective-permute-done((bf16[64,768]{1,0:T(8,128)(2,1)S(1)}, bf16[64,768]{1,0:T(8,128)(2,1)S(1)}, u32[]{:S(2)}, u32[]{:S(2)}) %collective-permute-start.27) | collective-permute-done | bytes 98336 | tf_op jit(solution)/shard_map/ppermute | solution.py:796
  80.4 2.6 %collective-permute-start.35 = (bf16[96,768]{1,0:T(8,128)(2,1)S(1)}, bf16[96,768]{1,0:T(8,128)(2,1)S(1)}, u32[]{:S(2)}, u32[]{:S(2)}) collective-permute-start(bf16[96,768]{1,0:T(8,128)(2,1)S(1)} %add_pair.6.a), channel_id=1, source_target_pairs={{0,16},{8,24},{16,0},{24,8},{1,17},{9,25},{17,1},{25,9},{2,18},{10... | collective-permute-start | bytes 442376 | tf_op jit(solution)/shard_map/ppermute | solution.py:796
  83.0 1.4 %collective-permute-start.29 = (bf16[64,768]{1,0:T(8,128)(2,1)S(1)}, bf16[64,768]{1,0:T(8,128)(2,1)S(1)}, u32[]{:S(2)}, u32[]{:S(2)}) collective-permute-start(bf16[64,768]{1,0:T(8,128)(2,1)S(1)} %add_parts.3.a), channel_id=1, source_target_pairs={{0,8},{8,0},{16,24},{24,16},{1,9},{9,1},{17,25},{25,17},{2,10},{10... | collective-permute-start | bytes 294920 | tf_op jit(solution)/shard_map/ppermute | solution.py:796
  84.5 4.0 %collective-permute-done.29.b = bf16[64,768]{1,0:T(8,128)(2,1)S(1)} collective-permute-done((bf16[64,768]{1,0:T(8,128)(2,1)S(1)}, bf16[64,768]{1,0:T(8,128)(2,1)S(1)}, u32[]{:S(2)}, u32[]{:S(2)}) %collective-permute-start.29) | collective-permute-done | bytes 98336 | tf_op jit(solution)/shard_map/ppermute | solution.py:796
  90.6 1.5 %collective-permute-start.36 = (bf16[96,768]{1,0:T(8,128)(2,1)S(1)}, bf16[96,768]{1,0:T(8,128)(2,1)S(1)}, u32[]{:S(2)}, u32[]{:S(2)}) collective-permute-start(bf16[96,768]{1,0:T(8,128)(2,1)S(1)} %add_pair.7.own), channel_id=1, source_target_pairs={{0,2},{1,3},{2,0},{3,1},{4,6},{5,7},{6,4},{7,5},{8,10},{9,11},{10,... | collective-permute-start | bytes 442376 | tf_op jit(solution)/shard_map/ppermute | solution.py:796
  92.1 2.5 %collective-permute-start.34 = (bf16[64,768]{1,0:T(8,128)(2,1)S(1)}, bf16[64,768]{1,0:T(8,128)(2,1)S(1)}, u32[]{:S(2)}, u32[]{:S(2)}) collective-permute-start(bf16[64,768]{1,0:T(8,128)(2,1)S(1)} %add_pair.4.a), channel_id=1, source_target_pairs={{0,16},{8,24},{16,0},{24,8},{1,17},{9,25},{17,1},{25,9},{2,18},{10... | collective-permute-start | bytes 294920 | tf_op jit(solution)/shard_map/ppermute | solution.py:796
  94.6 4.0 %collective-permute-done.34.b = bf16[64,768]{1,0:T(8,128)(2,1)S(1)} collective-permute-done((bf16[64,768]{1,0:T(8,128)(2,1)S(1)}, bf16[64,768]{1,0:T(8,128)(2,1)S(1)}, u32[]{:S(2)}, u32[]{:S(2)}) %collective-permute-start.34) | collective-permute-done | bytes 98336 | tf_op jit(solution)/shard_map/ppermute | solution.py:796
  99.9 2.5 %collective-permute-start.40 = (bf16[64,768]{1,0:T(8,128)(2,1)S(1)}, bf16[64,768]{1,0:T(8,128)(2,1)S(1)}, u32[]{:S(2)}, u32[]{:S(2)}) collective-permute-start(bf16[64,768]{1,0:T(8,128)(2,1)S(1)} %add_pair.5.own), channel_id=1, source_target_pairs={{0,2},{1,3},{2,0},{3,1},{4,6},{5,7},{6,4},{7,5},{8,10},{9,11},{10,... | collective-permute-start | bytes 294920 | tf_op jit(solution)/shard_map/ppermute | solution.py:796
  103.8 2.2 %first_results.1 = (f32[768,384]{1,0:T(8,128)}, f32[384,1536]{1,0:T(8,128)}) custom-call(s32[1]{0:T(128)} %bitcast.2.me.me_ref, bf16[384,768]{1,0:T(8,128)(2,1)S(1)} %order_parts.2.own, bf16[384,768]{1,0:T(8,128)(2,1)S(1)} %collective-permute-done.39.other), custom_call_target="tpu_custom_call" | custom-call | flops 1 | bytes 1 | tf_op jit(solution)/shard_map/first_results/pallas_call | solution.py:773
  108.0 1.8 %last_results.1 = (f32[384]{0:T(512)}, f32[384,1536]{1,0:T(8,128)}, f32[4,768]{1,0:T(4,128)}, f32[768]{0:T(1024)}, f32[56,768]{1,0:T(8,128)}, /*index=5*/f32[24,...) custom-call(s32[1]{0:T(128)} %bitcast.2.me.me_ref, ...), custom_call_target="tpu_custom_call", output_to_operand_aliasing={{1}: (3, {})} | custom-call | flops 1 | bytes 1 | tf_op jit(solution)/shard_map/last_results/pallas_call | solution.py:773
  (88 shorter events, 21.1 us)
Async XLA Ops:
  1.7 10.0 %collective-permute-start.2 = (bf16[272,384]{1,0:T(8,128)(2,1)S(1)}, bf16[272,384]{1,0:T(8,128)(2,1)S(1)}, u32[]{:S(2)}, u32[]{:S(2)}) collective-permute-start(bf16[272,384]{1,0:T(8,128)(2,1)S(1)} %tokens_and_order.1.refs_0_), channel_id=1, source_target_pairs={{0,6},{1,7},{2,4},{3,5},{4,2},{5,3},{6,0},{7,1},{8,14},{9,15},{10,... | collective-permute-start | bytes 626696 | tf_op jit(solution)/shard_map/ppermute | solution.py:796
  5.6 9.6 %collective-permute-start.1 = (bf16[272,384]{1,0:T(8,128)(2,1)S(1)}, bf16[272,384]{1,0:T(8,128)(2,1)S(1)}, u32[]{:S(2)}, u32[]{:S(2)}) collective-permute-start(bf16[272,384]{1,0:T(8,128)(2,1)S(1)} %tokens_and_order.1.refs_0_), channel_id=1, source_target_pairs={{0,4},{1,5},{2,6},{3,7},{4,0},{5,1},{6,2},{7,3},{8,12},{9,13},{10,... | collective-permute-start | bytes 626696 | tf_op jit(solution)/shard_map/ppermute | solution.py:796
  6.1 9.4 %collective-permute-start = (bf16[272,384]{1,0:T(8,128)(2,1)S(1)}, bf16[272,384]{1,0:T(8,128)(2,1)S(1)}, u32[]{:S(2)}, u32[]{:S(2)}) collective-permute-start(bf16[272,384]{1,0:T(8,128)(2,1)S(1)} %tokens_and_order.1.refs_0_), channel_id=1, source_target_pairs={{0,2},{1,3},{2,0},{3,1},{4,6},{5,7},{6,4},{7,5},{8,10},{9,11},{10,... | collective-permute-start | bytes 626696 | tf_op jit(solution)/shard_map/ppermute | solution.py:796
  6.3 11.3 %collective-permute-start.3 = (bf16[272,384]{1,0:T(8,128)(2,1)S(1)}, bf16[272,384]{1,0:T(8,128)(2,1)S(1)}, u32[]{:S(2)}, u32[]{:S(2)}) collective-permute-start(bf16[272,384]{1,0:T(8,128)(2,1)S(1)} %tokens_and_order.1.refs_0_), channel_id=1, source_target_pairs={{0,1},{1,0},{2,3},{3,2},{4,5},{5,4},{6,7},{7,6},{8,9},{9,8},{10,11... | collective-permute-start | bytes 626696 | tf_op jit(solution)/shard_map/ppermute | solution.py:796
  11.7 7.3 %collective-permute-start.6 = (bf16[272,384]{1,0:T(8,128)(2,1)S(1)}, bf16[272,384]{1,0:T(8,128)(2,1)S(1)}, u32[]{:S(2)}, u32[]{:S(2)}) collective-permute-start(bf16[272,384]{1,0:T(8,128)(2,1)S(1)} %collective-permute-done.2.refs_3_), channel_id=1, source_target_pairs={{0,1},{1,0},{2,3},{3,2},{4,5},{5,4},{6,7},{7,6},{8,9},{9,8},{10,11... | collective-permute-start | bytes 626696 | tf_op jit(solution)/shard_map/ppermute | solution.py:796
  15.8 11.6 %collective-permute-start.9 = (bf16[256,384]{1,0:T(8,128)(2,1)}, bf16[256,384]{1,0:T(8,128)(2,1)S(1)}, u32[]{:S(2)}, u32[]{:S(2)}) collective-permute-start(bf16[256,384]{1,0:T(8,128)(2,1)} %bitcast.11), channel_id=1, source_target_pairs={{0,6},{1,7},{2,4},{3,5},{4,2},{5,3},{6,0},{7,1},{8,14},{9,15},{10,... | collective-permute-start | bytes 589832 | tf_op jit(solution)/shard_map/ppermute | solution.py:796
  17.6 10.6 %collective-permute-start.8 = (bf16[256,384]{1,0:T(8,128)(2,1)}, bf16[256,384]{1,0:T(8,128)(2,1)S(1)}, u32[]{:S(2)}, u32[]{:S(2)}) collective-permute-start(bf16[256,384]{1,0:T(8,128)(2,1)} %bitcast.12), channel_id=1, source_target_pairs={{0,4},{1,5},{2,6},{3,7},{4,0},{5,1},{6,2},{7,3},{8,12},{9,13},{10,... | collective-permute-start | bytes 589832 | tf_op jit(solution)/shard_map/ppermute | solution.py:796
  18.9 9.3 %collective-permute-start.7 = (bf16[256,384]{1,0:T(8,128)(2,1)}, bf16[256,384]{1,0:T(8,128)(2,1)S(1)}, u32[]{:S(2)}, u32[]{:S(2)}) collective-permute-start(bf16[256,384]{1,0:T(8,128)(2,1)} %bitcast.13), channel_id=1, source_target_pairs={{0,2},{1,3},{2,0},{3,1},{4,6},{5,7},{6,4},{7,5},{8,10},{9,11},{10,... | collective-permute-start | bytes 589832 | tf_op jit(solution)/shard_map/ppermute | solution.py:796
  35.3 7.4 %collective-permute-start.18 = (bf16[256,384]{1,0:T(8,128)(2,1)S(1)}, bf16[256,384]{1,0:T(8,128)(2,1)S(1)}, u32[]{:S(2)}, u32[]{:S(2)}) collective-permute-start(bf16[256,384]{1,0:T(8,128)(2,1)S(1)} %get-tuple-element.123), channel_id=1, source_target_pairs={{0,1},{1,0},{2,3},{3,2},{4,5},{5,4},{6,7},{7,6},{8,9},{9,8},{10,11... | collective-permute-start | bytes 589832 | tf_op jit(solution)/shard_map/ppermute | solution.py:796
  37.0 4.8 %collective-permute-start.12 = (f32[16,896]{1,0:T(8,128)S(1)}, f32[16,896]{1,0:T(8,128)S(1)}, u32[]{:S(2)}, u32[]{:S(2)}) collective-permute-start(f32[16,896]{1,0:T(8,128)S(1)} %get-tuple-element.118), channel_id=1, source_target_pairs={{0,4},{1,5},{2,6},{3,7},{4,0},{5,1},{6,2},{7,3},{8,12},{9,13},{10,... | collective-permute-start | bytes 172040 | tf_op jit(solution)/shard_map/ppermute | solution.py:796
  37.6 5.1 %collective-permute-start.13 = (f32[16,896]{1,0:T(8,128)S(1)}, f32[16,896]{1,0:T(8,128)S(1)}, u32[]{:S(2)}, u32[]{:S(2)}) collective-permute-start(f32[16,896]{1,0:T(8,128)S(1)} %get-tuple-element.119), channel_id=1, source_target_pairs={{0,6},{1,7},{2,4},{3,5},{4,2},{5,3},{6,0},{7,1},{8,14},{9,15},{10,... | collective-permute-start | bytes 172040 | tf_op jit(solution)/shard_map/ppermute | solution.py:796
  50.4 16.8 %collective-permute-start.21 = (bf16[224,768]{1,0:T(8,128)(2,1)S(1)}, bf16[224,768]{1,0:T(8,128)(2,1)S(1)}, u32[]{:S(2)}, u32[]{:S(2)}) collective-permute-start(bf16[224,768]{1,0:T(8,128)(2,1)S(1)} %get-tuple-element.162), channel_id=1, source_target_pairs={{0,2},{1,3},{2,0},{3,1},{4,6},{5,7},{6,4},{7,5},{8,10},{9,11},{10,... | collective-permute-start | bytes 1032200 | tf_op jit(solution)/shard_map/ppermute | solution.py:796
  51.8 17.2 %collective-permute-start.22 = (bf16[224,768]{1,0:T(8,128)(2,1)S(1)}, bf16[224,768]{1,0:T(8,128)(2,1)S(1)}, u32[]{:S(2)}, u32[]{:S(2)}) collective-permute-start(bf16[224,768]{1,0:T(8,128)(2,1)S(1)} %get-tuple-element.163), channel_id=1, source_target_pairs={{0,4},{1,5},{2,6},{3,7},{4,0},{5,1},{6,2},{7,3},{8,12},{9,13},{10,... | collective-permute-start | bytes 1032200 | tf_op jit(solution)/shard_map/ppermute | solution.py:796
  52.4 16.6 %collective-permute-start.23 = (bf16[224,768]{1,0:T(8,128)(2,1)S(1)}, bf16[224,768]{1,0:T(8,128)(2,1)S(1)}, u32[]{:S(2)}, u32[]{:S(2)}) collective-permute-start(bf16[224,768]{1,0:T(8,128)(2,1)S(1)} %get-tuple-element.164), channel_id=1, source_target_pairs={{0,6},{1,7},{2,4},{3,5},{4,2},{5,3},{6,0},{7,1},{8,14},{9,15},{10,... | collective-permute-start | bytes 1032200 | tf_op jit(solution)/shard_map/ppermute | solution.py:796
  64.0 5.1 %collective-permute-start.19 = (f32[8,768]{1,0:T(8,128)S(1)}, f32[8,768]{1,0:T(8,128)S(1)}, u32[]{:S(2)}, u32[]{:S(2)}) collective-permute-start(f32[8,768]{1,0:T(8,128)S(1)} %get-tuple-element.156), channel_id=1, source_target_pairs={{1,0},{2,1},{3,2},{4,3},{5,4},{6,5},{7,6},{9,8},{10,9},{11,10},{12... | collective-permute-start | bytes 73736 | tf_op jit(solution)/shard_map/ppermute | solution.py:814
  70.1 6.8 %collective-permute-start.25 = (bf16[96,768]{1,0:T(8,128)(2,1)S(1)}, bf16[96,768]{1,0:T(8,128)(2,1)S(1)}, u32[]{:S(2)}, u32[]{:S(2)}) collective-permute-start(bf16[96,768]{1,0:T(8,128)(2,1)S(1)} %add_parts.2.a), channel_id=1, source_target_pairs={{0,8},{8,0},{16,24},{24,16},{1,9},{9,1},{17,25},{25,17},{2,10},{10... | collective-permute-start | bytes 442376 | tf_op jit(solution)/shard_map/ppermute | solution.py:796
  71.9 5.6 %collective-permute-start.26 = (bf16[64,768]{1,0:T(8,128)(2,1)S(1)}, bf16[64,768]{1,0:T(8,128)(2,1)S(1)}, u32[]{:S(2)}, u32[]{:S(2)}) collective-permute-start(bf16[64,768]{1,0:T(8,128)(2,1)S(1)} %get-tuple-element.171), channel_id=1, source_target_pairs={{0,2},{1,3},{2,0},{3,1},{4,6},{5,7},{6,4},{7,5},{8,10},{9,11},{10,... | collective-permute-start | bytes 294920 | tf_op jit(solution)/shard_map/ppermute | solution.py:796
  73.4 7.0 %collective-permute-start.27 = (bf16[64,768]{1,0:T(8,128)(2,1)S(1)}, bf16[64,768]{1,0:T(8,128)(2,1)S(1)}, u32[]{:S(2)}, u32[]{:S(2)}) collective-permute-start(bf16[64,768]{1,0:T(8,128)(2,1)S(1)} %get-tuple-element.172), channel_id=1, source_target_pairs={{0,4},{1,5},{2,6},{3,7},{4,0},{5,1},{6,2},{7,3},{8,12},{9,13},{10,... | collective-permute-start | bytes 294920 | tf_op jit(solution)/shard_map/ppermute | solution.py:796
  74.1 8.9 %collective-permute-start.28 = (bf16[64,768]{1,0:T(8,128)(2,1)S(1)}, bf16[64,768]{1,0:T(8,128)(2,1)S(1)}, u32[]{:S(2)}, u32[]{:S(2)}) collective-permute-start(bf16[64,768]{1,0:T(8,128)(2,1)S(1)} %get-tuple-element.173), channel_id=1, source_target_pairs={{0,6},{1,7},{2,4},{3,5},{4,2},{5,3},{6,0},{7,1},{8,14},{9,15},{10,... | collective-permute-start | bytes 294920 | tf_op jit(solution)/shard_map/ppermute | solution.py:796
  75.5 13.0 %collective-permute-start.30 = (bf16[256,384]{1,0:T(8,128)(2,1)S(1)}, bf16[256,384]{1,0:T(8,128)(2,1)S(1)}, u32[]{:S(2)}, u32[]{:S(2)}) collective-permute-start(bf16[256,384]{1,0:T(8,128)(2,1)S(1)} %get-tuple-element.176.refs_4_), channel_id=1, source_target_pairs={{0,2},{1,3},{2,0},{3,1},{4,6},{5,7},{6,4},{7,5},{8,10},{9,11},{10,... | collective-permute-start | bytes 589832 | tf_op jit(solution)/shard_map/ppermute | solution.py:796
  76.9 11.7 %collective-permute-start.31 = (bf16[256,384]{1,0:T(8,128)(2,1)S(1)}, bf16[256,384]{1,0:T(8,128)(2,1)S(1)}, u32[]{:S(2)}, u32[]{:S(2)}) collective-permute-start(bf16[256,384]{1,0:T(8,128)(2,1)S(1)} %get-tuple-element.176.refs_4_), channel_id=1, source_target_pairs={{0,4},{1,5},{2,6},{3,7},{4,0},{5,1},{6,2},{7,3},{8,12},{9,13},{10,... | collective-permute-start | bytes 589832 | tf_op jit(solution)/shard_map/ppermute | solution.py:796
  77.6 11.0 %collective-permute-start.32 = (bf16[256,384]{1,0:T(8,128)(2,1)S(1)}, bf16[256,384]{1,0:T(8,128)(2,1)S(1)}, u32[]{:S(2)}, u32[]{:S(2)}) collective-permute-start(bf16[256,384]{1,0:T(8,128)(2,1)S(1)} %get-tuple-element.176.refs_4_), channel_id=1, source_target_pairs={{0,6},{1,7},{2,4},{3,5},{4,2},{5,3},{6,0},{7,1},{8,14},{9,15},{10,... | collective-permute-start | bytes 589832 | tf_op jit(solution)/shard_map/ppermute | solution.py:796
  80.4 8.1 %collective-permute-start.35 = (bf16[96,768]{1,0:T(8,128)(2,1)S(1)}, bf16[96,768]{1,0:T(8,128)(2,1)S(1)}, u32[]{:S(2)}, u32[]{:S(2)}) collective-permute-start(bf16[96,768]{1,0:T(8,128)(2,1)S(1)} %add_pair.6.a), channel_id=1, source_target_pairs={{0,16},{8,24},{16,0},{24,8},{1,17},{9,25},{17,1},{25,9},{2,18},{10... | collective-permute-start | bytes 442376 | tf_op jit(solution)/shard_map/ppermute | solution.py:796
  83.0 5.4 %collective-permute-start.29 = (bf16[64,768]{1,0:T(8,128)(2,1)S(1)}, bf16[64,768]{1,0:T(8,128)(2,1)S(1)}, u32[]{:S(2)}, u32[]{:S(2)}) collective-permute-start(bf16[64,768]{1,0:T(8,128)(2,1)S(1)} %add_parts.3.a), channel_id=1, source_target_pairs={{0,8},{8,0},{16,24},{24,16},{1,9},{9,1},{17,25},{25,17},{2,10},{10... | collective-permute-start | bytes 294920 | tf_op jit(solution)/shard_map/ppermute | solution.py:796
  88.6 10.1 %collective-permute-start.38 = (bf16[96,768]{1,0:T(8,128)(2,1)S(1)}, bf16[96,768]{1,0:T(8,128)(2,1)S(1)}, u32[]{:S(2)}, u32[]{:S(2)}) collective-permute-start(bf16[96,768]{1,0:T(8,128)(2,1)S(1)} %add_pair.7.own), channel_id=1, source_target_pairs={{0,6},{1,7},{2,4},{3,5},{4,2},{5,3},{6,0},{7,1},{8,14},{9,15},{10,... | collective-permute-start | bytes 442376 | tf_op jit(solution)/shard_map/ppermute | solution.py:796
  89.7 9.0 %collective-permute-start.37 = (bf16[96,768]{1,0:T(8,128)(2,1)S(1)}, bf16[96,768]{1,0:T(8,128)(2,1)S(1)}, u32[]{:S(2)}, u32[]{:S(2)}) collective-permute-start(bf16[96,768]{1,0:T(8,128)(2,1)S(1)} %add_pair.7.own), channel_id=1, source_target_pairs={{0,4},{1,5},{2,6},{3,7},{4,0},{5,1},{6,2},{7,3},{8,12},{9,13},{10,... | collective-permute-start | bytes 442376 | tf_op jit(solution)/shard_map/ppermute | solution.py:796
  90.6 8.1 %collective-permute-start.36 = (bf16[96,768]{1,0:T(8,128)(2,1)S(1)}, bf16[96,768]{1,0:T(8,128)(2,1)S(1)}, u32[]{:S(2)}, u32[]{:S(2)}) collective-permute-start(bf16[96,768]{1,0:T(8,128)(2,1)S(1)} %add_pair.7.own), channel_id=1, source_target_pairs={{0,2},{1,3},{2,0},{3,1},{4,6},{5,7},{6,4},{7,5},{8,10},{9,11},{10,... | collective-permute-start | bytes 442376 | tf_op jit(solution)/shard_map/ppermute | solution.py:796
  92.1 6.6 %collective-permute-start.34 = (bf16[64,768]{1,0:T(8,128)(2,1)S(1)}, bf16[64,768]{1,0:T(8,128)(2,1)S(1)}, u32[]{:S(2)}, u32[]{:S(2)}) collective-permute-start(bf16[64,768]{1,0:T(8,128)(2,1)S(1)} %add_pair.4.a), channel_id=1, source_target_pairs={{0,16},{8,24},{16,0},{24,8},{1,17},{9,25},{17,1},{25,9},{2,18},{10... | collective-permute-start | bytes 294920 | tf_op jit(solution)/shard_map/ppermute | solution.py:796
  98.8 5.0 %collective-permute-start.39 = (bf16[384,768]{1,0:T(8,128)(2,1)S(1)}, bf16[384,768]{1,0:T(8,128)(2,1)S(1)}, u32[]{:S(2)}, u32[]{:S(2)}) collective-permute-start(bf16[384,768]{1,0:T(8,128)(2,1)S(1)} %order_parts.2.own), channel_id=1, source_target_pairs={{0,1},{1,0},{2,3},{3,2},{4,5},{5,4},{6,7},{7,6},{8,9},{9,8},{10,11... | collective-permute-start | bytes 1769480 | tf_op jit(solution)/shard_map/ppermute | solution.py:796
  98.9 7.1 %collective-permute-start.42 = (bf16[64,768]{1,0:T(8,128)(2,1)S(1)}, bf16[64,768]{1,0:T(8,128)(2,1)S(1)}, u32[]{:S(2)}, u32[]{:S(2)}) collective-permute-start(bf16[64,768]{1,0:T(8,128)(2,1)S(1)} %add_pair.5.own), channel_id=1, source_target_pairs={{0,6},{1,7},{2,4},{3,5},{4,2},{5,3},{6,0},{7,1},{8,14},{9,15},{10,... | collective-permute-start | bytes 294920 | tf_op jit(solution)/shard_map/ppermute | solution.py:796
  99.0 7.2 %collective-permute-start.41 = (bf16[64,768]{1,0:T(8,128)(2,1)S(1)}, bf16[64,768]{1,0:T(8,128)(2,1)S(1)}, u32[]{:S(2)}, u32[]{:S(2)}) collective-permute-start(bf16[64,768]{1,0:T(8,128)(2,1)S(1)} %add_pair.5.own), channel_id=1, source_target_pairs={{0,4},{1,5},{2,6},{3,7},{4,0},{5,1},{6,2},{7,3},{8,12},{9,13},{10,... | collective-permute-start | bytes 294920 | tf_op jit(solution)/shard_map/ppermute | solution.py:796
  99.9 6.3 %collective-permute-start.40 = (bf16[64,768]{1,0:T(8,128)(2,1)S(1)}, bf16[64,768]{1,0:T(8,128)(2,1)S(1)}, u32[]{:S(2)}, u32[]{:S(2)}) collective-permute-start(bf16[64,768]{1,0:T(8,128)(2,1)S(1)} %add_pair.5.own), channel_id=1, source_target_pairs={{0,2},{1,3},{2,0},{3,1},{4,6},{5,7},{6,4},{7,5},{8,10},{9,11},{10,... | collective-permute-start | bytes 294920 | tf_op jit(solution)/shard_map/ppermute | solution.py:796
  (16 other events, 74.0 us)

commit v6 on v5

--- a/solution.py
+++ b/solution.py
@@ -238,7 +238,7 @@
             )
 
         zero = jnp.zeros((CHUNKS, LANES), F32)
-        last = lax.fori_loop(0, steps, scan_body, (zero,) * state, unroll=8)
+        last = lax.fori_loop(0, steps, scan_body, (zero,) * state, unroll=True)
         for n in range(state):
             chunkf_o[lb, n * CHUNKS : (n + 1) * CHUNKS, :] = last[n]
     total = jnp.zeros((state, inner), F32)
@@ -297,7 +297,7 @@
             )
 
         zero = jnp.zeros((CHUNKS, LANES), F32)
-        last = lax.fori_loop(0, steps, scan_body, (zero,) * state, unroll=8)
+        last = lax.fori_loop(0, steps, scan_body, (zero,) * state, unroll=True)
         for n in range(state):
             chunkb_o[lb, n * CHUNKS : (n + 1) * CHUNKS, :] = last[n]
     total = jnp.zeros((state, inner), F32)
@@ -384,7 +384,7 @@
             mixed[r, ls] = out
             return tuple(new)
 
-        lax.fori_loop(0, steps, forward, tuple(begin), unroll=8)
+        lax.fori_loop(0, steps, forward, tuple(begin), unroll=True)
 
     second = jnp.bitwise_and(me, 1) == 1
 
@@ -489,7 +489,7 @@
                 return tuple(new_flows), tuple(new_sums)
 
             flows, sums_a = lax.fori_loop(
-                0, steps, backward, (tuple(begin), (zero,) * (pair * group)), unroll=8
+                0, steps, backward, (tuple(begin), (zero,) * (pair * group)), unroll=True
             )
             for q, n in enumerate(ns):
                 for x, ls in enumerate(lanes):

time: 110 us -> 109 us (level)
  transfers between devices with their start and end apart: 44 -> 44, of which waited for: 18 -> 19; matrix products, arithmetic and copies ran while one was open for 0% -> 0% of each run, Pallas kernels for 24% -> 23%
where the time goes in v6:
time: 109 us
  starting transfers between devices  40.2 us (37%)
  Pallas kernels  38.9 us (36%)
  waiting for transfers between devices  28.9 us (27%)
  between operations  1.16 us (1%)
    ppermute x43, starting transfers between devices, swap(): lax.ppermute(block, axis, [(i, i ^ distance) for i in range(devices)])  38.9 us
    pallas_call x24, Pallas kernels, run(): pl.pallas_call(kernel, out_shape=[jax.ShapeDtypeStruct(*part) if isinstan...  38.9 us
    ppermute x43, waiting for transfers between devices, swap(): lax.ppermute(block, axis, [(i, i ^ distance) for i in range(devices)])  28.9 us
  transfers between devices with their start and end apart: 44, of which 19 were waited for; matrix products, arithmetic and copies ran while one was open for 0% of the time, Pallas kernels for 23%

profile of v6, /device:TPU:0, one launch (start us, length us, event | category | flops | bytes accessed | tf_op | source)
XLA Modules:
  0.0 109.1 jit_solution(776414028705049161)
XLA Ops:
  1.7 4.0 %collective-permute-start.2 = (bf16[272,384]{1,0:T(8,128)(2,1)S(1)}, bf16[272,384]{1,0:T(8,128)(2,1)S(1)}, u32[]{:S(2)}, u32[]{:S(2)}) collective-permute-start(bf16[272,384]{1,0:T(8,128)(2,1)S(1)} %tokens_and_order.1.refs_0_), channel_id=1, source_target_pairs={{0,6},{1,7},{2,4},{3,5},{4,2},{5,3},{6,0},{7,1},{8,14},{9,15},{10,... | collective-permute-start | bytes 626696 | tf_op jit(solution)/shard_map/ppermute | solution.py:796
  6.3 5.4 %collective-permute-done.2.refs_3_ = bf16[272,384]{1,0:T(8,128)(2,1)S(1)} collective-permute-done((bf16[272,384]{1,0:T(8,128)(2,1)S(1)}, bf16[272,384]{1,0:T(8,128)(2,1)S(1)}, u32[]{:S(2)}, u32[]{:S(2)}) %collective-permute-start.2) | collective-permute-done | bytes 208928 | tf_op jit(solution)/shard_map/ppermute | solution.py:796
  11.7 3.6 %collective-permute-done.1.refs_2_ = bf16[272,384]{1,0:T(8,128)(2,1)S(1)} collective-permute-done((bf16[272,384]{1,0:T(8,128)(2,1)S(1)}, bf16[272,384]{1,0:T(8,128)(2,1)S(1)}, u32[]{:S(2)}, u32[]{:S(2)}) %collective-permute-start.1) | collective-permute-done | bytes 208928 | tf_op jit(solution)/shard_map/ppermute | solution.py:796
  15.8 1.8 %collective-permute-start.9 = (bf16[256,384]{1,0:T(8,128)(2,1)}, bf16[256,384]{1,0:T(8,128)(2,1)S(1)}, u32[]{:S(2)}, u32[]{:S(2)}) collective-permute-start(bf16[256,384]{1,0:T(8,128)(2,1)} %bitcast.11), channel_id=1, source_target_pairs={{0,6},{1,7},{2,4},{3,5},{4,2},{5,3},{6,0},{7,1},{8,14},{9,15},{10,... | collective-permute-start | bytes 589832 | tf_op jit(solution)/shard_map/ppermute | solution.py:796
  17.6 1.3 %collective-permute-start.8 = (bf16[256,384]{1,0:T(8,128)(2,1)}, bf16[256,384]{1,0:T(8,128)(2,1)S(1)}, u32[]{:S(2)}, u32[]{:S(2)}) collective-permute-start(bf16[256,384]{1,0:T(8,128)(2,1)} %bitcast.12), channel_id=1, source_target_pairs={{0,4},{1,5},{2,6},{3,7},{4,0},{5,1},{6,2},{7,3},{8,12},{9,13},{10,... | collective-permute-start | bytes 589832 | tf_op jit(solution)/shard_map/ppermute | solution.py:796
  19.3 7.5 %forward_local.1 = (bf16[256,384]{1,0:T(8,128)(2,1)S(1)}, bf16[256,384]{1,0:T(8,128)(2,1)S(1)}, f32[256,768]{1,0:T(8,128)S(1)}, f32[280,768]{1,0:T(8,128)S(1)}, ...) custom-call(s32[1]{0:T(128)} %bitcast.2.me.me_ref, ...), custom_call_target="tpu_custom_call" | custom-call | flops 1 | bytes 1 | tf_op jit(solution)/shard_map/forward_local/pallas_call | solution.py:773
  26.8 1.4 %collective-permute-done.8.four = bf16[256,384]{1,0:T(8,128)(2,1)S(1)} collective-permute-done((bf16[256,384]{1,0:T(8,128)(2,1)}, bf16[256,384]{1,0:T(8,128)(2,1)S(1)}, u32[]{:S(2)}, u32[]{:S(2)}) %collective-permute-start.8) | collective-permute-done | bytes 196640 | tf_op jit(solution)/shard_map/ppermute | solution.py:796
  30.2 5.0 %backward_local.1 = (bf16[256,384]{1,0:T(8,128)(2,1)S(1)}, f32[256,768]{1,0:T(8,128)S(1)}, f32[256,768]{1,0:T(8,128)S(1)}, f32[256,2048]{1,0:T(8,128)S(1)}, f32[...) custom-call(s32[1]{0:T(128)} %bitcast.2.me.me_ref, ...), custom_call_target="tpu_custom_call" | custom-call | flops 1 | bytes 1 | tf_op jit(solution)/shard_map/backward_local/pallas_call | solution.py:773
  35.3 1.5 %collective-permute-start.11 = (f32[16,896]{1,0:T(8,128)S(1)}, f32[16,896]{1,0:T(8,128)S(1)}, u32[]{:S(2)}, u32[]{:S(2)}) collective-permute-start(f32[16,896]{1,0:T(8,128)S(1)} %get-tuple-element.117), channel_id=1, source_target_pairs={{0,2},{1,3},{2,0},{3,1},{4,6},{5,7},{6,4},{7,5},{8,10},{9,11},{10,... | collective-permute-start | bytes 172040 | tf_op jit(solution)/shard_map/ppermute | solution.py:796
  37.4 1.4 %collective-permute-start.13 = (f32[16,896]{1,0:T(8,128)S(1)}, f32[16,896]{1,0:T(8,128)S(1)}, u32[]{:S(2)}, u32[]{:S(2)}) collective-permute-start(f32[16,896]{1,0:T(8,128)S(1)} %get-tuple-element.119), channel_id=1, source_target_pairs={{0,6},{1,7},{2,4},{3,5},{4,2},{5,3},{6,0},{7,1},{8,14},{9,15},{10,... | collective-permute-start | bytes 172040 | tf_op jit(solution)/shard_map/ppermute | solution.py:796
  39.5 2.1 %collective-permute-done.12.refs_1_ = f32[16,896]{1,0:T(8,128)S(1)} collective-permute-done((f32[16,896]{1,0:T(8,128)S(1)}, f32[16,896]{1,0:T(8,128)S(1)}, u32[]{:S(2)}, u32[]{:S(2)}) %collective-permute-start.12) | collective-permute-done | bytes 57376 | tf_op jit(solution)/shard_map/ppermute | solution.py:796
  43.8 4.0 %scan_forward.1 = (f32[16,264,128]{2,1,0:T(8,128)S(1)}, f32[16,264,128]{2,1,0:T(8,128)S(1)}, f32[16,264,128]{2,1,0:T(8,128)S(1)}, f32[16,264,128]{2,1,0:T(8,128)...) custom-call(s32[1]{0:T(128)} %bitcast.2.me.me_ref, ...), custom_call_target="tpu_custom_call" | custom-call | flops 1 | bytes 1 | tf_op jit(solution)/shard_map/scan_forward/pallas_call | solution.py:773
  50.0 1.4 %collective-permute-start.21 = (bf16[224,768]{1,0:T(8,128)(2,1)S(1)}, bf16[224,768]{1,0:T(8,128)(2,1)S(1)}, u32[]{:S(2)}, u32[]{:S(2)}) collective-permute-start(bf16[224,768]{1,0:T(8,128)(2,1)S(1)} %get-tuple-element.162), channel_id=1, source_target_pairs={{0,2},{1,3},{2,0},{3,1},{4,6},{5,7},{6,4},{7,5},{8,10},{9,11},{10,... | collective-permute-start | bytes 1032200 | tf_op jit(solution)/shard_map/ppermute | solution.py:796
  52.1 1.5 %collective-permute-start.23 = (bf16[224,768]{1,0:T(8,128)(2,1)S(1)}, bf16[224,768]{1,0:T(8,128)(2,1)S(1)}, u32[]{:S(2)}, u32[]{:S(2)}) collective-permute-start(bf16[224,768]{1,0:T(8,128)(2,1)S(1)} %get-tuple-element.164), channel_id=1, source_target_pairs={{0,6},{1,7},{2,4},{3,5},{4,2},{5,3},{6,0},{7,1},{8,14},{9,15},{10,... | collective-permute-start | bytes 1032200 | tf_op jit(solution)/shard_map/ppermute | solution.py:796
  53.6 9.7 %scan_backward.1 = (f32[256,768]{1,0:T(8,128)S(1)}, f32[8,768]{1,0:T(8,128)S(1)}, bf16[256,768]{1,0:T(8,128)(2,1)S(1)}, bf16[256,128]{1,0:T(8,128)(2,1)S(1)}, f32[16,768]{1,0:T(8,128)S(1)}) custom-call(f32[16,264,128]{2,1,0:T(8,128)S(1)} %get-tuple-element.137.refs_0_, f32[16,264,128]{2,1,0:T(8,128)S(1)} %get-tuple-element.138.refs_1_, ...), custom_call_target="tpu_custom_call" | custom-call | flops 1 | bytes 1 | tf_op jit(solution)/shard_map/scan_backward/pallas_call | solution.py:773
  63.3 1.3 %collective-permute-start.19 = (f32[8,768]{1,0:T(8,128)S(1)}, f32[8,768]{1,0:T(8,128)S(1)}, u32[]{:S(2)}, u32[]{:S(2)}) collective-permute-start(f32[8,768]{1,0:T(8,128)S(1)} %get-tuple-element.156), channel_id=1, source_target_pairs={{1,0},{2,1},{3,2},{4,3},{5,4},{6,5},{7,6},{9,8},{10,9},{11,10},{12... | collective-permute-start | bytes 73736 | tf_op jit(solution)/shard_map/ppermute | solution.py:814
  64.6 1.9 %small_grads.1 = (f32[104,768]{1,0:T(8,128)S(1)}, f32[256,768]{1,0:T(8,128)S(1)}) custom-call(bf16[256,768]{1,0:T(8,128)(2,1)S(1)} %get-tuple-element.150.gpre, bf16[256,128]{1,0:T(8,128)(2,1)S(1)} %get-tuple-element.151.gxproj, f32[256,128]{1,0:T(8,128)S(1)} %get-tuple-element.112.refs_4_.xproj, ...), custom_call_target="tpu_custom_call" | custom-call | flops 1 | bytes 1 | tf_op jit(solution)/shard_map/small_grads/pallas_call | solution.py:773
  66.6 2.1 %collective-permute-done.22.c.refs_2_ = bf16[224,768]{1,0:T(8,128)(2,1)S(1)} collective-permute-done((bf16[224,768]{1,0:T(8,128)(2,1)S(1)}, bf16[224,768]{1,0:T(8,128)(2,1)S(1)}, u32[]{:S(2)}, u32[]{:S(2)}) %collective-permute-start.22) | collective-permute-done | bytes 344096 | tf_op jit(solution)/shard_map/ppermute | solution.py:796
  69.8 1.6 %collective-permute-start.25 = (bf16[96,768]{1,0:T(8,128)(2,1)S(1)}, bf16[96,768]{1,0:T(8,128)(2,1)S(1)}, u32[]{:S(2)}, u32[]{:S(2)}) collective-permute-start(bf16[96,768]{1,0:T(8,128)(2,1)S(1)} %add_parts.2.a), channel_id=1, source_target_pairs={{0,8},{8,0},{16,24},{24,16},{1,9},{9,1},{17,25},{25,17},{2,10},{10... | collective-permute-start | bytes 442376 | tf_op jit(solution)/shard_map/ppermute | solution.py:796
  71.6 1.2 %collective-permute-start.26 = (bf16[64,768]{1,0:T(8,128)(2,1)S(1)}, bf16[64,768]{1,0:T(8,128)(2,1)S(1)}, u32[]{:S(2)}, u32[]{:S(2)}) collective-permute-start(bf16[64,768]{1,0:T(8,128)(2,1)S(1)} %get-tuple-element.171), channel_id=1, source_target_pairs={{0,2},{1,3},{2,0},{3,1},{4,6},{5,7},{6,4},{7,5},{8,10},{9,11},{10,... | collective-permute-start | bytes 294920 | tf_op jit(solution)/shard_map/ppermute | solution.py:796
  73.7 1.4 %collective-permute-start.28 = (bf16[64,768]{1,0:T(8,128)(2,1)S(1)}, bf16[64,768]{1,0:T(8,128)(2,1)S(1)}, u32[]{:S(2)}, u32[]{:S(2)}) collective-permute-start(bf16[64,768]{1,0:T(8,128)(2,1)S(1)} %get-tuple-element.173), channel_id=1, source_target_pairs={{0,6},{1,7},{2,4},{3,5},{4,2},{5,3},{6,0},{7,1},{8,14},{9,15},{10,... | collective-permute-start | bytes 294920 | tf_op jit(solution)/shard_map/ppermute | solution.py:796
  77.2 1.5 %collective-permute-start.32 = (bf16[256,384]{1,0:T(8,128)(2,1)S(1)}, bf16[256,384]{1,0:T(8,128)(2,1)S(1)}, u32[]{:S(2)}, u32[]{:S(2)}) collective-permute-start(bf16[256,384]{1,0:T(8,128)(2,1)S(1)} %get-tuple-element.176.refs_4_), channel_id=1, source_target_pairs={{0,6},{1,7},{2,4},{3,5},{4,2},{5,3},{6,0},{7,1},{8,14},{9,15},{10,... | collective-permute-start | bytes 589832 | tf_op jit(solution)/shard_map/ppermute | solution.py:796
  78.8 2.7 %collective-permute-start.35 = (bf16[96,768]{1,0:T(8,128)(2,1)S(1)}, bf16[96,768]{1,0:T(8,128)(2,1)S(1)}, u32[]{:S(2)}, u32[]{:S(2)}) collective-permute-start(bf16[96,768]{1,0:T(8,128)(2,1)S(1)} %add_pair.6.a), channel_id=1, source_target_pairs={{0,16},{8,24},{16,0},{24,8},{1,17},{9,25},{17,1},{25,9},{2,18},{10... | collective-permute-start | bytes 442376 | tf_op jit(solution)/shard_map/ppermute | solution.py:796
  81.5 1.6 %collective-permute-start.29 = (bf16[64,768]{1,0:T(8,128)(2,1)S(1)}, bf16[64,768]{1,0:T(8,128)(2,1)S(1)}, u32[]{:S(2)}, u32[]{:S(2)}) collective-permute-start(bf16[64,768]{1,0:T(8,128)(2,1)S(1)} %add_parts.3.a), channel_id=1, source_target_pairs={{0,8},{8,0},{16,24},{24,16},{1,9},{9,1},{17,25},{25,17},{2,10},{10... | collective-permute-start | bytes 294920 | tf_op jit(solution)/shard_map/ppermute | solution.py:796
  83.1 3.1 %collective-permute-done.29.b = bf16[64,768]{1,0:T(8,128)(2,1)S(1)} collective-permute-done((bf16[64,768]{1,0:T(8,128)(2,1)S(1)}, bf16[64,768]{1,0:T(8,128)(2,1)S(1)}, u32[]{:S(2)}, u32[]{:S(2)}) %collective-permute-start.29) | collective-permute-done | bytes 98336 | tf_op jit(solution)/shard_map/ppermute | solution.py:796
  87.9 1.3 %collective-permute-start.38 = (bf16[96,768]{1,0:T(8,128)(2,1)S(1)}, bf16[96,768]{1,0:T(8,128)(2,1)S(1)}, u32[]{:S(2)}, u32[]{:S(2)}) collective-permute-start(bf16[96,768]{1,0:T(8,128)(2,1)S(1)} %add_pair.7.own), channel_id=1, source_target_pairs={{0,6},{1,7},{2,4},{3,5},{4,2},{5,3},{6,0},{7,1},{8,14},{9,15},{10,... | collective-permute-start | bytes 442376 | tf_op jit(solution)/shard_map/ppermute | solution.py:796
  91.4 2.6 %collective-permute-start.34 = (bf16[64,768]{1,0:T(8,128)(2,1)S(1)}, bf16[64,768]{1,0:T(8,128)(2,1)S(1)}, u32[]{:S(2)}, u32[]{:S(2)}) collective-permute-start(bf16[64,768]{1,0:T(8,128)(2,1)S(1)} %add_pair.4.a), channel_id=1, source_target_pairs={{0,16},{8,24},{16,0},{24,8},{1,17},{9,25},{17,1},{25,9},{2,18},{10... | collective-permute-start | bytes 294920 | tf_op jit(solution)/shard_map/ppermute | solution.py:796
  94.0 2.9 %collective-permute-done.34.b = bf16[64,768]{1,0:T(8,128)(2,1)S(1)} collective-permute-done((bf16[64,768]{1,0:T(8,128)(2,1)S(1)}, bf16[64,768]{1,0:T(8,128)(2,1)S(1)}, u32[]{:S(2)}, u32[]{:S(2)}) %collective-permute-start.34) | collective-permute-done | bytes 98336 | tf_op jit(solution)/shard_map/ppermute | solution.py:796
  97.1 1.4 %collective-permute-start.42 = (bf16[64,768]{1,0:T(8,128)(2,1)S(1)}, bf16[64,768]{1,0:T(8,128)(2,1)S(1)}, u32[]{:S(2)}, u32[]{:S(2)}) collective-permute-start(bf16[64,768]{1,0:T(8,128)(2,1)S(1)} %add_pair.5.own), channel_id=1, source_target_pairs={{0,6},{1,7},{2,4},{3,5},{4,2},{5,3},{6,0},{7,1},{8,14},{9,15},{10,... | collective-permute-start | bytes 294920 | tf_op jit(solution)/shard_map/ppermute | solution.py:796
  100.7 1.3 %share_rows.1 = (bf16[256,384]{1,0:T(8,128)(2,1)S(1)}, bf16[256,384]{1,0:T(8,128)(2,1)S(1)}, bf16[256,768]{1,0:T(8,128)(2,1)S(1)}) custom-call(s32[1]{0:T(128)} %bitcast.2.me.me_ref, f32[4,256]{1,0:T(4,128)S(1)} %get-tuple-element.106.orders, bf16[256,384]{1,0:T(8,128)(2,1)S(1)} %get-tuple-element.174.rows.refs_0_, ...), custom_call_target="tpu_custom_call" | custom-call | flops 1 | bytes 1 | tf_op jit(solution)/shard_map/share_rows/pallas_call | solution.py:773
  102.0 2.2 %first_results.1 = (f32[768,384]{1,0:T(8,128)}, f32[384,1536]{1,0:T(8,128)}) custom-call(s32[1]{0:T(128)} %bitcast.2.me.me_ref, bf16[384,768]{1,0:T(8,128)(2,1)S(1)} %order_parts.2.own, bf16[384,768]{1,0:T(8,128)(2,1)S(1)} %collective-permute-done.39.other), custom_call_target="tpu_custom_call" | custom-call | flops 1 | bytes 1 | tf_op jit(solution)/shard_map/first_results/pallas_call | solution.py:773
  107.2 1.8 %last_results.1 = (f32[384]{0:T(512)}, f32[384,1536]{1,0:T(8,128)}, f32[4,768]{1,0:T(4,128)}, f32[768]{0:T(1024)}, f32[56,768]{1,0:T(8,128)}, /*index=5*/f32[24,...) custom-call(s32[1]{0:T(128)} %bitcast.2.me.me_ref, ...), custom_call_target="tpu_custom_call", output_to_operand_aliasing={{1}: (3, {})} | custom-call | flops 1 | bytes 1 | tf_op jit(solution)/shard_map/last_results/pallas_call | solution.py:773
  (88 shorter events, 24.5 us)
Async XLA Ops:
  1.7 10.0 %collective-permute-start.2 = (bf16[272,384]{1,0:T(8,128)(2,1)S(1)}, bf16[272,384]{1,0:T(8,128)(2,1)S(1)}, u32[]{:S(2)}, u32[]{:S(2)}) collective-permute-start(bf16[272,384]{1,0:T(8,128)(2,1)S(1)} %tokens_and_order.1.refs_0_), channel_id=1, source_target_pairs={{0,6},{1,7},{2,4},{3,5},{4,2},{5,3},{6,0},{7,1},{8,14},{9,15},{10,... | collective-permute-start | bytes 626696 | tf_op jit(solution)/shard_map/ppermute | solution.py:796
  5.6 9.6 %collective-permute-start.1 = (bf16[272,384]{1,0:T(8,128)(2,1)S(1)}, bf16[272,384]{1,0:T(8,128)(2,1)S(1)}, u32[]{:S(2)}, u32[]{:S(2)}) collective-permute-start(bf16[272,384]{1,0:T(8,128)(2,1)S(1)} %tokens_and_order.1.refs_0_), channel_id=1, source_target_pairs={{0,4},{1,5},{2,6},{3,7},{4,0},{5,1},{6,2},{7,3},{8,12},{9,13},{10,... | collective-permute-start | bytes 626696 | tf_op jit(solution)/shard_map/ppermute | solution.py:796
  6.1 9.4 %collective-permute-start = (bf16[272,384]{1,0:T(8,128)(2,1)S(1)}, bf16[272,384]{1,0:T(8,128)(2,1)S(1)}, u32[]{:S(2)}, u32[]{:S(2)}) collective-permute-start(bf16[272,384]{1,0:T(8,128)(2,1)S(1)} %tokens_and_order.1.refs_0_), channel_id=1, source_target_pairs={{0,2},{1,3},{2,0},{3,1},{4,6},{5,7},{6,4},{7,5},{8,10},{9,11},{10,... | collective-permute-start | bytes 626696 | tf_op jit(solution)/shard_map/ppermute | solution.py:796
  6.3 11.3 %collective-permute-start.3 = (bf16[272,384]{1,0:T(8,128)(2,1)S(1)}, bf16[272,384]{1,0:T(8,128)(2,1)S(1)}, u32[]{:S(2)}, u32[]{:S(2)}) collective-permute-start(bf16[272,384]{1,0:T(8,128)(2,1)S(1)} %tokens_and_order.1.refs_0_), channel_id=1, source_target_pairs={{0,1},{1,0},{2,3},{3,2},{4,5},{5,4},{6,7},{7,6},{8,9},{9,8},{10,11... | collective-permute-start | bytes 626696 | tf_op jit(solution)/shard_map/ppermute | solution.py:796
  11.7 7.3 %collective-permute-start.6 = (bf16[272,384]{1,0:T(8,128)(2,1)S(1)}, bf16[272,384]{1,0:T(8,128)(2,1)S(1)}, u32[]{:S(2)}, u32[]{:S(2)}) collective-permute-start(bf16[272,384]{1,0:T(8,128)(2,1)S(1)} %collective-permute-done.2.refs_3_), channel_id=1, source_target_pairs={{0,1},{1,0},{2,3},{3,2},{4,5},{5,4},{6,7},{7,6},{8,9},{9,8},{10,11... | collective-permute-start | bytes 626696 | tf_op jit(solution)/shard_map/ppermute | solution.py:796
  15.8 11.0 %collective-permute-start.9 = (bf16[256,384]{1,0:T(8,128)(2,1)}, bf16[256,384]{1,0:T(8,128)(2,1)S(1)}, u32[]{:S(2)}, u32[]{:S(2)}) collective-permute-start(bf16[256,384]{1,0:T(8,128)(2,1)} %bitcast.11), channel_id=1, source_target_pairs={{0,6},{1,7},{2,4},{3,5},{4,2},{5,3},{6,0},{7,1},{8,14},{9,15},{10,... | collective-permute-start | bytes 589832 | tf_op jit(solution)/shard_map/ppermute | solution.py:796
  17.6 10.6 %collective-permute-start.8 = (bf16[256,384]{1,0:T(8,128)(2,1)}, bf16[256,384]{1,0:T(8,128)(2,1)S(1)}, u32[]{:S(2)}, u32[]{:S(2)}) collective-permute-start(bf16[256,384]{1,0:T(8,128)(2,1)} %bitcast.12), channel_id=1, source_target_pairs={{0,4},{1,5},{2,6},{3,7},{4,0},{5,1},{6,2},{7,3},{8,12},{9,13},{10,... | collective-permute-start | bytes 589832 | tf_op jit(solution)/shard_map/ppermute | solution.py:796
  18.9 9.3 %collective-permute-start.7 = (bf16[256,384]{1,0:T(8,128)(2,1)}, bf16[256,384]{1,0:T(8,128)(2,1)S(1)}, u32[]{:S(2)}, u32[]{:S(2)}) collective-permute-start(bf16[256,384]{1,0:T(8,128)(2,1)} %bitcast.13), channel_id=1, source_target_pairs={{0,2},{1,3},{2,0},{3,1},{4,6},{5,7},{6,4},{7,5},{8,10},{9,11},{10,... | collective-permute-start | bytes 589832 | tf_op jit(solution)/shard_map/ppermute | solution.py:796
  35.1 7.4 %collective-permute-start.18 = (bf16[256,384]{1,0:T(8,128)(2,1)S(1)}, bf16[256,384]{1,0:T(8,128)(2,1)S(1)}, u32[]{:S(2)}, u32[]{:S(2)}) collective-permute-start(bf16[256,384]{1,0:T(8,128)(2,1)S(1)} %get-tuple-element.123), channel_id=1, source_target_pairs={{0,1},{1,0},{2,3},{3,2},{4,5},{5,4},{6,7},{7,6},{8,9},{9,8},{10,11... | collective-permute-start | bytes 589832 | tf_op jit(solution)/shard_map/ppermute | solution.py:796
  36.8 4.8 %collective-permute-start.12 = (f32[16,896]{1,0:T(8,128)S(1)}, f32[16,896]{1,0:T(8,128)S(1)}, u32[]{:S(2)}, u32[]{:S(2)}) collective-permute-start(f32[16,896]{1,0:T(8,128)S(1)} %get-tuple-element.118), channel_id=1, source_target_pairs={{0,4},{1,5},{2,6},{3,7},{4,0},{5,1},{6,2},{7,3},{8,12},{9,13},{10,... | collective-permute-start | bytes 172040 | tf_op jit(solution)/shard_map/ppermute | solution.py:796
  37.4 5.1 %collective-permute-start.13 = (f32[16,896]{1,0:T(8,128)S(1)}, f32[16,896]{1,0:T(8,128)S(1)}, u32[]{:S(2)}, u32[]{:S(2)}) collective-permute-start(f32[16,896]{1,0:T(8,128)S(1)} %get-tuple-element.119), channel_id=1, source_target_pairs={{0,6},{1,7},{2,4},{3,5},{4,2},{5,3},{6,0},{7,1},{8,14},{9,15},{10,... | collective-permute-start | bytes 172040 | tf_op jit(solution)/shard_map/ppermute | solution.py:796
  50.0 16.5 %collective-permute-start.21 = (bf16[224,768]{1,0:T(8,128)(2,1)S(1)}, bf16[224,768]{1,0:T(8,128)(2,1)S(1)}, u32[]{:S(2)}, u32[]{:S(2)}) collective-permute-start(bf16[224,768]{1,0:T(8,128)(2,1)S(1)} %get-tuple-element.162), channel_id=1, source_target_pairs={{0,2},{1,3},{2,0},{3,1},{4,6},{5,7},{6,4},{7,5},{8,10},{9,11},{10,... | collective-permute-start | bytes 1032200 | tf_op jit(solution)/shard_map/ppermute | solution.py:796
  51.5 17.2 %collective-permute-start.22 = (bf16[224,768]{1,0:T(8,128)(2,1)S(1)}, bf16[224,768]{1,0:T(8,128)(2,1)S(1)}, u32[]{:S(2)}, u32[]{:S(2)}) collective-permute-start(bf16[224,768]{1,0:T(8,128)(2,1)S(1)} %get-tuple-element.163), channel_id=1, source_target_pairs={{0,4},{1,5},{2,6},{3,7},{4,0},{5,1},{6,2},{7,3},{8,12},{9,13},{10,... | collective-permute-start | bytes 1032200 | tf_op jit(solution)/shard_map/ppermute | solution.py:796
  52.1 16.6 %collective-permute-start.23 = (bf16[224,768]{1,0:T(8,128)(2,1)S(1)}, bf16[224,768]{1,0:T(8,128)(2,1)S(1)}, u32[]{:S(2)}, u32[]{:S(2)}) collective-permute-start(bf16[224,768]{1,0:T(8,128)(2,1)S(1)} %get-tuple-element.164), channel_id=1, source_target_pairs={{0,6},{1,7},{2,4},{3,5},{4,2},{5,3},{6,0},{7,1},{8,14},{9,15},{10,... | collective-permute-start | bytes 1032200 | tf_op jit(solution)/shard_map/ppermute | solution.py:796
  63.3 5.5 %collective-permute-start.19 = (f32[8,768]{1,0:T(8,128)S(1)}, f32[8,768]{1,0:T(8,128)S(1)}, u32[]{:S(2)}, u32[]{:S(2)}) collective-permute-start(f32[8,768]{1,0:T(8,128)S(1)} %get-tuple-element.156), channel_id=1, source_target_pairs={{1,0},{2,1},{3,2},{4,3},{5,4},{6,5},{7,6},{9,8},{10,9},{11,10},{12... | collective-permute-start | bytes 73736 | tf_op jit(solution)/shard_map/ppermute | solution.py:814
  69.8 6.5 %collective-permute-start.25 = (bf16[96,768]{1,0:T(8,128)(2,1)S(1)}, bf16[96,768]{1,0:T(8,128)(2,1)S(1)}, u32[]{:S(2)}, u32[]{:S(2)}) collective-permute-start(bf16[96,768]{1,0:T(8,128)(2,1)S(1)} %add_parts.2.a), channel_id=1, source_target_pairs={{0,8},{8,0},{16,24},{24,16},{1,9},{9,1},{17,25},{25,17},{2,10},{10... | collective-permute-start | bytes 442376 | tf_op jit(solution)/shard_map/ppermute | solution.py:796
  71.6 5.6 %collective-permute-start.26 = (bf16[64,768]{1,0:T(8,128)(2,1)S(1)}, bf16[64,768]{1,0:T(8,128)(2,1)S(1)}, u32[]{:S(2)}, u32[]{:S(2)}) collective-permute-start(bf16[64,768]{1,0:T(8,128)(2,1)S(1)} %get-tuple-element.171), channel_id=1, source_target_pairs={{0,2},{1,3},{2,0},{3,1},{4,6},{5,7},{6,4},{7,5},{8,10},{9,11},{10,... | collective-permute-start | bytes 294920 | tf_op jit(solution)/shard_map/ppermute | solution.py:796
  72.8 6.0 %collective-permute-start.27 = (bf16[64,768]{1,0:T(8,128)(2,1)S(1)}, bf16[64,768]{1,0:T(8,128)(2,1)S(1)}, u32[]{:S(2)}, u32[]{:S(2)}) collective-permute-start(bf16[64,768]{1,0:T(8,128)(2,1)S(1)} %get-tuple-element.172), channel_id=1, source_target_pairs={{0,4},{1,5},{2,6},{3,7},{4,0},{5,1},{6,2},{7,3},{8,12},{9,13},{10,... | collective-permute-start | bytes 294920 | tf_op jit(solution)/shard_map/ppermute | solution.py:796
  73.7 7.7 %collective-permute-start.28 = (bf16[64,768]{1,0:T(8,128)(2,1)S(1)}, bf16[64,768]{1,0:T(8,128)(2,1)S(1)}, u32[]{:S(2)}, u32[]{:S(2)}) collective-permute-start(bf16[64,768]{1,0:T(8,128)(2,1)S(1)} %get-tuple-element.173), channel_id=1, source_target_pairs={{0,6},{1,7},{2,4},{3,5},{4,2},{5,3},{6,0},{7,1},{8,14},{9,15},{10,... | collective-permute-start | bytes 294920 | tf_op jit(solution)/shard_map/ppermute | solution.py:796
  75.1 12.0 %collective-permute-start.30 = (bf16[256,384]{1,0:T(8,128)(2,1)S(1)}, bf16[256,384]{1,0:T(8,128)(2,1)S(1)}, u32[]{:S(2)}, u32[]{:S(2)}) collective-permute-start(bf16[256,384]{1,0:T(8,128)(2,1)S(1)} %get-tuple-element.176.refs_4_), channel_id=1, source_target_pairs={{0,2},{1,3},{2,0},{3,1},{4,6},{5,7},{6,4},{7,5},{8,10},{9,11},{10,... | collective-permute-start | bytes 589832 | tf_op jit(solution)/shard_map/ppermute | solution.py:796
  76.2 11.7 %collective-permute-start.31 = (bf16[256,384]{1,0:T(8,128)(2,1)S(1)}, bf16[256,384]{1,0:T(8,128)(2,1)S(1)}, u32[]{:S(2)}, u32[]{:S(2)}) collective-permute-start(bf16[256,384]{1,0:T(8,128)(2,1)S(1)} %get-tuple-element.176.refs_4_), channel_id=1, source_target_pairs={{0,4},{1,5},{2,6},{3,7},{4,0},{5,1},{6,2},{7,3},{8,12},{9,13},{10,... | collective-permute-start | bytes 589832 | tf_op jit(solution)/shard_map/ppermute | solution.py:796
  77.2 10.7 %collective-permute-start.32 = (bf16[256,384]{1,0:T(8,128)(2,1)S(1)}, bf16[256,384]{1,0:T(8,128)(2,1)S(1)}, u32[]{:S(2)}, u32[]{:S(2)}) collective-permute-start(bf16[256,384]{1,0:T(8,128)(2,1)S(1)} %get-tuple-element.176.refs_4_), channel_id=1, source_target_pairs={{0,6},{1,7},{2,4},{3,5},{4,2},{5,3},{6,0},{7,1},{8,14},{9,15},{10,... | collective-permute-start | bytes 589832 | tf_op jit(solution)/shard_map/ppermute | solution.py:796
  78.8 8.4 %collective-permute-start.35 = (bf16[96,768]{1,0:T(8,128)(2,1)S(1)}, bf16[96,768]{1,0:T(8,128)(2,1)S(1)}, u32[]{:S(2)}, u32[]{:S(2)}) collective-permute-start(bf16[96,768]{1,0:T(8,128)(2,1)S(1)} %add_pair.6.a), channel_id=1, source_target_pairs={{0,16},{8,24},{16,0},{24,8},{1,17},{9,25},{17,1},{25,9},{2,18},{10... | collective-permute-start | bytes 442376 | tf_op jit(solution)/shard_map/ppermute | solution.py:796
  81.5 4.7 %collective-permute-start.29 = (bf16[64,768]{1,0:T(8,128)(2,1)S(1)}, bf16[64,768]{1,0:T(8,128)(2,1)S(1)}, u32[]{:S(2)}, u32[]{:S(2)}) collective-permute-start(bf16[64,768]{1,0:T(8,128)(2,1)S(1)} %add_parts.3.a), channel_id=1, source_target_pairs={{0,8},{8,0},{16,24},{24,16},{1,9},{9,1},{17,25},{25,17},{2,10},{10... | collective-permute-start | bytes 294920 | tf_op jit(solution)/shard_map/ppermute | solution.py:796
  87.9 9.1 %collective-permute-start.38 = (bf16[96,768]{1,0:T(8,128)(2,1)S(1)}, bf16[96,768]{1,0:T(8,128)(2,1)S(1)}, u32[]{:S(2)}, u32[]{:S(2)}) collective-permute-start(bf16[96,768]{1,0:T(8,128)(2,1)S(1)} %add_pair.7.own), channel_id=1, source_target_pairs={{0,6},{1,7},{2,4},{3,5},{4,2},{5,3},{6,0},{7,1},{8,14},{9,15},{10,... | collective-permute-start | bytes 442376 | tf_op jit(solution)/shard_map/ppermute | solution.py:796
  89.2 7.7 %collective-permute-start.37 = (bf16[96,768]{1,0:T(8,128)(2,1)S(1)}, bf16[96,768]{1,0:T(8,128)(2,1)S(1)}, u32[]{:S(2)}, u32[]{:S(2)}) collective-permute-start(bf16[96,768]{1,0:T(8,128)(2,1)S(1)} %add_pair.7.own), channel_id=1, source_target_pairs={{0,4},{1,5},{2,6},{3,7},{4,0},{5,1},{6,2},{7,3},{8,12},{9,13},{10,... | collective-permute-start | bytes 442376 | tf_op jit(solution)/shard_map/ppermute | solution.py:796
  90.3 6.7 %collective-permute-start.36 = (bf16[96,768]{1,0:T(8,128)(2,1)S(1)}, bf16[96,768]{1,0:T(8,128)(2,1)S(1)}, u32[]{:S(2)}, u32[]{:S(2)}) collective-permute-start(bf16[96,768]{1,0:T(8,128)(2,1)S(1)} %add_pair.7.own), channel_id=1, source_target_pairs={{0,2},{1,3},{2,0},{3,1},{4,6},{5,7},{6,4},{7,5},{8,10},{9,11},{10,... | collective-permute-start | bytes 442376 | tf_op jit(solution)/shard_map/ppermute | solution.py:796
  91.4 5.5 %collective-permute-start.34 = (bf16[64,768]{1,0:T(8,128)(2,1)S(1)}, bf16[64,768]{1,0:T(8,128)(2,1)S(1)}, u32[]{:S(2)}, u32[]{:S(2)}) collective-permute-start(bf16[64,768]{1,0:T(8,128)(2,1)S(1)} %add_pair.4.a), channel_id=1, source_target_pairs={{0,16},{8,24},{16,0},{24,8},{1,17},{9,25},{17,1},{25,9},{2,18},{10... | collective-permute-start | bytes 294920 | tf_op jit(solution)/shard_map/ppermute | solution.py:796
  97.1 5.0 %collective-permute-start.39 = (bf16[384,768]{1,0:T(8,128)(2,1)S(1)}, bf16[384,768]{1,0:T(8,128)(2,1)S(1)}, u32[]{:S(2)}, u32[]{:S(2)}) collective-permute-start(bf16[384,768]{1,0:T(8,128)(2,1)S(1)} %order_parts.2.own), channel_id=1, source_target_pairs={{0,1},{1,0},{2,3},{3,2},{4,5},{5,4},{6,7},{7,6},{8,9},{9,8},{10,11... | collective-permute-start | bytes 1769480 | tf_op jit(solution)/shard_map/ppermute | solution.py:796
  97.1 7.1 %collective-permute-start.42 = (bf16[64,768]{1,0:T(8,128)(2,1)S(1)}, bf16[64,768]{1,0:T(8,128)(2,1)S(1)}, u32[]{:S(2)}, u32[]{:S(2)}) collective-permute-start(bf16[64,768]{1,0:T(8,128)(2,1)S(1)} %add_pair.5.own), channel_id=1, source_target_pairs={{0,6},{1,7},{2,4},{3,5},{4,2},{5,3},{6,0},{7,1},{8,14},{9,15},{10,... | collective-permute-start | bytes 294920 | tf_op jit(solution)/shard_map/ppermute | solution.py:796
  98.5 6.8 %collective-permute-start.41 = (bf16[64,768]{1,0:T(8,128)(2,1)S(1)}, bf16[64,768]{1,0:T(8,128)(2,1)S(1)}, u32[]{:S(2)}, u32[]{:S(2)}) collective-permute-start(bf16[64,768]{1,0:T(8,128)(2,1)S(1)} %add_pair.5.own), channel_id=1, source_target_pairs={{0,4},{1,5},{2,6},{3,7},{4,0},{5,1},{6,2},{7,3},{8,12},{9,13},{10,... | collective-permute-start | bytes 294920 | tf_op jit(solution)/shard_map/ppermute | solution.py:796
  99.6 5.8 %collective-permute-start.40 = (bf16[64,768]{1,0:T(8,128)(2,1)S(1)}, bf16[64,768]{1,0:T(8,128)(2,1)S(1)}, u32[]{:S(2)}, u32[]{:S(2)}) collective-permute-start(bf16[64,768]{1,0:T(8,128)(2,1)S(1)} %add_pair.5.own), channel_id=1, source_target_pairs={{0,2},{1,3},{2,0},{3,1},{4,6},{5,7},{6,4},{7,5},{8,10},{9,11},{10,... | collective-permute-start | bytes 294920 | tf_op jit(solution)/shard_map/ppermute | solution.py:796
  (16 other events, 75.9 us)

commit v7 on v6

--- a/solution.py
+++ b/solution.py
@@ -951,7 +951,8 @@
             "first_halves",
             12,
         )(me, part, factor, got, branch)
-        away_one = [swap(block, "seq", d) for block, d in zip(sent, SENT)]
+        six, four, two = [swap(sent[k], "seq", SENT[k]) for k in (2, 1, 0)]
+        away_one = [two, four, six]
     gconv, rim, gpre, gxproj, galog = call(
         functools.partial(scan_backward_kernel, sizes),
         [(big, F32), ((CHUNKS, inner), F32), (big, BF16), (lane, BF16), ((state, inner), F32)],

time: 109 us -> 109 us (level)
  no operation moved by 1% of the time
where the time goes in v7:
time: 109 us
  starting transfers between devices  40.2 us (37%)
  Pallas kernels  38.9 us (36%)
  waiting for transfers between devices  28.9 us (27%)
  between operations  1.16 us (1%)
    ppermute x43, starting transfers between devices, swap(): lax.ppermute(block, axis, [(i, i ^ distance) for i in range(devices)])  38.9 us
    pallas_call x24, Pallas kernels, run(): pl.pallas_call(kernel, out_shape=[jax.ShapeDtypeStruct(*part) if isinstan...  38.9 us
    ppermute x43, waiting for transfers between devices, swap(): lax.ppermute(block, axis, [(i, i ^ distance) for i in range(devices)])  28.9 us
  transfers between devices with their start and end apart: 44, of which 19 were waited for; matrix products, arithmetic and copies ran while one was open for 0% of the time, Pallas kernels for 23%

profile of v7, /device:TPU:0, one launch (start us, length us, event | category | flops | bytes accessed | tf_op | source)
XLA Modules:
  0.0 109.1 jit_solution(776414028705049161)
XLA Ops:
  1.7 4.0 %collective-permute-start.2 = (bf16[272,384]{1,0:T(8,128)(2,1)S(1)}, bf16[272,384]{1,0:T(8,128)(2,1)S(1)}, u32[]{:S(2)}, u32[]{:S(2)}) collective-permute-start(bf16[272,384]{1,0:T(8,128)(2,1)S(1)} %tokens_and_order.1.refs_0_), channel_id=1, source_target_pairs={{0,6},{1,7},{2,4},{3,5},{4,2},{5,3},{6,0},{7,1},{8,14},{9,15},{10,... | collective-permute-start | bytes 626696 | tf_op jit(solution)/shard_map/ppermute | solution.py:796
  6.3 5.4 %collective-permute-done.2.refs_3_ = bf16[272,384]{1,0:T(8,128)(2,1)S(1)} collective-permute-done((bf16[272,384]{1,0:T(8,128)(2,1)S(1)}, bf16[272,384]{1,0:T(8,128)(2,1)S(1)}, u32[]{:S(2)}, u32[]{:S(2)}) %collective-permute-start.2) | collective-permute-done | bytes 208928 | tf_op jit(solution)/shard_map/ppermute | solution.py:796
  11.7 3.6 %collective-permute-done.1.refs_2_ = bf16[272,384]{1,0:T(8,128)(2,1)S(1)} collective-permute-done((bf16[272,384]{1,0:T(8,128)(2,1)S(1)}, bf16[272,384]{1,0:T(8,128)(2,1)S(1)}, u32[]{:S(2)}, u32[]{:S(2)}) %collective-permute-start.1) | collective-permute-done | bytes 208928 | tf_op jit(solution)/shard_map/ppermute | solution.py:796
  15.8 1.8 %collective-permute-start.9 = (bf16[256,384]{1,0:T(8,128)(2,1)}, bf16[256,384]{1,0:T(8,128)(2,1)S(1)}, u32[]{:S(2)}, u32[]{:S(2)}) collective-permute-start(bf16[256,384]{1,0:T(8,128)(2,1)} %bitcast.11), channel_id=1, source_target_pairs={{0,6},{1,7},{2,4},{3,5},{4,2},{5,3},{6,0},{7,1},{8,14},{9,15},{10,... | collective-permute-start | bytes 589832 | tf_op jit(solution)/shard_map/ppermute | solution.py:796
  17.6 1.3 %collective-permute-start.8 = (bf16[256,384]{1,0:T(8,128)(2,1)}, bf16[256,384]{1,0:T(8,128)(2,1)S(1)}, u32[]{:S(2)}, u32[]{:S(2)}) collective-permute-start(bf16[256,384]{1,0:T(8,128)(2,1)} %bitcast.12), channel_id=1, source_target_pairs={{0,4},{1,5},{2,6},{3,7},{4,0},{5,1},{6,2},{7,3},{8,12},{9,13},{10,... | collective-permute-start | bytes 589832 | tf_op jit(solution)/shard_map/ppermute | solution.py:796
  19.3 7.5 %forward_local.1 = (bf16[256,384]{1,0:T(8,128)(2,1)S(1)}, bf16[256,384]{1,0:T(8,128)(2,1)S(1)}, f32[256,768]{1,0:T(8,128)S(1)}, f32[280,768]{1,0:T(8,128)S(1)}, ...) custom-call(s32[1]{0:T(128)} %bitcast.2.me.me_ref, ...), custom_call_target="tpu_custom_call" | custom-call | flops 1 | bytes 1 | tf_op jit(solution)/shard_map/forward_local/pallas_call | solution.py:773
  26.8 1.4 %collective-permute-done.8.four = bf16[256,384]{1,0:T(8,128)(2,1)S(1)} collective-permute-done((bf16[256,384]{1,0:T(8,128)(2,1)}, bf16[256,384]{1,0:T(8,128)(2,1)S(1)}, u32[]{:S(2)}, u32[]{:S(2)}) %collective-permute-start.8) | collective-permute-done | bytes 196640 | tf_op jit(solution)/shard_map/ppermute | solution.py:796
  30.2 5.0 %backward_local.1 = (bf16[256,384]{1,0:T(8,128)(2,1)S(1)}, f32[256,768]{1,0:T(8,128)S(1)}, f32[256,768]{1,0:T(8,128)S(1)}, f32[256,2048]{1,0:T(8,128)S(1)}, f32[...) custom-call(s32[1]{0:T(128)} %bitcast.2.me.me_ref, ...), custom_call_target="tpu_custom_call" | custom-call | flops 1 | bytes 1 | tf_op jit(solution)/shard_map/backward_local/pallas_call | solution.py:773
  35.3 1.5 %collective-permute-start.11 = (f32[16,896]{1,0:T(8,128)S(1)}, f32[16,896]{1,0:T(8,128)S(1)}, u32[]{:S(2)}, u32[]{:S(2)}) collective-permute-start(f32[16,896]{1,0:T(8,128)S(1)} %get-tuple-element.117), channel_id=1, source_target_pairs={{0,2},{1,3},{2,0},{3,1},{4,6},{5,7},{6,4},{7,5},{8,10},{9,11},{10,... | collective-permute-start | bytes 172040 | tf_op jit(solution)/shard_map/ppermute | solution.py:796
  37.4 1.4 %collective-permute-start.13 = (f32[16,896]{1,0:T(8,128)S(1)}, f32[16,896]{1,0:T(8,128)S(1)}, u32[]{:S(2)}, u32[]{:S(2)}) collective-permute-start(f32[16,896]{1,0:T(8,128)S(1)} %get-tuple-element.119), channel_id=1, source_target_pairs={{0,6},{1,7},{2,4},{3,5},{4,2},{5,3},{6,0},{7,1},{8,14},{9,15},{10,... | collective-permute-start | bytes 172040 | tf_op jit(solution)/shard_map/ppermute | solution.py:796
  39.5 2.1 %collective-permute-done.12.refs_1_ = f32[16,896]{1,0:T(8,128)S(1)} collective-permute-done((f32[16,896]{1,0:T(8,128)S(1)}, f32[16,896]{1,0:T(8,128)S(1)}, u32[]{:S(2)}, u32[]{:S(2)}) %collective-permute-start.12) | collective-permute-done | bytes 57376 | tf_op jit(solution)/shard_map/ppermute | solution.py:796
  43.8 4.0 %scan_forward.1 = (f32[16,264,128]{2,1,0:T(8,128)S(1)}, f32[16,264,128]{2,1,0:T(8,128)S(1)}, f32[16,264,128]{2,1,0:T(8,128)S(1)}, f32[16,264,128]{2,1,0:T(8,128)...) custom-call(s32[1]{0:T(128)} %bitcast.2.me.me_ref, ...), custom_call_target="tpu_custom_call" | custom-call | flops 1 | bytes 1 | tf_op jit(solution)/shard_map/scan_forward/pallas_call | solution.py:773
  50.0 1.4 %collective-permute-start.21 = (bf16[224,768]{1,0:T(8,128)(2,1)S(1)}, bf16[224,768]{1,0:T(8,128)(2,1)S(1)}, u32[]{:S(2)}, u32[]{:S(2)}) collective-permute-start(bf16[224,768]{1,0:T(8,128)(2,1)S(1)} %get-tuple-element.162), channel_id=1, source_target_pairs={{0,2},{1,3},{2,0},{3,1},{4,6},{5,7},{6,4},{7,5},{8,10},{9,11},{10,... | collective-permute-start | bytes 1032200 | tf_op jit(solution)/shard_map/ppermute | solution.py:796
  52.1 1.5 %collective-permute-start.23 = (bf16[224,768]{1,0:T(8,128)(2,1)S(1)}, bf16[224,768]{1,0:T(8,128)(2,1)S(1)}, u32[]{:S(2)}, u32[]{:S(2)}) collective-permute-start(bf16[224,768]{1,0:T(8,128)(2,1)S(1)} %get-tuple-element.164), channel_id=1, source_target_pairs={{0,6},{1,7},{2,4},{3,5},{4,2},{5,3},{6,0},{7,1},{8,14},{9,15},{10,... | collective-permute-start | bytes 1032200 | tf_op jit(solution)/shard_map/ppermute | solution.py:796
  53.6 9.7 %scan_backward.1 = (f32[256,768]{1,0:T(8,128)S(1)}, f32[8,768]{1,0:T(8,128)S(1)}, bf16[256,768]{1,0:T(8,128)(2,1)S(1)}, bf16[256,128]{1,0:T(8,128)(2,1)S(1)}, f32[16,768]{1,0:T(8,128)S(1)}) custom-call(f32[16,264,128]{2,1,0:T(8,128)S(1)} %get-tuple-element.137.refs_0_, f32[16,264,128]{2,1,0:T(8,128)S(1)} %get-tuple-element.138.refs_1_, ...), custom_call_target="tpu_custom_call" | custom-call | flops 1 | bytes 1 | tf_op jit(solution)/shard_map/scan_backward/pallas_call | solution.py:773
  63.3 1.3 %collective-permute-start.19 = (f32[8,768]{1,0:T(8,128)S(1)}, f32[8,768]{1,0:T(8,128)S(1)}, u32[]{:S(2)}, u32[]{:S(2)}) collective-permute-start(f32[8,768]{1,0:T(8,128)S(1)} %get-tuple-element.156), channel_id=1, source_target_pairs={{1,0},{2,1},{3,2},{4,3},{5,4},{6,5},{7,6},{9,8},{10,9},{11,10},{12... | collective-permute-start | bytes 73736 | tf_op jit(solution)/shard_map/ppermute | solution.py:814
  64.6 1.9 %small_grads.1 = (f32[104,768]{1,0:T(8,128)S(1)}, f32[256,768]{1,0:T(8,128)S(1)}) custom-call(bf16[256,768]{1,0:T(8,128)(2,1)S(1)} %get-tuple-element.150.gpre, bf16[256,128]{1,0:T(8,128)(2,1)S(1)} %get-tuple-element.151.gxproj, f32[256,128]{1,0:T(8,128)S(1)} %get-tuple-element.112.refs_4_.xproj, ...), custom_call_target="tpu_custom_call" | custom-call | flops 1 | bytes 1 | tf_op jit(solution)/shard_map/small_grads/pallas_call | solution.py:773
  66.6 2.1 %collective-permute-done.22.c.refs_2_ = bf16[224,768]{1,0:T(8,128)(2,1)S(1)} collective-permute-done((bf16[224,768]{1,0:T(8,128)(2,1)S(1)}, bf16[224,768]{1,0:T(8,128)(2,1)S(1)}, u32[]{:S(2)}, u32[]{:S(2)}) %collective-permute-start.22) | collective-permute-done | bytes 344096 | tf_op jit(solution)/shard_map/ppermute | solution.py:796
  69.8 1.6 %collective-permute-start.25 = (bf16[96,768]{1,0:T(8,128)(2,1)S(1)}, bf16[96,768]{1,0:T(8,128)(2,1)S(1)}, u32[]{:S(2)}, u32[]{:S(2)}) collective-permute-start(bf16[96,768]{1,0:T(8,128)(2,1)S(1)} %add_parts.2.a), channel_id=1, source_target_pairs={{0,8},{8,0},{16,24},{24,16},{1,9},{9,1},{17,25},{25,17},{2,10},{10... | collective-permute-start | bytes 442376 | tf_op jit(solution)/shard_map/ppermute | solution.py:796
  71.6 1.2 %collective-permute-start.26 = (bf16[64,768]{1,0:T(8,128)(2,1)S(1)}, bf16[64,768]{1,0:T(8,128)(2,1)S(1)}, u32[]{:S(2)}, u32[]{:S(2)}) collective-permute-start(bf16[64,768]{1,0:T(8,128)(2,1)S(1)} %get-tuple-element.171), channel_id=1, source_target_pairs={{0,2},{1,3},{2,0},{3,1},{4,6},{5,7},{6,4},{7,5},{8,10},{9,11},{10,... | collective-permute-start | bytes 294920 | tf_op jit(solution)/shard_map/ppermute | solution.py:796
  73.7 1.4 %collective-permute-start.28 = (bf16[64,768]{1,0:T(8,128)(2,1)S(1)}, bf16[64,768]{1,0:T(8,128)(2,1)S(1)}, u32[]{:S(2)}, u32[]{:S(2)}) collective-permute-start(bf16[64,768]{1,0:T(8,128)(2,1)S(1)} %get-tuple-element.173), channel_id=1, source_target_pairs={{0,6},{1,7},{2,4},{3,5},{4,2},{5,3},{6,0},{7,1},{8,14},{9,15},{10,... | collective-permute-start | bytes 294920 | tf_op jit(solution)/shard_map/ppermute | solution.py:796
  77.2 1.5 %collective-permute-start.32 = (bf16[256,384]{1,0:T(8,128)(2,1)S(1)}, bf16[256,384]{1,0:T(8,128)(2,1)S(1)}, u32[]{:S(2)}, u32[]{:S(2)}) collective-permute-start(bf16[256,384]{1,0:T(8,128)(2,1)S(1)} %get-tuple-element.176.refs_4_), channel_id=1, source_target_pairs={{0,6},{1,7},{2,4},{3,5},{4,2},{5,3},{6,0},{7,1},{8,14},{9,15},{10,... | collective-permute-start | bytes 589832 | tf_op jit(solution)/shard_map/ppermute | solution.py:796
  78.8 2.7 %collective-permute-start.35 = (bf16[96,768]{1,0:T(8,128)(2,1)S(1)}, bf16[96,768]{1,0:T(8,128)(2,1)S(1)}, u32[]{:S(2)}, u32[]{:S(2)}) collective-permute-start(bf16[96,768]{1,0:T(8,128)(2,1)S(1)} %add_pair.6.a), channel_id=1, source_target_pairs={{0,16},{8,24},{16,0},{24,8},{1,17},{9,25},{17,1},{25,9},{2,18},{10... | collective-permute-start | bytes 442376 | tf_op jit(solution)/shard_map/ppermute | solution.py:796
  81.5 1.6 %collective-permute-start.29 = (bf16[64,768]{1,0:T(8,128)(2,1)S(1)}, bf16[64,768]{1,0:T(8,128)(2,1)S(1)}, u32[]{:S(2)}, u32[]{:S(2)}) collective-permute-start(bf16[64,768]{1,0:T(8,128)(2,1)S(1)} %add_parts.3.a), channel_id=1, source_target_pairs={{0,8},{8,0},{16,24},{24,16},{1,9},{9,1},{17,25},{25,17},{2,10},{10... | collective-permute-start | bytes 294920 | tf_op jit(solution)/shard_map/ppermute | solution.py:796
  83.1 3.1 %collective-permute-done.29.b = bf16[64,768]{1,0:T(8,128)(2,1)S(1)} collective-permute-done((bf16[64,768]{1,0:T(8,128)(2,1)S(1)}, bf16[64,768]{1,0:T(8,128)(2,1)S(1)}, u32[]{:S(2)}, u32[]{:S(2)}) %collective-permute-start.29) | collective-permute-done | bytes 98336 | tf_op jit(solution)/shard_map/ppermute | solution.py:796
  87.9 1.3 %collective-permute-start.38 = (bf16[96,768]{1,0:T(8,128)(2,1)S(1)}, bf16[96,768]{1,0:T(8,128)(2,1)S(1)}, u32[]{:S(2)}, u32[]{:S(2)}) collective-permute-start(bf16[96,768]{1,0:T(8,128)(2,1)S(1)} %add_pair.7.own), channel_id=1, source_target_pairs={{0,6},{1,7},{2,4},{3,5},{4,2},{5,3},{6,0},{7,1},{8,14},{9,15},{10,... | collective-permute-start | bytes 442376 | tf_op jit(solution)/shard_map/ppermute | solution.py:796
  91.4 2.6 %collective-permute-start.34 = (bf16[64,768]{1,0:T(8,128)(2,1)S(1)}, bf16[64,768]{1,0:T(8,128)(2,1)S(1)}, u32[]{:S(2)}, u32[]{:S(2)}) collective-permute-start(bf16[64,768]{1,0:T(8,128)(2,1)S(1)} %add_pair.4.a), channel_id=1, source_target_pairs={{0,16},{8,24},{16,0},{24,8},{1,17},{9,25},{17,1},{25,9},{2,18},{10... | collective-permute-start | bytes 294920 | tf_op jit(solution)/shard_map/ppermute | solution.py:796
  94.0 2.9 %collective-permute-done.34.b = bf16[64,768]{1,0:T(8,128)(2,1)S(1)} collective-permute-done((bf16[64,768]{1,0:T(8,128)(2,1)S(1)}, bf16[64,768]{1,0:T(8,128)(2,1)S(1)}, u32[]{:S(2)}, u32[]{:S(2)}) %collective-permute-start.34) | collective-permute-done | bytes 98336 | tf_op jit(solution)/shard_map/ppermute | solution.py:796
  97.1 1.4 %collective-permute-start.42 = (bf16[64,768]{1,0:T(8,128)(2,1)S(1)}, bf16[64,768]{1,0:T(8,128)(2,1)S(1)}, u32[]{:S(2)}, u32[]{:S(2)}) collective-permute-start(bf16[64,768]{1,0:T(8,128)(2,1)S(1)} %add_pair.5.own), channel_id=1, source_target_pairs={{0,6},{1,7},{2,4},{3,5},{4,2},{5,3},{6,0},{7,1},{8,14},{9,15},{10,... | collective-permute-start | bytes 294920 | tf_op jit(solution)/shard_map/ppermute | solution.py:796
  100.7 1.3 %share_rows.1 = (bf16[256,384]{1,0:T(8,128)(2,1)S(1)}, bf16[256,384]{1,0:T(8,128)(2,1)S(1)}, bf16[256,768]{1,0:T(8,128)(2,1)S(1)}) custom-call(s32[1]{0:T(128)} %bitcast.2.me.me_ref, f32[4,256]{1,0:T(4,128)S(1)} %get-tuple-element.106.orders, bf16[256,384]{1,0:T(8,128)(2,1)S(1)} %get-tuple-element.174.rows.refs_0_, ...), custom_call_target="tpu_custom_call" | custom-call | flops 1 | bytes 1 | tf_op jit(solution)/shard_map/share_rows/pallas_call | solution.py:773
  102.0 2.2 %first_results.1 = (f32[768,384]{1,0:T(8,128)}, f32[384,1536]{1,0:T(8,128)}) custom-call(s32[1]{0:T(128)} %bitcast.2.me.me_ref, bf16[384,768]{1,0:T(8,128)(2,1)S(1)} %order_parts.2.own, bf16[384,768]{1,0:T(8,128)(2,1)S(1)} %collective-permute-done.39.other), custom_call_target="tpu_custom_call" | custom-call | flops 1 | bytes 1 | tf_op jit(solution)/shard_map/first_results/pallas_call | solution.py:773
  107.2 1.8 %last_results.1 = (f32[384]{0:T(512)}, f32[384,1536]{1,0:T(8,128)}, f32[4,768]{1,0:T(4,128)}, f32[768]{0:T(1024)}, f32[56,768]{1,0:T(8,128)}, /*index=5*/f32[24,...) custom-call(s32[1]{0:T(128)} %bitcast.2.me.me_ref, ...), custom_call_target="tpu_custom_call", output_to_operand_aliasing={{1}: (3, {})} | custom-call | flops 1 | bytes 1 | tf_op jit(solution)/shard_map/last_results/pallas_call | solution.py:773
  (88 shorter events, 24.5 us)
Async XLA Ops:
  1.7 10.0 %collective-permute-start.2 = (bf16[272,384]{1,0:T(8,128)(2,1)S(1)}, bf16[272,384]{1,0:T(8,128)(2,1)S(1)}, u32[]{:S(2)}, u32[]{:S(2)}) collective-permute-start(bf16[272,384]{1,0:T(8,128)(2,1)S(1)} %tokens_and_order.1.refs_0_), channel_id=1, source_target_pairs={{0,6},{1,7},{2,4},{3,5},{4,2},{5,3},{6,0},{7,1},{8,14},{9,15},{10,... | collective-permute-start | bytes 626696 | tf_op jit(solution)/shard_map/ppermute | solution.py:796
  5.6 9.6 %collective-permute-start.1 = (bf16[272,384]{1,0:T(8,128)(2,1)S(1)}, bf16[272,384]{1,0:T(8,128)(2,1)S(1)}, u32[]{:S(2)}, u32[]{:S(2)}) collective-permute-start(bf16[272,384]{1,0:T(8,128)(2,1)S(1)} %tokens_and_order.1.refs_0_), channel_id=1, source_target_pairs={{0,4},{1,5},{2,6},{3,7},{4,0},{5,1},{6,2},{7,3},{8,12},{9,13},{10,... | collective-permute-start | bytes 626696 | tf_op jit(solution)/shard_map/ppermute | solution.py:796
  6.1 9.4 %collective-permute-start = (bf16[272,384]{1,0:T(8,128)(2,1)S(1)}, bf16[272,384]{1,0:T(8,128)(2,1)S(1)}, u32[]{:S(2)}, u32[]{:S(2)}) collective-permute-start(bf16[272,384]{1,0:T(8,128)(2,1)S(1)} %tokens_and_order.1.refs_0_), channel_id=1, source_target_pairs={{0,2},{1,3},{2,0},{3,1},{4,6},{5,7},{6,4},{7,5},{8,10},{9,11},{10,... | collective-permute-start | bytes 626696 | tf_op jit(solution)/shard_map/ppermute | solution.py:796
  6.3 11.3 %collective-permute-start.3 = (bf16[272,384]{1,0:T(8,128)(2,1)S(1)}, bf16[272,384]{1,0:T(8,128)(2,1)S(1)}, u32[]{:S(2)}, u32[]{:S(2)}) collective-permute-start(bf16[272,384]{1,0:T(8,128)(2,1)S(1)} %tokens_and_order.1.refs_0_), channel_id=1, source_target_pairs={{0,1},{1,0},{2,3},{3,2},{4,5},{5,4},{6,7},{7,6},{8,9},{9,8},{10,11... | collective-permute-start | bytes 626696 | tf_op jit(solution)/shard_map/ppermute | solution.py:796
  11.7 7.3 %collective-permute-start.6 = (bf16[272,384]{1,0:T(8,128)(2,1)S(1)}, bf16[272,384]{1,0:T(8,128)(2,1)S(1)}, u32[]{:S(2)}, u32[]{:S(2)}) collective-permute-start(bf16[272,384]{1,0:T(8,128)(2,1)S(1)} %collective-permute-done.2.refs_3_), channel_id=1, source_target_pairs={{0,1},{1,0},{2,3},{3,2},{4,5},{5,4},{6,7},{7,6},{8,9},{9,8},{10,11... | collective-permute-start | bytes 626696 | tf_op jit(solution)/shard_map/ppermute | solution.py:796
  15.8 11.0 %collective-permute-start.9 = (bf16[256,384]{1,0:T(8,128)(2,1)}, bf16[256,384]{1,0:T(8,128)(2,1)S(1)}, u32[]{:S(2)}, u32[]{:S(2)}) collective-permute-start(bf16[256,384]{1,0:T(8,128)(2,1)} %bitcast.11), channel_id=1, source_target_pairs={{0,6},{1,7},{2,4},{3,5},{4,2},{5,3},{6,0},{7,1},{8,14},{9,15},{10,... | collective-permute-start | bytes 589832 | tf_op jit(solution)/shard_map/ppermute | solution.py:796
  17.6 10.6 %collective-permute-start.8 = (bf16[256,384]{1,0:T(8,128)(2,1)}, bf16[256,384]{1,0:T(8,128)(2,1)S(1)}, u32[]{:S(2)}, u32[]{:S(2)}) collective-permute-start(bf16[256,384]{1,0:T(8,128)(2,1)} %bitcast.12), channel_id=1, source_target_pairs={{0,4},{1,5},{2,6},{3,7},{4,0},{5,1},{6,2},{7,3},{8,12},{9,13},{10,... | collective-permute-start | bytes 589832 | tf_op jit(solution)/shard_map/ppermute | solution.py:796
  18.9 9.3 %collective-permute-start.7 = (bf16[256,384]{1,0:T(8,128)(2,1)}, bf16[256,384]{1,0:T(8,128)(2,1)S(1)}, u32[]{:S(2)}, u32[]{:S(2)}) collective-permute-start(bf16[256,384]{1,0:T(8,128)(2,1)} %bitcast.13), channel_id=1, source_target_pairs={{0,2},{1,3},{2,0},{3,1},{4,6},{5,7},{6,4},{7,5},{8,10},{9,11},{10,... | collective-permute-start | bytes 589832 | tf_op jit(solution)/shard_map/ppermute | solution.py:796
  35.1 7.4 %collective-permute-start.18 = (bf16[256,384]{1,0:T(8,128)(2,1)S(1)}, bf16[256,384]{1,0:T(8,128)(2,1)S(1)}, u32[]{:S(2)}, u32[]{:S(2)}) collective-permute-start(bf16[256,384]{1,0:T(8,128)(2,1)S(1)} %get-tuple-element.123), channel_id=1, source_target_pairs={{0,1},{1,0},{2,3},{3,2},{4,5},{5,4},{6,7},{7,6},{8,9},{9,8},{10,11... | collective-permute-start | bytes 589832 | tf_op jit(solution)/shard_map/ppermute | solution.py:796
  36.8 4.8 %collective-permute-start.12 = (f32[16,896]{1,0:T(8,128)S(1)}, f32[16,896]{1,0:T(8,128)S(1)}, u32[]{:S(2)}, u32[]{:S(2)}) collective-permute-start(f32[16,896]{1,0:T(8,128)S(1)} %get-tuple-element.118), channel_id=1, source_target_pairs={{0,4},{1,5},{2,6},{3,7},{4,0},{5,1},{6,2},{7,3},{8,12},{9,13},{10,... | collective-permute-start | bytes 172040 | tf_op jit(solution)/shard_map/ppermute | solution.py:796
  37.4 5.1 %collective-permute-start.13 = (f32[16,896]{1,0:T(8,128)S(1)}, f32[16,896]{1,0:T(8,128)S(1)}, u32[]{:S(2)}, u32[]{:S(2)}) collective-permute-start(f32[16,896]{1,0:T(8,128)S(1)} %get-tuple-element.119), channel_id=1, source_target_pairs={{0,6},{1,7},{2,4},{3,5},{4,2},{5,3},{6,0},{7,1},{8,14},{9,15},{10,... | collective-permute-start | bytes 172040 | tf_op jit(solution)/shard_map/ppermute | solution.py:796
  50.0 16.5 %collective-permute-start.21 = (bf16[224,768]{1,0:T(8,128)(2,1)S(1)}, bf16[224,768]{1,0:T(8,128)(2,1)S(1)}, u32[]{:S(2)}, u32[]{:S(2)}) collective-permute-start(bf16[224,768]{1,0:T(8,128)(2,1)S(1)} %get-tuple-element.162), channel_id=1, source_target_pairs={{0,2},{1,3},{2,0},{3,1},{4,6},{5,7},{6,4},{7,5},{8,10},{9,11},{10,... | collective-permute-start | bytes 1032200 | tf_op jit(solution)/shard_map/ppermute | solution.py:796
  51.5 17.2 %collective-permute-start.22 = (bf16[224,768]{1,0:T(8,128)(2,1)S(1)}, bf16[224,768]{1,0:T(8,128)(2,1)S(1)}, u32[]{:S(2)}, u32[]{:S(2)}) collective-permute-start(bf16[224,768]{1,0:T(8,128)(2,1)S(1)} %get-tuple-element.163), channel_id=1, source_target_pairs={{0,4},{1,5},{2,6},{3,7},{4,0},{5,1},{6,2},{7,3},{8,12},{9,13},{10,... | collective-permute-start | bytes 1032200 | tf_op jit(solution)/shard_map/ppermute | solution.py:796
  52.1 16.6 %collective-permute-start.23 = (bf16[224,768]{1,0:T(8,128)(2,1)S(1)}, bf16[224,768]{1,0:T(8,128)(2,1)S(1)}, u32[]{:S(2)}, u32[]{:S(2)}) collective-permute-start(bf16[224,768]{1,0:T(8,128)(2,1)S(1)} %get-tuple-element.164), channel_id=1, source_target_pairs={{0,6},{1,7},{2,4},{3,5},{4,2},{5,3},{6,0},{7,1},{8,14},{9,15},{10,... | collective-permute-start | bytes 1032200 | tf_op jit(solution)/shard_map/ppermute | solution.py:796
  63.3 5.5 %collective-permute-start.19 = (f32[8,768]{1,0:T(8,128)S(1)}, f32[8,768]{1,0:T(8,128)S(1)}, u32[]{:S(2)}, u32[]{:S(2)}) collective-permute-start(f32[8,768]{1,0:T(8,128)S(1)} %get-tuple-element.156), channel_id=1, source_target_pairs={{1,0},{2,1},{3,2},{4,3},{5,4},{6,5},{7,6},{9,8},{10,9},{11,10},{12... | collective-permute-start | bytes 73736 | tf_op jit(solution)/shard_map/ppermute | solution.py:814
  69.8 6.5 %collective-permute-start.25 = (bf16[96,768]{1,0:T(8,128)(2,1)S(1)}, bf16[96,768]{1,0:T(8,128)(2,1)S(1)}, u32[]{:S(2)}, u32[]{:S(2)}) collective-permute-start(bf16[96,768]{1,0:T(8,128)(2,1)S(1)} %add_parts.2.a), channel_id=1, source_target_pairs={{0,8},{8,0},{16,24},{24,16},{1,9},{9,1},{17,25},{25,17},{2,10},{10... | collective-permute-start | bytes 442376 | tf_op jit(solution)/shard_map/ppermute | solution.py:796
  71.6 5.6 %collective-permute-start.26 = (bf16[64,768]{1,0:T(8,128)(2,1)S(1)}, bf16[64,768]{1,0:T(8,128)(2,1)S(1)}, u32[]{:S(2)}, u32[]{:S(2)}) collective-permute-start(bf16[64,768]{1,0:T(8,128)(2,1)S(1)} %get-tuple-element.171), channel_id=1, source_target_pairs={{0,2},{1,3},{2,0},{3,1},{4,6},{5,7},{6,4},{7,5},{8,10},{9,11},{10,... | collective-permute-start | bytes 294920 | tf_op jit(solution)/shard_map/ppermute | solution.py:796
  72.8 6.0 %collective-permute-start.27 = (bf16[64,768]{1,0:T(8,128)(2,1)S(1)}, bf16[64,768]{1,0:T(8,128)(2,1)S(1)}, u32[]{:S(2)}, u32[]{:S(2)}) collective-permute-start(bf16[64,768]{1,0:T(8,128)(2,1)S(1)} %get-tuple-element.172), channel_id=1, source_target_pairs={{0,4},{1,5},{2,6},{3,7},{4,0},{5,1},{6,2},{7,3},{8,12},{9,13},{10,... | collective-permute-start | bytes 294920 | tf_op jit(solution)/shard_map/ppermute | solution.py:796
  73.7 7.7 %collective-permute-start.28 = (bf16[64,768]{1,0:T(8,128)(2,1)S(1)}, bf16[64,768]{1,0:T(8,128)(2,1)S(1)}, u32[]{:S(2)}, u32[]{:S(2)}) collective-permute-start(bf16[64,768]{1,0:T(8,128)(2,1)S(1)} %get-tuple-element.173), channel_id=1, source_target_pairs={{0,6},{1,7},{2,4},{3,5},{4,2},{5,3},{6,0},{7,1},{8,14},{9,15},{10,... | collective-permute-start | bytes 294920 | tf_op jit(solution)/shard_map/ppermute | solution.py:796
  75.1 12.0 %collective-permute-start.30 = (bf16[256,384]{1,0:T(8,128)(2,1)S(1)}, bf16[256,384]{1,0:T(8,128)(2,1)S(1)}, u32[]{:S(2)}, u32[]{:S(2)}) collective-permute-start(bf16[256,384]{1,0:T(8,128)(2,1)S(1)} %get-tuple-element.176.refs_4_), channel_id=1, source_target_pairs={{0,2},{1,3},{2,0},{3,1},{4,6},{5,7},{6,4},{7,5},{8,10},{9,11},{10,... | collective-permute-start | bytes 589832 | tf_op jit(solution)/shard_map/ppermute | solution.py:796
  76.2 11.7 %collective-permute-start.31 = (bf16[256,384]{1,0:T(8,128)(2,1)S(1)}, bf16[256,384]{1,0:T(8,128)(2,1)S(1)}, u32[]{:S(2)}, u32[]{:S(2)}) collective-permute-start(bf16[256,384]{1,0:T(8,128)(2,1)S(1)} %get-tuple-element.176.refs_4_), channel_id=1, source_target_pairs={{0,4},{1,5},{2,6},{3,7},{4,0},{5,1},{6,2},{7,3},{8,12},{9,13},{10,... | collective-permute-start | bytes 589832 | tf_op jit(solution)/shard_map/ppermute | solution.py:796
  77.2 10.7 %collective-permute-start.32 = (bf16[256,384]{1,0:T(8,128)(2,1)S(1)}, bf16[256,384]{1,0:T(8,128)(2,1)S(1)}, u32[]{:S(2)}, u32[]{:S(2)}) collective-permute-start(bf16[256,384]{1,0:T(8,128)(2,1)S(1)} %get-tuple-element.176.refs_4_), channel_id=1, source_target_pairs={{0,6},{1,7},{2,4},{3,5},{4,2},{5,3},{6,0},{7,1},{8,14},{9,15},{10,... | collective-permute-start | bytes 589832 | tf_op jit(solution)/shard_map/ppermute | solution.py:796
  78.8 8.4 %collective-permute-start.35 = (bf16[96,768]{1,0:T(8,128)(2,1)S(1)}, bf16[96,768]{1,0:T(8,128)(2,1)S(1)}, u32[]{:S(2)}, u32[]{:S(2)}) collective-permute-start(bf16[96,768]{1,0:T(8,128)(2,1)S(1)} %add_pair.6.a), channel_id=1, source_target_pairs={{0,16},{8,24},{16,0},{24,8},{1,17},{9,25},{17,1},{25,9},{2,18},{10... | collective-permute-start | bytes 442376 | tf_op jit(solution)/shard_map/ppermute | solution.py:796
  81.5 4.7 %collective-permute-start.29 = (bf16[64,768]{1,0:T(8,128)(2,1)S(1)}, bf16[64,768]{1,0:T(8,128)(2,1)S(1)}, u32[]{:S(2)}, u32[]{:S(2)}) collective-permute-start(bf16[64,768]{1,0:T(8,128)(2,1)S(1)} %add_parts.3.a), channel_id=1, source_target_pairs={{0,8},{8,0},{16,24},{24,16},{1,9},{9,1},{17,25},{25,17},{2,10},{10... | collective-permute-start | bytes 294920 | tf_op jit(solution)/shard_map/ppermute | solution.py:796
  87.9 9.1 %collective-permute-start.38 = (bf16[96,768]{1,0:T(8,128)(2,1)S(1)}, bf16[96,768]{1,0:T(8,128)(2,1)S(1)}, u32[]{:S(2)}, u32[]{:S(2)}) collective-permute-start(bf16[96,768]{1,0:T(8,128)(2,1)S(1)} %add_pair.7.own), channel_id=1, source_target_pairs={{0,6},{1,7},{2,4},{3,5},{4,2},{5,3},{6,0},{7,1},{8,14},{9,15},{10,... | collective-permute-start | bytes 442376 | tf_op jit(solution)/shard_map/ppermute | solution.py:796
  89.2 7.7 %collective-permute-start.37 = (bf16[96,768]{1,0:T(8,128)(2,1)S(1)}, bf16[96,768]{1,0:T(8,128)(2,1)S(1)}, u32[]{:S(2)}, u32[]{:S(2)}) collective-permute-start(bf16[96,768]{1,0:T(8,128)(2,1)S(1)} %add_pair.7.own), channel_id=1, source_target_pairs={{0,4},{1,5},{2,6},{3,7},{4,0},{5,1},{6,2},{7,3},{8,12},{9,13},{10,... | collective-permute-start | bytes 442376 | tf_op jit(solution)/shard_map/ppermute | solution.py:796
  90.3 6.7 %collective-permute-start.36 = (bf16[96,768]{1,0:T(8,128)(2,1)S(1)}, bf16[96,768]{1,0:T(8,128)(2,1)S(1)}, u32[]{:S(2)}, u32[]{:S(2)}) collective-permute-start(bf16[96,768]{1,0:T(8,128)(2,1)S(1)} %add_pair.7.own), channel_id=1, source_target_pairs={{0,2},{1,3},{2,0},{3,1},{4,6},{5,7},{6,4},{7,5},{8,10},{9,11},{10,... | collective-permute-start | bytes 442376 | tf_op jit(solution)/shard_map/ppermute | solution.py:796
  91.4 5.5 %collective-permute-start.34 = (bf16[64,768]{1,0:T(8,128)(2,1)S(1)}, bf16[64,768]{1,0:T(8,128)(2,1)S(1)}, u32[]{:S(2)}, u32[]{:S(2)}) collective-permute-start(bf16[64,768]{1,0:T(8,128)(2,1)S(1)} %add_pair.4.a), channel_id=1, source_target_pairs={{0,16},{8,24},{16,0},{24,8},{1,17},{9,25},{17,1},{25,9},{2,18},{10... | collective-permute-start | bytes 294920 | tf_op jit(solution)/shard_map/ppermute | solution.py:796
  97.1 5.0 %collective-permute-start.39 = (bf16[384,768]{1,0:T(8,128)(2,1)S(1)}, bf16[384,768]{1,0:T(8,128)(2,1)S(1)}, u32[]{:S(2)}, u32[]{:S(2)}) collective-permute-start(bf16[384,768]{1,0:T(8,128)(2,1)S(1)} %order_parts.2.own), channel_id=1, source_target_pairs={{0,1},{1,0},{2,3},{3,2},{4,5},{5,4},{6,7},{7,6},{8,9},{9,8},{10,11... | collective-permute-start | bytes 1769480 | tf_op jit(solution)/shard_map/ppermute | solution.py:796
  97.1 7.1 %collective-permute-start.42 = (bf16[64,768]{1,0:T(8,128)(2,1)S(1)}, bf16[64,768]{1,0:T(8,128)(2,1)S(1)}, u32[]{:S(2)}, u32[]{:S(2)}) collective-permute-start(bf16[64,768]{1,0:T(8,128)(2,1)S(1)} %add_pair.5.own), channel_id=1, source_target_pairs={{0,6},{1,7},{2,4},{3,5},{4,2},{5,3},{6,0},{7,1},{8,14},{9,15},{10,... | collective-permute-start | bytes 294920 | tf_op jit(solution)/shard_map/ppermute | solution.py:796
  98.5 6.8 %collective-permute-start.41 = (bf16[64,768]{1,0:T(8,128)(2,1)S(1)}, bf16[64,768]{1,0:T(8,128)(2,1)S(1)}, u32[]{:S(2)}, u32[]{:S(2)}) collective-permute-start(bf16[64,768]{1,0:T(8,128)(2,1)S(1)} %add_pair.5.own), channel_id=1, source_target_pairs={{0,4},{1,5},{2,6},{3,7},{4,0},{5,1},{6,2},{7,3},{8,12},{9,13},{10,... | collective-permute-start | bytes 294920 | tf_op jit(solution)/shard_map/ppermute | solution.py:796
  99.6 5.8 %collective-permute-start.40 = (bf16[64,768]{1,0:T(8,128)(2,1)S(1)}, bf16[64,768]{1,0:T(8,128)(2,1)S(1)}, u32[]{:S(2)}, u32[]{:S(2)}) collective-permute-start(bf16[64,768]{1,0:T(8,128)(2,1)S(1)} %add_pair.5.own), channel_id=1, source_target_pairs={{0,2},{1,3},{2,0},{3,1},{4,6},{5,7},{6,4},{7,5},{8,10},{9,11},{10,... | collective-permute-start | bytes 294920 | tf_op jit(solution)/shard_map/ppermute | solution.py:796
  (16 other events, 75.9 us)
